TPU v7x, 32 devices: a whole 2x2x4 slice. The times are simulated.
32 devices in a mesh: dp: 2 (over y), seq: 16 (over z, x, core).
Axes of the slice: x: 2, y: 2, z: 4, core: 2. Of those that a mesh axis runs over, the one named last changes fastest.
Arguments:
- tokens: bfloat16 [1024, 16, 768], P('seq', 'dp'), may hold values from -6 to 6
- norm_gain1: bfloat16 [768], P(('dp', 'seq')), may hold values from 0.25 to 1.75
- value_weight: bfloat16 [768, 768], P(('dp', 'seq')), may hold values from -0.21875 to 0.21875
- mixer_logits: bfloat16 [12, 1024, 1024], P(None, 'seq'), may hold values from -8 to 8
- out_weight: bfloat16 [768, 768], P(('dp', 'seq')), may hold values from -0.625 to 0.625
- norm_gain2: bfloat16 [768], P(('dp', 'seq')), may hold values from 0.25 to 1.75
- up_weight: bfloat16 [768, 3072], P(('dp', 'seq')), may hold values from -0.21875 to 0.21875
- down_weight: bfloat16 [3072, 768], P(('dp', 'seq')), may hold values from -0.109375 to 0.109375
- out_grad: bfloat16 [1024, 16, 768], P('seq', 'dp'), may hold values from -6 to 6
Outputs:
- layer_out: bfloat16 [1024, 16, 768], P('seq', 'dp')
- tokens_grad: float32 [1024, 16, 768], P('seq', 'dp')
- gain1_grad: float32 [768], P(('dp', 'seq'))
- value_weight_grad: float32 [768, 768], P(('dp', 'seq'))
- logits_grad: float32 [12, 1024, 1024], P(None, 'seq', 'dp')
- out_weight_grad: float32 [768, 768], P(('dp', 'seq'))
- gain2_grad: float32 [768], P(('dp', 'seq'))
- up_weight_grad: float32 [768, 3072], P(('dp', 'seq'))
- down_weight_grad: float32 [3072, 768], P(('dp', 'seq'))
All inputs are finite; a program needn't handle non-finite values.
Results may differ from a plain program's by a relative error of at most 0.015.
Values may be sent and summed in bfloat16 or wider, within the bound.
No kernel may reach another device: no remote copies, remote signals or barrier semaphores. Data moves between devices by JAX's collectives and lax.ppermute only.
A program may use at most 256 MiB of HBM per device.

v0:
```python
import jax
import jax.numpy as jnp
from jax import lax
from jax.sharding import PartitionSpec as P


def rms_scale(inputs, gain):
    return inputs * lax.rsqrt(jnp.mean(inputs * inputs, axis=-1, keepdims=True) + 1e-06) * gain


def outer_sum(left, right):
    return lax.dot_general(
        left.reshape(-1, left.shape[-1]),
        right.reshape(-1, right.shape[-1]),
        (((0,), (0,)), ((), ())),
        preferred_element_type=jnp.float32,
    )


def back_dot(grad, weight):
    return lax.dot_general(
        grad, weight, (((grad.ndim - 1,), (1,)), ((), ())), preferred_element_type=jnp.float32
    )


def on_device(
    tokens,
    norm_gain1,
    value_weight,
    mixer_logits,
    out_weight,
    norm_gain2,
    up_weight,
    down_weight,
    out_grad,
):
    positions, sequences, model_width = tokens.shape
    head_count = mixer_logits.shape[0]
    length = mixer_logits.shape[2]
    head_size = model_width // head_count
    inputs = tokens.astype(jnp.float32)
    gain_one, w_value, w_out = (
        lax.all_gather(norm_gain1, ("dp", "seq"), axis=0, tiled=True),
        lax.all_gather(value_weight, ("dp", "seq"), axis=0, tiled=True),
        lax.all_gather(out_weight, ("dp", "seq"), axis=0, tiled=True),
    )
    gain_one = gain_one.astype(jnp.float32)
    low_one = rms_scale(inputs, gain_one).astype(jnp.bfloat16)
    values = jnp.dot(low_one, w_value, preferred_element_type=jnp.float32).astype(jnp.bfloat16)
    row_index = lax.axis_index("seq") * positions + lax.broadcasted_iota(
        jnp.int32, (positions, length), 0
    )
    col_index = lax.broadcasted_iota(jnp.int32, (positions, length), 1)
    allowed = col_index <= row_index
    masked = jnp.where(allowed[None], mixer_logits.astype(jnp.float32), -jnp.inf)
    row_max = jnp.max(masked, axis=-1, keepdims=True)
    expo_rows = jnp.exp(masked - row_max)
    row_total = jnp.sum(expo_rows, axis=-1, keepdims=True)
    mix_soft = expo_rows / row_total
    mix_low = mix_soft.astype(jnp.bfloat16)
    gathered = lax.all_gather(values, "seq", axis=0, tiled=True)
    gathered_heads = gathered.reshape(length, sequences, head_count, head_size)
    mixed = jnp.einsum(
        "hij,jbhc->ibhc", mix_low, gathered_heads, preferred_element_type=jnp.float32
    )
    mixed_low = mixed.reshape(positions, sequences, model_width).astype(jnp.bfloat16)
    residual = inputs + jnp.dot(mixed_low, w_out, preferred_element_type=jnp.float32)
    gain_two, w_up, w_down = (
        lax.all_gather(norm_gain2, ("dp", "seq"), axis=0, tiled=True),
        lax.all_gather(up_weight, ("dp", "seq"), axis=0, tiled=True),
        lax.all_gather(down_weight, ("dp", "seq"), axis=0, tiled=True),
    )
    gain_two = gain_two.astype(jnp.float32)
    low_two = rms_scale(residual, gain_two).astype(jnp.bfloat16)
    pre_act = jnp.dot(low_two, w_up, preferred_element_type=jnp.float32)
    hidden = jax.nn.gelu(pre_act).astype(jnp.bfloat16)
    layer_out = (residual + jnp.dot(hidden, w_down, preferred_element_type=jnp.float32)).astype(
        jnp.bfloat16
    )
    down_grad = outer_sum(hidden, out_grad)
    hidden_grad = back_dot(out_grad, w_down)
    unused_act, gelu_back = jax.vjp(jax.nn.gelu, pre_act)
    pre_grad = gelu_back(hidden_grad)[0].astype(jnp.bfloat16)
    up_grad = outer_sum(low_two, pre_grad)
    normed_two_grad = back_dot(pre_grad, w_up)
    unused_two, norm_back_two = jax.vjp(rms_scale, residual, gain_two)
    residual_part, gain_two_grad = norm_back_two(normed_two_grad)
    gain_two_grad = jnp.sum(gain_two_grad.reshape(-1, model_width), axis=0)
    residual_grad = out_grad.astype(jnp.float32) + residual_part
    attn_grad = residual_grad.astype(jnp.bfloat16)
    out_wgrad = outer_sum(mixed_low, attn_grad)
    mixed_grad = back_dot(attn_grad, w_out).astype(jnp.bfloat16)
    mixed_grad_heads = mixed_grad.reshape(positions, sequences, head_count, head_size)
    soft_grad = jnp.einsum(
        "ibhc,jbhc->hij", mixed_grad_heads, gathered_heads, preferred_element_type=jnp.float32
    )
    local_logit_grad = mix_soft * (
        soft_grad - jnp.sum(mix_soft * soft_grad, axis=-1, keepdims=True)
    )
    logits_grad = lax.psum_scatter(
        local_logit_grad.astype(jnp.bfloat16), "dp", scatter_dimension=2, tiled=True
    ).astype(jnp.float32)
    term = jnp.einsum(
        "hij,ibhc->jbhc", mix_low, mixed_grad_heads, preferred_element_type=jnp.float32
    )
    value_sum = lax.psum_scatter(
        term.reshape(positions * lax.axis_size("seq"), sequences, model_width).astype(jnp.bfloat16),
        "seq",
        scatter_dimension=0,
        tiled=True,
    )
    value_wgrad = outer_sum(low_one, value_sum)
    normed_one_grad = back_dot(value_sum, w_value)
    unused_one, norm_back_one = jax.vjp(rms_scale, inputs, gain_one)
    input_part, gain_one_grad = norm_back_one(normed_one_grad)
    gain_one_grad = jnp.sum(gain_one_grad.reshape(-1, model_width), axis=0)
    tokens_grad = residual_grad + input_part
    summed = (
        lax.psum_scatter(gain_one_grad, ("dp", "seq"), scatter_dimension=0, tiled=True),
        lax.psum_scatter(value_wgrad, ("dp", "seq"), scatter_dimension=0, tiled=True),
        lax.psum_scatter(out_wgrad, ("dp", "seq"), scatter_dimension=0, tiled=True),
        lax.psum_scatter(gain_two_grad, ("dp", "seq"), scatter_dimension=0, tiled=True),
        lax.psum_scatter(up_grad, ("dp", "seq"), scatter_dimension=0, tiled=True),
        lax.psum_scatter(down_grad, ("dp", "seq"), scatter_dimension=0, tiled=True),
    )
    return (
        layer_out,
        tokens_grad,
        summed[0],
        summed[1],
        logits_grad,
        summed[2],
        summed[3],
        summed[4],
        summed[5],
    )


def solution(mesh):
    placed = (
        P("seq", "dp", None),
        P(("dp", "seq")),
        P(("dp", "seq"), None),
        P(None, "seq", None),
        P(("dp", "seq"), None),
        P(("dp", "seq")),
        P(("dp", "seq"), None),
        P(("dp", "seq"), None),
        P("seq", "dp", None),
    )
    return jax.shard_map(
        on_device,
        mesh=mesh,
        in_specs=placed,
        out_specs=(
            P("seq", "dp", None),
            P("seq", "dp", None),
            P(("dp", "seq")),
            P(("dp", "seq"), None),
            P(None, "seq", "dp"),
            P(("dp", "seq"), None),
            P(("dp", "seq")),
            P(("dp", "seq"), None),
            P(("dp", "seq"), None),
        ),
        check_vma=False,
    )
```

profile of v0, /device:TPU:0, one launch (start us, length us, event | category | flops | bytes accessed | tf_op | source)
XLA Modules:
  0.0 1072.0 jit_solution(10616083030389804871)
XLA Ops:
  7.2 0.7 all-gather.6.cloned.1.call-update
  8.0 0.8 dynamic-update-slice
  8.8 0.8 dynamic-update-slice.1
  9.7 42.1 %all-reduce.5 = (bf16[768]{0:T(1024)(128)(2,1)S(1)}, bf16[768]{0:T(1024)(128)(2,1)S(1)}) all-reduce(bf16[768]{0:T(1024)(128)(2,1)S(1)} %dynamic-update-slice, bf16[768]{0:T(1024)(128)(2,1)S(1)} %dynamic-update-slice.1), channel_id=1, replica_groups=mesh['dp'=2,'seq'=16] {'dp','seq'}, use_global_device_ids=true, to_apply=%add | all-reduce | flops 1536 | bytes 6144
  51.8 1.4 fusion.35
  53.3 14.3 %all-gather.6.cloned.1.call-done = bf16[768,768]{1,0:T(8,128)(2,1)} async-done(((bf16[24,768]{1,0:T(8,128)(2,1)}), bf16[768,768]{1,0:T(8,128)(2,1)}) %all-gather.6.cloned.1.call-update) | async-done | bytes 1179664 | tf_op jit(solution)/shard_map/all_gather | solution.py:44
  67.6 3.2 convolution_convert_fusion.1
  70.9 0.7 all-gather.10.cloned.1.call-update
  73.1 2.9 fusion.65
  76.1 94.6 %all-gather.8.cloned.1.call-done = bf16[1024,8,768]{2,1,0:T(8,128)(2,1)} async-done(((bf16[64,8,768]{2,1,0:T(8,128)(2,1)}), bf16[1024,8,768]{2,1,0:T(8,128)(2,1)}) %all-gather.8.cloned.1.call-update) | async-done | bytes 12582928 | tf_op jit(solution)/shard_map/all_gather | solution.py:61
  170.7 16.5 %copy.68 = bf16[1024,8,768]{0,2,1:T(8,128)(2,1)} copy(bf16[1024,8,768]{2,1,0:T(8,128)(2,1)} %all-gather.8.cloned.1.call-done) | data formatting | bytes 25165824 | tf_op jit(solution)/shard_map/all_gather | solution.py:61
  187.2 8.2 fusion.41
  195.5 3.7 copy.70
  199.2 2.0 convert_element_type.74
  201.2 24.6 %all-gather.10.cloned.1.call-done = bf16[768,768]{1,0:T(8,128)(2,1)} async-done(((bf16[24,768]{1,0:T(8,128)(2,1)}), bf16[768,768]{1,0:T(8,128)(2,1)}) %all-gather.10.cloned.1.call-update) | async-done | bytes 1179664 | tf_op jit(solution)/shard_map/all_gather | solution.py:45
  225.8 2.4 multiply_reduce_fusion.2
  228.4 62.7 %all-gather.12.cloned.1.call-done = bf16[768,3072]{1,0:T(8,128)(2,1)} async-done(((bf16[24,3072]{1,0:T(8,128)(2,1)}), bf16[768,3072]{1,0:T(8,128)(2,1)}) %all-gather.12.cloned.1.call-update) | async-done | bytes 4718608 | tf_op jit(solution)/shard_map/all_gather | solution.py:70
  291.1 7.0 fusion.19
  298.1 58.2 %all-gather.14.cloned.1.call-done = bf16[3072,768]{1,0:T(8,128)(2,1)} async-done(((bf16[96,768]{1,0:T(8,128)(2,1)}), bf16[3072,768]{1,0:T(8,128)(2,1)}) %all-gather.14.cloned.1.call-update) | async-done | bytes 4718608 | tf_op jit(solution)/shard_map/all_gather | solution.py:71
  356.3 9.0 fusion.12
  365.3 3.4 multiply_reduce_fusion
  368.9 1.6 fusion.33
  370.6 1.1 copy-done
  371.7 0.8 convolution_convert_fusion
  372.6 1.3 reshape.101
  373.8 9.5 convert_bitcast_fusion
  383.4 10.7 %copy.76 = bf16[1024,8,12,64]{0,3,2,1:T(8,128)(2,1)} copy(bf16[1024,8,12,64]{0,3,1,2:T(8,128)(2,1)} %convert_bitcast_fusion) | data formatting | bytes 25165824 | tf_op jit(solution)/shard_map/convert_element_type | solution.py:107
  394.1 17.0 %copy.77 = bf16[1024,8,768]{2,1,0:T(8,128)(2,1)} copy(bf16[1024,8,768]{0,2,1:T(8,128)(2,1)} %bitcast.72) | data formatting | bytes 25165824 | tf_op jit(solution)/shard_map/convert_element_type | solution.py:107
  411.2 7.0 fusion.2
  418.3 5.5 fusion.22
  423.9 2.2 convolution_bitcast_fusion.2
  426.5 10.6 convolution_bitcast_fusion
  437.2 1.3 copy-done.4
  438.5 7.5 convolution_bitcast_fusion.1
  446.1 98.8 %reduce-scatter.7.cloned.1.call-done = bf16[64,8,768]{2,1,0:T(8,128)(2,1)} async-done(((bf16[1024,8,768]{2,1,0:T(8,128)(2,1)}), bf16[64,8,768]{2,1,0:T(8,128)(2,1)}) %reduce-scatter.7.cloned.1.call-update) | async-done | bytes 786448 | tf_op jit(solution)/shard_map/reduce_scatter | solution.py:106
  544.9 3.4 convolution_bitcast_fusion.3
  548.4 9.0 add_convert_fusion
  557.4 15.0 %reduce-scatter.11.cloned.1.call-done = bf16[12,64,512]{2,1,0:T(8,128)(2,1)} async-done(((bf16[12,64,1024]{2,1,0:T(8,128)(2,1)}), bf16[12,64,512]{2,1,0:T(8,128)(2,1)}) %reduce-scatter.11.cloned.1.call-update) | async-done | bytes 786448 | tf_op jit(solution)/shard_map/reduce_scatter | solution.py:100
  572.4 2.5 convert_element_type.87
  574.9 3.6 fusion.32
  578.5 39.4 %all-reduce.4 = (f32[768]{0:T(1024)S(1)}, f32[768]{0:T(1024)S(1)}) all-reduce(f32[768]{0:T(1024)S(1)} %get-tuple-element.11, f32[768]{0:T(1024)S(1)} %copy-done.22), channel_id=3, replica_groups=mesh['dp'=2,'seq'=16] {'dp','seq'}, use_global_device_ids=true, to_apply=%region_8.9.clone | all-reduce | flops 1536 | bytes 12288
  617.8 0.6 dynamic-slice
  618.4 0.6 dynamic-slice.1
  619.2 3.0 fusion.34
  622.2 56.0 %reduce-scatter.13.cloned.1.call-done = f32[24,768]{1,0:T(8,128)} async-done(((f32[768,768]{1,0:T(8,128)}), f32[24,768]{1,0:T(8,128)}) %reduce-scatter.13.cloned.1.call-update) | async-done | bytes 73744 | tf_op jit(solution)/shard_map/reduce_scatter | solution.py:121
  678.2 141.0 %reduce-scatter.17.cloned.1.call-done = f32[96,768]{1,0:T(8,128)} async-done(((f32[3072,768]{1,0:T(8,128)}), f32[96,768]{1,0:T(8,128)}) %reduce-scatter.17.cloned.1.call-update) | async-done | bytes 294928 | tf_op jit(solution)/shard_map/reduce_scatter | solution.py:124
  819.2 141.9 %reduce-scatter.15.cloned.1.call-done = f32[24,3072]{1,0:T(8,128)} async-done(((f32[768,3072]{1,0:T(8,128)}), f32[24,3072]{1,0:T(8,128)}) %reduce-scatter.15.cloned.1.call-update) | async-done | bytes 294928 | tf_op jit(solution)/shard_map/reduce_scatter | solution.py:123
  961.1 104.0 %reduce-scatter.9.cloned.1.call-done = f32[24,768]{1,0:T(8,128)} async-done(((f32[768,768]{1,0:T(8,128)}), f32[24,768]{1,0:T(8,128)}) %reduce-scatter.9.cloned.1.call-update) | async-done | bytes 73744 | tf_op jit(solution)/shard_map/reduce_scatter | solution.py:120
  (90 shorter events, 2.9 us)
Async XLA Ops:
  7.2 66.0 %copy-start.19 = (bf16[12,64,1024]{2,1,0:T(8,128)(2,1)S(1)}, bf16[12,64,1024]{2,1,0:T(8,128)(2,1)}, u32[]{:S(2)}) copy-start(bf16[12,64,1024]{2,1,0:T(8,128)(2,1)} %param.12) | copy-start | bytes 4718596
  7.2 60.4 %all-gather.6.cloned.1.call-start = ((), (), s32[]{:S(2)}) async-start(), calls=%async_computation.6 | async-start | bytes 1216512 | tf_op jit(solution)/shard_map/all_gather | solution.py:44
  7.9 162.8 %all-gather.8.cloned.1.call-start = ((), (), s32[]{:S(2)}) async-start(), calls=%async_computation.7 | async-start | bytes 13369344 | tf_op jit(solution)/shard_map/all_gather | solution.py:61
  51.8 24.3 %copy-start.20 = (f32[768]{0:T(1024)}, f32[768]{0:T(1024)S(1)}, u32[]{:S(2)}) copy-start(f32[768]{0:T(1024)S(1)} %convert_element_type.67) | copy-start | bytes 9220
  53.2 22.8 %copy-start.17 = (f32[64,8]{0,1:T(8,128)}, f32[64,8]{0,1:T(8,128)S(1)}, u32[]{:S(2)}) copy-start(f32[64,8]{0,1:T(8,128)S(1)} %copy.66) | copy-start | bytes 6148
  53.3 22.7 %copy-start.15 = (f32[64,8]{1,0:T(8,128)}, f32[64,8]{1,0:T(8,128)S(1)}, u32[]{:S(2)}) copy-start(f32[64,8]{1,0:T(8,128)S(1)} %copy.67) | copy-start | bytes 6148
  70.9 154.9 %all-gather.10.cloned.1.call-start = ((), (), s32[]{:S(2)}) async-start(), calls=%async_computation.8 | async-start | bytes 1216512 | tf_op jit(solution)/shard_map/all_gather | solution.py:45
  71.6 219.5 %all-gather.12.cloned.1.call-start = ((), (), s32[]{:S(2)}) async-start(), calls=%async_computation.9 | async-start | bytes 4866048 | tf_op jit(solution)/shard_map/all_gather | solution.py:70
  72.2 284.1 %all-gather.14.cloned.1.call-start = ((), (), s32[]{:S(2)}) async-start(), calls=%async_computation.10 | async-start | bytes 4866048 | tf_op jit(solution)/shard_map/all_gather | solution.py:71
  72.8 472.1 %reduce-scatter.7.cloned.1.call-start = ((), (), s32[]{:S(2)}) async-start(), calls=%async_computation.11 | async-start | bytes 13369344 | tf_op jit(solution)/shard_map/reduce_scatter | solution.py:106
  73.0 295.9 %copy-start.13 = (f32[768]{0:T(1024)}, f32[768]{0:T(1024)S(1)}, u32[]{:S(2)}) copy-start(f32[768]{0:T(1024)S(1)} %convert_element_type.75) | copy-start | bytes 9220
  195.5 30.3 %copy-start.6 = (bf16[64,8,768]{2,1,0:T(8,128)(2,1)S(1)}, bf16[64,8,768]{2,1,0:T(8,128)(2,1)}, u32[]{:S(2)}) copy-start(bf16[64,8,768]{2,1,0:T(8,128)(2,1)} %param.9) | copy-start | bytes 2359300
  228.2 140.7 %copy-start.3 = (f32[64,8,768]{2,1,0:T(8,128)}, f32[64,8,768]{2,1,0:T(8,128)S(1)}, u32[]{:S(2)}) copy-start(f32[64,8,768]{2,1,0:T(8,128)S(1)} %get-tuple-element.20) | copy-start | bytes 4718596
  228.4 140.5 %copy-start.8 = (f32[64,8]{1,0:T(8,128)}, f32[64,8]{1,0:T(8,128)S(1)}, u32[]{:S(2)}) copy-start(f32[64,8]{1,0:T(8,128)S(1)} %copy.72) | copy-start | bytes 6148
  291.1 65.2 %copy-start.10 = (bf16[64,8,768]{2,1,0:T(8,128)(2,1)S(1)}, bf16[64,8,768]{2,1,0:T(8,128)(2,1)}, u32[]{:S(2)}) copy-start(bf16[64,8,768]{2,1,0:T(8,128)(2,1)} %param.17) | copy-start | bytes 2359300
  356.3 9.0 copy-start.5
  365.3 3.5 copy-start.26
  368.9 2.8 copy-start.23
  370.6 1.1 copy-start
  411.2 161.2 %reduce-scatter.11.cloned.1.call-start = ((), (), s32[]{:S(2)}) async-start(), calls=%async_computation.13 | async-start | bytes 2359296 | tf_op jit(solution)/shard_map/reduce_scatter | solution.py:100
  411.2 7.0 copy-start.25
  418.2 5.7 copy-start.1
  418.2 5.6 copy-start.12
  423.8 2.6 copy-start.11
  423.8 254.3 %reduce-scatter.13.cloned.1.call-start = ((), (), s32[]{:S(2)}) async-start(), calls=%async_computation.14 | async-start | bytes 2433024 | tf_op jit(solution)/shard_map/reduce_scatter | solution.py:121
  426.2 393.0 %reduce-scatter.17.cloned.1.call-start = ((), (), s32[]{:S(2)}) async-start(), calls=%async_computation.16 | async-start | bytes 9732096 | tf_op jit(solution)/shard_map/reduce_scatter | solution.py:124
  437.1 1.4 copy-start.4
  437.1 1.4 copy-start.9
  437.1 1.4 copy-start.14
  437.1 524.0 %reduce-scatter.15.cloned.1.call-start = ((), (), s32[]{:S(2)}) async-start(), calls=%async_computation.15 | async-start | bytes 9732096 | tf_op jit(solution)/shard_map/reduce_scatter | solution.py:123
  446.0 98.9 %copy-start.7 = (bf16[64,8,768]{2,1,0:T(8,128)(2,1)S(1)}, bf16[64,8,768]{2,1,0:T(8,128)(2,1)}, u32[]{:S(2)}) copy-start(bf16[64,8,768]{2,1,0:T(8,128)(2,1)} %param.9) | copy-start | bytes 2359300
  446.0 98.9 %copy-start.16 = (f32[64,8]{1,0:T(8,128)S(1)}, f32[64,8]{1,0:T(8,128)}, u32[]{:S(2)}) copy-start(f32[64,8]{1,0:T(8,128)} %copy-done.15) | copy-start | bytes 6148
  446.0 98.9 %copy-start.21 = (f32[768]{0:T(1024)S(1)}, f32[768]{0:T(1024)}, u32[]{:S(2)}) copy-start(f32[768]{0:T(1024)} %copy-done.20) | copy-start | bytes 9220
  446.0 619.0 %reduce-scatter.9.cloned.1.call-start = ((), (), s32[]{:S(2)}) async-start(), calls=%async_computation.12 | async-start | bytes 2433024 | tf_op jit(solution)/shard_map/reduce_scatter | solution.py:120
  548.4 26.5 %copy-start.24 = (bf16[64,8,768]{2,1,0:T(8,128)(2,1)S(1)}, bf16[64,8,768]{2,1,0:T(8,128)(2,1)}, u32[]{:S(2)}) copy-start(bf16[64,8,768]{2,1,0:T(8,128)(2,1)} %reduce-scatter.7.cloned.1.call-done) | copy-start | bytes 2359300
  574.9 3.6 copy-start.22
  574.9 44.2 %copy-start.18 = (f32[64,8]{0,1:T(8,128)S(1)}, f32[64,8]{0,1:T(8,128)}, u32[]{:S(2)}) copy-start(f32[64,8]{0,1:T(8,128)} %copy-done.17) | copy-start | bytes 6148
  574.9 44.3 %copy-start.2 = (f32[64,8,768]{2,1,0:T(8,128)S(1)}, f32[64,8,768]{2,1,0:T(8,128)}, u32[]{:S(2)}) copy-start(f32[64,8,768]{2,1,0:T(8,128)} %copy-done) | copy-start | bytes 4718596
Sparse Core Ops, SparseCore 0:
  10.9 56.6 all-gather.5
  71.0 99.6 all-gather.7
  173.6 52.1 all-gather.9
  228.5 62.5 all-gather.11
  293.8 62.3 all-gather.13
  411.3 133.5 reduce-scatter.6
  547.1 25.2 reduce-scatter.10
  579.1 99.0 reduce-scatter.12
  684.6 134.4 reduce-scatter.16
  826.5 134.5 reduce-scatter.14
  967.0 98.0 reduce-scatter.8
where the time goes:
time: 1080 us; the launch traced here: 1070 us
  waiting for transfers between devices  814 us (75%)
  matrix products  87 us (8%)
  blocking collectives  81.5 us (8%)
  local copies, waits for them, and re-layouts  57.3 us (5%)
  other arithmetic  17.1 us (2%)
  between operations  14.7 us (1%)
    reduce_scatter x1, waiting for transfers between devices, on_device(): lax.psum_scatter(up_grad, ('dp', 'seq'), scatter_dimension=0, tiled=True)  142 us
    reduce_scatter x1, waiting for transfers between devices, on_device(): lax.psum_scatter(down_grad, ('dp', 'seq'), scatter_dimension=0, tiled=True)  141 us
    reduce_scatter x1, waiting for transfers between devices, on_device(): lax.psum_scatter(value_wgrad, ('dp', 'seq'), scatter_dimension=0, tiled=T...  104 us
    reduce_scatter x1, waiting for transfers between devices, on_device(): lax.psum_scatter(term.reshape(positions * lax.axis_size('seq'), sequences...  98.8 us
    all_gather x1, waiting for transfers between devices, on_device(): gathered = lax.all_gather(values, 'seq', axis=0, tiled=True)  94.6 us
    unnamed x2, blocking collectives  81.5 us
    all_gather x1, waiting for transfers between devices, on_device(): lax.all_gather(up_weight, ('dp', 'seq'), axis=0, tiled=True)  62.7 us
    all_gather x1, waiting for transfers between devices, on_device(): lax.all_gather(down_weight, ('dp', 'seq'), axis=0, tiled=True)  58.2 us
  transfers between devices with their start and end apart: 11, of which 11 were waited for; matrix products, arithmetic and copies ran while one was open for 10% of the time, Pallas kernels for 0%

commit v1 on v0

v1 whole, which is shorter than its diff:
```python
import functools

import jax
import jax.numpy as jnp
from jax import lax
from jax.experimental import pallas as pl
from jax.experimental.pallas import tpu as pltpu
from jax.sharding import PartitionSpec as P

F32 = jnp.float32
BF16 = jnp.bfloat16
AXES = ("dp", "seq")
HEAD = 64
GROUPS = 4
EPS = 1e-06
MIB = 1 << 20


def smem():
    return pl.BlockSpec(memory_space=pltpu.SMEM)


def vmem():
    return pl.BlockSpec(memory_space=pltpu.VMEM)


def params(mib):
    return pltpu.CompilerParams(vmem_limit_bytes=mib * MIB)


def cost(flops, moved, trans=0):
    return pl.CostEstimate(flops=int(flops), bytes_accessed=int(moved), transcendentals=int(trans))


def shape(dims, kind=BF16):
    return jax.ShapeDtypeStruct(tuple(dims), kind)


def dot_nn(left, right):
    return lax.dot_general(left, right, (((1,), (0,)), ((), ())), preferred_element_type=F32)


def dot_nt(left, right):
    return lax.dot_general(left, right, (((1,), (1,)), ((), ())), preferred_element_type=F32)


def dot_tn(left, right):
    return lax.dot_general(left, right, (((0,), (0,)), ((), ())), preferred_element_type=F32)


class Layout:
    def __init__(self, tokens, logits):
        self.positions, self.sequences, self.width = tokens.shape
        self.heads, _, self.length = logits.shape
        self.dp, self.seq = lax.axis_size("dp"), lax.axis_size("seq")
        self.xs = self.seq // (2 * GROUPS)
        self.rows = self.positions * self.sequences
        self.group = self.heads // GROUPS
        self.lanes = self.sequences * HEAD
        self.devices = self.dp * self.seq
        dp, seq = lax.axis_index("dp"), lax.axis_index("seq")
        self.z, self.x, self.c = seq // (2 * self.xs), (seq // 2) % self.xs, seq % 2
        self.me = jnp.stack([dp, self.z, self.x, self.c, seq, seq, seq, seq]).astype(jnp.int32)
        self.small = self.dp == 2 and self.xs == 2

    def swap(self, array, dp=0, z=0, x=0, c=0):
        mask = ((dp * GROUPS + z) * self.xs + x) * 2 + c
        return lax.ppermute(array, AXES, [(i, i ^ mask) for i in range(self.devices)])


def add_low(left, right):
    return (left.astype(F32) + right.astype(F32)).astype(BF16)


def to_heads(source, target, positions, sequences, heads):
    group = heads // GROUPS
    low = lax.broadcasted_iota(jnp.int32, (positions, 2 * HEAD), 1) < HEAD
    for pair in range(sequences // 2):
        for two in range(heads // 2):
            a = source[two, pl.ds(2 * pair, positions, stride=sequences), :]
            b = source[two, pl.ds(2 * pair + 1, positions, stride=sequences), :]
            even = jnp.where(low, a, pltpu.roll(b, HEAD, 1))
            odd = jnp.where(low, pltpu.roll(a, HEAD, 1), b)
            for head, tile in ((2 * two, even), (2 * two + 1, odd)):
                target[head // group, head % group, :, 128 * pair : 128 * pair + 128] = tile.astype(BF16)


def from_heads(source, target, positions, sequences, heads):
    group = heads // GROUPS
    low = lax.broadcasted_iota(jnp.int32, (positions, 2 * HEAD), 1) < HEAD
    for pair in range(sequences // 2):
        for two in range(heads // 2):
            even, odd = (
                source[head // group, head % group, :, 128 * pair : 128 * pair + 128].astype(F32)
                for head in (2 * two, 2 * two + 1)
            )
            first = jnp.where(low, even, pltpu.roll(odd, HEAD, 1))
            second = jnp.where(low, pltpu.roll(even, HEAD, 1), odd)
            target[two, pl.ds(2 * pair, positions, stride=sequences), :] = first
            target[two, pl.ds(2 * pair + 1, positions, stride=sequences), :] = second


def split_lanes(value, target):
    for two in range(target.shape[0]):
        target[two] = value[:, 128 * two : 128 * two + 128]


def join_lanes(source, target):
    for two in range(source.shape[0]):
        target[:, 128 * two : 128 * two + 128] = source[two].astype(target.dtype)


def softmax_kernel(me, logits, own, *others):
    positions, length = logits.shape[2], logits.shape[3]
    z, seq, side = me[1], me[4], me[0] % 2
    half = positions // 2
    column = lax.broadcasted_iota(jnp.int32, (positions, length), 1)
    row = lax.broadcasted_iota(jnp.int32, (positions, length), 0) + seq * positions

    def soft(values, allowed):
        masked = jnp.where(allowed, values.astype(F32), -jnp.inf)
        expo = jnp.exp(masked - jnp.max(masked, axis=-1, keepdims=True))
        return (expo * (1.0 / jnp.sum(expo, axis=-1, keepdims=True))).astype(BF16)

    allowed = column <= row
    for head in range(logits.shape[1]):
        own[head] = soft(logits[z, head], allowed)
    start = pl.multiple_of(side * half, half)
    allowed = column[:half] <= row[:half] + start
    for k, out in enumerate(others, 1):
        for head in range(logits.shape[1]):
            out[head] = soft(logits[z ^ k, head, pl.ds(start, half), :], allowed)


def softmax_rows(lay, logits):
    group, positions, length = lay.group, lay.positions, lay.length
    return pl.pallas_call(
        softmax_kernel,
        in_specs=[smem(), vmem()],
        out_specs=[vmem()] * GROUPS,
        out_shape=[shape((group, positions, length))]
        + [shape((group, positions // 2, length))] * (GROUPS - 1),
        compiler_params=params(24),
        cost_estimate=cost(1e7, 4 * logits.size, logits.size),
        name="mix_rows",
    )(lay.me, logits.reshape(GROUPS, group, positions, length))


def gather_rows(me, own, other, store, xs, dps):
    first = me[3] == 0
    for r in range(own.shape[0]):
        xr, yr, zr = r // (GROUPS * dps), (r // GROUPS) % dps, r % GROUPS
        chip = ((me[0] ^ yr) * GROUPS + (me[1] ^ zr)) * xs + (me[2] ^ xr)
        mine, theirs = own[r].astype(F32), other[r].astype(F32)
        block = jnp.concatenate([jnp.where(first, mine, theirs), jnp.where(first, theirs, mine)], 0)
        store(chip, block.astype(BF16))


def value_body(me, tokens, weight, scratch, parts, outs, normed, positions, sequences, heads):
    inputs = tokens[...].astype(F32)
    scale = lax.rsqrt(jnp.mean(inputs * inputs, axis=-1, keepdims=True) + EPS)
    low = (inputs * scale).astype(BF16)
    normed[...] = low
    split_lanes(dot_nn(low, weight[...]), scratch)
    to_heads(scratch, parts, positions, sequences, heads)
    for k, out in enumerate(outs):
        out[...] = parts[me[1] ^ k]


def value_kernel(me, tokens, *rest, positions, sequences, heads, blocks):
    if blocks:
        own, other, normed, whole, *outs = rest[:8]
        rows = whole.shape[0] // blocks

        def store(chip, block):
            whole[pl.ds(pl.multiple_of(chip * rows, rows), rows), :] = block

        gather_rows(me, own, other, store, 2, 2)
    else:
        whole, normed, *outs = rest[:6]
    parts, scratch = rest[-2:]
    value_body(me, tokens, whole, scratch, parts, outs, normed, positions, sequences, heads)


def make_values(lay, tokens, weight):
    rows, width = tokens.shape
    piece = (lay.group, lay.positions, lay.lanes)
    blocks = 0 if len(weight) == 1 else lay.devices // 2
    outs = [shape((rows, width))] + ([shape((width, width))] if blocks else []) + [shape(piece)] * GROUPS
    result = pl.pallas_call(
        functools.partial(
            value_kernel,
            positions=lay.positions,
            sequences=lay.sequences,
            heads=lay.heads,
            blocks=blocks,
        ),
        in_specs=[smem()] + [vmem()] * (1 + len(weight)),
        out_specs=[vmem()] * len(outs),
        out_shape=outs,
        scratch_shapes=[pltpu.VMEM((GROUPS,) + piece, BF16), pltpu.VMEM((width // 128, rows, 128), F32)],
        compiler_params=params(24),
        cost_estimate=cost(2 * rows * width * width, 6 * rows * width + 4 * width * width),
        name="make_values",
    )(lay.me, tokens, *weight)
    normed = result[0]
    whole = result[1] if blocks else weight[0]
    return normed, whole, list(result[-GROUPS:])


def mix_kernel(me, *refs, xs, positions):
    values = refs[: 2 * xs * GROUPS]
    refs = refs[2 * xs * GROUPS :]
    own, near, far = refs[0], refs[1:GROUPS], refs[GROUPS : 2 * GROUPS - 1]
    rows_out, values_out, *outs, mixed = refs[2 * GROUPS - 1 :]
    z, x, c, side = me[1], me[2], me[3], me[0] % 2
    half = positions // 2
    rows_out[:, pl.ds(pl.multiple_of(z * positions, positions), positions), :] = own[...]
    for k in range(1, GROUPS):
        base = (z ^ k) * positions
        rows_out[:, pl.ds(pl.multiple_of(base + side * half, half), half), :] = near[k - 1][...]
        rows_out[:, pl.ds(pl.multiple_of(base + (1 - side) * half, half), half), :] = far[k - 1][...]
    index = 0
    for m in range(2):
        for j in range(xs):
            for k in range(GROUPS):
                block = ((z ^ k) * xs + (x ^ j)) * 2 + (c ^ m)
                values_out[:, pl.ds(pl.multiple_of(block * positions, positions), positions), :] = values[
                    index
                ][...]
                index += 1
    for head in range(rows_out.shape[0]):
        mixed[head] = dot_nn(rows_out[head], values_out[head]).astype(BF16)
    for k, out in enumerate(outs):
        out[...] = mixed[:, pl.ds(pl.multiple_of((z ^ k) * positions, positions), positions), :]


def mix_values(lay, values, rows):
    group, positions, length, lanes = lay.group, lay.positions, lay.length, lay.lanes
    inputs = list(values) + list(rows)
    result = pl.pallas_call(
        functools.partial(mix_kernel, xs=lay.xs, positions=positions),
        in_specs=[smem()] + [vmem()] * len(inputs),
        out_specs=[vmem()] * (2 + GROUPS),
        out_shape=[shape((group, GROUPS * positions, length)), shape((group, length, lanes))]
        + [shape((group, positions, lanes))] * GROUPS,
        scratch_shapes=[pltpu.VMEM((group, GROUPS * positions, lanes), BF16)],
        compiler_params=params(40),
        cost_estimate=cost(2 * group * GROUPS * positions * length * lanes, 8 * group * length * lanes),
        name="mix_values",
    )(lay.me, *inputs)
    return result[0], result[1], list(result[2:])


def up_front_kernel(me, out_grad, *refs, blocks):
    if blocks:
        up_own, up_other, down_own, down_other, up_whole, down_whole, grad = refs
        rows, tall = up_whole.shape[0] // blocks, 2 * down_own.shape[1]
        part = pl.program_id(0)

        def store(chip, block):
            up_whole[pl.ds(pl.multiple_of(chip * rows, rows), rows), :] = block

        gather_rows(me, up_own, up_other, store, 2, 2)

        @pl.when(part == 0)
        def _():
            for r in range(down_own.shape[0]):
                yr, xr, zr = r // (GROUPS * 2), (r // GROUPS) % 2, r % GROUPS
                chip = ((me[0] ^ yr) * GROUPS + (me[1] ^ zr)) * 2 + (me[2] ^ xr)
                for ref, core in ((down_own, me[3]), (down_other, 1 - me[3])):
                    start = pl.multiple_of(chip * tall + core * (tall // 2), tall // 2)
                    down_whole[pl.ds(start, tall // 2), :] = ref[r]

        @pl.when(part < pl.num_programs(0) - 1)
        def _():
            start = pl.multiple_of(part * up_whole.shape[1], up_whole.shape[1])
            grad[...] = dot_nt(
                out_grad[...], down_whole[pl.ds(start, up_whole.shape[1]), :]
            ).astype(BF16)


def prepare_weights(lay, out_grad, up_own, up_other, down_own, down_other):
    rows, width = out_grad.shape
    chips, short, wide = up_own.shape
    tall = down_own.shape[1]
    hidden = wide - width
    steps = hidden // width

    def part(i, me):
        return (0, 0, i)

    def fixed(i, me):
        return (0, 0, 0)

    return pl.pallas_call(
        functools.partial(up_front_kernel, blocks=chips),
        grid_spec=pltpu.PrefetchScalarGridSpec(
            num_scalar_prefetch=1,
            grid=(steps + 1,),
            in_specs=[
                pl.BlockSpec((rows, width), lambda i, me: (0, 0)),
                pl.BlockSpec((chips, short, width), part),
                pl.BlockSpec((chips, short, width), part),
                pl.BlockSpec((chips, tall, width), fixed),
                pl.BlockSpec((chips, tall, width), fixed),
            ],
            out_specs=[
                pl.BlockSpec((width, width), lambda i, me: (0, i)),
                pl.BlockSpec((hidden, width), lambda i, me: (0, 0)),
                pl.BlockSpec((rows, width), lambda i, me: (0, jnp.minimum(i, steps - 1))),
            ],
        ),
        out_shape=[shape((width, wide)), shape((hidden, width)), shape((rows, hidden))],
        compiler_params=params(40),
        cost_estimate=cost(2 * rows * width * hidden, 8 * width * hidden),
        name="prepare_weights",
    )(lay.me, out_grad, up_own, up_other, down_own, down_other)


def hidden_grad_kernel(out_grad, down, grad):
    grad[...] = dot_nt(out_grad[...], down[...]).astype(BF16)


def hidden_grads(out_grad, down):
    rows, width = out_grad.shape
    hidden = down.shape[0]
    return pl.pallas_call(
        hidden_grad_kernel,
        grid=(hidden // width,),
        in_specs=[
            pl.BlockSpec((rows, width), lambda i: (0, 0)),
            pl.BlockSpec((width, width), lambda i: (i, 0)),
        ],
        out_specs=pl.BlockSpec((rows, width), lambda i: (0, i)),
        out_shape=shape((rows, hidden)),
        name="hidden_grads",
    )(out_grad, down)


ROOT = 0.7978845608028654
CUBE = 0.044715


def middle_kernel(
    me,
    *refs,
    positions,
    sequences,
    heads,
):
    pieces = refs[:GROUPS]
    tokens, out_grad, w_out, w_up, hidden_grad = refs[GROUPS : GROUPS + 5]
    rest = refs[GROUPS + 5 :]
    mixed, residual, normed, hidden, pre_grad, residual_grad, attn_grad = rest[:7]
    outs = rest[7 : 7 + GROUPS]
    parts, scratch, total = rest[7 + GROUPS :]
    step, last = pl.program_id(0), pl.num_programs(0) - 1
    z = me[1]

    @pl.when(step == 0)
    def _():
        for k, piece in enumerate(pieces):
            parts[z ^ k] = piece[...]
        from_heads(parts, scratch, positions, sequences, heads)
        join_lanes(scratch, mixed)
        value = tokens[...].astype(F32) + dot_nn(mixed[...], w_out[...])
        residual[...] = value
        scale = lax.rsqrt(jnp.mean(value * value, axis=-1, keepdims=True) + EPS)
        normed[...] = (value * scale).astype(BF16)

    u = dot_nn(normed[...], w_up[...])
    square = u * u
    tanh = jnp.tanh(ROOT * u * (1.0 + CUBE * square))
    half = 0.5 * (1.0 + tanh)
    hidden[...] = (u * half).astype(BF16)
    slope = half + 0.5 * u * (1.0 - tanh * tanh) * (ROOT * (1.0 + 3.0 * CUBE * square))
    pre = (slope * hidden_grad[...].astype(F32)).astype(BF16)
    pre_grad[...] = pre
    add = dot_nt(pre, w_up[...])

    @pl.when(step == 0)
    def _():
        total[...] = add

    @pl.when(step > 0)
    def _():
        total[...] += add

    @pl.when(step == last)
    def _():
        value = residual[...]
        scale = lax.rsqrt(jnp.mean(value * value, axis=-1, keepdims=True) + EPS)
        norm = value * scale
        grad = total[...]
        back = scale * (grad - norm * jnp.mean(grad * norm, axis=-1, keepdims=True))
        grad = out_grad[...].astype(F32) + back
        residual_grad[...] = grad
        attn_grad[...] = grad.astype(BF16)
        split_lanes(dot_nt(attn_grad[...], w_out[...]), scratch)
        to_heads(scratch, parts, positions, sequences, heads)
        for k, out in enumerate(outs):
            out[...] = parts[z ^ k]


def middle(lay, pieces, tokens, out_grad, out_weight, up_weight, hidden_grad, where):
    rows, width = tokens.shape
    hidden = hidden_grad.shape[1]
    steps = hidden // width
    piece = (lay.group, lay.positions, lay.lanes)

    def whole(*dims):
        return pl.BlockSpec(dims, lambda i, me: (0,) * len(dims))

    def part(i, me):
        return (0, i)

    out = pl.pallas_call(
        functools.partial(
            middle_kernel, positions=lay.positions, sequences=lay.sequences, heads=lay.heads
        ),
        grid_spec=pltpu.PrefetchScalarGridSpec(
            num_scalar_prefetch=1,
            grid=(steps,),
            in_specs=[whole(*piece)] * GROUPS
            + [
                whole(rows, width),
                whole(rows, width),
                pl.BlockSpec((width, width), lambda i, me: (0, where)),
                pl.BlockSpec((width, width), part),
                pl.BlockSpec((rows, width), part),
            ],
            out_specs=[
                whole(rows, width),
                whole(rows, width),
                whole(rows, width),
                pl.BlockSpec((rows, width), part),
                pl.BlockSpec((rows, width), part),
                whole(rows, width),
                whole(rows, width),
            ]
            + [whole(*piece)] * GROUPS,
            scratch_shapes=[
                pltpu.VMEM((GROUPS,) + piece, BF16),
                pltpu.VMEM((width // 128, rows, 128), F32),
                pltpu.VMEM((rows, width), F32),
            ],
        ),
        out_shape=[
            shape((rows, width)),
            shape((rows, width), F32),
            shape((rows, width)),
            shape((rows, hidden)),
            shape((rows, hidden)),
            shape((rows, width), F32),
            shape((rows, width)),
        ]
        + [shape(piece)] * GROUPS,
        compiler_params=params(48),
        cost_estimate=cost(4 * rows * width * (hidden + width), 16 * rows * hidden, rows * hidden),
        name="middle",
    )(lay.me, *pieces, tokens, out_grad, out_weight, up_weight, hidden_grad)
    return out[:7], list(out[7:])


def layer_out_kernel(residual, hidden, down, out):
    out[...] = (residual[...] + dot_nn(hidden[...], down[...])).astype(BF16)


def make_layer_out(residual, hidden, down):
    rows, width = residual.shape
    return pl.pallas_call(
        layer_out_kernel,
        out_shape=shape((rows, width)),
        in_specs=[vmem()] * 3,
        out_specs=vmem(),
        compiler_params=params(32),
        cost_estimate=cost(2 * hidden.size * width, 2 * (hidden.size + down.size) + 6 * residual.size),
        name="make_layer_out",
    )(residual, hidden, down)


def down_grad_kernel(me, hidden, out_grad, own, other, result, *, tall):
    part = pl.program_id(0)
    result[...] = dot_tn(hidden[...], out_grad[...]).astype(BF16)
    count = result.shape[0] // (2 * tall)
    for i in range(count):
        chip = part * count + i
        yr, zr, xr = (chip // 8) ^ me[0], ((chip // 2) % 4) ^ me[1], (chip % 2) ^ me[2]
        slot = (yr * 2 + xr) * 4 + zr
        for ref, core in ((own, me[3]), (other, 1 - me[3])):
            start = pl.multiple_of((2 * i + core) * tall, tall)
            ref[slot] = result[pl.ds(start, tall), :]


def down_grads(lay, hidden, out_grad):
    rows, width = out_grad.shape
    units = hidden.shape[1]
    tall = units // lay.devices
    chips = lay.devices // 2
    return pl.pallas_call(
        functools.partial(down_grad_kernel, tall=tall),
        grid_spec=pltpu.PrefetchScalarGridSpec(
            num_scalar_prefetch=1,
            grid=(units // width,),
            in_specs=[
                pl.BlockSpec((rows, width), lambda i, me: (0, i)),
                pl.BlockSpec((rows, width), lambda i, me: (0, 0)),
            ],
            out_specs=[pl.BlockSpec((chips, tall, width), lambda i, me: (0, 0, 0))] * 2,
            scratch_shapes=[pltpu.VMEM((width, width), BF16)],
        ),
        out_shape=[shape((chips, tall, width))] * 2,
        compiler_params=params(32),
        cost_estimate=cost(2 * rows * units * width, 2 * (rows + width) * units),
        name="down_grads",
    )(lay.me, hidden, out_grad)


def spread_rows(me, result, own, other, short, xs, dps):
    for chip in range(result.shape[0] // (2 * short)):
        yr, zr, xr = (chip // (GROUPS * xs)) ^ me[0], ((chip // xs) % GROUPS) ^ me[1], (chip % xs) ^ me[2]
        slot = (xr * dps + yr) * GROUPS + zr
        for ref, core in ((own, me[3]), (other, 1 - me[3])):
            start = pl.multiple_of(2 * short * chip + short * core, short)
            ref[slot] = result[pl.ds(start, short), :].astype(BF16)


def up_grad_kernel(me, normed, mixed, pre_grad, attn_grad, own, other, result):
    part, last = pl.program_id(0), pl.num_programs(0) - 1

    @pl.when(part < last)
    def _():
        result[...] = dot_tn(normed[...], pre_grad[...])

    @pl.when(part == last)
    def _():
        result[...] = dot_tn(mixed[...], attn_grad[...])

    spread_rows(me, result, own, other, own.shape[1], 2, 2)


def up_grads(lay, normed, mixed, pre_grad, attn_grad):
    rows, width = normed.shape
    units = pre_grad.shape[1]
    steps = units // width
    chips, short = lay.devices // 2, width // lay.devices

    def whole(i, me):
        return (0, 0)

    return pl.pallas_call(
        up_grad_kernel,
        grid_spec=pltpu.PrefetchScalarGridSpec(
            num_scalar_prefetch=1,
            grid=(steps + 1,),
            in_specs=[
                pl.BlockSpec((rows, width), whole),
                pl.BlockSpec((rows, width), whole),
                pl.BlockSpec((rows, width), lambda i, me: (0, jnp.minimum(i, steps - 1))),
                pl.BlockSpec((rows, width), whole),
            ],
            out_specs=[pl.BlockSpec((chips, short, width), lambda i, me: (0, 0, i))] * 2,
            scratch_shapes=[pltpu.VMEM((width, width), F32)],
        ),
        out_shape=[shape((chips, short, units + width))] * 2,
        compiler_params=params(32),
        cost_estimate=cost(2 * rows * width * (units + width), 4 * (rows + width) * units),
        name="up_grads",
    )(lay.me, normed, mixed, pre_grad, attn_grad)


def back_kernel(me, *refs, xs, dps, positions):
    pieces, rows, values = refs[:GROUPS], refs[GROUPS], refs[GROUPS + 1]
    outs = refs[GROUPS + 2 :]
    logit_outs, term_outs = outs[:dps], outs[dps : dps + 2 * GROUPS]
    grads, term, logit = outs[dps + 2 * GROUPS :]
    dp, z, x, c = me[0], me[1], me[2], me[3]
    part = logit_outs[0].shape[-1]
    for k, piece in enumerate(pieces):
        grads[:, pl.ds(pl.multiple_of((z ^ k) * positions, positions), positions), :] = piece[...]
    for head in range(rows.shape[0]):
        term[head] = dot_tn(rows[head], grads[head]).astype(BF16)
        soft = rows[head].astype(F32)
        product = soft * dot_nt(grads[head], values[head])
        logit[...] = (product - soft * jnp.sum(product, axis=-1, keepdims=True)).astype(BF16)
        for r, out in enumerate(logit_outs):
            start = pl.multiple_of((dp ^ r) * part, part)
            for k in range(GROUPS):
                base = pl.multiple_of((z ^ k) * positions, positions)
                out[k, head] = logit[pl.ds(base, positions), pl.ds(start, part)]
    index = 0
    for m in range(2):
        for k in range(GROUPS):
            for j in range(xs):
                block = ((z ^ k) * xs + (x ^ j)) * 2 + (c ^ m)
                term_outs[index][j] = term[:, pl.ds(pl.multiple_of(block * positions, positions), positions), :]
            index += 1


def mix_back(lay, pieces, rows, values):
    group, positions, length, lanes = lay.group, lay.positions, lay.length, lay.lanes
    part = length // lay.dp
    result = pl.pallas_call(
        functools.partial(back_kernel, xs=lay.xs, dps=lay.dp, positions=positions),
        in_specs=[smem()] + [vmem()] * (GROUPS + 2),
        out_specs=[vmem()] * (lay.dp + 2 * GROUPS),
        out_shape=[shape((GROUPS, group, positions, part))] * lay.dp
        + [shape((lay.xs, group, positions, lanes))] * (2 * GROUPS),
        scratch_shapes=[
            pltpu.VMEM((group, GROUPS * positions, lanes), BF16),
            pltpu.VMEM((group, length, lanes), BF16),
            pltpu.VMEM((GROUPS * positions, length), BF16),
        ],
        compiler_params=params(48),
        cost_estimate=cost(
            4 * group * GROUPS * positions * length * lanes, 8 * group * length * lanes
        ),
        name="mix_back",
    )(lay.me, *pieces, rows, values)
    return list(result[: lay.dp]), list(result[lay.dp :])


def value_grad_kernel(me, *refs, positions, sequences, heads, spread):
    pieces, normed = refs[:GROUPS], refs[GROUPS]
    if spread:
        total, own, other, parts, scratch, result = refs[GROUPS + 1 :]
    else:
        total, parts, scratch, result = refs[GROUPS + 1 :]
    for k, piece in enumerate(pieces):
        parts[me[1] ^ k] = piece[...]
    from_heads(parts, scratch, positions, sequences, heads)
    join_lanes(scratch, total)
    if spread:
        result[...] = dot_tn(normed[...], total[...])
        spread_rows(me, result, own, other, own.shape[1], 2, 2)


def value_grads(lay, pieces, normed):
    rows, width = normed.shape
    piece = (lay.group, lay.positions, lay.lanes)
    chips, short = lay.devices // 2, width // lay.devices
    outs = [shape((rows, width))] + ([shape((chips, short, width))] * 2 if lay.small else [])
    return pl.pallas_call(
        functools.partial(
            value_grad_kernel,
            positions=lay.positions,
            sequences=lay.sequences,
            heads=lay.heads,
            spread=lay.small,
        ),
        in_specs=[smem()] + [vmem()] * (GROUPS + 1),
        out_specs=[vmem()] * len(outs),
        out_shape=outs,
        scratch_shapes=[
            pltpu.VMEM((GROUPS,) + piece, BF16),
            pltpu.VMEM((width // 128, rows, 128), F32),
            pltpu.VMEM((width, width), F32),
        ],
        compiler_params=params(32),
        cost_estimate=cost(2 * rows * width * width, 8 * rows * width),
        name="value_grads",
    )(lay.me, *pieces, normed)


def tokens_grad_kernel(total, weight, tokens, residual_grad, out):
    grad = dot_nt(total[...], weight[...])
    inputs = tokens[...].astype(F32)
    scale = lax.rsqrt(jnp.mean(inputs * inputs, axis=-1, keepdims=True) + EPS)
    norm = inputs * scale
    back = scale * (grad - norm * jnp.mean(grad * norm, axis=-1, keepdims=True))
    out[...] = residual_grad[...] + back


def make_tokens_grad(total, weight, tokens, residual_grad):
    rows, width = tokens.shape
    return pl.pallas_call(
        tokens_grad_kernel,
        out_shape=shape((rows, width), F32),
        in_specs=[vmem()] * 4,
        out_specs=vmem(),
        compiler_params=params(24),
        cost_estimate=cost(2 * rows * width * width, 12 * rows * width),
        name="make_tokens_grad",
    )(total, weight, tokens, residual_grad)


def logits_out_kernel(me, *refs):
    pieces, out = refs[:GROUPS], refs[GROUPS]
    for k, piece in enumerate(pieces):
        out[me[1] ^ k] = piece[...].astype(F32)


def make_logits_grad(lay, pieces):
    group, positions, part = pieces[0].shape
    out = pl.pallas_call(
        logits_out_kernel,
        out_shape=shape((GROUPS, group, positions, part), F32),
        in_specs=[smem()] + [vmem()] * GROUPS,
        out_specs=vmem(),
        compiler_params=params(16),
        cost_estimate=cost(1e6, 24 * pieces[0].size),
        name="make_logits_grad",
    )(lay.me, *pieces)
    return out.reshape(lay.heads, positions, part)


def along_z(lay, pieces):
    return [pieces[0]] + [lay.swap(pieces[k], z=k) for k in range(1, GROUPS)]


def along_z_gather(lay, array):
    return jnp.stack([array] + [lay.swap(array, z=k) for k in range(1, GROUPS)])


def double(lay, array, **way):
    return jnp.concatenate([array, lay.swap(array, **way)])


def halve(lay, array, **way):
    half = array.shape[0] // 2
    return add_low(array[:half], lay.swap(array[half:], **way))


def sum_z(lay, array):
    total = array[0].astype(F32)
    for k in range(1, GROUPS):
        total = total + lay.swap(array[k], z=k).astype(F32)
    return total


def on_device(
    tokens,
    norm_gain1,
    value_weight,
    mixer_logits,
    out_weight,
    norm_gain2,
    up_weight,
    down_weight,
    out_grad,
):
    lay = Layout(tokens, mixer_logits)
    out_shape = tokens.shape
    width = lay.width
    tokens = tokens.reshape(lay.rows, width)
    out_grad = out_grad.reshape(lay.rows, width)
    gain_one = norm_gain1.astype(F32)[:, None]
    gain_two = norm_gain2.astype(F32)[:, None]
    value_rows = (gain_one * value_weight.astype(F32)).astype(BF16)
    up_rows = (gain_two * up_weight.astype(F32)).astype(BF16)
    small = lay.small

    with jax.named_scope("value_weight_gather"):
        if small:
            own = along_z_gather(lay, value_rows)
            four = [own, lay.swap(own, dp=1), lay.swap(own, x=1), lay.swap(own, dp=1, x=1)]
            own = jnp.concatenate(four)
            w_value = [own, lay.swap(own, c=1)]
        else:
            w_value = [lax.all_gather(value_rows, AXES, axis=0, tiled=True)]
    with jax.named_scope("mixing_rows"):
        pieces = softmax_rows(lay, mixer_logits)
        near = [lay.swap(pieces[k], z=k) for k in range(1, GROUPS)]
        far = [lay.swap(piece, dp=1) for piece in near]
        rows = [pieces[0]] + near + far
    with jax.named_scope("weight_gather"):
        if small:
            wide = along_z_gather(lay, jnp.concatenate([up_rows, out_weight], axis=1))
            wide = double(lay, double(lay, wide, dp=1).reshape((8,) + wide.shape[1:]), x=1)
            tall = along_z_gather(lay, down_weight)
            tall = double(lay, double(lay, tall, x=1), dp=1)
            wide_other, tall_other = lay.swap(wide, c=1), lay.swap(tall, c=1)
        else:
            w_up = lax.all_gather(up_rows, AXES, axis=0, tiled=True)
            w_out = lax.all_gather(out_weight, AXES, axis=0, tiled=True)
            w_down = lax.all_gather(down_weight, AXES, axis=0, tiled=True)

    with jax.named_scope("values"):
        normed_one, w_value, pieces = make_values(lay, tokens, w_value)
        first = along_z(lay, pieces)
        values = list(first)
        for j in range(1, lay.xs):
            values += [lay.swap(piece, x=j) for piece in first]
        values += [lay.swap(piece, c=1) for piece in values]
    with jax.named_scope("mixing"):
        mix_low, values, pieces = mix_values(lay, values, rows)
        pieces = along_z(lay, pieces)
    with jax.named_scope("weights"):
        if small:
            w_wide, w_down, hidden_grad = prepare_weights(
                lay, out_grad, wide, wide_other, tall, tall_other
            )
            w_out, w_up, where = w_wide, w_wide, w_down.shape[0] // width
        else:
            hidden_grad = hidden_grads(out_grad, w_down)
            where = 0
    with jax.named_scope("feed_forward"):
        kept, pieces = middle(lay, pieces, tokens, out_grad, w_out, w_up, hidden_grad, where)
        mixed, residual, normed_two, hidden, pre_grad, residual_grad, attn_grad = kept
        pieces = along_z(lay, pieces)
    with jax.named_scope("weight_grads"):
        if small:
            tall, tall_other = down_grads(lay, hidden, out_grad)
            wide, wide_other = up_grads(lay, normed_two, mixed, pre_grad, attn_grad)
            tall = add_low(tall, lay.swap(tall_other, c=1))
            wide = add_low(wide, lay.swap(wide_other, c=1))
            tall = halve(lay, halve(lay, tall, dp=1), x=1)
            wide = halve(lay, halve(lay, wide, x=1), dp=1)
            down_grad = sum_z(lay, tall)
            wide = sum_z(lay, wide)
            up_sum, out_wgrad = wide[:, : up_rows.shape[1]], wide[:, up_rows.shape[1] :]
        else:
            down_grad = scatter_sum(dot_tn(hidden, out_grad))
            up_sum = scatter_sum(dot_tn(normed_two, pre_grad))
            out_wgrad = scatter_sum(dot_tn(mixed, attn_grad))
        layer_out = make_layer_out(residual, hidden, w_down)
        up_grad = gain_two * up_sum
        gain_two_grad = jnp.sum(up_sum * up_weight.astype(F32), axis=1)
    with jax.named_scope("mixing_back"):
        logit_parts, terms = mix_back(lay, pieces, mix_low, values)
        arrived = []
        for k in range(GROUPS):
            piece = add_low(terms[k], lay.swap(terms[GROUPS + k], c=1))
            bit = lay.xs // 2
            while bit:
                piece = add_low(piece[:bit], lay.swap(piece[bit:], x=bit))
                bit //= 2
            arrived.append(piece[0])
        pieces = along_z(lay, arrived)
        while len(logit_parts) > 1:
            bit = len(logit_parts) // 2
            logit_parts = [
                add_low(logit_parts[r], lay.swap(logit_parts[r + bit], dp=bit)) for r in range(bit)
            ]
        logit_pieces = along_z(lay, [logit_parts[0][k] for k in range(GROUPS)])
        logits_grad = make_logits_grad(lay, logit_pieces)
    with jax.named_scope("value_grads"):
        total, *spread = value_grads(lay, pieces, normed_one)
        if small:
            own, other = spread
            own = add_low(own, lay.swap(other, c=1))
            four = own.reshape((4, GROUPS) + own.shape[1:])
            own = (
                four[0].astype(F32)
                + lay.swap(four[1], dp=1).astype(F32)
                + lay.swap(four[2], x=1).astype(F32)
                + lay.swap(four[3], dp=1, x=1).astype(F32)
            ).astype(BF16)
            value_sum = sum_z(lay, own)
        else:
            value_sum = scatter_sum(dot_tn(normed_one, total))
        tokens_grad = make_tokens_grad(total, w_value, tokens, residual_grad)
        value_wgrad = gain_one * value_sum
        gain_one_grad = jnp.sum(value_sum * value_weight.astype(F32), axis=1)
    return (
        layer_out.reshape(out_shape),
        tokens_grad.reshape(out_shape),
        gain_one_grad,
        value_wgrad,
        logits_grad,
        out_wgrad,
        gain_two_grad,
        up_grad,
        down_grad,
    )


def scatter_sum(array):
    return lax.psum_scatter(array.astype(BF16), AXES, scatter_dimension=0, tiled=True).astype(F32)


def solution(mesh):
    placed = (
        P("seq", "dp", None),
        P(("dp", "seq")),
        P(("dp", "seq"), None),
        P(None, "seq", None),
        P(("dp", "seq"), None),
        P(("dp", "seq")),
        P(("dp", "seq"), None),
        P(("dp", "seq"), None),
        P("seq", "dp", None),
    )
    return jax.shard_map(
        on_device,
        mesh=mesh,
        in_specs=placed,
        out_specs=(
            P("seq", "dp", None),
            P("seq", "dp", None),
            P(("dp", "seq")),
            P(("dp", "seq"), None),
            P(None, "seq", "dp"),
            P(("dp", "seq"), None),
            P(("dp", "seq")),
            P(("dp", "seq"), None),
            P(("dp", "seq"), None),
        ),
        check_vma=False,
    )
```

time: 1080 us -> 428 us (0.40)
  waiting for transfers between devices: 814 us -> 234 us
  starting transfers between devices: 0.87 us -> 103 us
  matrix products: 87 us -> 0 us
  blocking collectives: 81.5 us -> 0 us
  Pallas kernels: 0 us -> 59 us
  local copies, waits for them, and re-layouts: 57.3 us -> 14.3 us
  between operations: 14.7 us -> 1.33 us
    reduce_scatter x6 -> x0, waiting for transfers between devices: 557 us -> none  [the longest x1 142 us: on_device(): lax.psum_scatter(up_grad, ('dp', 'seq'), scatter_dimension=0, tiled=True)]
    all_gather x5 -> x0, waiting for transfers between devices: 254 us -> none  [the longest x1 94.6 us: on_device(): gathered = lax.all_gather(values, 'seq', axis=0, tiled=True)]
    ppermute x0 -> x80, waiting for transfers between devices: none -> 234 us  [swap(): lax.ppermute(array, AXES, [(i, i ^ mask) for i in range(self.devices)])]
    ppermute x0 -> x80, starting transfers between devices: none -> 103 us  [swap(): lax.ppermute(array, AXES, [(i, i ^ mask) for i in range(self.devices)])]
    dot_general x15 -> x0, matrix products: 87 us -> none  [the longest x4 23.8 us: outer_sum(): lax.dot_general(left.reshape(-1, left.shape[-1]), right.reshape(-1, right...]
    unnamed x2 -> x0, blocking collectives: 81.5 us -> none
    pallas_call x0 -> x12, Pallas kernels: none -> 59 us  [the longest x1 16.9 us: middle(): pl.pallas_call(functools.partial(middle_kernel, positions=lay.positions,...]
    convert_element_type x4 -> x0, local copies, waits for them, and re-layouts: 33.4 us -> none  [the longest x2 27.7 us: on_device(): term.reshape(positions * lax.axis_size('seq'), sequences, model_width)]
  transfers between devices with their start and end apart: 11 -> 80, of which waited for: 11 -> 35; matrix products, arithmetic and copies ran while one was open for 10% -> 4% of each run, Pallas kernels for 0% -> 9%
where the time goes in v1:
time: 428 us; the launch traced here: 427 us
  waiting for transfers between devices  234 us (55%)
  starting transfers between devices  103 us (24%)
  Pallas kernels  59 us (14%)
  other arithmetic  15 us (4%)
  local copies, waits for them, and re-layouts  14.3 us (3%)
    ppermute x80, waiting for transfers between devices, swap(): lax.ppermute(array, AXES, [(i, i ^ mask) for i in range(self.devices)])  234 us
    ppermute x80, starting transfers between devices, swap(): lax.ppermute(array, AXES, [(i, i ^ mask) for i in range(self.devices)])  103 us
    pallas_call x1, Pallas kernels, middle(): pl.pallas_call(functools.partial(middle_kernel, positions=lay.positions,...  16.9 us
    pallas_call x1, Pallas kernels, prepare_weights(): pl.pallas_call(functools.partial(up_front_kernel, blocks=chips), grid_spe...  11.5 us
    unnamed x54, local copies, waits for them, and re-layouts  10.8 us
  transfers between devices with their start and end apart: 80, of which 35 were waited for; matrix products, arithmetic and copies ran while one was open for 4% of the time, Pallas kernels for 9%

profile of v1, /device:TPU:0, one launch (start us, length us, event | category | flops | bytes accessed | tf_op | source)
XLA Modules:
  0.0 427.1 jit_solution(7496022730039466294)
XLA Ops:
  0.6 3.1 collective-permute-start.37
  3.7 2.5 collective-permute-start.39
  10.6 2.5 collective-permute-start.33
  14.6 7.8 %collective-permute-done.32 = bf16[24,3840]{1,0:T(8,128)(2,1)S(1)} collective-permute-done((bf16[24,3840]{1,0:T(8,128)(2,1)S(1)}, bf16[24,3840]{1,0:T(8,128)(2,1)S(1)}, u32[]{:S(2)}, u32[]{:S(2)}) %collective-permute-start.32) | collective-permute-done | bytes 184352 | tf_op jit(solution)/shard_map/weight_gather/ppermute | solution.py:68
  22.3 2.8 collective-permute-done.33
  26.9 16.9 %collective-permute-done.34 = bf16[4,24,3840]{2,1,0:T(8,128)(2,1)S(1)} collective-permute-done((bf16[4,24,3840]{2,1,0:T(8,128)(2,1)S(1)}, bf16[4,24,3840]{2,1,0:T(8,128)(2,1)S(1)}, u32[]{:S(2)}, u32[]{:S(2)}) %collective-permute-start.34) | collective-permute-done | bytes 737312 | tf_op jit(solution)/shard_map/weight_gather/ppermute | solution.py:68
  48.8 41.2 %collective-permute-done.40 = bf16[4,96,768]{2,1,0:T(8,128)(2,1)S(1)} collective-permute-done((bf16[4,96,768]{2,1,0:T(8,128)(2,1)S(1)}, bf16[4,96,768]{2,1,0:T(8,128)(2,1)S(1)}, u32[]{:S(2)}, u32[]{:S(2)}) %collective-permute-start.40) | collective-permute-done | bytes 589856 | tf_op jit(solution)/shard_map/weight_gather/ppermute | solution.py:68
  92.6 5.5 %collective-permute-start.1 = (bf16[24,768]{1,0:T(8,128)(2,1)S(1)}, bf16[24,768]{1,0:T(8,128)(2,1)S(1)}, u32[]{:S(2)}, u32[]{:S(2)}) collective-permute-start(bf16[24,768]{1,0:T(8,128)(2,1)S(1)} %get-tuple-element.104), channel_id=1, source_target_pairs={{0,8},{1,9},{2,10},{3,11},{4,12},{5,13},{6,14},{7,15},{8,0},{9,1},... | collective-permute-start | bytes 110600 | tf_op jit(solution)/shard_map/value_weight_gather/ppermute | solution.py:68
  105.8 16.0 %collective-permute-done.41 = bf16[8,96,768]{2,1,0:T(8,128)(2,1)S(1)} collective-permute-done((bf16[8,96,768]{2,1,0:T(8,128)(2,1)S(1)}, bf16[8,96,768]{2,1,0:T(8,128)(2,1)S(1)}, u32[]{:S(2)}, u32[]{:S(2)}) %collective-permute-start.41) | collective-permute-done | bytes 1179680 | tf_op jit(solution)/shard_map/weight_gather/ppermute | solution.py:68
  129.5 8.5 %collective-permute-done.22.refs_17_ = bf16[3,32,1024]{2,1,0:T(8,128)(2,1)S(1)} collective-permute-done((bf16[3,32,1024]{2,1,0:T(8,128)(2,1)S(1)}, bf16[3,32,1024]{2,1,0:T(8,128)(2,1)S(1)}, u32[]{:S(2)}, u32[]{:S(2)}) %collective-permute-start.22) | collective-permute-done | bytes 196640 | tf_op jit(solution)/shard_map/mixing_rows/ppermute | solution.py:68
  142.2 4.3 %collective-permute-done.24.refs_19_ = bf16[3,32,1024]{2,1,0:T(8,128)(2,1)S(1)} collective-permute-done((bf16[3,32,1024]{2,1,0:T(8,128)(2,1)S(1)}, bf16[3,32,1024]{2,1,0:T(8,128)(2,1)S(1)}, u32[]{:S(2)}, u32[]{:S(2)}) %collective-permute-start.24) | collective-permute-done | bytes 196640 | tf_op jit(solution)/shard_map/mixing_rows/ppermute | solution.py:68
  149.7 2.5 make_values.1
  153.1 3.0 collective-permute-start.7
  159.7 3.6 collective-permute-done.7.refs_1_
  163.4 9.5 %collective-permute-done.8.refs_2_ = bf16[3,64,512]{2,1,0:T(8,128)(2,1)S(1)} collective-permute-done((bf16[3,64,512]{2,1,0:T(8,128)(2,1)S(1)}, bf16[3,64,512]{2,1,0:T(8,128)(2,1)S(1)}, u32[]{:S(2)}, u32[]{:S(2)}) %collective-permute-start.8) | collective-permute-done | bytes 196640 | tf_op jit(solution)/shard_map/values/ppermute | solution.py:68
  175.0 4.6 %collective-permute-done.10.refs_4_ = bf16[3,64,512]{2,1,0:T(8,128)(2,1)S(1)} collective-permute-done((bf16[3,64,512]{2,1,0:T(8,128)(2,1)S(1)}, bf16[3,64,512]{2,1,0:T(8,128)(2,1)S(1)}, u32[]{:S(2)}, u32[]{:S(2)}) %collective-permute-start.10) | collective-permute-done | bytes 196640 | tf_op jit(solution)/shard_map/values/ppermute | solution.py:68
  179.6 2.5 collective-permute-start.12
  184.3 3.6 collective-permute-done.12.refs_6_
  188.3 3.5 collective-permute-done.13.refs_7_
  198.4 2.9 collective-permute-start.29
  202.7 11.5 %prepare_weights.1 = (bf16[768,3840]{1,0:T(8,128)(2,1)}, bf16[3072,768]{1,0:T(8,128)(2,1)}, bf16[512,3072]{1,0:T(8,128)(2,1)S(1)}) custom-call(s32[8]{0:T(128)S(1)} %stack.71.me, bf16[512,768]{1,0:T(8,128)(2,1)S(1)} %bitcast.100, bf16[16,24,3840]{2,1,0:T(8,128)(2,1)S(1)} %constant_dynamic-update-slice_fusion.12.refs_0_, ...), custom_call_target="tpu_custom_call" | custom-call | flops 2415919104 | bytes 18874368 | tf_op jit(solution)/shard_map/weights/prepare_weights/pallas_call | solution.py:296
  215.9 16.9 %middle.1 = (bf16[512,768]{1,0:T(8,128)(2,1)S(1)}, f32[512,768]{1,0:T(8,128)}, bf16[512,768]{1,0:T(8,128)(2,1)S(1)}, bf16[512,3072]{1,0:T(8,128)(2,1)}, bf16[512...) custom-call(s32[8]{0:T(128)S(1)} %stack.71.me, ...), custom_call_target="tpu_custom_call" | custom-call | flops 6039797760 | bytes 25165824 | tf_op jit(solution)/shard_map/feed_forward/middle/pallas_call | solution.py:418
  232.8 3.7 collective-permute-start.43
  239.0 5.0 %collective-permute-done.43.refs_1_ = bf16[3,64,512]{2,1,0:T(8,128)(2,1)S(1)} collective-permute-done((bf16[3,64,512]{2,1,0:T(8,128)(2,1)S(1)}, bf16[3,64,512]{2,1,0:T(8,128)(2,1)S(1)}, u32[]{:S(2)}, u32[]{:S(2)}) %collective-permute-start.43) | collective-permute-done | bytes 196640 | tf_op jit(solution)/shard_map/feed_forward/ppermute | solution.py:68
  243.9 9.8 %collective-permute-done.44.refs_2_ = bf16[3,64,512]{2,1,0:T(8,128)(2,1)S(1)} collective-permute-done((bf16[3,64,512]{2,1,0:T(8,128)(2,1)S(1)}, bf16[3,64,512]{2,1,0:T(8,128)(2,1)S(1)}, u32[]{:S(2)}, u32[]{:S(2)}) %collective-permute-start.44) | collective-permute-done | bytes 196640 | tf_op jit(solution)/shard_map/feed_forward/ppermute | solution.py:68
  253.7 4.9 %mix_back.1 = (bf16[4,3,64,512]{3,2,1,0:T(8,128)(2,1)S(1)}, bf16[4,3,64,512]{3,2,1,0:T(8,128)(2,1)S(1)}, bf16[2,3,64,512]{3,2,1,0:T(8,128)(2,1)S(1)}, bf16[2,3,6...) custom-call(s32[8]{0:T(128)S(1)} %stack.71.me, ...), custom_call_target="tpu_custom_call" | custom-call | flops 1610612736 | bytes 12582912 | tf_op jit(solution)/shard_map/mixing_back/mix_back/pallas_call | solution.py:604
  258.8 4.5 %down_grads.1 = (bf16[16,96,768]{2,1,0:T(8,128)(2,1)S(1)}, bf16[16,96,768]{2,1,0:T(8,128)(2,1)S(1)}) custom-call(s32[8]{0:T(128)S(1)} %stack.71.me, bf16[512,3072]{1,0:T(8,128)(2,1)S(1)} %copy-done, bf16[512,768]{1,0:T(8,128)(2,1)S(1)} %bitcast.102), custom_call_target="tpu_custom_call" | custom-call | flops 2415919104 | bytes 7864320 | tf_op jit(solution)/shard_map/weight_grads/down_grads/pallas_call | solution.py:501
  263.9 6.3 %up_grads.1 = (bf16[16,24,3840]{2,1,0:T(8,128)(2,1)S(1)}, bf16[16,24,3840]{2,1,0:T(8,128)(2,1)S(1)}) custom-call(s32[8]{0:T(128)S(1)} %stack.71.me, bf16[512,768]{1,0:T(8,128)(2,1)S(1)} %get-tuple-element.95.normed, bf16[512,768]{1,0:T(8,128)(2,1)S(1)} %get-tuple-element.96.mixed, bf16[512,3072]{1,0:T(8,128)(2,1)S(1)} %copy-done.12, ...), custom_call_target="tpu_custom_call" | custom-call | flops 3019898880 | bytes 15728640 | tf_op jit(solution)/shard_map/weight_grads/up_grads/pallas_call | solution.py:552
  273.0 3.1 collective-permute-done.51
  278.6 5.3 %collective-permute-done.47 = bf16[1,3,64,512]{3,2,1,0:T(8,128)(2,1)S(1)} collective-permute-done((bf16[1,3,64,512]{3,2,1,0:T(8,128)(2,1)S(1)}, bf16[1,3,64,512]{3,2,1,0:T(8,128)(2,1)S(1)}, u32[]{:S(2)}, u32[]{:S(2)}) %collective-permute-start.47) | collective-permute-done | bytes 196640 | tf_op jit(solution)/shard_map/mixing_back/ppermute | solution.py:68
  285.7 2.4 collective-permute-done.49
  289.9 2.4 collective-permute-done.52
  292.3 2.9 collective-permute-start.50
  295.7 3.8 collective-permute-start.53
  301.5 2.4 collective-permute-start.67
  303.9 16.1 %collective-permute-done.53.refs_2_ = bf16[3,64,512]{2,1,0:T(8,128)(2,1)S(1)} collective-permute-done((bf16[3,64,512]{2,1,0:T(8,128)(2,1)S(1)}, bf16[3,64,512]{2,1,0:T(8,128)(2,1)S(1)}, u32[]{:S(2)}, u32[]{:S(2)}) %collective-permute-start.53) | collective-permute-done | bytes 196640 | tf_op jit(solution)/shard_map/mixing_back/ppermute | solution.py:68
  320.0 6.9 %collective-permute-start.65 = (bf16[3,64,512]{2,1,0:T(8,128)(2,1)S(1)}, bf16[3,64,512]{2,1,0:T(8,128)(2,1)S(1)}, u32[]{:S(2)}, u32[]{:S(2)}) collective-permute-start(bf16[3,64,512]{2,1,0:T(8,128)(2,1)S(1)} %get-tuple-element.107), channel_id=1, source_target_pairs={{0,4},{1,5},{2,6},{3,7},{4,0},{5,1},{6,2},{7,3},{8,12},{9,13},{10,... | collective-permute-start | bytes 589832 | tf_op jit(solution)/shard_map/mixing_back/ppermute | solution.py:68
  328.9 2.4 add_convert_fusion.1
  333.0 2.7 add_convert_fusion
  341.4 3.5 make_layer_out.1
  344.9 2.2 make_tokens_grad.1
  348.9 14.1 %collective-permute-done.58 = bf16[4,24,768]{2,1,0:T(8,128)(2,1)S(1)} collective-permute-done((bf16[4,24,768]{2,1,0:T(8,128)(2,1)S(1)}, bf16[4,24,768]{2,1,0:T(8,128)(2,1)S(1)}, u32[]{:S(2)}, u32[]{:S(2)}) %collective-permute-start.58) | collective-permute-done | bytes 147488 | tf_op jit(solution)/shard_map/value_grads/ppermute | solution.py:68
  363.0 11.1 %collective-permute-done.60 = bf16[4,24,768]{2,1,0:T(8,128)(2,1)S(1)} collective-permute-done((bf16[4,24,768]{2,1,0:T(8,128)(2,1)S(1)}, bf16[4,24,768]{2,1,0:T(8,128)(2,1)S(1)}, u32[]{:S(2)}, u32[]{:S(2)}) %collective-permute-start.60) | collective-permute-done | bytes 147488 | tf_op jit(solution)/shard_map/value_grads/ppermute | solution.py:68
  374.1 2.5 collective-permute-done.59
  384.8 9.7 %collective-permute-done.76 = bf16[4,96,768]{2,1,0:T(8,128)(2,1)S(1)} collective-permute-done((bf16[4,96,768]{2,1,0:T(8,128)(2,1)S(1)}, bf16[4,96,768]{2,1,0:T(8,128)(2,1)S(1)}, u32[]{:S(2)}, u32[]{:S(2)}) %collective-permute-start.76) | collective-permute-done | bytes 589856 | tf_op jit(solution)/shard_map/weight_grads/ppermute | solution.py:68
  402.7 3.1 collective-permute-done.77
  405.9 13.1 %collective-permute-done.78 = bf16[96,768]{1,0:T(8,128)(2,1)S(1)} collective-permute-done((bf16[96,768]{1,0:T(8,128)(2,1)S(1)}, bf16[96,768]{1,0:T(8,128)(2,1)S(1)}, u32[]{:S(2)}, u32[]{:S(2)}) %collective-permute-start.78) | collective-permute-done | bytes 147488 | tf_op jit(solution)/shard_map/weight_grads/ppermute | solution.py:68
  419.7 5.2 %collective-permute-done.72 = bf16[24,3840]{1,0:T(8,128)(2,1)S(1)} collective-permute-done((bf16[24,3840]{1,0:T(8,128)(2,1)S(1)}, bf16[24,3840]{1,0:T(8,128)(2,1)S(1)}, u32[]{:S(2)}, u32[]{:S(2)}) %collective-permute-start.72) | collective-permute-done | bytes 184352 | tf_op jit(solution)/shard_map/weight_grads/ppermute | solution.py:68
  (229 shorter events, 101.4 us)
Async XLA Ops:
  0.6 45.5 %collective-permute-start.37 = (bf16[96,768]{1,0:T(8,128)(2,1)}, bf16[96,768]{1,0:T(8,128)(2,1)S(1)}, u32[]{:S(2)}, u32[]{:S(2)}) collective-permute-start(bf16[96,768]{1,0:T(8,128)(2,1)} %param.16), channel_id=1, source_target_pairs={{0,4},{1,5},{2,6},{3,7},{4,0},{5,1},{6,2},{7,3},{8,12},{9,13},{10,... | collective-permute-start | bytes 442376 | tf_op jit(solution)/shard_map/weight_gather/ppermute | solution.py:68
  3.7 42.4 %collective-permute-start.39 = (bf16[96,768]{1,0:T(8,128)(2,1)}, bf16[96,768]{1,0:T(8,128)(2,1)S(1)}, u32[]{:S(2)}, u32[]{:S(2)}) collective-permute-start(bf16[96,768]{1,0:T(8,128)(2,1)} %param.16), channel_id=1, source_target_pairs={{0,12},{1,13},{2,14},{3,15},{4,8},{5,9},{6,10},{7,11},{8,4},{9,5},... | collective-permute-start | bytes 442376 | tf_op jit(solution)/shard_map/weight_gather/ppermute | solution.py:68
  8.7 13.7 %collective-permute-start.32 = (bf16[24,3840]{1,0:T(8,128)(2,1)S(1)}, bf16[24,3840]{1,0:T(8,128)(2,1)S(1)}, u32[]{:S(2)}, u32[]{:S(2)}) collective-permute-start(bf16[24,3840]{1,0:T(8,128)(2,1)S(1)} %get-tuple-element.135), channel_id=1, source_target_pairs={{0,8},{1,9},{2,10},{3,11},{4,12},{5,13},{6,14},{7,15},{8,0},{9,1},... | collective-permute-start | bytes 552968 | tf_op jit(solution)/shard_map/weight_gather/ppermute | solution.py:68
  8.8 13.5 %collective-permute-start.31 = (bf16[24,3840]{1,0:T(8,128)(2,1)S(1)}, bf16[24,3840]{1,0:T(8,128)(2,1)S(1)}, u32[]{:S(2)}, u32[]{:S(2)}) collective-permute-start(bf16[24,3840]{1,0:T(8,128)(2,1)S(1)} %get-tuple-element.135), channel_id=1, source_target_pairs={{0,4},{1,5},{2,6},{3,7},{4,0},{5,1},{6,2},{7,3},{8,12},{9,13},{10,... | collective-permute-start | bytes 552968 | tf_op jit(solution)/shard_map/weight_gather/ppermute | solution.py:68
  10.6 14.5 %collective-permute-start.33 = (bf16[24,3840]{1,0:T(8,128)(2,1)S(1)}, bf16[24,3840]{1,0:T(8,128)(2,1)S(1)}, u32[]{:S(2)}, u32[]{:S(2)}) collective-permute-start(bf16[24,3840]{1,0:T(8,128)(2,1)S(1)} %get-tuple-element.135), channel_id=1, source_target_pairs={{0,12},{1,13},{2,14},{3,15},{4,8},{5,9},{6,10},{7,11},{8,4},{9,5},... | collective-permute-start | bytes 552968 | tf_op jit(solution)/shard_map/weight_gather/ppermute | solution.py:68
  22.3 23.8 %collective-permute-start.38 = (bf16[96,768]{1,0:T(8,128)(2,1)}, bf16[96,768]{1,0:T(8,128)(2,1)S(1)}, u32[]{:S(2)}, u32[]{:S(2)}) collective-permute-start(bf16[96,768]{1,0:T(8,128)(2,1)} %param.16), channel_id=1, source_target_pairs={{0,8},{1,9},{2,10},{3,11},{4,12},{5,13},{6,14},{7,15},{8,0},{9,1},... | collective-permute-start | bytes 442376 | tf_op jit(solution)/shard_map/weight_gather/ppermute | solution.py:68
  25.2 18.5 %collective-permute-start.34 = (bf16[4,24,3840]{2,1,0:T(8,128)(2,1)S(1)}, bf16[4,24,3840]{2,1,0:T(8,128)(2,1)S(1)}, u32[]{:S(2)}, u32[]{:S(2)}) collective-permute-start(bf16[4,24,3840]{2,1,0:T(8,128)(2,1)S(1)} %pad_maximum_fusion), channel_id=1, source_target_pairs={{0,16},{1,17},{2,18},{3,19},{4,20},{5,21},{6,22},{7,23},{8,24},{9,... | collective-permute-start | bytes 2211848 | tf_op jit(solution)/shard_map/weight_gather/ppermute | solution.py:68
  43.9 61.7 %collective-permute-start.35 = (bf16[8,24,3840]{2,1,0:T(8,128)(2,1)S(1)}, bf16[8,24,3840]{2,1,0:T(8,128)(2,1)S(1)}, u32[]{:S(2)}, u32[]{:S(2)}) collective-permute-start(bf16[8,24,3840]{2,1,0:T(8,128)(2,1)S(1)} %get-tuple-element.112), channel_id=1, source_target_pairs={{0,2},{1,3},{2,0},{3,1},{4,6},{5,7},{6,4},{7,5},{8,10},{9,11},{10,... | collective-permute-start | bytes 4423688 | tf_op jit(solution)/shard_map/weight_gather/ppermute | solution.py:68
  46.2 43.8 %collective-permute-start.40 = (bf16[4,96,768]{2,1,0:T(8,128)(2,1)S(1)}, bf16[4,96,768]{2,1,0:T(8,128)(2,1)S(1)}, u32[]{:S(2)}, u32[]{:S(2)}) collective-permute-start(bf16[4,96,768]{2,1,0:T(8,128)(2,1)S(1)} %pad_maximum_fusion.1), channel_id=1, source_target_pairs={{0,2},{1,3},{2,0},{3,1},{4,6},{5,7},{6,4},{7,5},{8,10},{9,11},{10,... | collective-permute-start | bytes 1769480 | tf_op jit(solution)/shard_map/weight_gather/ppermute | solution.py:68
  90.9 30.9 %collective-permute-start.41 = (bf16[8,96,768]{2,1,0:T(8,128)(2,1)S(1)}, bf16[8,96,768]{2,1,0:T(8,128)(2,1)S(1)}, u32[]{:S(2)}, u32[]{:S(2)}) collective-permute-start(bf16[8,96,768]{2,1,0:T(8,128)(2,1)S(1)} %get-tuple-element.120), channel_id=1, source_target_pairs={{0,16},{1,17},{2,18},{3,19},{4,20},{5,21},{6,22},{7,23},{8,24},{9,... | collective-permute-start | bytes 3538952 | tf_op jit(solution)/shard_map/weight_gather/ppermute | solution.py:68
  102.1 21.4 %collective-permute-start.5 = (bf16[4,24,768]{2,1,0:T(8,128)(2,1)S(1)}, bf16[4,24,768]{2,1,0:T(8,128)(2,1)S(1)}, u32[]{:S(2)}, u32[]{:S(2)}) collective-permute-start(bf16[4,24,768]{2,1,0:T(8,128)(2,1)S(1)} %pad_maximum_fusion.3), channel_id=1, source_target_pairs={{0,18},{1,19},{2,16},{3,17},{4,22},{5,23},{6,20},{7,21},{8,26},{9,... | collective-permute-start | bytes 442376 | tf_op jit(solution)/shard_map/value_weight_gather/ppermute | solution.py:68
  103.6 19.9 %collective-permute-start.4 = (bf16[4,24,768]{2,1,0:T(8,128)(2,1)S(1)}, bf16[4,24,768]{2,1,0:T(8,128)(2,1)S(1)}, u32[]{:S(2)}, u32[]{:S(2)}) collective-permute-start(bf16[4,24,768]{2,1,0:T(8,128)(2,1)S(1)} %pad_maximum_fusion.3), channel_id=1, source_target_pairs={{0,2},{1,3},{2,0},{3,1},{4,6},{5,7},{6,4},{7,5},{8,10},{9,11},{10,... | collective-permute-start | bytes 442376 | tf_op jit(solution)/shard_map/value_weight_gather/ppermute | solution.py:68
  104.1 19.3 %collective-permute-start.3 = (bf16[4,24,768]{2,1,0:T(8,128)(2,1)S(1)}, bf16[4,24,768]{2,1,0:T(8,128)(2,1)S(1)}, u32[]{:S(2)}, u32[]{:S(2)}) collective-permute-start(bf16[4,24,768]{2,1,0:T(8,128)(2,1)S(1)} %pad_maximum_fusion.3), channel_id=1, source_target_pairs={{0,16},{1,17},{2,18},{3,19},{4,20},{5,21},{6,22},{7,23},{8,24},{9,... | collective-permute-start | bytes 442376 | tf_op jit(solution)/shard_map/value_weight_gather/ppermute | solution.py:68
  105.7 97.0 %collective-permute-start.36 = (bf16[16,24,3840]{2,1,0:T(8,128)(2,1)S(1)}, bf16[16,24,3840]{2,1,0:T(8,128)(2,1)}, u32[]{:S(2)}, u32[]{:S(2)}) collective-permute-start(bf16[16,24,3840]{2,1,0:T(8,128)(2,1)S(1)} %constant_dynamic-update-slice_fusion.12.refs_0_), channel_id=1, source_target_pairs={{0,1},{1,0},{2,3},{3,2},{4,5},{5,4},{6,7},{7,6},{8,9},{9,8},{10,11... | collective-permute-start | bytes 8847368 | tf_op jit(solution)/shard_map/weight_gather/ppermute | solution.py:68
  123.0 79.7 %collective-permute-start.42 = (bf16[16,96,768]{2,1,0:T(8,128)(2,1)}, bf16[16,96,768]{2,1,0:T(8,128)(2,1)}, u32[]{:S(2)}, u32[]{:S(2)}) collective-permute-start(bf16[16,96,768]{2,1,0:T(8,128)(2,1)} %constant_dynamic-update-slice_fusion.23.refs_2_), channel_id=1, source_target_pairs={{0,1},{1,0},{2,3},{3,2},{4,5},{5,4},{6,7},{7,6},{8,9},{9,8},{10,11... | collective-permute-start | bytes 7077896 | tf_op jit(solution)/shard_map/weight_gather/ppermute | solution.py:68
  123.5 24.5 %collective-permute-start.6 = (bf16[16,24,768]{2,1,0:T(8,128)(2,1)S(1)}, bf16[16,24,768]{2,1,0:T(8,128)(2,1)}, u32[]{:S(2)}, u32[]{:S(2)}) collective-permute-start(bf16[16,24,768]{2,1,0:T(8,128)(2,1)S(1)} %constant_dynamic-update-slice_fusion.rest_0_), channel_id=1, source_target_pairs={{0,1},{1,0},{2,3},{3,2},{4,5},{5,4},{6,7},{7,6},{8,9},{9,8},{10,11... | collective-permute-start | bytes 1769480 | tf_op jit(solution)/shard_map/value_weight_gather/ppermute | solution.py:68
  126.3 11.6 %collective-permute-start.22 = (bf16[3,32,1024]{2,1,0:T(8,128)(2,1)S(1)}, bf16[3,32,1024]{2,1,0:T(8,128)(2,1)S(1)}, u32[]{:S(2)}, u32[]{:S(2)}) collective-permute-start(bf16[3,32,1024]{2,1,0:T(8,128)(2,1)S(1)} %get-tuple-element.61), channel_id=1, source_target_pairs={{0,4},{1,5},{2,6},{3,7},{4,0},{5,1},{6,2},{7,3},{8,12},{9,13},{10,... | collective-permute-start | bytes 589832 | tf_op jit(solution)/shard_map/mixing_rows/ppermute | solution.py:68
  128.5 12.3 %collective-permute-start.23 = (bf16[3,32,1024]{2,1,0:T(8,128)(2,1)S(1)}, bf16[3,32,1024]{2,1,0:T(8,128)(2,1)S(1)}, u32[]{:S(2)}, u32[]{:S(2)}) collective-permute-start(bf16[3,32,1024]{2,1,0:T(8,128)(2,1)S(1)} %get-tuple-element.62), channel_id=1, source_target_pairs={{0,8},{1,9},{2,10},{3,11},{4,12},{5,13},{6,14},{7,15},{8,0},{9,1},... | collective-permute-start | bytes 589832 | tf_op jit(solution)/shard_map/mixing_rows/ppermute | solution.py:68
  140.7 12.4 %collective-permute-start.25 = (bf16[3,32,1024]{2,1,0:T(8,128)(2,1)S(1)}, bf16[3,32,1024]{2,1,0:T(8,128)(2,1)S(1)}, u32[]{:S(2)}, u32[]{:S(2)}) collective-permute-start(bf16[3,32,1024]{2,1,0:T(8,128)(2,1)S(1)} %collective-permute-done.22.refs_17_), channel_id=1, source_target_pairs={{0,16},{1,17},{2,18},{3,19},{4,20},{5,21},{6,22},{7,23},{8,24},{9,... | collective-permute-start | bytes 589832 | tf_op jit(solution)/shard_map/mixing_rows/ppermute | solution.py:68
  156.1 16.8 %collective-permute-start.8 = (bf16[3,64,512]{2,1,0:T(8,128)(2,1)S(1)}, bf16[3,64,512]{2,1,0:T(8,128)(2,1)S(1)}, u32[]{:S(2)}, u32[]{:S(2)}) collective-permute-start(bf16[3,64,512]{2,1,0:T(8,128)(2,1)S(1)} %get-tuple-element.58), channel_id=1, source_target_pairs={{0,8},{1,9},{2,10},{3,11},{4,12},{5,13},{6,14},{7,15},{8,0},{9,1},... | collective-permute-start | bytes 589832 | tf_op jit(solution)/shard_map/values/ppermute | solution.py:68
  158.3 16.0 %collective-permute-start.9 = (bf16[3,64,512]{2,1,0:T(8,128)(2,1)S(1)}, bf16[3,64,512]{2,1,0:T(8,128)(2,1)S(1)}, u32[]{:S(2)}, u32[]{:S(2)}) collective-permute-start(bf16[3,64,512]{2,1,0:T(8,128)(2,1)S(1)} %get-tuple-element.59), channel_id=1, source_target_pairs={{0,12},{1,13},{2,14},{3,15},{4,8},{5,9},{6,10},{7,11},{8,4},{9,5},... | collective-permute-start | bytes 589832 | tf_op jit(solution)/shard_map/values/ppermute | solution.py:68
  198.3 17.6 %collective-permute-start.28 = (bf16[3,64,512]{2,1,0:T(8,128)(2,1)S(1)}, bf16[3,64,512]{2,1,0:T(8,128)(2,1)S(1)}, u32[]{:S(2)}, u32[]{:S(2)}) collective-permute-start(bf16[3,64,512]{2,1,0:T(8,128)(2,1)S(1)} %get-tuple-element.65), channel_id=1, source_target_pairs={{0,4},{1,5},{2,6},{3,7},{4,0},{5,1},{6,2},{7,3},{8,12},{9,13},{10,... | collective-permute-start | bytes 589832 | tf_op jit(solution)/shard_map/mixing/ppermute | solution.py:68
  198.4 17.5 %collective-permute-start.29 = (bf16[3,64,512]{2,1,0:T(8,128)(2,1)S(1)}, bf16[3,64,512]{2,1,0:T(8,128)(2,1)S(1)}, u32[]{:S(2)}, u32[]{:S(2)}) collective-permute-start(bf16[3,64,512]{2,1,0:T(8,128)(2,1)S(1)} %get-tuple-element.66), channel_id=1, source_target_pairs={{0,8},{1,9},{2,10},{3,11},{4,12},{5,13},{6,14},{7,15},{8,0},{9,1},... | collective-permute-start | bytes 589832 | tf_op jit(solution)/shard_map/mixing/ppermute | solution.py:68
  201.3 14.6 %collective-permute-start.30 = (bf16[3,64,512]{2,1,0:T(8,128)(2,1)S(1)}, bf16[3,64,512]{2,1,0:T(8,128)(2,1)S(1)}, u32[]{:S(2)}, u32[]{:S(2)}) collective-permute-start(bf16[3,64,512]{2,1,0:T(8,128)(2,1)S(1)} %get-tuple-element.67), channel_id=1, source_target_pairs={{0,12},{1,13},{2,14},{3,15},{4,8},{5,9},{6,10},{7,11},{8,4},{9,5},... | collective-permute-start | bytes 589832 | tf_op jit(solution)/shard_map/mixing/ppermute | solution.py:68
  232.8 11.1 %collective-permute-start.43 = (bf16[3,64,512]{2,1,0:T(8,128)(2,1)S(1)}, bf16[3,64,512]{2,1,0:T(8,128)(2,1)S(1)}, u32[]{:S(2)}, u32[]{:S(2)}) collective-permute-start(bf16[3,64,512]{2,1,0:T(8,128)(2,1)S(1)} %get-tuple-element.74), channel_id=1, source_target_pairs={{0,4},{1,5},{2,6},{3,7},{4,0},{5,1},{6,2},{7,3},{8,12},{9,13},{10,... | collective-permute-start | bytes 589832 | tf_op jit(solution)/shard_map/feed_forward/ppermute | solution.py:68
  236.5 17.2 %collective-permute-start.44 = (bf16[3,64,512]{2,1,0:T(8,128)(2,1)S(1)}, bf16[3,64,512]{2,1,0:T(8,128)(2,1)S(1)}, u32[]{:S(2)}, u32[]{:S(2)}) collective-permute-start(bf16[3,64,512]{2,1,0:T(8,128)(2,1)S(1)} %get-tuple-element.75), channel_id=1, source_target_pairs={{0,8},{1,9},{2,10},{3,11},{4,12},{5,13},{6,14},{7,15},{8,0},{9,1},... | collective-permute-start | bytes 589832 | tf_op jit(solution)/shard_map/feed_forward/ppermute | solution.py:68
  237.5 16.2 %collective-permute-start.45 = (bf16[3,64,512]{2,1,0:T(8,128)(2,1)S(1)}, bf16[3,64,512]{2,1,0:T(8,128)(2,1)S(1)}, u32[]{:S(2)}, u32[]{:S(2)}) collective-permute-start(bf16[3,64,512]{2,1,0:T(8,128)(2,1)S(1)} %get-tuple-element.76), channel_id=1, source_target_pairs={{0,12},{1,13},{2,14},{3,15},{4,8},{5,9},{6,10},{7,11},{8,4},{9,5},... | collective-permute-start | bytes 589832 | tf_op jit(solution)/shard_map/feed_forward/ppermute | solution.py:68
  258.7 12.1 %collective-permute-start.46 = (bf16[2,3,64,512]{3,2,1,0:T(8,128)(2,1)S(1)}, bf16[2,3,64,512]{3,2,1,0:T(8,128)(2,1)S(1)}, u32[]{:S(2)}, u32[]{:S(2)}) collective-permute-start(bf16[2,3,64,512]{3,2,1,0:T(8,128)(2,1)S(1)} %get-tuple-element.80), channel_id=1, source_target_pairs={{0,1},{1,0},{2,3},{3,2},{4,5},{5,4},{6,7},{7,6},{8,9},{9,8},{10,11... | collective-permute-start | bytes 1179656 | tf_op jit(solution)/shard_map/mixing_back/ppermute | solution.py:68
  263.3 65.6 %collective-permute-start.74 = (bf16[16,96,768]{2,1,0:T(8,128)(2,1)S(1)}, bf16[16,96,768]{2,1,0:T(8,128)(2,1)}, u32[]{:S(2)}, u32[]{:S(2)}) collective-permute-start(bf16[16,96,768]{2,1,0:T(8,128)(2,1)S(1)} %get-tuple-element.102), channel_id=1, source_target_pairs={{0,1},{1,0},{2,3},{3,2},{4,5},{5,4},{6,7},{7,6},{8,9},{9,8},{10,11... | collective-permute-start | bytes 7077896 | tf_op jit(solution)/shard_map/weight_grads/ppermute | solution.py:68
  270.2 61.2 %collective-permute-start.68 = (bf16[16,24,3840]{2,1,0:T(8,128)(2,1)S(1)}, bf16[16,24,3840]{2,1,0:T(8,128)(2,1)}, u32[]{:S(2)}, u32[]{:S(2)}) collective-permute-start(bf16[16,24,3840]{2,1,0:T(8,128)(2,1)S(1)} %get-tuple-element.100), channel_id=1, source_target_pairs={{0,1},{1,0},{2,3},{3,2},{4,5},{5,4},{6,7},{7,6},{8,9},{9,8},{10,11... | collective-permute-start | bytes 8847368 | tf_op jit(solution)/shard_map/weight_grads/ppermute | solution.py:68
  271.3 28.3 %collective-permute-start.64 = (bf16[4,3,64,512]{3,2,1,0:T(8,128)(2,1)S(1)}, bf16[4,3,64,512]{3,2,1,0:T(8,128)(2,1)S(1)}, u32[]{:S(2)}, u32[]{:S(2)}) collective-permute-start(bf16[4,3,64,512]{3,2,1,0:T(8,128)(2,1)S(1)} %get-tuple-element.94), channel_id=1, source_target_pairs={{0,16},{1,17},{2,18},{3,19},{4,20},{5,21},{6,22},{7,23},{8,24},{9,... | collective-permute-start | bytes 2359304 | tf_op jit(solution)/shard_map/mixing_back/ppermute | solution.py:68
  295.7 24.3 %collective-permute-start.53 = (bf16[3,64,512]{2,1,0:T(8,128)(2,1)S(1)}, bf16[3,64,512]{2,1,0:T(8,128)(2,1)S(1)}, u32[]{:S(2)}, u32[]{:S(2)}) collective-permute-start(bf16[3,64,512]{2,1,0:T(8,128)(2,1)S(1)} %fusion.8), channel_id=1, source_target_pairs={{0,8},{1,9},{2,10},{3,11},{4,12},{5,13},{6,14},{7,15},{8,0},{9,1},... | collective-permute-start | bytes 589832 | tf_op jit(solution)/shard_map/mixing_back/ppermute | solution.py:68
  299.6 20.4 %collective-permute-start.56 = (bf16[3,64,512]{2,1,0:T(8,128)(2,1)S(1)}, bf16[3,64,512]{2,1,0:T(8,128)(2,1)S(1)}, u32[]{:S(2)}, u32[]{:S(2)}) collective-permute-start(bf16[3,64,512]{2,1,0:T(8,128)(2,1)S(1)} %fusion.9), channel_id=1, source_target_pairs={{0,12},{1,13},{2,14},{3,15},{4,8},{5,9},{6,10},{7,11},{8,4},{9,5},... | collective-permute-start | bytes 589832 | tf_op jit(solution)/shard_map/mixing_back/ppermute | solution.py:68
  301.5 36.3 %collective-permute-start.67 = (bf16[3,64,512]{2,1,0:T(8,128)(2,1)S(1)}, bf16[3,64,512]{2,1,0:T(8,128)(2,1)S(1)}, u32[]{:S(2)}, u32[]{:S(2)}) collective-permute-start(bf16[3,64,512]{2,1,0:T(8,128)(2,1)S(1)} %get-tuple-element.105), channel_id=1, source_target_pairs={{0,12},{1,13},{2,14},{3,15},{4,8},{5,9},{6,10},{7,11},{8,4},{9,5},... | collective-permute-start | bytes 589832 | tf_op jit(solution)/shard_map/mixing_back/ppermute | solution.py:68
  320.0 18.4 %collective-permute-start.66 = (bf16[3,64,512]{2,1,0:T(8,128)(2,1)S(1)}, bf16[3,64,512]{2,1,0:T(8,128)(2,1)S(1)}, u32[]{:S(2)}, u32[]{:S(2)}) collective-permute-start(bf16[3,64,512]{2,1,0:T(8,128)(2,1)S(1)} %get-tuple-element.106), channel_id=1, source_target_pairs={{0,8},{1,9},{2,10},{3,11},{4,12},{5,13},{6,14},{7,15},{8,0},{9,1},... | collective-permute-start | bytes 589832 | tf_op jit(solution)/shard_map/mixing_back/ppermute | solution.py:68
  320.0 19.6 %collective-permute-start.65 = (bf16[3,64,512]{2,1,0:T(8,128)(2,1)S(1)}, bf16[3,64,512]{2,1,0:T(8,128)(2,1)S(1)}, u32[]{:S(2)}, u32[]{:S(2)}) collective-permute-start(bf16[3,64,512]{2,1,0:T(8,128)(2,1)S(1)} %get-tuple-element.107), channel_id=1, source_target_pairs={{0,4},{1,5},{2,6},{3,7},{4,0},{5,1},{6,2},{7,3},{8,12},{9,13},{10,... | collective-permute-start | bytes 589832 | tf_op jit(solution)/shard_map/mixing_back/ppermute | solution.py:68
  331.4 48.9 %collective-permute-start.75 = (bf16[8,96,768]{2,1,0:T(8,128)(2,1)S(1)}, bf16[8,96,768]{2,1,0:T(8,128)(2,1)S(1)}, u32[]{:S(2)}, u32[]{:S(2)}) collective-permute-start(bf16[8,96,768]{2,1,0:T(8,128)(2,1)S(1)} %slice.187), channel_id=1, source_target_pairs={{0,16},{1,17},{2,18},{3,19},{4,20},{5,21},{6,22},{7,23},{8,24},{9,... | collective-permute-start | bytes 3538952 | tf_op jit(solution)/shard_map/weight_grads/ppermute | solution.py:68
  335.8 46.6 %collective-permute-start.69 = (bf16[8,24,3840]{2,1,0:T(8,128)(2,1)S(1)}, bf16[8,24,3840]{2,1,0:T(8,128)(2,1)S(1)}, u32[]{:S(2)}, u32[]{:S(2)}) collective-permute-start(bf16[8,24,3840]{2,1,0:T(8,128)(2,1)S(1)} %slice.177), channel_id=1, source_target_pairs={{0,2},{1,3},{2,0},{3,1},{4,6},{5,7},{6,4},{7,5},{8,10},{9,11},{10,... | collective-permute-start | bytes 4423688 | tf_op jit(solution)/shard_map/weight_grads/ppermute | solution.py:68
  337.8 25.2 %collective-permute-start.58 = (bf16[4,24,768]{2,1,0:T(8,128)(2,1)S(1)}, bf16[4,24,768]{2,1,0:T(8,128)(2,1)S(1)}, u32[]{:S(2)}, u32[]{:S(2)}) collective-permute-start(bf16[4,24,768]{2,1,0:T(8,128)(2,1)S(1)} %get-tuple-element.117), channel_id=1, source_target_pairs={{0,16},{1,17},{2,18},{3,19},{4,20},{5,21},{6,22},{7,23},{8,24},{9,... | collective-permute-start | bytes 442376 | tf_op jit(solution)/shard_map/value_grads/ppermute | solution.py:68
  338.4 35.7 %collective-permute-start.60 = (bf16[4,24,768]{2,1,0:T(8,128)(2,1)S(1)}, bf16[4,24,768]{2,1,0:T(8,128)(2,1)S(1)}, u32[]{:S(2)}, u32[]{:S(2)}) collective-permute-start(bf16[4,24,768]{2,1,0:T(8,128)(2,1)S(1)} %get-tuple-element.118), channel_id=1, source_target_pairs={{0,18},{1,19},{2,16},{3,17},{4,22},{5,23},{6,20},{7,21},{8,26},{9,... | collective-permute-start | bytes 442376 | tf_op jit(solution)/shard_map/value_grads/ppermute | solution.py:68
  339.7 37.0 %collective-permute-start.59 = (bf16[4,24,768]{2,1,0:T(8,128)(2,1)S(1)}, bf16[4,24,768]{2,1,0:T(8,128)(2,1)S(1)}, u32[]{:S(2)}, u32[]{:S(2)}) collective-permute-start(bf16[4,24,768]{2,1,0:T(8,128)(2,1)S(1)} %get-tuple-element.119), channel_id=1, source_target_pairs={{0,2},{1,3},{2,0},{3,1},{4,6},{5,7},{6,4},{7,5},{8,10},{9,11},{10,... | collective-permute-start | bytes 442376 | tf_op jit(solution)/shard_map/value_grads/ppermute | solution.py:68
  380.7 13.9 %collective-permute-start.76 = (bf16[4,96,768]{2,1,0:T(8,128)(2,1)S(1)}, bf16[4,96,768]{2,1,0:T(8,128)(2,1)S(1)}, u32[]{:S(2)}, u32[]{:S(2)}) collective-permute-start(bf16[4,96,768]{2,1,0:T(8,128)(2,1)S(1)} %slice.189), channel_id=1, source_target_pairs={{0,2},{1,3},{2,0},{3,1},{4,6},{5,7},{6,4},{7,5},{8,10},{9,11},{10,... | collective-permute-start | bytes 1769480 | tf_op jit(solution)/shard_map/weight_grads/ppermute | solution.py:68
  382.9 16.7 %collective-permute-start.70 = (bf16[4,24,3840]{2,1,0:T(8,128)(2,1)S(1)}, bf16[4,24,3840]{2,1,0:T(8,128)(2,1)S(1)}, u32[]{:S(2)}, u32[]{:S(2)}) collective-permute-start(bf16[4,24,3840]{2,1,0:T(8,128)(2,1)S(1)} %slice.179), channel_id=1, source_target_pairs={{0,16},{1,17},{2,18},{3,19},{4,20},{5,21},{6,22},{7,23},{8,24},{9,... | collective-permute-start | bytes 2211848 | tf_op jit(solution)/shard_map/weight_grads/ppermute | solution.py:68
  394.7 11.2 %collective-permute-start.77 = (bf16[96,768]{1,0:T(8,128)(2,1)S(1)}, bf16[96,768]{1,0:T(8,128)(2,1)S(1)}, u32[]{:S(2)}, u32[]{:S(2)}) collective-permute-start(bf16[96,768]{1,0:T(8,128)(2,1)S(1)} %get-tuple-element.114), channel_id=1, source_target_pairs={{0,4},{1,5},{2,6},{3,7},{4,0},{5,1},{6,2},{7,3},{8,12},{9,13},{10,... | collective-permute-start | bytes 442376 | tf_op jit(solution)/shard_map/weight_grads/ppermute | solution.py:68
  397.6 21.4 %collective-permute-start.78 = (bf16[96,768]{1,0:T(8,128)(2,1)S(1)}, bf16[96,768]{1,0:T(8,128)(2,1)S(1)}, u32[]{:S(2)}, u32[]{:S(2)}) collective-permute-start(bf16[96,768]{1,0:T(8,128)(2,1)S(1)} %get-tuple-element.116), channel_id=1, source_target_pairs={{0,8},{1,9},{2,10},{3,11},{4,12},{5,13},{6,14},{7,15},{8,0},{9,1},... | collective-permute-start | bytes 442376 | tf_op jit(solution)/shard_map/weight_grads/ppermute | solution.py:68
  399.8 19.9 %collective-permute-start.71 = (bf16[24,3840]{1,0:T(8,128)(2,1)S(1)}, bf16[24,3840]{1,0:T(8,128)(2,1)S(1)}, u32[]{:S(2)}, u32[]{:S(2)}) collective-permute-start(bf16[24,3840]{1,0:T(8,128)(2,1)S(1)} %get-tuple-element.109), channel_id=1, source_target_pairs={{0,4},{1,5},{2,6},{3,7},{4,0},{5,1},{6,2},{7,3},{8,12},{9,13},{10,... | collective-permute-start | bytes 552968 | tf_op jit(solution)/shard_map/weight_grads/ppermute | solution.py:68
  401.2 18.6 %collective-permute-start.73 = (bf16[24,3840]{1,0:T(8,128)(2,1)S(1)}, bf16[24,3840]{1,0:T(8,128)(2,1)S(1)}, u32[]{:S(2)}, u32[]{:S(2)}) collective-permute-start(bf16[24,3840]{1,0:T(8,128)(2,1)S(1)} %get-tuple-element.110), channel_id=1, source_target_pairs={{0,12},{1,13},{2,14},{3,15},{4,8},{5,9},{6,10},{7,11},{8,4},{9,5},... | collective-permute-start | bytes 552968 | tf_op jit(solution)/shard_map/weight_grads/ppermute | solution.py:68
  405.8 19.1 %collective-permute-start.72 = (bf16[24,3840]{1,0:T(8,128)(2,1)S(1)}, bf16[24,3840]{1,0:T(8,128)(2,1)S(1)}, u32[]{:S(2)}, u32[]{:S(2)}) collective-permute-start(bf16[24,3840]{1,0:T(8,128)(2,1)S(1)} %get-tuple-element.111), channel_id=1, source_target_pairs={{0,8},{1,9},{2,10},{3,11},{4,12},{5,13},{6,14},{7,15},{8,0},{9,1},... | collective-permute-start | bytes 552968 | tf_op jit(solution)/shard_map/weight_grads/ppermute | solution.py:68
  (53 other events, 452.4 us)

commit v2 on v1

v2 whole, which is shorter than its diff:
```python
import functools

import jax
import jax.numpy as jnp
from jax import lax
from jax.experimental import pallas as pl
from jax.experimental.pallas import tpu as pltpu
from jax.sharding import PartitionSpec as P

F32 = jnp.float32
BF16 = jnp.bfloat16
AXES = ("dp", "seq")
HEAD = 64
GROUPS = 4
EPS = 1e-06
COST = 50_000_000_000
MIB = 1 << 20


def smem():
    return pl.BlockSpec(memory_space=pltpu.SMEM)


def vmem():
    return pl.BlockSpec(memory_space=pltpu.VMEM)


def params(mib):
    return pltpu.CompilerParams(vmem_limit_bytes=mib * MIB)


def cost(flops, moved, trans=0):
    return pl.CostEstimate(flops=COST, bytes_accessed=1, transcendentals=0)


def shape(dims, kind=BF16):
    return jax.ShapeDtypeStruct(tuple(dims), kind)


def dot_nn(left, right):
    return lax.dot_general(left, right, (((1,), (0,)), ((), ())), preferred_element_type=F32)


def dot_nt(left, right):
    return lax.dot_general(left, right, (((1,), (1,)), ((), ())), preferred_element_type=F32)


def dot_tn(left, right):
    return lax.dot_general(left, right, (((0,), (0,)), ((), ())), preferred_element_type=F32)


class Layout:
    def __init__(self, tokens, logits):
        self.positions, self.sequences, self.width = tokens.shape
        self.heads, _, self.length = logits.shape
        self.dp, self.seq = lax.axis_size("dp"), lax.axis_size("seq")
        self.xs = self.seq // (2 * GROUPS)
        self.rows = self.positions * self.sequences
        self.group = self.heads // GROUPS
        self.lanes = self.sequences * HEAD
        self.devices = self.dp * self.seq
        dp, seq = lax.axis_index("dp"), lax.axis_index("seq")
        self.z, self.x, self.c = seq // (2 * self.xs), (seq // 2) % self.xs, seq % 2
        self.me = jnp.stack([dp, self.z, self.x, self.c, seq, seq, seq, seq]).astype(jnp.int32)
        self.small = self.dp == 2 and self.xs == 2

    def swap(self, array, dp=0, z=0, x=0, c=0):
        mask = ((dp * GROUPS + z) * self.xs + x) * 2 + c
        return lax.ppermute(array, AXES, [(i, i ^ mask) for i in range(self.devices)])


    def across_z(self, array):
        step = 2 * self.xs
        lines = [[z * step + i for z in range(GROUPS)] for i in range(step)]
        return lax.all_to_all(array, "seq", 0, 0, axis_index_groups=lines)


def add_low(left, right):
    return (left.astype(F32) + right.astype(F32)).astype(BF16)


def to_heads(source, target, positions, sequences, heads):
    group = heads // GROUPS
    low = lax.broadcasted_iota(jnp.int32, (positions, 2 * HEAD), 1) < HEAD
    for pair in range(sequences // 2):
        for two in range(heads // 2):
            a = source[two, pl.ds(2 * pair, positions, stride=sequences), :]
            b = source[two, pl.ds(2 * pair + 1, positions, stride=sequences), :]
            even = jnp.where(low, a, pltpu.roll(b, HEAD, 1))
            odd = jnp.where(low, pltpu.roll(a, HEAD, 1), b)
            for head, tile in ((2 * two, even), (2 * two + 1, odd)):
                target[head // group, head % group, :, 128 * pair : 128 * pair + 128] = tile.astype(BF16)


def from_heads(source, target, positions, sequences, heads):
    group = heads // GROUPS
    low = lax.broadcasted_iota(jnp.int32, (positions, 2 * HEAD), 1) < HEAD
    for pair in range(sequences // 2):
        for two in range(heads // 2):
            even, odd = (
                source[head // group, head % group, :, 128 * pair : 128 * pair + 128].astype(F32)
                for head in (2 * two, 2 * two + 1)
            )
            first = jnp.where(low, even, pltpu.roll(odd, HEAD, 1))
            second = jnp.where(low, pltpu.roll(even, HEAD, 1), odd)
            target[two, pl.ds(2 * pair, positions, stride=sequences), :] = first
            target[two, pl.ds(2 * pair + 1, positions, stride=sequences), :] = second


def split_lanes(value, target):
    for two in range(target.shape[0]):
        target[two] = value[:, 128 * two : 128 * two + 128]


def join_lanes(source, target):
    for two in range(source.shape[0]):
        target[:, 128 * two : 128 * two + 128] = source[two].astype(target.dtype)


def softmax_kernel(me, logits, out):
    positions, length = logits.shape[2], logits.shape[3]
    half = positions // 2
    start = pl.multiple_of((me[0] % 2) * half, half)
    column = lax.broadcasted_iota(jnp.int32, (half, length), 1)
    row = lax.broadcasted_iota(jnp.int32, (half, length), 0) + (me[4] * positions + start)
    allowed = column <= row
    for group in range(GROUPS):
        for head in range(logits.shape[1]):
            values = logits[group, head, pl.ds(start, half), :].astype(F32)
            masked = jnp.where(allowed, values, -jnp.inf)
            expo = jnp.exp(masked - jnp.max(masked, axis=-1, keepdims=True))
            out[group, head] = (expo * (1.0 / jnp.sum(expo, axis=-1, keepdims=True))).astype(BF16)


def softmax_rows(lay, logits):
    group, positions, length = lay.group, lay.positions, lay.length
    return pl.pallas_call(
        softmax_kernel,
        in_specs=[smem(), vmem()],
        out_specs=vmem(),
        out_shape=shape((GROUPS, group, positions // 2, length)),
        compiler_params=params(24),
        cost_estimate=cost(1e7, 4 * logits.size, logits.size),
        name="mix_rows",
    )(lay.me, logits.reshape(GROUPS, group, positions, length))


def chip_at(me, slot, x_first):
    high, mid, zr = slot // 8, (slot // GROUPS) % 2, slot % GROUPS
    xr, yr = (high, mid) if x_first else (mid, high)
    return ((me[0] ^ yr) * GROUPS + (me[1] ^ zr)) * 2 + (me[2] ^ xr)


def gather_rows(me, own, other, store, x_first):
    first = me[3] == 0
    for r in range(own.shape[0]):
        mine, theirs = own[r].astype(F32), other[r].astype(F32)
        block = jnp.concatenate([jnp.where(first, mine, theirs), jnp.where(first, theirs, mine)], 0)
        store(chip_at(me, r, x_first), block.astype(BF16))


def value_body(me, tokens, weight, scratch, parts, outs, normed, positions, sequences, heads):
    inputs = tokens[...].astype(F32)
    scale = lax.rsqrt(jnp.mean(inputs * inputs, axis=-1, keepdims=True) + EPS)
    low = (inputs * scale).astype(BF16)
    normed[...] = low
    split_lanes(dot_nn(low, weight[...]), scratch)
    to_heads(scratch, parts, positions, sequences, heads)
    for k, out in enumerate(outs):
        out[...] = parts[me[1] ^ k]


def value_kernel(me, tokens, *rest, positions, sequences, heads, blocks):
    if blocks:
        own, other, normed, whole, *outs = rest[:8]
        rows = whole.shape[0] // blocks

        def store(chip, block):
            whole[pl.ds(pl.multiple_of(chip * rows, rows), rows), :] = block

        gather_rows(me, own, other, store, True)
    else:
        whole, normed, *outs = rest[:6]
    parts, scratch = rest[-2:]
    value_body(me, tokens, whole, scratch, parts, outs, normed, positions, sequences, heads)


def make_values(lay, tokens, weight):
    rows, width = tokens.shape
    piece = (lay.group, lay.positions, lay.lanes)
    blocks = 0 if len(weight) == 1 else lay.devices // 2
    outs = [shape((rows, width))] + ([shape((width, width))] if blocks else []) + [shape(piece)] * GROUPS
    result = pl.pallas_call(
        functools.partial(
            value_kernel,
            positions=lay.positions,
            sequences=lay.sequences,
            heads=lay.heads,
            blocks=blocks,
        ),
        in_specs=[smem()] + [vmem()] * (1 + len(weight)),
        out_specs=[vmem()] * len(outs),
        out_shape=outs,
        scratch_shapes=[pltpu.VMEM((GROUPS,) + piece, BF16), pltpu.VMEM((width // 128, rows, 128), F32)],
        compiler_params=params(24),
        cost_estimate=cost(2 * rows * width * width, 6 * rows * width + 4 * width * width),
        name="make_values",
    )(lay.me, tokens, *weight)
    normed = result[0]
    whole = result[1] if blocks else weight[0]
    return normed, whole, list(result[-GROUPS:])


def mix_kernel(me, *refs, xs, positions):
    values = refs[: 2 * xs * GROUPS]
    refs = refs[2 * xs * GROUPS :]
    near, far, rows_out, values_out, mixed = refs
    z, x, c, side = me[1], me[2], me[3], me[0] % 2
    half = positions // 2
    for k in range(GROUPS):
        base = k * positions
        rows_out[:, pl.ds(pl.multiple_of(base + side * half, half), half), :] = near[k]
        rows_out[:, pl.ds(pl.multiple_of(base + (1 - side) * half, half), half), :] = far[k]
    index = 0
    for m in range(2):
        for j in range(xs):
            for k in range(GROUPS):
                block = ((z ^ k) * xs + (x ^ j)) * 2 + (c ^ m)
                values_out[:, pl.ds(pl.multiple_of(block * positions, positions), positions), :] = values[
                    index
                ][...]
                index += 1
    for head in range(rows_out.shape[0]):
        result = dot_nn(rows_out[head], values_out[head]).astype(BF16)
        for k in range(GROUPS):
            mixed[k, head] = result[k * positions : (k + 1) * positions]


def mix_values(lay, values, rows):
    group, positions, length, lanes = lay.group, lay.positions, lay.length, lay.lanes
    inputs = list(values) + list(rows)
    result = pl.pallas_call(
        functools.partial(mix_kernel, xs=lay.xs, positions=positions),
        in_specs=[smem()] + [vmem()] * len(inputs),
        out_specs=[vmem()] * 3,
        out_shape=[
            shape((group, GROUPS * positions, length)),
            shape((group, length, lanes)),
            shape((GROUPS, group, positions, lanes)),
        ],
        compiler_params=params(40),
        cost_estimate=cost(2 * group * GROUPS * positions * length * lanes, 8 * group * length * lanes),
        name="mix_values",
    )(lay.me, *inputs)
    return result


def dense(block):
    value = block[...]
    if value.ndim == 2:
        return value
    return value.astype(F32).reshape(-1, value.shape[-1]).astype(BF16)


def down_block(down, width):
    if down.ndim == 2:
        return pl.BlockSpec((width, width), lambda i, *_: (i, 0))
    devices, kinds, short, _ = down.shape
    parts = (kinds - 1) // 2
    return pl.BlockSpec((devices // parts, parts, short, width), lambda i, *_: (i, 0, 0, 0))


def up_block(up, width):
    if up.ndim == 2:
        return pl.BlockSpec((width, width), lambda i, *_: (0, i))
    devices, kinds, short, _ = up.shape
    parts = (kinds - 1) // 2
    return pl.BlockSpec((devices, 1, short, width), lambda i, *_: (0, parts + i, 0, 0))


def out_block(out, width):
    if out.ndim == 2:
        return pl.BlockSpec((width, width), lambda i, *_: (0, 0))
    devices, kinds, short, _ = out.shape
    return pl.BlockSpec((devices, 1, short, width), lambda i, *_: (0, kinds - 1, 0, 0))


ROOT = 0.7978845608028654
CUBE = 0.044715


def middle_kernel(me, *refs, positions, sequences, heads, spread):
    pieces, tokens, out_grad, w_out, w_up, w_down, layer_out, residual_grad, parts = refs[:9]
    grads = refs[9:-7]
    residual, normed, mixed, total, layer, scratch, result = refs[-7:]
    step, last = pl.program_id(0), pl.num_programs(0) - 1

    @pl.when(step == 0)
    def _():
        from_heads(pieces, scratch, positions, sequences, heads)
        join_lanes(scratch, mixed)
        value = tokens[...].astype(F32) + dot_nn(mixed[...], dense(w_out))
        residual[...] = value
        scale = lax.rsqrt(jnp.mean(value * value, axis=-1, keepdims=True) + EPS)
        normed[...] = (value * scale).astype(BF16)
        layer[...] = value
        total[...] = jnp.zeros_like(total)

    up, down = dense(w_up), dense(w_down)
    u = dot_nn(normed[...], up)
    back = dot_nt(out_grad[...], down)
    square = u * u
    tanh = jnp.tanh(ROOT * u * (1.0 + CUBE * square))
    half = 0.5 * (1.0 + tanh)
    hidden = (u * half).astype(BF16)
    slope = half + 0.5 * u * (1.0 - tanh * tanh) * (ROOT * (1.0 + 3.0 * CUBE * square))
    pre = (slope * back).astype(BF16)
    total[...] += dot_nt(pre, up)
    layer[...] += dot_nn(hidden, down)
    if spread:
        a_own, a_other, b_own, b_other, d_down = grads
        short = a_own.shape[1]
        width = result.shape[0]
        d_down[...] = dot_tn(hidden, out_grad[...]).astype(BF16)
        result[...] = dot_tn(normed[...], pre)

        @pl.when(step < last)
        def _():
            spread_rows(me, result, a_own, a_other, short, False)

        @pl.when(step == last)
        def _():
            spread_rows(me, result, b_own.at[:, :, :width], b_other.at[:, :, :width], short, True)
    else:
        d_up, d_down, d_out = grads
        d_down[...] = dot_tn(hidden, out_grad[...]).astype(BF16)
        d_up[...] = dot_tn(normed[...], pre).astype(BF16)

    @pl.when(step == last)
    def _():
        layer_out[...] = layer[...].astype(BF16)
        value = residual[...]
        scale = lax.rsqrt(jnp.mean(value * value, axis=-1, keepdims=True) + EPS)
        norm = value * scale
        grad = total[...]
        back = scale * (grad - norm * jnp.mean(grad * norm, axis=-1, keepdims=True))
        grad = out_grad[...].astype(F32) + back
        residual_grad[...] = grad
        attn_grad = grad.astype(BF16)
        split_lanes(dot_nt(attn_grad, dense(w_out)), scratch)
        to_heads(scratch, parts, positions, sequences, heads)
        if spread:
            result[...] = dot_tn(mixed[...], attn_grad)
            spread_rows(me, result, b_own.at[:, :, width:], b_other.at[:, :, width:], short, True)
        else:
            d_out[...] = dot_tn(mixed[...], attn_grad).astype(BF16)


def middle(lay, pieces, tokens, out_grad, out_weight, up_weight, down_weight, hidden):
    rows, width = tokens.shape
    steps = hidden // width
    piece = (GROUPS, lay.group, lay.positions, lay.lanes)
    chips, short = lay.devices // 2, width // lay.devices
    flat = (rows, width)

    def whole(*dims):
        return pl.BlockSpec(dims, lambda i, me: (0,) * len(dims))

    if lay.small:
        grads = [(chips, short, (steps - 1) * width)] * 2 + [(chips, short, 2 * width)] * 2
        grads += [(hidden, width)]
        block = (chips, short, width)
        specs = [pl.BlockSpec(block, lambda i, me: (0, 0, jnp.minimum(i, steps - 2)))] * 2
        specs += [whole(*dims) for dims in grads[2:4]]
        specs += [pl.BlockSpec((width, width), lambda i, me: (i, 0))]
    else:
        grads = [(width, hidden), (hidden, width), (width, width)]
        specs = [
            pl.BlockSpec((width, width), lambda i, me: (0, i)),
            pl.BlockSpec((width, width), lambda i, me: (i, 0)),
            whole(width, width),
        ]
    out = pl.pallas_call(
        functools.partial(
            middle_kernel,
            positions=lay.positions,
            sequences=lay.sequences,
            heads=lay.heads,
            spread=lay.small,
        ),
        grid_spec=pltpu.PrefetchScalarGridSpec(
            num_scalar_prefetch=1,
            grid=(steps,),
            in_specs=[whole(*piece), whole(*flat), whole(*flat)]
            + [out_block(out_weight, width), up_block(up_weight, width), down_block(down_weight, width)],
            out_specs=[whole(*flat), whole(*flat), whole(*piece)] + specs,
            scratch_shapes=[
                pltpu.VMEM(flat, F32),
                pltpu.VMEM(flat, BF16),
                pltpu.VMEM(flat, BF16),
                pltpu.VMEM(flat, F32),
                pltpu.VMEM(flat, F32),
                pltpu.VMEM((width // 128, rows, 128), F32),
                pltpu.VMEM((width, width), F32),
            ],
        ),
        out_shape=[shape(flat), shape(flat, F32), shape(piece)] + [shape(dims) for dims in grads],
        compiler_params=params(60),
        cost_estimate=cost(12 * rows * width * hidden, 16 * width * hidden, rows * hidden),
        name="middle",
    )(lay.me, pieces, tokens, out_grad, out_weight, up_weight, down_weight)
    return out[0], out[1], out[2], list(out[3:])


def slot_of(me, chip, x_first, z_plain=False):
    yr, zr, xr = (chip // 8) ^ me[0], (chip // 2) % 4, (chip % 2) ^ me[2]
    zr = zr if z_plain else zr ^ me[1]
    return ((xr * 2 + yr) if x_first else (yr * 2 + xr)) * GROUPS + zr


def spread_rows(me, result, own, other, short, x_first):
    for chip in range(result.shape[0] // (2 * short)):
        slot = slot_of(me, chip, x_first)
        for ref, core in ((own, me[3]), (other, 1 - me[3])):
            start = pl.multiple_of(2 * short * chip + short * core, short)
            ref[slot] = result[pl.ds(start, short), :].astype(BF16)


def back_kernel(me, *refs, xs, dps, positions, by_distance):
    pieces, rows, values = refs[:3]
    outs = refs[3:]
    logit_out, term_outs = outs[0], outs[1:5]
    grads, term, logit = outs[5:]
    dp, z, x, c = me[0], me[1], me[2], me[3]
    part = logit_out.shape[-1]
    for k in range(GROUPS):
        grads[:, k * positions : (k + 1) * positions, :] = pieces[k]
    for head in range(rows.shape[0]):
        term[head] = dot_tn(rows[head], grads[head]).astype(BF16)
        soft = rows[head].astype(F32)
        product = soft * dot_nt(grads[head], values[head])
        logit[...] = (product - soft * jnp.sum(product, axis=-1, keepdims=True)).astype(BF16)
        for r in range(dps):
            for k in range(GROUPS):
                start = pl.multiple_of((dp ^ r if by_distance else r) * part, part)
                base = pl.multiple_of((z ^ k) * positions, positions)
                logit_out[r, k, head] = logit[pl.ds(base, positions), pl.ds(start, part)]
    for m in range(2):
        for k in range(GROUPS):
            for j in range(xs):
                block = ((z ^ k) * xs + (x ^ j)) * 2 + (c ^ m)
                out = term_outs[2 * m + k // 2]
                out[j, k % 2] = term[:, pl.ds(pl.multiple_of(block * positions, positions), positions), :]


def mix_back(lay, pieces, rows, values):
    group, positions, length, lanes = lay.group, lay.positions, lay.length, lay.lanes
    part = length // lay.dp
    result = pl.pallas_call(
        functools.partial(
            back_kernel, xs=lay.xs, dps=lay.dp, positions=positions, by_distance=lay.small
        ),
        in_specs=[smem()] + [vmem()] * 3,
        out_specs=[vmem()] * 5,
        out_shape=[shape((lay.dp, GROUPS, group, positions, part))]
        + [shape((lay.xs, 2, group, positions, lanes))] * 4,
        scratch_shapes=[
            pltpu.VMEM((group, GROUPS * positions, lanes), BF16),
            pltpu.VMEM((group, length, lanes), BF16),
            pltpu.VMEM((GROUPS * positions, length), BF16),
        ],
        compiler_params=params(48),
        cost_estimate=cost(
            4 * group * GROUPS * positions * length * lanes, 8 * group * length * lanes
        ),
        name="mix_back",
    )(lay.me, pieces, rows, values)
    return result[0], list(result[1:])


def value_grad_kernel(me, *refs, positions, sequences, heads, spread):
    pieces, normed = refs[:GROUPS], refs[GROUPS]
    if spread:
        total, own, other, parts, scratch, result = refs[GROUPS + 1 :]
    else:
        total, parts, scratch, result = refs[GROUPS + 1 :]
    for k, piece in enumerate(pieces):
        parts[me[1] ^ k] = piece[...]
    from_heads(parts, scratch, positions, sequences, heads)
    join_lanes(scratch, total)
    if spread:
        result[...] = dot_tn(normed[...], total[...])
        spread_rows(me, result, own, other, own.shape[1], True)


def value_grads(lay, pieces, normed):
    rows, width = normed.shape
    piece = (lay.group, lay.positions, lay.lanes)
    chips, short = lay.devices // 2, width // lay.devices
    outs = [shape((rows, width))] + ([shape((chips, short, width))] * 2 if lay.small else [])
    return pl.pallas_call(
        functools.partial(
            value_grad_kernel,
            positions=lay.positions,
            sequences=lay.sequences,
            heads=lay.heads,
            spread=lay.small,
        ),
        in_specs=[smem()] + [vmem()] * (GROUPS + 1),
        out_specs=[vmem()] * len(outs),
        out_shape=outs,
        scratch_shapes=[
            pltpu.VMEM((GROUPS,) + piece, BF16),
            pltpu.VMEM((width // 128, rows, 128), F32),
            pltpu.VMEM((width, width), F32),
        ],
        compiler_params=params(32),
        cost_estimate=cost(2 * rows * width * width, 8 * rows * width),
        name="value_grads",
    )(lay.me, *pieces, normed)


def tokens_grad_kernel(total, weight, tokens, residual_grad, out):
    grad = dot_nt(total[...], weight[...])
    inputs = tokens[...].astype(F32)
    scale = lax.rsqrt(jnp.mean(inputs * inputs, axis=-1, keepdims=True) + EPS)
    norm = inputs * scale
    back = scale * (grad - norm * jnp.mean(grad * norm, axis=-1, keepdims=True))
    out[...] = residual_grad[...] + back


def make_tokens_grad(total, weight, tokens, residual_grad):
    rows, width = tokens.shape
    return pl.pallas_call(
        tokens_grad_kernel,
        out_shape=shape((rows, width), F32),
        in_specs=[vmem()] * 4,
        out_specs=vmem(),
        compiler_params=params(24),
        cost_estimate=cost(2 * rows * width * width, 12 * rows * width),
        name="make_tokens_grad",
    )(total, weight, tokens, residual_grad)


def logits_out_kernel(me, *refs):
    pieces, out = refs[:GROUPS], refs[GROUPS]
    for k, piece in enumerate(pieces):
        out[me[1] ^ k] = piece[...].astype(F32)


def make_logits_grad(lay, pieces):
    group, positions, part = pieces[0].shape
    out = pl.pallas_call(
        logits_out_kernel,
        out_shape=shape((GROUPS, group, positions, part), F32),
        in_specs=[smem()] + [vmem()] * GROUPS,
        out_specs=vmem(),
        compiler_params=params(16),
        cost_estimate=cost(1e6, 24 * pieces[0].size),
        name="make_logits_grad",
    )(lay.me, *pieces)
    return out.reshape(lay.heads, positions, part)


def after(value, *done):
    return lax.optimization_barrier((value, done))[0]


def along_z(lay, pieces):
    return [pieces[0]] + [lay.swap(pieces[k], z=k) for k in range(1, GROUPS)]


def along_z_gather(lay, array):
    return jnp.stack([array] + [lay.swap(array, z=k) for k in range(1, GROUPS)])


def double(lay, array, **way):
    return jnp.concatenate([array, lay.swap(array, **way)])


def halves(own, other):
    half = own.shape[0] // 2
    return add_low(own[:half], other[:half]), add_low(own[half:], other[half:])


def sum_z(lay, array):
    total = array[0].astype(F32)
    for k in range(1, GROUPS):
        total = total + lay.swap(array[k], z=k).astype(F32)
    return total


def on_device(
    tokens,
    norm_gain1,
    value_weight,
    mixer_logits,
    out_weight,
    norm_gain2,
    up_weight,
    down_weight,
    out_grad,
):
    lay = Layout(tokens, mixer_logits)
    out_shape = tokens.shape
    width = lay.width
    tokens = tokens.reshape(lay.rows, width)
    out_grad = out_grad.reshape(lay.rows, width)
    gain_one = norm_gain1.astype(F32)[:, None]
    gain_two = norm_gain2.astype(F32)[:, None]
    value_rows = (gain_one * value_weight.astype(F32)).astype(BF16)
    up_rows = (gain_two * up_weight.astype(F32)).astype(BF16)
    small = lay.small

    with jax.named_scope("weight_gather"):
        if small:
            packed = jnp.concatenate(
                [
                    down_weight.reshape((-1,) + value_rows.shape),
                    up_rows.reshape(up_rows.shape[0], -1, width).swapaxes(0, 1),
                    out_weight[None],
                ]
            )
            w_down = w_up = w_out = lax.all_gather(packed, AXES, axis=0)
        else:
            w_up = lax.all_gather(up_rows, AXES, axis=0, tiled=True)
            w_out = lax.all_gather(out_weight, AXES, axis=0, tiled=True)
            w_down = lax.all_gather(down_weight, AXES, axis=0, tiled=True)
    rows = softmax_rows(lay, mixer_logits)
    with jax.named_scope("mixing_rows"):
        rows = lay.across_z(rows)
    with jax.named_scope("value_weight_gather"):
        if small:
            own = along_z_gather(lay, value_rows)
            four = [own, lay.swap(own, dp=1), lay.swap(own, x=1), lay.swap(own, dp=1, x=1)]
            own = jnp.concatenate(four)
            w_value = [own, lay.swap(own, c=1)]
        else:
            w_value = [lax.all_gather(value_rows, AXES, axis=0, tiled=True)]
        w_value = after(w_value, rows)
    with jax.named_scope("values"):
        normed_one, w_value, value_parts = make_values(lay, tokens, w_value)
        first = along_z(lay, value_parts)
    with jax.named_scope("mixing_rows"):
        rows = [rows, lay.swap(rows, dp=1)]
    with jax.named_scope("values"):
        values = list(first)
        for j in range(1, lay.xs):
            values += [lay.swap(piece, x=j) for piece in first]
        values = values + [lay.swap(piece, c=1) for piece in after(values, rows[1])]
    with jax.named_scope("mixing"):
        mix_low, values, pieces = mix_values(lay, values, rows)
        pieces = lay.across_z(pieces)
    with jax.named_scope("feed_forward"):
        layer_out, residual_grad, pieces, grads = middle(
            lay, pieces, tokens, out_grad, w_out, w_up, w_down, up_rows.shape[1]
        )
        pieces = lay.across_z(pieces)
    with jax.named_scope("weight_grads"):
        if small:
            a_own, a_other, b_own, b_other, c_grad = grads
            down_grad = scatter_sum(c_grad)
            b_own, b_send = halves(b_own, lay.swap(b_other, c=1))
            b_other = lay.swap(b_send, x=1)
            a_own, a_send = halves(a_own, lay.swap(a_other, c=1))
            pieces = after(pieces, b_other, a_send)
            a_other = lay.swap(a_send, dp=1)
            b_own, b_send = halves(b_own, after(b_other, a_send))
            b_other = lay.swap(b_send, dp=1)
    with jax.named_scope("mixing_back"):
        logit_parts, terms = mix_back(lay, pieces, mix_low, values)
        others = [lay.swap(terms[2 + k], c=1) for k in (0, 1)]
        if small:
            others = after(others, b_other)
        arrived = []
        for k in (1, 0):
            piece, other = terms[k], others[k]
            bit = lay.xs // 2
            while bit:
                piece, send = halves(piece, other)
                other = lay.swap(send, x=bit)
                bit //= 2
            if small and k == 1:
                other = after(other, a_other)
            arrived.append(add_low(piece[0], other[0]))
        arrived = [arrived[1][0], arrived[1][1], arrived[0][0], arrived[0][1]]
    with jax.named_scope("weight_grads"):
        if small:
            a_own, a_send = halves(a_own, a_other)
            b_sum = add_low(b_own, b_other)
            b_parts = [lay.swap(b_sum[k], z=k) for k in range(1, GROUPS)]
            arrived = after(arrived, b_parts)
            a_other = lay.swap(after(a_send, arrived), x=1)
    with jax.named_scope("mixing_back"):
        pieces = along_z(lay, arrived)
        if small:
            logit_other = lay.swap(after(logit_parts[1], a_send), dp=1)
            pieces = after(pieces, a_other, logit_other)
        else:
            logit_parts = lax.psum_scatter(logit_parts, "dp", scatter_dimension=0)
    with jax.named_scope("value_grads"):
        total, *spread = value_grads(lay, pieces, normed_one)
        if small:
            own, other = spread
            own = add_low(own, lay.swap(other, c=1))
            four = own.reshape((4, GROUPS) + own.shape[1:])
            parts = [lay.swap(four[1], dp=1), lay.swap(four[2], x=1), lay.swap(four[3], dp=1, x=1)]
            own = four[0].astype(F32)
            for part in parts:
                own = own + part.astype(F32)
            own = own.astype(BF16)
            value_sum = sum_z(lay, own)
        else:
            value_sum = scatter_sum(dot_tn(normed_one, total))
        value_wgrad = gain_one * value_sum
        gain_one_grad = jnp.sum(value_sum * value_weight.astype(F32), axis=1)
    with jax.named_scope("mixing_back"):
        if small:
            logit_parts = add_low(logit_parts[0], after(logit_other, total))
        logits_grad = make_logits_grad(lay, along_z(lay, logit_parts))
    with jax.named_scope("weight_grads"):
        if small:
            a_sum = sum_z(lay, add_low(a_own, after(a_other, own)))
            b_total = b_sum[0].astype(F32)
            for part in b_parts:
                b_total = b_total + part.astype(F32)
            up_sum = jnp.concatenate([a_sum, b_total[:, :width]], axis=1)
            out_wgrad = b_total[:, width:]
            total = after(total, own)
        else:
            up_sum, down_grad, out_wgrad = (scatter_sum(grad) for grad in grads)
        tokens_grad = make_tokens_grad(total, w_value, tokens, residual_grad)
        up_grad = gain_two * up_sum
        gain_two_grad = jnp.sum(up_sum * up_weight.astype(F32), axis=1)
    return (
        layer_out.reshape(out_shape),
        tokens_grad.reshape(out_shape),
        gain_one_grad,
        value_wgrad,
        logits_grad,
        out_wgrad,
        gain_two_grad,
        up_grad,
        down_grad,
    )


def scatter_sum(array):
    return lax.psum_scatter(array.astype(BF16), AXES, scatter_dimension=0, tiled=True).astype(F32)


def solution(mesh):
    placed = (
        P("seq", "dp", None),
        P(("dp", "seq")),
        P(("dp", "seq"), None),
        P(None, "seq", None),
        P(("dp", "seq"), None),
        P(("dp", "seq")),
        P(("dp", "seq"), None),
        P(("dp", "seq"), None),
        P("seq", "dp", None),
    )
    return jax.shard_map(
        on_device,
        mesh=mesh,
        in_specs=placed,
        out_specs=(
            P("seq", "dp", None),
            P("seq", "dp", None),
            P(("dp", "seq")),
            P(("dp", "seq"), None),
            P(None, "seq", "dp"),
            P(("dp", "seq"), None),
            P(("dp", "seq")),
            P(("dp", "seq"), None),
            P(("dp", "seq"), None),
        ),
        check_vma=False,
    )
```

time: 428 us -> 314 us (0.73)
  waiting for transfers between devices: 234 us -> 120 us
  blocking collectives: 0 us -> 38.9 us
  starting transfers between devices: 103 us -> 73.1 us
  Pallas kernels: 59 us -> 43.5 us
  between operations: 1.33 us -> 14.5 us
  local copies, waits for them, and re-layouts: 14.3 us -> 4.88 us
    ppermute x80 -> x53, waiting for transfers between devices: 234 us -> 104 us  [swap(): lax.ppermute(array, AXES, [(i, i ^ mask) for i in range(self.devices)])]
    all_to_all x0 -> x1, blocking collectives: none -> 38.9 us  [across_z(): return lax.all_to_all(array, 'seq', 0, 0, axis_index_groups=lines)]
    ppermute x80 -> x53, starting transfers between devices: 103 us -> 64.2 us  [swap(): lax.ppermute(array, AXES, [(i, i ^ mask) for i in range(self.devices)])]
    pallas_call x5 -> x1, Pallas kernels: 26.9 us -> 1.91 us  [softmax_rows(): pl.pallas_call(softmax_kernel, in_specs=[smem(), vmem()], out_specs=vmem(...]
    all_to_all x0 -> x2, waiting for transfers between devices: none -> 15.1 us  [across_z(): return lax.all_to_all(array, 'seq', 0, 0, axis_index_groups=lines)]
    pallas_call x1, Pallas kernels: 16.9 us -> 27 us  [middle(): pl.pallas_call(functools.partial(middle_kernel, positions=lay.positions,...]
    all_to_all x0 -> x2, starting transfers between devices: none -> 8.87 us  [across_z(): return lax.all_to_all(array, 'seq', 0, 0, axis_index_groups=lines)]
    unnamed x54 -> x43, local copies, waits for them, and re-layouts: 10.8 us -> 3.88 us
  transfers between devices with their start and end apart: 80 -> 57, of which waited for: 35 -> 27; matrix products, arithmetic and copies ran while one was open for 4% -> 5% of each run, Pallas kernels for 9% -> 5%
where the time goes in v2:
time: 314 us; the launch traced here: 313 us
  waiting for transfers between devices  120 us (38%)
  starting transfers between devices  73.1 us (23%)
  Pallas kernels  43.5 us (14%)
  blocking collectives  38.9 us (12%)
  other arithmetic  18.4 us (6%)
  between operations  14.5 us (5%)
  local copies, waits for them, and re-layouts  4.88 us (2%)
    ppermute x53, waiting for transfers between devices, swap(): lax.ppermute(array, AXES, [(i, i ^ mask) for i in range(self.devices)])  104 us
    ppermute x53, starting transfers between devices, swap(): lax.ppermute(array, AXES, [(i, i ^ mask) for i in range(self.devices)])  64.2 us
    all_to_all x1, blocking collectives, across_z(): return lax.all_to_all(array, 'seq', 0, 0, axis_index_groups=lines)  38.9 us
    pallas_call x1, Pallas kernels, middle(): pl.pallas_call(functools.partial(middle_kernel, positions=lay.positions,...  27 us
    all_to_all x2, waiting for transfers between devices, across_z(): return lax.all_to_all(array, 'seq', 0, 0, axis_index_groups=lines)  15.1 us
    convert_element_type x12, other arithmetic, add_low(): return (left.astype(F32) + right.astype(F32)).astype(BF16)  10.3 us
    all_to_all x2, starting transfers between devices, across_z(): return lax.all_to_all(array, 'seq', 0, 0, axis_index_groups=lines)  8.87 us
  transfers between devices with their start and end apart: 57, of which 27 were waited for; matrix products, arithmetic and copies ran while one was open for 5% of the time, Pallas kernels for 5%

profile of v2, /device:TPU:0, one launch (start us, length us, event | category | flops | bytes accessed | tf_op | source)
XLA Modules:
  0.0 313.0 jit_solution(14833869698436517194)
XLA Ops:
  9.1 1.7 pad_maximum_fusion
  10.9 5.1 %collective-permute-start.2 = (bf16[24,768]{1,0:T(8,128)(2,1)S(1)}, bf16[24,768]{1,0:T(8,128)(2,1)S(1)}, u32[]{:S(2)}, u32[]{:S(2)}) collective-permute-start(bf16[24,768]{1,0:T(8,128)(2,1)S(1)} %get-tuple-element.116), channel_id=1, source_target_pairs={{0,12},{1,13},{2,14},{3,15},{4,8},{5,9},{6,10},{7,11},{8,4},{9,5},... | collective-permute-start | bytes 110600 | tf_op jit(solution)/shard_map/value_weight_gather/ppermute | solution.py:69
  16.7 1.9 mix_rows.1
  18.6 5.1 %all-to-all-start = ((bf16[4,3,32,1024]{3,2,1,0:T(8,128)(2,1)}), bf16[4,3,32,1024]{3,2,1,0:T(8,128)(2,1)S(1)}, u32[]{:S(2)}, u32[]{:S(2)}) async-start(bf16[4,3,32,1024]{3,2,1,0:T(8,128)(2,1)} %mix_rows.1), calls=%async_computation | async-start | bytes 1572864 | tf_op jit(solution)/shard_map/mixing_rows/all_to_all | solution.py:75
  23.8 2.5 collective-permute-start.5
  27.4 6.9 %collective-permute-done.3 = bf16[4,24,768]{2,1,0:T(8,128)(2,1)S(1)} collective-permute-done((bf16[4,24,768]{2,1,0:T(8,128)(2,1)S(1)}, bf16[4,24,768]{2,1,0:T(8,128)(2,1)S(1)}, u32[]{:S(2)}, u32[]{:S(2)}) %collective-permute-start.3) | collective-permute-done | bytes 147488 | tf_op jit(solution)/shard_map/value_weight_gather/ppermute | solution.py:69
  34.4 2.0 collective-permute-done.6.rest_1_
  36.4 13.7 %all-to-all-done.refs_16_ = bf16[4,3,32,1024]{3,2,1,0:T(8,128)(2,1)S(1)} async-done(((bf16[4,3,32,1024]{3,2,1,0:T(8,128)(2,1)}), bf16[4,3,32,1024]{3,2,1,0:T(8,128)(2,1)S(1)}, u32[]{:S(2)}, u32[]{:S(2)}) %all-to-all-start) | async-done | bytes 786464 | tf_op jit(solution)/shard_map/mixing_rows/all_to_all | solution.py:75
  50.1 1.5 collective-permute-start.14
  51.7 2.0 make_values.1
  54.6 2.0 collective-permute-start.8
  56.6 2.4 collective-permute-start.9
  60.5 11.9 %collective-permute-done.7.refs_1_ = bf16[3,64,512]{2,1,0:T(8,128)(2,1)S(1)} collective-permute-done((bf16[3,64,512]{2,1,0:T(8,128)(2,1)S(1)}, bf16[3,64,512]{2,1,0:T(8,128)(2,1)S(1)}, u32[]{:S(2)}, u32[]{:S(2)}) %collective-permute-start.7) | collective-permute-done | bytes 196640 | tf_op jit(solution)/shard_map/values/ppermute | solution.py:69
  72.4 1.9 collective-permute-start.11
  75.4 1.5 collective-permute-start.12
  76.9 5.3 %collective-permute-done.9.refs_3_ = bf16[3,64,512]{2,1,0:T(8,128)(2,1)S(1)} collective-permute-done((bf16[3,64,512]{2,1,0:T(8,128)(2,1)S(1)}, bf16[3,64,512]{2,1,0:T(8,128)(2,1)S(1)}, u32[]{:S(2)}, u32[]{:S(2)}) %collective-permute-start.9) | collective-permute-done | bytes 196640 | tf_op jit(solution)/shard_map/values/ppermute | solution.py:69
  83.7 4.2 %collective-permute-done.13.refs_7_ = bf16[3,64,512]{2,1,0:T(8,128)(2,1)S(1)} collective-permute-done((bf16[3,64,512]{2,1,0:T(8,128)(2,1)S(1)}, bf16[3,64,512]{2,1,0:T(8,128)(2,1)S(1)}, u32[]{:S(2)}, u32[]{:S(2)}) %collective-permute-start.13) | collective-permute-done | bytes 196640 | tf_op jit(solution)/shard_map/values/ppermute | solution.py:69
  93.6 1.8 mix_values.1
  95.4 1.6 copy-done.5
  98.2 38.9 %all_to_all.15.refs_0_ = bf16[4,3,64,512]{3,2,1,0:T(8,128)(2,1)} all-to-all(bf16[4,3,64,512]{3,2,1,0:T(8,128)(2,1)S(1)} %get-tuple-element.76), channel_id=1, replica_groups={{0,4,8,12},{1,5,9,13},{2,6,10,14},{3,7,11,15},{16,20,24,28},{17,21,25,2..., dimensions={0} | all-to-all | bytes 1572864 | tf_op jit(solution)/shard_map/mixing/all_to_all | solution.py:75
  137.4 27.0 %middle.1 = (bf16[512,768]{1,0:T(8,128)(2,1)}, f32[512,768]{1,0:T(8,128)}, bf16[4,3,64,512]{3,2,1,0:T(8,128)(2,1)}, bf16[16,24,2304]{2,1,0:T(8,128)(2,1)}, bf16[...) custom-call(s32[8]{0:T(128)} %copy-done, ...), custom_call_target="tpu_custom_call" | custom-call | flops 49999998976 | bytes 1 | tf_op jit(solution)/shard_map/feed_forward/middle/pallas_call | solution.py:383
  165.0 3.7 %all-to-all-start.2 = ((bf16[4,3,64,512]{3,2,1,0:T(8,128)(2,1)}), bf16[4,3,64,512]{3,2,1,0:T(8,128)(2,1)S(1)}, u32[]{:S(2)}, u32[]{:S(2)}) async-start(bf16[4,3,64,512]{3,2,1,0:T(8,128)(2,1)} %get-tuple-element.78), calls=%async_computation.2 | async-start | bytes 1572864 | tf_op jit(solution)/shard_map/feed_forward/all_to_all | solution.py:75
  170.2 2.1 add_convert_fusion.3
  173.4 2.9 add_convert_fusion
  177.7 10.2 %collective-permute-done.24 = bf16[8,24,1536]{2,1,0:T(8,128)(2,1)} collective-permute-done((bf16[8,24,1536]{2,1,0:T(8,128)(2,1)S(1)}, bf16[8,24,1536]{2,1,0:T(8,128)(2,1)}, u32[]{:S(2)}, u32[]{:S(2)}) %collective-permute-start.24) | collective-permute-done | bytes 589856 | tf_op jit(solution)/shard_map/weight_grads/ppermute | solution.py:69
  191.5 4.9 %mix_back.1 = (bf16[2,4,3,64,512]{4,3,2,1,0:T(8,128)(2,1)S(1)}, bf16[2,2,3,64,512]{4,3,2,1,0:T(8,128)(2,1)S(1)}, bf16[2,2,3,64,512]{4,3,2,1,0:T(8,128)(2,1)S(1)}...) custom-call(s32[8]{0:T(128)S(1)} %copy-done.1, ...), custom_call_target="tpu_custom_call" | custom-call | flops 49999998976 | bytes 1 | tf_op jit(solution)/shard_map/mixing_back/mix_back/pallas_call | solution.py:459
  197.0 7.3 %collective-permute-done.28 = bf16[4,24,1536]{2,1,0:T(8,128)(2,1)S(1)} collective-permute-done((bf16[4,24,1536]{2,1,0:T(8,128)(2,1)S(1)}, bf16[4,24,1536]{2,1,0:T(8,128)(2,1)S(1)}, u32[]{:S(2)}, u32[]{:S(2)}) %collective-permute-start.28) | collective-permute-done | bytes 294944 | tf_op jit(solution)/shard_map/weight_grads/ppermute | solution.py:69
  205.4 1.9 collective-permute-start.34
  207.3 2.5 collective-permute-start.32
  213.4 15.0 %collective-permute-done.30 = bf16[1,2,3,64,512]{4,3,2,1,0:T(8,128)(2,1)S(1)} collective-permute-done((bf16[1,2,3,64,512]{4,3,2,1,0:T(8,128)(2,1)S(1)}, bf16[1,2,3,64,512]{4,3,2,1,0:T(8,128)(2,1)S(1)}, u32[]{:S(2)}, u32[]{:S(2)}) %collective-permute-start.30) | collective-permute-done | bytes 393248 | tf_op jit(solution)/shard_map/mixing_back/ppermute | solution.py:69
  229.9 6.2 %collective-permute-done.29 = bf16[1,2,3,64,512]{4,3,2,1,0:T(8,128)(2,1)S(1)} collective-permute-done((bf16[1,2,3,64,512]{4,3,2,1,0:T(8,128)(2,1)S(1)}, bf16[1,2,3,64,512]{4,3,2,1,0:T(8,128)(2,1)S(1)}, u32[]{:S(2)}, u32[]{:S(2)}) %collective-permute-start.29) | collective-permute-done | bytes 393248 | tf_op jit(solution)/shard_map/mixing_back/ppermute | solution.py:69
  236.8 1.8 collective-permute-start.36
  238.6 2.3 collective-permute-start.37
  242.0 8.0 %collective-permute-done.35.refs_1_ = bf16[3,64,512]{2,1,0:T(8,128)(2,1)S(1)} collective-permute-done((bf16[3,64,512]{2,1,0:T(8,128)(2,1)S(1)}, bf16[3,64,512]{2,1,0:T(8,128)(2,1)S(1)}, u32[]{:S(2)}, u32[]{:S(2)}) %collective-permute-start.35) | collective-permute-done | bytes 196640 | tf_op jit(solution)/shard_map/mixing_back/ppermute | solution.py:69
  249.9 4.9 %collective-permute-done.36.refs_2_ = bf16[3,64,512]{2,1,0:T(8,128)(2,1)S(1)} collective-permute-done((bf16[3,64,512]{2,1,0:T(8,128)(2,1)S(1)}, bf16[3,64,512]{2,1,0:T(8,128)(2,1)S(1)}, u32[]{:S(2)}, u32[]{:S(2)}) %collective-permute-start.36) | collective-permute-done | bytes 196640 | tf_op jit(solution)/shard_map/mixing_back/ppermute | solution.py:69
  254.8 1.9 value_grads.1
  257.8 3.9 %collective-permute-start.49 = (bf16[3,64,512]{2,1,0:T(8,128)(2,1)S(1)}, bf16[3,64,512]{2,1,0:T(8,128)(2,1)S(1)}, u32[]{:S(2)}, u32[]{:S(2)}) collective-permute-start(bf16[3,64,512]{2,1,0:T(8,128)(2,1)S(1)} %get-tuple-element.121), channel_id=1, source_target_pairs={{0,12},{1,13},{2,14},{3,15},{4,8},{5,9},{6,10},{7,11},{8,4},{9,5},... | collective-permute-start | bytes 589832 | tf_op jit(solution)/shard_map/mixing_back/ppermute | solution.py:69
  261.7 5.3 %collective-permute-start.48 = (bf16[3,64,512]{2,1,0:T(8,128)(2,1)S(1)}, bf16[3,64,512]{2,1,0:T(8,128)(2,1)S(1)}, u32[]{:S(2)}, u32[]{:S(2)}) collective-permute-start(bf16[3,64,512]{2,1,0:T(8,128)(2,1)S(1)} %get-tuple-element.122), channel_id=1, source_target_pairs={{0,8},{1,9},{2,10},{3,11},{4,12},{5,13},{6,14},{7,15},{8,0},{9,1},... | collective-permute-start | bytes 589832 | tf_op jit(solution)/shard_map/mixing_back/ppermute | solution.py:69
  267.6 4.6 %collective-permute-start.41 = (bf16[4,24,768]{2,1,0:T(8,128)(2,1)S(1)}, bf16[4,24,768]{2,1,0:T(8,128)(2,1)S(1)}, u32[]{:S(2)}, u32[]{:S(2)}) collective-permute-start(bf16[4,24,768]{2,1,0:T(8,128)(2,1)S(1)} %get-tuple-element.125), channel_id=1, source_target_pairs={{0,16},{1,17},{2,18},{3,19},{4,20},{5,21},{6,22},{7,23},{8,24},{9,... | collective-permute-start | bytes 442376 | tf_op jit(solution)/shard_map/value_grads/ppermute | solution.py:69
  272.2 1.5 collective-permute-start.42
  273.7 9.6 %collective-permute-done.48.refs_2_ = bf16[3,64,512]{2,1,0:T(8,128)(2,1)S(1)} collective-permute-done((bf16[3,64,512]{2,1,0:T(8,128)(2,1)S(1)}, bf16[3,64,512]{2,1,0:T(8,128)(2,1)S(1)}, u32[]{:S(2)}, u32[]{:S(2)}) %collective-permute-start.48) | collective-permute-done | bytes 196640 | tf_op jit(solution)/shard_map/mixing_back/ppermute | solution.py:69
  283.4 1.8 make_logits_grad.1
  285.6 2.3 collective-permute-start.46
  291.3 2.3 collective-permute-start.52
  293.6 2.3 make_tokens_grad.1
  297.3 1.9 collective-permute-done.52
  299.2 3.9 %collective-permute-done.51 = bf16[24,2304]{1,0:T(8,128)(2,1)S(1)} collective-permute-done((bf16[24,2304]{1,0:T(8,128)(2,1)S(1)}, bf16[24,2304]{1,0:T(8,128)(2,1)S(1)}, u32[]{:S(2)}, u32[]{:S(2)}) %collective-permute-start.51) | collective-permute-done | bytes 110624 | tf_op jit(solution)/shard_map/weight_grads/ppermute | solution.py:69
  304.5 1.6 convert_element_type.335
  (156 shorter events, 41.1 us)
Async XLA Ops:
  7.2 130.2 %all-gather.3.cloned.1.call-start = ((), (), s32[]{:S(2)}) async-start(), calls=%async_computation.5 | async-start | bytes 10948608 | tf_op jit(solution)/shard_map/weight_gather/all_gather | solution.py:624
  10.9 12.9 %collective-permute-start.2 = (bf16[24,768]{1,0:T(8,128)(2,1)S(1)}, bf16[24,768]{1,0:T(8,128)(2,1)S(1)}, u32[]{:S(2)}, u32[]{:S(2)}) collective-permute-start(bf16[24,768]{1,0:T(8,128)(2,1)S(1)} %get-tuple-element.116), channel_id=1, source_target_pairs={{0,12},{1,13},{2,14},{3,15},{4,8},{5,9},{6,10},{7,11},{8,4},{9,5},... | collective-permute-start | bytes 110600 | tf_op jit(solution)/shard_map/value_weight_gather/ppermute | solution.py:69
  16.0 7.8 %collective-permute-start.1 = (bf16[24,768]{1,0:T(8,128)(2,1)S(1)}, bf16[24,768]{1,0:T(8,128)(2,1)S(1)}, u32[]{:S(2)}, u32[]{:S(2)}) collective-permute-start(bf16[24,768]{1,0:T(8,128)(2,1)S(1)} %get-tuple-element.116), channel_id=1, source_target_pairs={{0,8},{1,9},{2,10},{3,11},{4,12},{5,13},{6,14},{7,15},{8,0},{9,1},... | collective-permute-start | bytes 110600 | tf_op jit(solution)/shard_map/value_weight_gather/ppermute | solution.py:69
  16.0 7.8 %collective-permute-start = (bf16[24,768]{1,0:T(8,128)(2,1)S(1)}, bf16[24,768]{1,0:T(8,128)(2,1)S(1)}, u32[]{:S(2)}, u32[]{:S(2)}) collective-permute-start(bf16[24,768]{1,0:T(8,128)(2,1)S(1)} %get-tuple-element.116), channel_id=1, source_target_pairs={{0,4},{1,5},{2,6},{3,7},{4,0},{5,1},{6,2},{7,3},{8,12},{9,13},{10,... | collective-permute-start | bytes 110600 | tf_op jit(solution)/shard_map/value_weight_gather/ppermute | solution.py:69
  18.6 31.5 %all-to-all-start = ((bf16[4,3,32,1024]{3,2,1,0:T(8,128)(2,1)}), bf16[4,3,32,1024]{3,2,1,0:T(8,128)(2,1)S(1)}, u32[]{:S(2)}, u32[]{:S(2)}) async-start(bf16[4,3,32,1024]{3,2,1,0:T(8,128)(2,1)} %mix_rows.1), calls=%async_computation | async-start | bytes 1572864 | tf_op jit(solution)/shard_map/mixing_rows/all_to_all | solution.py:75
  23.8 280.8 %reduce-scatter.2.cloned.1.call-start = ((), (), s32[]{:S(2)}) async-start(), calls=%async_computation.4 | async-start | bytes 4866048 | tf_op jit(solution)/shard_map/weight_grads/reduce_scatter | solution.py:749
  23.8 10.5 %collective-permute-start.5 = (bf16[4,24,768]{2,1,0:T(8,128)(2,1)S(1)}, bf16[4,24,768]{2,1,0:T(8,128)(2,1)S(1)}, u32[]{:S(2)}, u32[]{:S(2)}) collective-permute-start(bf16[4,24,768]{2,1,0:T(8,128)(2,1)S(1)} %pad_maximum_fusion.2), channel_id=1, source_target_pairs={{0,18},{1,19},{2,16},{3,17},{4,22},{5,23},{6,20},{7,21},{8,26},{9,... | collective-permute-start | bytes 442376 | tf_op jit(solution)/shard_map/value_weight_gather/ppermute | solution.py:69
  26.3 8.0 %collective-permute-start.4 = (bf16[4,24,768]{2,1,0:T(8,128)(2,1)S(1)}, bf16[4,24,768]{2,1,0:T(8,128)(2,1)S(1)}, u32[]{:S(2)}, u32[]{:S(2)}) collective-permute-start(bf16[4,24,768]{2,1,0:T(8,128)(2,1)S(1)} %pad_maximum_fusion.2), channel_id=1, source_target_pairs={{0,2},{1,3},{2,0},{3,1},{4,6},{5,7},{6,4},{7,5},{8,10},{9,11},{10,... | collective-permute-start | bytes 442376 | tf_op jit(solution)/shard_map/value_weight_gather/ppermute | solution.py:69
  26.9 7.4 %collective-permute-start.3 = (bf16[4,24,768]{2,1,0:T(8,128)(2,1)S(1)}, bf16[4,24,768]{2,1,0:T(8,128)(2,1)S(1)}, u32[]{:S(2)}, u32[]{:S(2)}) collective-permute-start(bf16[4,24,768]{2,1,0:T(8,128)(2,1)S(1)} %pad_maximum_fusion.2), channel_id=1, source_target_pairs={{0,16},{1,17},{2,18},{3,19},{4,20},{5,21},{6,22},{7,23},{8,24},{9,... | collective-permute-start | bytes 442376 | tf_op jit(solution)/shard_map/value_weight_gather/ppermute | solution.py:69
  50.1 37.8 %collective-permute-start.14 = (bf16[4,3,32,1024]{3,2,1,0:T(8,128)(2,1)S(1)}, bf16[4,3,32,1024]{3,2,1,0:T(8,128)(2,1)S(1)}, u32[]{:S(2)}, u32[]{:S(2)}) collective-permute-start(bf16[4,3,32,1024]{3,2,1,0:T(8,128)(2,1)S(1)} %all-to-all-done.refs_16_), channel_id=1, source_target_pairs={{0,16},{1,17},{2,18},{3,19},{4,20},{5,21},{6,22},{7,23},{8,24},{9,... | collective-permute-start | bytes 2359304 | tf_op jit(solution)/shard_map/mixing_rows/ppermute | solution.py:69
  54.6 17.7 %collective-permute-start.7 = (bf16[3,64,512]{2,1,0:T(8,128)(2,1)S(1)}, bf16[3,64,512]{2,1,0:T(8,128)(2,1)S(1)}, u32[]{:S(2)}, u32[]{:S(2)}) collective-permute-start(bf16[3,64,512]{2,1,0:T(8,128)(2,1)S(1)} %get-tuple-element.65), channel_id=1, source_target_pairs={{0,4},{1,5},{2,6},{3,7},{4,0},{5,1},{6,2},{7,3},{8,12},{9,13},{10,... | collective-permute-start | bytes 589832 | tf_op jit(solution)/shard_map/values/ppermute | solution.py:69
  54.6 20.8 %collective-permute-start.8 = (bf16[3,64,512]{2,1,0:T(8,128)(2,1)S(1)}, bf16[3,64,512]{2,1,0:T(8,128)(2,1)S(1)}, u32[]{:S(2)}, u32[]{:S(2)}) collective-permute-start(bf16[3,64,512]{2,1,0:T(8,128)(2,1)S(1)} %get-tuple-element.66), channel_id=1, source_target_pairs={{0,8},{1,9},{2,10},{3,11},{4,12},{5,13},{6,14},{7,15},{8,0},{9,1},... | collective-permute-start | bytes 589832 | tf_op jit(solution)/shard_map/values/ppermute | solution.py:69
  56.6 25.6 %collective-permute-start.9 = (bf16[3,64,512]{2,1,0:T(8,128)(2,1)S(1)}, bf16[3,64,512]{2,1,0:T(8,128)(2,1)S(1)}, u32[]{:S(2)}, u32[]{:S(2)}) collective-permute-start(bf16[3,64,512]{2,1,0:T(8,128)(2,1)S(1)} %get-tuple-element.67), channel_id=1, source_target_pairs={{0,12},{1,13},{2,14},{3,15},{4,8},{5,9},{6,10},{7,11},{8,4},{9,5},... | collective-permute-start | bytes 589832 | tf_op jit(solution)/shard_map/values/ppermute | solution.py:69
  59.0 24.7 %collective-permute-start.10 = (bf16[3,64,512]{2,1,0:T(8,128)(2,1)S(1)}, bf16[3,64,512]{2,1,0:T(8,128)(2,1)S(1)}, u32[]{:S(2)}, u32[]{:S(2)}) collective-permute-start(bf16[3,64,512]{2,1,0:T(8,128)(2,1)S(1)} %get-tuple-element.68.refs_0_), channel_id=1, source_target_pairs={{0,2},{1,3},{2,0},{3,1},{4,6},{5,7},{6,4},{7,5},{8,10},{9,11},{10,... | collective-permute-start | bytes 589832 | tf_op jit(solution)/shard_map/values/ppermute | solution.py:69
  72.4 11.3 %collective-permute-start.11 = (bf16[3,64,512]{2,1,0:T(8,128)(2,1)S(1)}, bf16[3,64,512]{2,1,0:T(8,128)(2,1)S(1)}, u32[]{:S(2)}, u32[]{:S(2)}) collective-permute-start(bf16[3,64,512]{2,1,0:T(8,128)(2,1)S(1)} %collective-permute-done.7.refs_1_), channel_id=1, source_target_pairs={{0,2},{1,3},{2,0},{3,1},{4,6},{5,7},{6,4},{7,5},{8,10},{9,11},{10,... | collective-permute-start | bytes 589832 | tf_op jit(solution)/shard_map/values/ppermute | solution.py:69
  75.4 8.3 %collective-permute-start.12 = (bf16[3,64,512]{2,1,0:T(8,128)(2,1)S(1)}, bf16[3,64,512]{2,1,0:T(8,128)(2,1)S(1)}, u32[]{:S(2)}, u32[]{:S(2)}) collective-permute-start(bf16[3,64,512]{2,1,0:T(8,128)(2,1)S(1)} %collective-permute-done.8.refs_2_), channel_id=1, source_target_pairs={{0,2},{1,3},{2,0},{3,1},{4,6},{5,7},{6,4},{7,5},{8,10},{9,11},{10,... | collective-permute-start | bytes 589832 | tf_op jit(solution)/shard_map/values/ppermute | solution.py:69
  82.2 5.7 %collective-permute-start.13 = (bf16[3,64,512]{2,1,0:T(8,128)(2,1)S(1)}, bf16[3,64,512]{2,1,0:T(8,128)(2,1)S(1)}, u32[]{:S(2)}, u32[]{:S(2)}) collective-permute-start(bf16[3,64,512]{2,1,0:T(8,128)(2,1)S(1)} %collective-permute-done.9.refs_3_), channel_id=1, source_target_pairs={{0,2},{1,3},{2,0},{3,1},{4,6},{5,7},{6,4},{7,5},{8,10},{9,11},{10,... | collective-permute-start | bytes 589832 | tf_op jit(solution)/shard_map/values/ppermute | solution.py:69
  164.5 8.9 %collective-permute-start.25 = (bf16[16,24,2304]{2,1,0:T(8,128)(2,1)}, bf16[16,24,2304]{2,1,0:T(8,128)(2,1)}, u32[]{:S(2)}, u32[]{:S(2)}) collective-permute-start(bf16[16,24,2304]{2,1,0:T(8,128)(2,1)} %get-tuple-element.82), channel_id=1, source_target_pairs={{0,1},{1,0},{2,3},{3,2},{4,5},{5,4},{6,7},{7,6},{8,9},{9,8},{10,11... | collective-permute-start | bytes 5308424 | tf_op jit(solution)/shard_map/weight_grads/ppermute | solution.py:69
  164.7 5.5 %collective-permute-start.23 = (bf16[16,24,1536]{2,1,0:T(8,128)(2,1)}, bf16[16,24,1536]{2,1,0:T(8,128)(2,1)}, u32[]{:S(2)}, u32[]{:S(2)}) collective-permute-start(bf16[16,24,1536]{2,1,0:T(8,128)(2,1)} %get-tuple-element.80), channel_id=1, source_target_pairs={{0,1},{1,0},{2,3},{3,2},{4,5},{5,4},{6,7},{7,6},{8,9},{9,8},{10,11... | collective-permute-start | bytes 3538952 | tf_op jit(solution)/shard_map/weight_grads/ppermute | solution.py:69
  165.0 24.3 %all-to-all-start.2 = ((bf16[4,3,64,512]{3,2,1,0:T(8,128)(2,1)}), bf16[4,3,64,512]{3,2,1,0:T(8,128)(2,1)S(1)}, u32[]{:S(2)}, u32[]{:S(2)}) async-start(bf16[4,3,64,512]{3,2,1,0:T(8,128)(2,1)} %get-tuple-element.78), calls=%async_computation.2 | async-start | bytes 1572864 | tf_op jit(solution)/shard_map/feed_forward/all_to_all | solution.py:75
  172.3 15.7 %collective-permute-start.24 = (bf16[8,24,1536]{2,1,0:T(8,128)(2,1)S(1)}, bf16[8,24,1536]{2,1,0:T(8,128)(2,1)}, u32[]{:S(2)}, u32[]{:S(2)}) collective-permute-start(bf16[8,24,1536]{2,1,0:T(8,128)(2,1)S(1)} %get-tuple-element.120), channel_id=1, source_target_pairs={{0,2},{1,3},{2,0},{3,1},{4,6},{5,7},{6,4},{7,5},{8,10},{9,11},{10,... | collective-permute-start | bytes 1769480 | tf_op jit(solution)/shard_map/weight_grads/ppermute | solution.py:69
  176.3 34.9 %collective-permute-start.31 = (bf16[8,24,2304]{2,1,0:T(8,128)(2,1)}, bf16[8,24,2304]{2,1,0:T(8,128)(2,1)}, u32[]{:S(2)}, u32[]{:S(2)}) collective-permute-start(bf16[8,24,2304]{2,1,0:T(8,128)(2,1)} %get-tuple-element.118), channel_id=1, source_target_pairs={{0,16},{1,17},{2,18},{3,19},{4,20},{5,21},{6,22},{7,23},{8,24},{9,... | collective-permute-start | bytes 2654216 | tf_op jit(solution)/shard_map/weight_grads/ppermute | solution.py:69
  190.4 13.9 %collective-permute-start.28 = (bf16[4,24,1536]{2,1,0:T(8,128)(2,1)S(1)}, bf16[4,24,1536]{2,1,0:T(8,128)(2,1)S(1)}, u32[]{:S(2)}, u32[]{:S(2)}) collective-permute-start(bf16[4,24,1536]{2,1,0:T(8,128)(2,1)S(1)} %add_convert_fusion.16), channel_id=1, source_target_pairs={{0,16},{1,17},{2,18},{3,19},{4,20},{5,21},{6,22},{7,23},{8,24},{9,... | collective-permute-start | bytes 884744 | tf_op jit(solution)/shard_map/weight_grads/ppermute | solution.py:69
  196.4 10.9 %collective-permute-start.26 = (bf16[2,2,3,64,512]{4,3,2,1,0:T(8,128)(2,1)S(1)}, bf16[2,2,3,64,512]{4,3,2,1,0:T(8,128)(2,1)S(1)}, u32[]{:S(2)}, u32[]{:S(2)}) collective-permute-start(bf16[2,2,3,64,512]{4,3,2,1,0:T(8,128)(2,1)S(1)} %get-tuple-element.87), channel_id=1, source_target_pairs={{0,1},{1,0},{2,3},{3,2},{4,5},{5,4},{6,7},{7,6},{8,9},{9,8},{10,11... | collective-permute-start | bytes 2359304 | tf_op jit(solution)/shard_map/mixing_back/ppermute | solution.py:69
  196.5 13.4 %collective-permute-start.27 = (bf16[2,2,3,64,512]{4,3,2,1,0:T(8,128)(2,1)S(1)}, bf16[2,2,3,64,512]{4,3,2,1,0:T(8,128)(2,1)S(1)}, u32[]{:S(2)}, u32[]{:S(2)}) collective-permute-start(bf16[2,2,3,64,512]{4,3,2,1,0:T(8,128)(2,1)S(1)} %get-tuple-element.88), channel_id=1, source_target_pairs={{0,1},{1,0},{2,3},{3,2},{4,5},{5,4},{6,7},{7,6},{8,9},{9,8},{10,11... | collective-permute-start | bytes 2359304 | tf_op jit(solution)/shard_map/mixing_back/ppermute | solution.py:69
  205.4 31.0 %collective-permute-start.34 = (bf16[24,1536]{1,0:T(8,128)(2,1)S(1)}, bf16[24,1536]{1,0:T(8,128)(2,1)S(1)}, u32[]{:S(2)}, u32[]{:S(2)}) collective-permute-start(bf16[24,1536]{1,0:T(8,128)(2,1)S(1)} %get-tuple-element.137), channel_id=1, source_target_pairs={{0,12},{1,13},{2,14},{3,15},{4,8},{5,9},{6,10},{7,11},{8,4},{9,5},... | collective-permute-start | bytes 221192 | tf_op jit(solution)/shard_map/weight_grads/ppermute | solution.py:69
  207.3 29.1 %collective-permute-start.33 = (bf16[24,1536]{1,0:T(8,128)(2,1)S(1)}, bf16[24,1536]{1,0:T(8,128)(2,1)S(1)}, u32[]{:S(2)}, u32[]{:S(2)}) collective-permute-start(bf16[24,1536]{1,0:T(8,128)(2,1)S(1)} %get-tuple-element.138), channel_id=1, source_target_pairs={{0,8},{1,9},{2,10},{3,11},{4,12},{5,13},{6,14},{7,15},{8,0},{9,1},... | collective-permute-start | bytes 221192 | tf_op jit(solution)/shard_map/weight_grads/ppermute | solution.py:69
  207.3 29.1 %collective-permute-start.32 = (bf16[24,1536]{1,0:T(8,128)(2,1)S(1)}, bf16[24,1536]{1,0:T(8,128)(2,1)S(1)}, u32[]{:S(2)}, u32[]{:S(2)}) collective-permute-start(bf16[24,1536]{1,0:T(8,128)(2,1)S(1)} %get-tuple-element.139), channel_id=1, source_target_pairs={{0,4},{1,5},{2,6},{3,7},{4,0},{5,1},{6,2},{7,3},{8,12},{9,13},{10,... | collective-permute-start | bytes 221192 | tf_op jit(solution)/shard_map/weight_grads/ppermute | solution.py:69
  210.0 18.5 %collective-permute-start.30 = (bf16[1,2,3,64,512]{4,3,2,1,0:T(8,128)(2,1)S(1)}, bf16[1,2,3,64,512]{4,3,2,1,0:T(8,128)(2,1)S(1)}, u32[]{:S(2)}, u32[]{:S(2)}) collective-permute-start(bf16[1,2,3,64,512]{4,3,2,1,0:T(8,128)(2,1)S(1)} %add_convert_fusion.9), channel_id=1, source_target_pairs={{0,2},{1,3},{2,0},{3,1},{4,6},{5,7},{6,4},{7,5},{8,10},{9,11},{10,... | collective-permute-start | bytes 1179656 | tf_op jit(solution)/shard_map/mixing_back/ppermute | solution.py:69
  211.1 25.0 %collective-permute-start.29 = (bf16[1,2,3,64,512]{4,3,2,1,0:T(8,128)(2,1)S(1)}, bf16[1,2,3,64,512]{4,3,2,1,0:T(8,128)(2,1)S(1)}, u32[]{:S(2)}, u32[]{:S(2)}) collective-permute-start(bf16[1,2,3,64,512]{4,3,2,1,0:T(8,128)(2,1)S(1)} %add_convert_fusion.12), channel_id=1, source_target_pairs={{0,2},{1,3},{2,0},{3,1},{4,6},{5,7},{6,4},{7,5},{8,10},{9,11},{10,... | collective-permute-start | bytes 1179656 | tf_op jit(solution)/shard_map/mixing_back/ppermute | solution.py:69
  228.4 26.4 %collective-permute-start.39 = (bf16[4,3,64,512]{3,2,1,0:T(8,128)(2,1)S(1)}, bf16[4,3,64,512]{3,2,1,0:T(8,128)(2,1)S(1)}, u32[]{:S(2)}, u32[]{:S(2)}) collective-permute-start(bf16[4,3,64,512]{3,2,1,0:T(8,128)(2,1)S(1)} %slice_bitcast_fusion), channel_id=1, source_target_pairs={{0,16},{1,17},{2,18},{3,19},{4,20},{5,21},{6,22},{7,23},{8,24},{9,... | collective-permute-start | bytes 2359304 | tf_op jit(solution)/shard_map/mixing_back/ppermute | solution.py:69
  236.4 13.5 %collective-permute-start.35 = (bf16[3,64,512]{2,1,0:T(8,128)(2,1)S(1)}, bf16[3,64,512]{2,1,0:T(8,128)(2,1)S(1)}, u32[]{:S(2)}, u32[]{:S(2)}) collective-permute-start(bf16[3,64,512]{2,1,0:T(8,128)(2,1)S(1)} %get-tuple-element.95), channel_id=1, source_target_pairs={{0,4},{1,5},{2,6},{3,7},{4,0},{5,1},{6,2},{7,3},{8,12},{9,13},{10,... | collective-permute-start | bytes 589832 | tf_op jit(solution)/shard_map/mixing_back/ppermute | solution.py:69
  236.8 18.0 %collective-permute-start.36 = (bf16[3,64,512]{2,1,0:T(8,128)(2,1)S(1)}, bf16[3,64,512]{2,1,0:T(8,128)(2,1)S(1)}, u32[]{:S(2)}, u32[]{:S(2)}) collective-permute-start(bf16[3,64,512]{2,1,0:T(8,128)(2,1)S(1)} %get-tuple-element.96), channel_id=1, source_target_pairs={{0,8},{1,9},{2,10},{3,11},{4,12},{5,13},{6,14},{7,15},{8,0},{9,1},... | collective-permute-start | bytes 589832 | tf_op jit(solution)/shard_map/mixing_back/ppermute | solution.py:69
  238.6 16.2 %collective-permute-start.37 = (bf16[3,64,512]{2,1,0:T(8,128)(2,1)S(1)}, bf16[3,64,512]{2,1,0:T(8,128)(2,1)S(1)}, u32[]{:S(2)}, u32[]{:S(2)}) collective-permute-start(bf16[3,64,512]{2,1,0:T(8,128)(2,1)S(1)} %get-tuple-element.97), channel_id=1, source_target_pairs={{0,12},{1,13},{2,14},{3,15},{4,8},{5,9},{6,10},{7,11},{8,4},{9,5},... | collective-permute-start | bytes 589832 | tf_op jit(solution)/shard_map/mixing_back/ppermute | solution.py:69
  240.9 13.9 %collective-permute-start.38 = (bf16[4,24,2304]{2,1,0:T(8,128)(2,1)S(1)}, bf16[4,24,2304]{2,1,0:T(8,128)(2,1)S(1)}, u32[]{:S(2)}, u32[]{:S(2)}) collective-permute-start(bf16[4,24,2304]{2,1,0:T(8,128)(2,1)S(1)} %add_convert_fusion.7), channel_id=1, source_target_pairs={{0,2},{1,3},{2,0},{3,1},{4,6},{5,7},{6,4},{7,5},{8,10},{9,11},{10,... | collective-permute-start | bytes 1327112 | tf_op jit(solution)/shard_map/weight_grads/ppermute | solution.py:69
  256.7 10.6 %collective-permute-start.40 = (bf16[16,24,768]{2,1,0:T(8,128)(2,1)S(1)}, bf16[16,24,768]{2,1,0:T(8,128)(2,1)S(1)}, u32[]{:S(2)}, u32[]{:S(2)}) collective-permute-start(bf16[16,24,768]{2,1,0:T(8,128)(2,1)S(1)} %get-tuple-element.108), channel_id=1, source_target_pairs={{0,1},{1,0},{2,3},{3,2},{4,5},{5,4},{6,7},{7,6},{8,9},{9,8},{10,11... | collective-permute-start | bytes 1769480 | tf_op jit(solution)/shard_map/value_grads/ppermute | solution.py:69
  257.8 14.4 %collective-permute-start.49 = (bf16[3,64,512]{2,1,0:T(8,128)(2,1)S(1)}, bf16[3,64,512]{2,1,0:T(8,128)(2,1)S(1)}, u32[]{:S(2)}, u32[]{:S(2)}) collective-permute-start(bf16[3,64,512]{2,1,0:T(8,128)(2,1)S(1)} %get-tuple-element.121), channel_id=1, source_target_pairs={{0,12},{1,13},{2,14},{3,15},{4,8},{5,9},{6,10},{7,11},{8,4},{9,5},... | collective-permute-start | bytes 589832 | tf_op jit(solution)/shard_map/mixing_back/ppermute | solution.py:69
  261.7 21.7 %collective-permute-start.48 = (bf16[3,64,512]{2,1,0:T(8,128)(2,1)S(1)}, bf16[3,64,512]{2,1,0:T(8,128)(2,1)S(1)}, u32[]{:S(2)}, u32[]{:S(2)}) collective-permute-start(bf16[3,64,512]{2,1,0:T(8,128)(2,1)S(1)} %get-tuple-element.122), channel_id=1, source_target_pairs={{0,8},{1,9},{2,10},{3,11},{4,12},{5,13},{6,14},{7,15},{8,0},{9,1},... | collective-permute-start | bytes 589832 | tf_op jit(solution)/shard_map/mixing_back/ppermute | solution.py:69
  266.9 16.4 %collective-permute-start.47 = (bf16[3,64,512]{2,1,0:T(8,128)(2,1)S(1)}, bf16[3,64,512]{2,1,0:T(8,128)(2,1)S(1)}, u32[]{:S(2)}, u32[]{:S(2)}) collective-permute-start(bf16[3,64,512]{2,1,0:T(8,128)(2,1)S(1)} %get-tuple-element.123), channel_id=1, source_target_pairs={{0,4},{1,5},{2,6},{3,7},{4,0},{5,1},{6,2},{7,3},{8,12},{9,13},{10,... | collective-permute-start | bytes 589832 | tf_op jit(solution)/shard_map/mixing_back/ppermute | solution.py:69
  267.6 17.6 %collective-permute-start.41 = (bf16[4,24,768]{2,1,0:T(8,128)(2,1)S(1)}, bf16[4,24,768]{2,1,0:T(8,128)(2,1)S(1)}, u32[]{:S(2)}, u32[]{:S(2)}) collective-permute-start(bf16[4,24,768]{2,1,0:T(8,128)(2,1)S(1)} %get-tuple-element.125), channel_id=1, source_target_pairs={{0,16},{1,17},{2,18},{3,19},{4,20},{5,21},{6,22},{7,23},{8,24},{9,... | collective-permute-start | bytes 442376 | tf_op jit(solution)/shard_map/value_grads/ppermute | solution.py:69
  272.2 13.0 %collective-permute-start.43 = (bf16[4,24,768]{2,1,0:T(8,128)(2,1)S(1)}, bf16[4,24,768]{2,1,0:T(8,128)(2,1)S(1)}, u32[]{:S(2)}, u32[]{:S(2)}) collective-permute-start(bf16[4,24,768]{2,1,0:T(8,128)(2,1)S(1)} %get-tuple-element.126), channel_id=1, source_target_pairs={{0,18},{1,19},{2,16},{3,17},{4,22},{5,23},{6,20},{7,21},{8,26},{9,... | collective-permute-start | bytes 442376 | tf_op jit(solution)/shard_map/value_grads/ppermute | solution.py:69
  272.2 13.0 %collective-permute-start.42 = (bf16[4,24,768]{2,1,0:T(8,128)(2,1)S(1)}, bf16[4,24,768]{2,1,0:T(8,128)(2,1)S(1)}, u32[]{:S(2)}, u32[]{:S(2)}) collective-permute-start(bf16[4,24,768]{2,1,0:T(8,128)(2,1)S(1)} %get-tuple-element.127), channel_id=1, source_target_pairs={{0,2},{1,3},{2,0},{3,1},{4,6},{5,7},{6,4},{7,5},{8,10},{9,11},{10,... | collective-permute-start | bytes 442376 | tf_op jit(solution)/shard_map/value_grads/ppermute | solution.py:69
  285.3 10.6 %collective-permute-start.44 = (bf16[24,768]{1,0:T(8,128)(2,1)S(1)}, bf16[24,768]{1,0:T(8,128)(2,1)S(1)}, u32[]{:S(2)}, u32[]{:S(2)}) collective-permute-start(bf16[24,768]{1,0:T(8,128)(2,1)S(1)} %get-tuple-element.144), channel_id=1, source_target_pairs={{0,4},{1,5},{2,6},{3,7},{4,0},{5,1},{6,2},{7,3},{8,12},{9,13},{10,... | collective-permute-start | bytes 110600 | tf_op jit(solution)/shard_map/value_grads/ppermute | solution.py:69
  285.6 10.3 %collective-permute-start.46 = (bf16[24,768]{1,0:T(8,128)(2,1)S(1)}, bf16[24,768]{1,0:T(8,128)(2,1)S(1)}, u32[]{:S(2)}, u32[]{:S(2)}) collective-permute-start(bf16[24,768]{1,0:T(8,128)(2,1)S(1)} %get-tuple-element.145), channel_id=1, source_target_pairs={{0,12},{1,13},{2,14},{3,15},{4,8},{5,9},{6,10},{7,11},{8,4},{9,5},... | collective-permute-start | bytes 110600 | tf_op jit(solution)/shard_map/value_grads/ppermute | solution.py:69
  287.9 8.0 %collective-permute-start.45 = (bf16[24,768]{1,0:T(8,128)(2,1)S(1)}, bf16[24,768]{1,0:T(8,128)(2,1)S(1)}, u32[]{:S(2)}, u32[]{:S(2)}) collective-permute-start(bf16[24,768]{1,0:T(8,128)(2,1)S(1)} %get-tuple-element.146), channel_id=1, source_target_pairs={{0,8},{1,9},{2,10},{3,11},{4,12},{5,13},{6,14},{7,15},{8,0},{9,1},... | collective-permute-start | bytes 110600 | tf_op jit(solution)/shard_map/value_grads/ppermute | solution.py:69
  290.1 7.2 %collective-permute-start.50 = (bf16[24,2304]{1,0:T(8,128)(2,1)S(1)}, bf16[24,2304]{1,0:T(8,128)(2,1)S(1)}, u32[]{:S(2)}, u32[]{:S(2)}) collective-permute-start(bf16[24,2304]{1,0:T(8,128)(2,1)S(1)} %get-tuple-element.128), channel_id=1, source_target_pairs={{0,4},{1,5},{2,6},{3,7},{4,0},{5,1},{6,2},{7,3},{8,12},{9,13},{10,... | collective-permute-start | bytes 331784 | tf_op jit(solution)/shard_map/weight_grads/ppermute | solution.py:69
  291.3 7.9 %collective-permute-start.52 = (bf16[24,2304]{1,0:T(8,128)(2,1)S(1)}, bf16[24,2304]{1,0:T(8,128)(2,1)S(1)}, u32[]{:S(2)}, u32[]{:S(2)}) collective-permute-start(bf16[24,2304]{1,0:T(8,128)(2,1)S(1)} %get-tuple-element.129), channel_id=1, source_target_pairs={{0,12},{1,13},{2,14},{3,15},{4,8},{5,9},{6,10},{7,11},{8,4},{9,5},... | collective-permute-start | bytes 331784 | tf_op jit(solution)/shard_map/weight_grads/ppermute | solution.py:69
  295.9 7.2 %collective-permute-start.51 = (bf16[24,2304]{1,0:T(8,128)(2,1)S(1)}, bf16[24,2304]{1,0:T(8,128)(2,1)S(1)}, u32[]{:S(2)}, u32[]{:S(2)}) collective-permute-start(bf16[24,2304]{1,0:T(8,128)(2,1)S(1)} %get-tuple-element.130), channel_id=1, source_target_pairs={{0,8},{1,9},{2,10},{3,11},{4,12},{5,13},{6,14},{7,15},{8,0},{9,1},... | collective-permute-start | bytes 331784 | tf_op jit(solution)/shard_map/weight_grads/ppermute | solution.py:69
  (28 other events, 241.6 us)
Sparse Core Ops, SparseCore 0:
  11.5 125.8 all-gather.2
  165.1 126.6 reduce-scatter.1

commit v3 on v2

--- a/solution.py
+++ b/solution.py
@@ -14,6 +14,8 @@
 GROUPS = 4
 EPS = 1e-06
 COST = 50_000_000_000
+FIRST = 2
+SPLIT = 3
 MIB = 1 << 20
 
 
@@ -212,8 +214,8 @@
 
 
 def mix_kernel(me, *refs, xs, positions):
-    values = refs[: 2 * xs * GROUPS]
-    refs = refs[2 * xs * GROUPS :]
+    values = refs[: 2 * xs]
+    refs = refs[2 * xs :]
     near, far, rows_out, values_out, mixed = refs
     z, x, c, side = me[1], me[2], me[3], me[0] % 2
     half = positions // 2
@@ -226,10 +228,9 @@
         for j in range(xs):
             for k in range(GROUPS):
                 block = ((z ^ k) * xs + (x ^ j)) * 2 + (c ^ m)
-                values_out[:, pl.ds(pl.multiple_of(block * positions, positions), positions), :] = values[
-                    index
-                ][...]
-                index += 1
+                start = pl.multiple_of(block * positions, positions)
+                values_out[:, pl.ds(start, positions), :] = values[index][k]
+            index += 1
     for head in range(rows_out.shape[0]):
         result = dot_nn(rows_out[head], values_out[head]).astype(BF16)
         for k in range(GROUPS):
@@ -255,82 +256,115 @@
     return result
 
 
-def dense(block):
-    value = block[...]
-    if value.ndim == 2:
-        return value
-    return value.astype(F32).reshape(-1, value.shape[-1]).astype(BF16)
-
-
-def down_block(down, width):
-    if down.ndim == 2:
-        return pl.BlockSpec((width, width), lambda i, *_: (i, 0))
-    devices, kinds, short, _ = down.shape
-    parts = (kinds - 1) // 2
-    return pl.BlockSpec((devices // parts, parts, short, width), lambda i, *_: (i, 0, 0, 0))
-
-
-def up_block(up, width):
-    if up.ndim == 2:
-        return pl.BlockSpec((width, width), lambda i, *_: (0, i))
-    devices, kinds, short, _ = up.shape
-    parts = (kinds - 1) // 2
-    return pl.BlockSpec((devices, 1, short, width), lambda i, *_: (0, parts + i, 0, 0))
-
-
-def out_block(out, width):
-    if out.ndim == 2:
-        return pl.BlockSpec((width, width), lambda i, *_: (0, 0))
-    devices, kinds, short, _ = out.shape
-    return pl.BlockSpec((devices, 1, short, width), lambda i, *_: (0, kinds - 1, 0, 0))
-
-
 ROOT = 0.7978845608028654
 CUBE = 0.044715
 
 
+def prepare_kernel(me, *refs):
+    ups, out = refs[:4], refs[4]
+    step, rows = pl.program_id(0), out.shape[0] // refs[0].shape[0]
+
+    def store(chip, block):
+        out[pl.ds(pl.multiple_of(chip * rows, rows), rows), :] = block
+
+    pl.when(step < SPLIT)(lambda: gather_rows(me, ups[0].at[:, 0], ups[1].at[:, 0], store, True))
+    pl.when(step >= SPLIT)(lambda: gather_rows(me, ups[2].at[:, 0], ups[3].at[:, 0], store, False))
+
+
+def prepare_weights(lay, ups):
+    chips, _, short, width = ups[0].shape
+    kinds = ups[0].shape[1] + ups[2].shape[1]
+    block = (chips, 1, short, width)
+    specs = [pl.BlockSpec(block, lambda i, me: (0, jnp.minimum(i, SPLIT - 1), 0, 0))] * 2
+    specs += [pl.BlockSpec(block, lambda i, me: (0, jnp.maximum(i - SPLIT, 0), 0, 0))] * 2
+    return pl.pallas_call(
+        prepare_kernel,
+        grid_spec=pltpu.PrefetchScalarGridSpec(
+            num_scalar_prefetch=1,
+            grid=(kinds,),
+            in_specs=specs,
+            out_specs=pl.BlockSpec((width, width), lambda i, me: (0, i)),
+        ),
+        out_shape=shape((width, kinds * width)),
+        compiler_params=params(24),
+        cost_estimate=cost(width * width * kinds, 4 * width * width * kinds),
+        name="prepare_weights",
+    )(lay.me, *ups)
+
+
 def middle_kernel(me, *refs, positions, sequences, heads, spread):
-    pieces, tokens, out_grad, w_out, w_up, w_down, layer_out, residual_grad, parts = refs[:9]
-    grads = refs[9:-7]
+    step, last = pl.program_id(0), pl.num_programs(0) - 1
+    if spread:
+        *refs, w_down = refs
+        pieces, tokens, out_grad, w_out, up = refs[:5]
+        downs = refs[5:13]
+        layer_out, residual_grad, parts = refs[13:16]
+        grads = refs[16:-7]
+        first, half_tall = me[3] == 0, downs[0].shape[1]
+        count = w_down.shape[0] // (4 * half_tall)
+        for i in range(count):
+            for part in range(2):
+                slot = slot_of(me, step * count + i, part == 0)
+                far, slot = slot >= 8, slot % 8
+                near_own, far_own, near_other, far_other = downs[4 * part : 4 * part + 4]
+                mine = jnp.where(far, far_own[slot], near_own[slot])
+                theirs = jnp.where(far, far_other[slot], near_other[slot])
+                start = (4 * i + part) * half_tall
+                w_down[start : start + half_tall, :] = jnp.where(first, mine, theirs)
+                start += 2 * half_tall
+                w_down[start : start + half_tall, :] = jnp.where(first, theirs, mine)
+    else:
+        pieces, tokens, out_grad, w_out, up, w_down, layer_out, residual_grad, parts = refs[:9]
+        grads = refs[9:-7]
     residual, normed, mixed, total, layer, scratch, result = refs[-7:]
-    step, last = pl.program_id(0), pl.num_programs(0) - 1
 
     @pl.when(step == 0)
     def _():
         from_heads(pieces, scratch, positions, sequences, heads)
         join_lanes(scratch, mixed)
-        value = tokens[...].astype(F32) + dot_nn(mixed[...], dense(w_out))
+        value = tokens[...].astype(F32) + dot_nn(mixed[...], w_out[...])
         residual[...] = value
         scale = lax.rsqrt(jnp.mean(value * value, axis=-1, keepdims=True) + EPS)
         normed[...] = (value * scale).astype(BF16)
         layer[...] = value
         total[...] = jnp.zeros_like(total)
 
-    up, down = dense(w_up), dense(w_down)
-    u = dot_nn(normed[...], up)
+    down = w_down[...]
+    u = dot_nn(normed[...], up[...])
     back = dot_nt(out_grad[...], down)
     square = u * u
-    tanh = jnp.tanh(ROOT * u * (1.0 + CUBE * square))
-    half = 0.5 * (1.0 + tanh)
-    hidden = (u * half).astype(BF16)
-    slope = half + 0.5 * u * (1.0 - tanh * tanh) * (ROOT * (1.0 + 3.0 * CUBE * square))
+    tanh = jnp.tanh(u * (ROOT + ROOT * CUBE * square))
+    half = 0.5 + 0.5 * tanh
+    active = u * half
+    hidden = active.astype(BF16)
+    slope = half + active * (1.0 - tanh) * (ROOT + 3.0 * ROOT * CUBE * square)
     pre = (slope * back).astype(BF16)
-    total[...] += dot_nt(pre, up)
+    total[...] += dot_nt(pre, up[...])
     layer[...] += dot_nn(hidden, down)
     if spread:
-        a_own, a_other, b_own, b_other, d_down = grads
-        short = a_own.shape[1]
+        a_own, a_other, b_own, b_other, *c_parts = grads
+        short, half_tall = a_own.shape[1], c_parts[0].shape[1]
         width = result.shape[0]
-        d_down[...] = dot_tn(hidden, out_grad[...]).astype(BF16)
+        result[...] = dot_tn(hidden, out_grad[...])
+        for i in range(width // (4 * half_tall)):
+            chip = step * (width // (4 * half_tall)) + i
+            for part in range(2):
+                slot = slot_of(me, chip, part == 0)
+                for ref, core in ((c_parts[2 * part], me[3]), (c_parts[2 * part + 1], 1 - me[3])):
+                    start = pl.multiple_of(((2 * i + core) * 2 + part) * half_tall, half_tall)
+                    ref[slot] = result[pl.ds(start, half_tall), :].astype(BF16)
         result[...] = dot_tn(normed[...], pre)
 
-        @pl.when(step < last)
+        @pl.when(step < FIRST)
         def _():
             spread_rows(me, result, a_own, a_other, short, False)
 
-        @pl.when(step == last)
-        def _():
-            spread_rows(me, result, b_own.at[:, :, :width], b_other.at[:, :, :width], short, True)
+        for kind in range(b_own.shape[2] // width - 1):
+
+            @pl.when(step == FIRST + kind)
+            def _(kind=kind):
+                part = pl.ds(kind * width, width)
+                spread_rows(me, result, b_own.at[:, :, part], b_other.at[:, :, part], short, True)
     else:
         d_up, d_down, d_out = grads
         d_down[...] = dot_tn(hidden, out_grad[...]).astype(BF16)
@@ -347,11 +381,12 @@
         grad = out_grad[...].astype(F32) + back
         residual_grad[...] = grad
         attn_grad = grad.astype(BF16)
-        split_lanes(dot_nt(attn_grad, dense(w_out)), scratch)
+        split_lanes(dot_nt(attn_grad, w_out[...]), scratch)
         to_heads(scratch, parts, positions, sequences, heads)
         if spread:
             result[...] = dot_tn(mixed[...], attn_grad)
-            spread_rows(me, result, b_own.at[:, :, width:], b_other.at[:, :, width:], short, True)
+            part = pl.ds(b_own.shape[2] - width, width)
+            spread_rows(me, result, b_own.at[:, :, part], b_other.at[:, :, part], short, True)
         else:
             d_out[...] = dot_tn(mixed[...], attn_grad).astype(BF16)
 
@@ -360,20 +395,31 @@
     rows, width = tokens.shape
     steps = hidden // width
     piece = (GROUPS, lay.group, lay.positions, lay.lanes)
-    chips, short = lay.devices // 2, width // lay.devices
+    chips, short, tall = lay.devices // 2, width // lay.devices, hidden // lay.devices
     flat = (rows, width)
 
     def whole(*dims):
         return pl.BlockSpec(dims, lambda i, me: (0,) * len(dims))
 
     if lay.small:
-        grads = [(chips, short, (steps - 1) * width)] * 2 + [(chips, short, 2 * width)] * 2
-        grads += [(hidden, width)]
+        weights = [up_weight, up_weight, *down_weight]
+        weight_specs = [
+            pl.BlockSpec((width, width), lambda i, me: (0, steps)),
+            pl.BlockSpec((width, width), lambda i, me: (0, i)),
+        ]
+        weight_specs += [whole(*array.shape) for array in down_weight]
+        grads = [(chips, short, FIRST * width)] * 2 + [(chips, short, (steps + 1 - FIRST) * width)] * 2
+        grads += [(chips, tall // 2, width)] * 4
         block = (chips, short, width)
-        specs = [pl.BlockSpec(block, lambda i, me: (0, 0, jnp.minimum(i, steps - 2)))] * 2
-        specs += [whole(*dims) for dims in grads[2:4]]
-        specs += [pl.BlockSpec((width, width), lambda i, me: (i, 0))]
+        specs = [pl.BlockSpec(block, lambda i, me: (0, 0, jnp.minimum(i, FIRST - 1)))] * 2
+        specs += [whole(*dims) for dims in grads[2:]]
     else:
+        weights = [out_weight, up_weight, down_weight]
+        weight_specs = [
+            whole(width, width),
+            pl.BlockSpec((width, width), lambda i, me: (0, i)),
+            pl.BlockSpec((width, width), lambda i, me: (i, 0)),
+        ]
         grads = [(width, hidden), (hidden, width), (width, width)]
         specs = [
             pl.BlockSpec((width, width), lambda i, me: (0, i)),
@@ -392,7 +438,7 @@
             num_scalar_prefetch=1,
             grid=(steps,),
             in_specs=[whole(*piece), whole(*flat), whole(*flat)]
-            + [out_block(out_weight, width), up_block(up_weight, width), down_block(down_weight, width)],
+            + weight_specs,
             out_specs=[whole(*flat), whole(*flat), whole(*piece)] + specs,
             scratch_shapes=[
                 pltpu.VMEM(flat, F32),
@@ -402,13 +448,14 @@
                 pltpu.VMEM(flat, F32),
                 pltpu.VMEM((width // 128, rows, 128), F32),
                 pltpu.VMEM((width, width), F32),
-            ],
+            ]
+            + [pltpu.VMEM((width, width), BF16)] * (1 if lay.small else 0),
         ),
         out_shape=[shape(flat), shape(flat, F32), shape(piece)] + [shape(dims) for dims in grads],
         compiler_params=params(60),
         cost_estimate=cost(12 * rows * width * hidden, 16 * width * hidden, rows * hidden),
         name="middle",
-    )(lay.me, pieces, tokens, out_grad, out_weight, up_weight, down_weight)
+    )(lay.me, pieces, tokens, out_grad, *weights)
     return out[0], out[1], out[2], list(out[3:])
 
 
@@ -429,8 +476,8 @@
 def back_kernel(me, *refs, xs, dps, positions, by_distance):
     pieces, rows, values = refs[:3]
     outs = refs[3:]
-    logit_out, term_outs = outs[0], outs[1:5]
-    grads, term, logit = outs[5:]
+    logit_out, term_outs = outs[0], outs[1:3]
+    grads, term, logit = outs[3:]
     dp, z, x, c = me[0], me[1], me[2], me[3]
     part = logit_out.shape[-1]
     for k in range(GROUPS):
@@ -443,14 +490,15 @@
         for r in range(dps):
             for k in range(GROUPS):
                 start = pl.multiple_of((dp ^ r if by_distance else r) * part, part)
-                base = pl.multiple_of((z ^ k) * positions, positions)
-                logit_out[r, k, head] = logit[pl.ds(base, positions), pl.ds(start, part)]
+                logit_out[r, k, head] = logit[
+                    k * positions : (k + 1) * positions, pl.ds(start, part)
+                ]
     for m in range(2):
         for k in range(GROUPS):
             for j in range(xs):
                 block = ((z ^ k) * xs + (x ^ j)) * 2 + (c ^ m)
-                out = term_outs[2 * m + k // 2]
-                out[j, k % 2] = term[:, pl.ds(pl.multiple_of(block * positions, positions), positions), :]
+                start = pl.multiple_of(block * positions, positions)
+                term_outs[m][j, k] = term[:, pl.ds(start, positions), :]
 
 
 def mix_back(lay, pieces, rows, values):
@@ -461,9 +509,9 @@
             back_kernel, xs=lay.xs, dps=lay.dp, positions=positions, by_distance=lay.small
         ),
         in_specs=[smem()] + [vmem()] * 3,
-        out_specs=[vmem()] * 5,
+        out_specs=[vmem()] * 3,
         out_shape=[shape((lay.dp, GROUPS, group, positions, part))]
-        + [shape((lay.xs, 2, group, positions, lanes))] * 4,
+        + [shape((lay.xs, GROUPS, group, positions, lanes))] * 2,
         scratch_shapes=[
             pltpu.VMEM((group, GROUPS * positions, lanes), BF16),
             pltpu.VMEM((group, length, lanes), BF16),
@@ -562,6 +610,65 @@
     return out.reshape(lay.heads, positions, part)
 
 
+def add_kernel(*refs):
+    left, right, *outs = refs
+    half = outs[0].shape[0]
+    for i, out in enumerate(outs):
+        part = pl.ds(i * half, half)
+        out[...] = (left[part].astype(F32) + right[part].astype(F32)).astype(BF16)
+
+
+def add_split(left, right, parts=2):
+    dims = (left.shape[0] // parts,) + left.shape[1:]
+    return pl.pallas_call(
+        add_kernel,
+        out_shape=[shape(dims)] * parts,
+        in_specs=[vmem()] * 2,
+        out_specs=[vmem()] * parts,
+        compiler_params=params(24),
+        cost_estimate=cost(left.size, 6 * left.size),
+        name="add_split",
+    )(left, right)
+
+
+def stack_kernel(*refs):
+    *parts, out = refs
+    for i, part in enumerate(parts):
+        out[i] = part[...]
+
+
+def stack_all(parts):
+    return pl.pallas_call(
+        stack_kernel,
+        out_shape=shape((len(parts),) + parts[0].shape),
+        in_specs=[vmem()] * len(parts),
+        out_specs=vmem(),
+        compiler_params=params(24),
+        cost_estimate=cost(0, 4 * len(parts) * parts[0].size),
+        name="stack_all",
+    )(*parts)
+
+
+def total_kernel(*refs):
+    *parts, out = refs
+    total = parts[0][...].astype(F32)
+    for part in parts[1:]:
+        total = total + part[...].astype(F32)
+    out[...] = total.astype(BF16)
+
+
+def add_all(parts):
+    return pl.pallas_call(
+        total_kernel,
+        out_shape=shape(parts[0].shape),
+        in_specs=[vmem()] * len(parts),
+        out_specs=vmem(),
+        compiler_params=params(24),
+        cost_estimate=cost(len(parts) * parts[0].size, 4 * len(parts) * parts[0].size),
+        name="add_all",
+    )(*parts)
+
+
 def after(value, *done):
     return lax.optimization_barrier((value, done))[0]
 
@@ -612,43 +719,67 @@
     up_rows = (gain_two * up_weight.astype(F32)).astype(BF16)
     small = lay.small
 
-    with jax.named_scope("weight_gather"):
-        if small:
-            packed = jnp.concatenate(
-                [
-                    down_weight.reshape((-1,) + value_rows.shape),
-                    up_rows.reshape(up_rows.shape[0], -1, width).swapaxes(0, 1),
-                    out_weight[None],
-                ]
-            )
-            w_down = w_up = w_out = lax.all_gather(packed, AXES, axis=0)
-        else:
-            w_up = lax.all_gather(up_rows, AXES, axis=0, tiled=True)
-            w_out = lax.all_gather(out_weight, AXES, axis=0, tiled=True)
-            w_down = lax.all_gather(down_weight, AXES, axis=0, tiled=True)
+    tie = lax.optimization_barrier
     rows = softmax_rows(lay, mixer_logits)
-    with jax.named_scope("mixing_rows"):
-        rows = lay.across_z(rows)
-    with jax.named_scope("value_weight_gather"):
-        if small:
-            own = along_z_gather(lay, value_rows)
+    if small:
+        with jax.named_scope("round_one"):
+            kinds = up_rows.reshape(up_rows.shape[0], -1, width).swapaxes(0, 1)
+            wide = jnp.concatenate([kinds, out_weight[None], value_rows[None]])
+            wide = [wide] + [lay.swap(wide, z=k) for k in range(1, GROUPS)]
+            *wide, rows = tie((*wide, rows))
+        with jax.named_scope("round_two"):
+            rows = lay.across_z(rows)
+            own = jnp.stack([part[-1] for part in wide])
+            wide = jnp.stack([part[:-1] for part in wide])
+            one, two = wide[:, :SPLIT], wide[:, SPLIT:]
             four = [own, lay.swap(own, dp=1), lay.swap(own, x=1), lay.swap(own, dp=1, x=1)]
+            one_other, two_other = lay.swap(one, dp=1), lay.swap(two, x=1)
             own = jnp.concatenate(four)
             w_value = [own, lay.swap(own, c=1)]
-        else:
-            w_value = [lax.all_gather(value_rows, AXES, axis=0, tiled=True)]
-        w_value = after(w_value, rows)
-    with jax.named_scope("values"):
+            w_value, one_other, two_other, rows = tie((w_value, one_other, two_other, rows))
+        with jax.named_scope("round_three"):
+            normed_one, w_value, value_parts = make_values(lay, tokens, w_value)
+            first = along_z(lay, value_parts)
+            one, two = jnp.concatenate([one, one_other]), jnp.concatenate([two, two_other])
+            one_other, two_other = lay.swap(one, x=1), lay.swap(two, dp=1)
+            first, one_other, two_other = tie((first, one_other, two_other))
+        with jax.named_scope("round_four"):
+            values = stack_all(first)
+            values_other = lay.swap(values, x=1)
+            rows_other = lay.swap(rows, dp=1)
+            tall = [down_weight] + [lay.swap(down_weight, z=k) for k in range(1, GROUPS)]
+            values_other, rows_other, tall = tie((values_other, rows_other, tall))
+            rows = [rows, rows_other]
+        with jax.named_scope("round_five"):
+            values = [values, values_other, lay.swap(values, c=1), lay.swap(values_other, c=1)]
+            mix_low, values, pieces = mix_values(lay, values, rows)
+            pieces = lay.across_z(pieces)
+            tall, one, two, one_other, two_other = after(
+                (tall, one, two, one_other, two_other), mix_low
+            )
+            tall = jnp.stack(tall)
+            cut = tall.shape[1] // 2
+            three, four = tall[:, :cut], tall[:, cut:]
+            three_other, four_other = lay.swap(three, dp=1), lay.swap(four, x=1)
+            one, two = jnp.concatenate([one, one_other]), jnp.concatenate([two, two_other])
+            w_up = prepare_weights(lay, [one, lay.swap(one, c=1), two, lay.swap(two, c=1)])
+            three, four = jnp.concatenate([three, three_other]), jnp.concatenate([four, four_other])
+            three_other, four_other = lay.swap(three, x=1), lay.swap(four, dp=1)
+            w_down = [three, three_other, four, four_other]
+            w_down += [lay.swap(array, c=1) for array in w_down]
+            w_down = [w_down[i] for i in (0, 1, 4, 5, 2, 3, 6, 7)]
+            w_out = None
+    else:
+        w_up = lax.all_gather(up_rows, AXES, axis=0, tiled=True)
+        w_out = lax.all_gather(out_weight, AXES, axis=0, tiled=True)
+        w_down = lax.all_gather(down_weight, AXES, axis=0, tiled=True)
+        w_value = [lax.all_gather(value_rows, AXES, axis=0, tiled=True)]
+        rows = lay.across_z(rows)
+        rows = [rows, lay.swap(rows, dp=1)]
         normed_one, w_value, value_parts = make_values(lay, tokens, w_value)
-        first = along_z(lay, value_parts)
-    with jax.named_scope("mixing_rows"):
-        rows = [rows, lay.swap(rows, dp=1)]
-    with jax.named_scope("values"):
-        values = list(first)
-        for j in range(1, lay.xs):
-            values += [lay.swap(piece, x=j) for piece in first]
-        values = values + [lay.swap(piece, c=1) for piece in after(values, rows[1])]
-    with jax.named_scope("mixing"):
+        values = [jnp.stack(along_z(lay, value_parts))]
+        values += [lay.swap(values[0], x=j) for j in range(1, lay.xs)]
+        values += [lay.swap(piece, c=1) for piece in values]
         mix_low, values, pieces = mix_values(lay, values, rows)
         pieces = lay.across_z(pieces)
     with jax.named_scope("feed_forward"):
@@ -658,78 +789,85 @@
         pieces = lay.across_z(pieces)
     with jax.named_scope("weight_grads"):
         if small:
-            a_own, a_other, b_own, b_other, c_grad = grads
-            down_grad = scatter_sum(c_grad)
+            a_own, a_other, b_own, b_other, *c_parts = grads
+            c_one, one_send = halves(c_parts[0], lay.swap(c_parts[1], c=1))
+            c_two, two_send = halves(c_parts[2], lay.swap(c_parts[3], c=1))
+            one_other, two_other = lay.swap(one_send, x=1), lay.swap(two_send, dp=1)
+            a_own, a_send = halves(a_own, lay.swap(a_other, c=1))
             b_own, b_send = halves(b_own, lay.swap(b_other, c=1))
-            b_other = lay.swap(b_send, x=1)
-            a_own, a_send = halves(a_own, lay.swap(a_other, c=1))
-            pieces = after(pieces, b_other, a_send)
-            a_other = lay.swap(a_send, dp=1)
-            b_own, b_send = halves(b_own, after(b_other, a_send))
-            b_other = lay.swap(b_send, dp=1)
+            pieces, one_other, two_other, a_send, b_send = tie(
+                (pieces, one_other, two_other, a_send, b_send)
+            )
+            c_one, one_send = halves(c_one, one_other)
+            c_two, two_send = halves(c_two, two_other)
+            one_other, two_other = lay.swap(one_send, dp=1), lay.swap(two_send, x=1)
     with jax.named_scope("mixing_back"):
         logit_parts, terms = mix_back(lay, pieces, mix_low, values)
-        others = [lay.swap(terms[2 + k], c=1) for k in (0, 1)]
-        if small:
-            others = after(others, b_other)
-        arrived = []
-        for k in (1, 0):
-            piece, other = terms[k], others[k]
+    if small:
+        with jax.named_scope("mixing_back"):
+            terms, one_other, two_other = tie((terms, one_other, two_other))
+            term, term_send = add_split(terms[0], lay.swap(terms[1], c=1))
+            term_other = lay.swap(term_send, x=1)
+            logit_other = lay.swap(logit_parts[1], dp=1)
+        with jax.named_scope("weight_grads"):
+            c_sum = jnp.concatenate([add_low(c_one, one_other), add_low(c_two, two_other)], axis=1)
+            c_rest = [lay.swap(c_sum[k], z=k) for k in range(1, GROUPS)]
+        with jax.named_scope("mixing_back"):
+            term_other, logit_other, c_rest = tie((term_other, logit_other, c_rest))
+            (term,) = add_split(term[0], term_other[0], 1)
+            pieces = along_z(lay, [term[k] for k in range(GROUPS)])
+        with jax.named_scope("weight_grads"):
+            a_other = lay.swap(after(a_send, term), dp=1)
+            b_other = lay.swap(after(b_send, term), x=1)
+            pieces, a_other, b_other = tie((pieces, a_other, b_other))
+        with jax.named_scope("value_grads"):
+            total, own, other = value_grads(lay, pieces, normed_one)
+            other = lay.swap(other, c=1)
+        with jax.named_scope("mixing_back"):
+            logit_parts = add_low(logit_parts[0], after(logit_other, total))
+            logit_parts = lay.across_z(logit_parts)
+        with jax.named_scope("value_grads"):
+            own = add_split(own, other, 4)
+            parts = [lay.swap(own[1], dp=1), lay.swap(own[2], x=1), lay.swap(own[3], dp=1, x=1)]
+        with jax.named_scope("weight_grads"):
+            a_own, a_send = halves(a_own, after(a_other, own))
+            b_own, b_send = halves(b_own, after(b_other, own))
+            a_other, b_other = lay.swap(a_send, x=1), lay.swap(b_send, dp=1)
+        with jax.named_scope("value_grads"):
+            parts, a_other, b_other, logit_parts = tie((parts, a_other, b_other, logit_parts))
+            own = add_all([own[0]] + list(parts))
+        with jax.named_scope("weight_grads"):
+            last = jnp.concatenate([own, add_low(a_own, a_other), add_low(b_own, b_other)], axis=2)
+            last = sum_z(lay, last)
+            value_sum, up_sum, out_wgrad = last[:, :width], last[:, width:-width], last[:, -width:]
+            down_grad = c_sum[0].astype(F32)
+            for part in c_rest:
+                down_grad = down_grad + part.astype(F32)
+            down_grad, total, logit_parts = after((down_grad, total, logit_parts), own)
+        with jax.named_scope("mixing_back"):
+            logits_grad = logit_parts.astype(F32).reshape(lay.heads, lay.positions, -1)
+    else:
+        with jax.named_scope("mixing_back"):
+            piece, other = terms[0], lay.swap(terms[1], c=1)
             bit = lay.xs // 2
             while bit:
                 piece, send = halves(piece, other)
                 other = lay.swap(send, x=bit)
                 bit //= 2
-            if small and k == 1:
-                other = after(other, a_other)
-            arrived.append(add_low(piece[0], other[0]))
-        arrived = [arrived[1][0], arrived[1][1], arrived[0][0], arrived[0][1]]
-    with jax.named_scope("weight_grads"):
-        if small:
-            a_own, a_send = halves(a_own, a_other)
-            b_sum = add_low(b_own, b_other)
-            b_parts = [lay.swap(b_sum[k], z=k) for k in range(1, GROUPS)]
-            arrived = after(arrived, b_parts)
-            a_other = lay.swap(after(a_send, arrived), x=1)
-    with jax.named_scope("mixing_back"):
-        pieces = along_z(lay, arrived)
-        if small:
-            logit_other = lay.swap(after(logit_parts[1], a_send), dp=1)
-            pieces = after(pieces, a_other, logit_other)
-        else:
+            piece = add_low(piece[0], other[0])
+            pieces = along_z(lay, [piece[k] for k in range(GROUPS)])
             logit_parts = lax.psum_scatter(logit_parts, "dp", scatter_dimension=0)
+            logits_grad = lay.across_z(logit_parts).astype(F32).reshape(lay.heads, lay.positions, -1)
+        with jax.named_scope("value_grads"):
+            (total,) = value_grads(lay, pieces, normed_one)
+            value_sum = scatter_sum(dot_tn(normed_one, total))
+        with jax.named_scope("weight_grads"):
+            up_sum, down_grad, out_wgrad = (scatter_sum(grad) for grad in grads)
     with jax.named_scope("value_grads"):
-        total, *spread = value_grads(lay, pieces, normed_one)
-        if small:
-            own, other = spread
-            own = add_low(own, lay.swap(other, c=1))
-            four = own.reshape((4, GROUPS) + own.shape[1:])
-            parts = [lay.swap(four[1], dp=1), lay.swap(four[2], x=1), lay.swap(four[3], dp=1, x=1)]
-            own = four[0].astype(F32)
-            for part in parts:
-                own = own + part.astype(F32)
-            own = own.astype(BF16)
-            value_sum = sum_z(lay, own)
-        else:
-            value_sum = scatter_sum(dot_tn(normed_one, total))
+        tokens_grad = make_tokens_grad(total, w_value, tokens, residual_grad)
         value_wgrad = gain_one * value_sum
         gain_one_grad = jnp.sum(value_sum * value_weight.astype(F32), axis=1)
-    with jax.named_scope("mixing_back"):
-        if small:
-            logit_parts = add_low(logit_parts[0], after(logit_other, total))
-        logits_grad = make_logits_grad(lay, along_z(lay, logit_parts))
     with jax.named_scope("weight_grads"):
-        if small:
-            a_sum = sum_z(lay, add_low(a_own, after(a_other, own)))
-            b_total = b_sum[0].astype(F32)
-            for part in b_parts:
-                b_total = b_total + part.astype(F32)
-            up_sum = jnp.concatenate([a_sum, b_total[:, :width]], axis=1)
-            out_wgrad = b_total[:, width:]
-            total = after(total, own)
-        else:
-            up_sum, down_grad, out_wgrad = (scatter_sum(grad) for grad in grads)
-        tokens_grad = make_tokens_grad(total, w_value, tokens, residual_grad)
         up_grad = gain_two * up_sum
         gain_two_grad = jnp.sum(up_sum * up_weight.astype(F32), axis=1)
     return (

time: 314 us -> 311 us (level)
  blocking collectives: 38.9 us -> 0 us
  waiting for transfers between devices: 120 us -> 143 us
  between operations: 14.5 us -> 1.49 us
  Pallas kernels: 43.5 us -> 51.6 us
  local copies, waits for them, and re-layouts: 4.88 us -> 12.9 us
  other arithmetic: 18.4 us -> 26.3 us
    all_to_all x1 -> x0, blocking collectives: 38.9 us -> none  [across_z(): return lax.all_to_all(array, 'seq', 0, 0, axis_index_groups=lines)]
    ppermute x53 -> x59, waiting for transfers between devices: 104 us -> 131 us  [swap(): lax.ppermute(array, AXES, [(i, i ^ mask) for i in range(self.devices)])]
    all_to_all x2 -> x4, starting transfers between devices: 8.87 us -> 17.8 us  [across_z(): return lax.all_to_all(array, 'seq', 0, 0, axis_index_groups=lines)]
    unnamed x43 -> x116, local copies, waits for them, and re-layouts: 3.88 us -> 12.4 us
    ppermute x53 -> x59, starting transfers between devices: 64.2 us -> 56.9 us  [swap(): lax.ppermute(array, AXES, [(i, i ^ mask) for i in range(self.devices)])]
    convert_element_type x12 -> x13, other arithmetic: 10.3 us -> 15 us  [add_low(): return (left.astype(F32) + right.astype(F32)).astype(BF16)]
    pallas_call x1 -> x6, Pallas kernels: 1.79 us -> 5.81 us  [the longest x1 5 us: prepare_weights(): pl.pallas_call(prepare_kernel, grid_spec=pltpu.PrefetchScalarGridSpec(num...]
    pallas_call x1, Pallas kernels: 27 us -> 30.3 us  [middle(): pl.pallas_call(functools.partial(middle_kernel, positions=lay.positions,...]
  transfers between devices with their start and end apart: 57 -> 63, of which waited for: 27 -> 29; matrix products, arithmetic and copies ran while one was open for 5% -> 5% of each run, Pallas kernels for 5% -> 5%
where the time goes in v3:
time: 311 us; the launch traced here: 310 us
  waiting for transfers between devices  143 us (46%)
  starting transfers between devices  74.7 us (24%)
  Pallas kernels  51.6 us (17%)
  other arithmetic  26.3 us (8%)
  local copies, waits for them, and re-layouts  12.9 us (4%)
    ppermute x59, waiting for transfers between devices, swap(): lax.ppermute(array, AXES, [(i, i ^ mask) for i in range(self.devices)])  131 us
    ppermute x59, starting transfers between devices, swap(): lax.ppermute(array, AXES, [(i, i ^ mask) for i in range(self.devices)])  56.9 us
    pallas_call x1, Pallas kernels, middle(): pl.pallas_call(functools.partial(middle_kernel, positions=lay.positions,...  30.3 us
    all_to_all x4, starting transfers between devices, across_z(): return lax.all_to_all(array, 'seq', 0, 0, axis_index_groups=lines)  17.8 us
    convert_element_type x13, other arithmetic, add_low(): return (left.astype(F32) + right.astype(F32)).astype(BF16)  15 us
    unnamed x116, local copies, waits for them, and re-layouts  12.4 us
    all_to_all x4, waiting for transfers between devices, across_z(): return lax.all_to_all(array, 'seq', 0, 0, axis_index_groups=lines)  12.1 us
  transfers between devices with their start and end apart: 63, of which 29 were waited for; matrix products, arithmetic and copies ran while one was open for 5% of the time, Pallas kernels for 5%

profile of v3, /device:TPU:0, one launch (start us, length us, event | category | flops | bytes accessed | tf_op | source)
XLA Modules:
  0.0 310.1 jit_solution(13072471829515416913)
XLA Ops:
  4.6 5.1 %collective-permute-start.2 = (bf16[6,24,768]{2,1,0:T(8,128)(2,1)S(1)}, bf16[6,24,768]{2,1,0:T(8,128)(2,1)S(1)}, u32[]{:S(2)}, u32[]{:S(2)}) collective-permute-start(bf16[6,24,768]{2,1,0:T(8,128)(2,1)S(1)} %pad_maximum_fusion.8), channel_id=1, source_target_pairs={{0,12},{1,13},{2,14},{3,15},{4,8},{5,9},{6,10},{7,11},{8,4},{9,5},... | collective-permute-start | bytes 663560 | tf_op jit(solution)/shard_map/round_one/ppermute | solution.py:71
  11.9 1.9 mix_rows.1
  13.8 2.3 collective-permute-done.2
  16.2 12.4 %collective-permute-done.1 = bf16[6,24,768]{2,1,0:T(8,128)(2,1)S(1)} collective-permute-done((bf16[6,24,768]{2,1,0:T(8,128)(2,1)S(1)}, bf16[6,24,768]{2,1,0:T(8,128)(2,1)S(1)}, u32[]{:S(2)}, u32[]{:S(2)}) %collective-permute-start.1) | collective-permute-done | bytes 221216 | tf_op jit(solution)/shard_map/round_one/ppermute | solution.py:71
  31.7 3.7 %all-to-all-start = ((bf16[4,3,32,1024]{3,2,1,0:T(8,128)(2,1)}), bf16[4,3,32,1024]{3,2,1,0:T(8,128)(2,1)S(1)}, u32[]{:S(2)}, u32[]{:S(2)}) async-start(bf16[4,3,32,1024]{3,2,1,0:T(8,128)(2,1)} %mix_rows.1), calls=%async_computation | async-start | bytes 1572864 | tf_op jit(solution)/shard_map/round_two/all_to_all | solution.py:77
  36.1 5.5 %collective-permute-done.5 = bf16[4,24,768]{2,1,0:T(8,128)(2,1)S(1)} collective-permute-done((bf16[4,24,768]{2,1,0:T(8,128)(2,1)S(1)}, bf16[4,24,768]{2,1,0:T(8,128)(2,1)S(1)}, u32[]{:S(2)}, u32[]{:S(2)}) %collective-permute-start.5) | collective-permute-done | bytes 147488 | tf_op jit(solution)/shard_map/round_two/ppermute | solution.py:71
  43.1 8.6 %collective-permute-done.8 = bf16[4,2,24,768]{3,2,1,0:T(8,128)(2,1)S(1)} collective-permute-done((bf16[4,2,24,768]{3,2,1,0:T(8,128)(2,1)S(1)}, bf16[4,2,24,768]{3,2,1,0:T(8,128)(2,1)S(1)}, u32[]{:S(2)}, u32[]{:S(2)}) %collective-permute-start.8) | collective-permute-done | bytes 294944 | tf_op jit(solution)/shard_map/round_two/ppermute | solution.py:71
  51.7 2.8 collective-permute-done.7
  57.2 1.9 make_values.1
  59.2 2.1 collective-permute-start.9
  61.3 2.4 collective-permute-start.10
  63.7 5.6 %collective-permute-done.9.refs_1_ = bf16[3,64,512]{2,1,0:T(8,128)(2,1)S(1)} collective-permute-done((bf16[3,64,512]{2,1,0:T(8,128)(2,1)S(1)}, bf16[3,64,512]{2,1,0:T(8,128)(2,1)S(1)}, u32[]{:S(2)}, u32[]{:S(2)}) %collective-permute-start.9) | collective-permute-done | bytes 196640 | tf_op jit(solution)/shard_map/round_three/ppermute | solution.py:71
  69.3 9.2 %collective-permute-done.10.refs_2_ = bf16[3,64,512]{2,1,0:T(8,128)(2,1)S(1)} collective-permute-done((bf16[3,64,512]{2,1,0:T(8,128)(2,1)S(1)}, bf16[3,64,512]{2,1,0:T(8,128)(2,1)S(1)}, u32[]{:S(2)}, u32[]{:S(2)}) %collective-permute-start.10) | collective-permute-done | bytes 196640 | tf_op jit(solution)/shard_map/round_three/ppermute | solution.py:71
  79.7 3.8 %collective-permute-start.17 = (bf16[96,768]{1,0:T(8,128)(2,1)S(1)}, bf16[96,768]{1,0:T(8,128)(2,1)S(1)}, u32[]{:S(2)}, u32[]{:S(2)}) collective-permute-start(bf16[96,768]{1,0:T(8,128)(2,1)S(1)} %copy-done.43), channel_id=1, source_target_pairs={{0,8},{1,9},{2,10},{3,11},{4,12},{5,13},{6,14},{7,15},{8,0},{9,1},... | collective-permute-start | bytes 442376 | tf_op jit(solution)/shard_map/round_four/ppermute | solution.py:71
  84.9 7.2 %collective-permute-done.17 = bf16[96,768]{1,0:T(8,128)(2,1)S(1)} collective-permute-done((bf16[96,768]{1,0:T(8,128)(2,1)S(1)}, bf16[96,768]{1,0:T(8,128)(2,1)S(1)}, u32[]{:S(2)}, u32[]{:S(2)}) %collective-permute-start.17) | collective-permute-done | bytes 147488 | tf_op jit(solution)/shard_map/round_four/ppermute | solution.py:71
  95.3 2.3 collective-permute-done.20.refs_3_
  97.6 2.7 mix_values.1
  106.1 7.0 %collective-permute-done.23 = bf16[4,48,768]{2,1,0:T(8,128)(2,1)S(1)} collective-permute-done((bf16[4,48,768]{2,1,0:T(8,128)(2,1)S(1)}, bf16[4,48,768]{2,1,0:T(8,128)(2,1)S(1)}, u32[]{:S(2)}, u32[]{:S(2)}) %collective-permute-start.23) | collective-permute-done | bytes 294944 | tf_op jit(solution)/shard_map/round_five/ppermute | solution.py:71
  116.2 6.5 %all-to-all-start.1 = ((bf16[4,3,64,512]{3,2,1,0:T(8,128)(2,1)}), bf16[4,3,64,512]{3,2,1,0:T(8,128)(2,1)}, u32[]{:S(2)}, u32[]{:S(2)}) async-start(bf16[4,3,64,512]{3,2,1,0:T(8,128)(2,1)} %get-tuple-element.125), calls=%async_computation.1 | async-start | bytes 1572864 | tf_op jit(solution)/shard_map/round_five/all_to_all | solution.py:77
  122.7 5.1 %collective-permute-done.24.refs_6_ = bf16[8,48,768]{2,1,0:T(8,128)(2,1)} collective-permute-done((bf16[8,48,768]{2,1,0:T(8,128)(2,1)S(1)}, bf16[8,48,768]{2,1,0:T(8,128)(2,1)}, u32[]{:S(2)}, u32[]{:S(2)}) %collective-permute-start.24) | collective-permute-done | bytes 589856 | tf_op jit(solution)/shard_map/round_five/ppermute | solution.py:71
  127.9 1.9 collective-permute-done.28.refs_10_
  130.3 5.0 %prepare_weights.1.refs_3_.refs_4_ = bf16[768,3840]{1,0:T(8,128)(2,1)S(1)} custom-call(s32[8]{0:T(128)S(1)} %stack.59.me, bf16[16,3,24,768]{3,2,1,0:T(8,128)(2,1)S(1)} %constant_dynamic-update-slice_fusion.7.refs_0_, bf16[16,3,24,768]{3,2,1,0:T(8,128)(2,1)} %collective-permute-done.21.refs_1_, ...), custom_call_target="tpu_custom_call" | custom-call | flops 49999998976 | bytes 1 | tf_op jit(solution)/shard_map/round_five/prepare_weights/pallas_call | solution.py:280
  135.3 2.5 copy-done.7
  138.6 4.0 %all-to-all-done.1.refs_0_ = bf16[4,3,64,512]{3,2,1,0:T(8,128)(2,1)} async-done(((bf16[4,3,64,512]{3,2,1,0:T(8,128)(2,1)}), bf16[4,3,64,512]{3,2,1,0:T(8,128)(2,1)}, u32[]{:S(2)}, u32[]{:S(2)}) %all-to-all-start.1) | async-done | bytes 786464 | tf_op jit(solution)/shard_map/round_five/all_to_all | solution.py:77
  142.6 30.3 %middle.1 = (bf16[512,768]{1,0:T(8,128)(2,1)}, f32[512,768]{1,0:T(8,128)}, bf16[4,3,64,512]{3,2,1,0:T(8,128)(2,1)}, bf16[16,24,1536]{2,1,0:T(8,128)(2,1)}, bf16[...) custom-call(s32[8]{0:T(128)} %copy-done.2, ...), custom_call_target="tpu_custom_call" | custom-call | flops 49999998976 | bytes 1 | tf_op jit(solution)/shard_map/feed_forward/middle/pallas_call | solution.py:429
  174.0 3.7 %all-to-all-start.2 = ((bf16[4,3,64,512]{3,2,1,0:T(8,128)(2,1)}), bf16[4,3,64,512]{3,2,1,0:T(8,128)(2,1)S(1)}, u32[]{:S(2)}, u32[]{:S(2)}) async-start(bf16[4,3,64,512]{3,2,1,0:T(8,128)(2,1)} %get-tuple-element.144), calls=%async_computation.2 | async-start | bytes 1572864 | tf_op jit(solution)/shard_map/feed_forward/all_to_all | solution.py:77
  177.7 2.5 add_convert_fusion.7
  184.1 2.7 add_convert_fusion.2
  186.8 3.1 %add_convert_fusion = (bf16[8,24,2304]{2,1,0:T(8,128)(2,1)}, bf16[8,24,2304]{2,1,0:T(8,128)(2,1)}) fusion(bf16[16,24,2304]{2,1,0:T(8,128)(2,1)} %collective-permute-done.36, bf16[16,24,2304]{2,1,0:T(8,128)(2,1)S(1)} %copy-done.27), kind=kLoop, calls=%fused_computation | loop fusion | flops 3538944 | bytes 5308416 | tf_op jit(solution)/shard_map/weight_grads/convert_element_type | solution.py:81
  189.9 8.1 %all-to-all-done.2.refs_0_ = bf16[4,3,64,512]{3,2,1,0:T(8,128)(2,1)S(1)} async-done(((bf16[4,3,64,512]{3,2,1,0:T(8,128)(2,1)}), bf16[4,3,64,512]{3,2,1,0:T(8,128)(2,1)S(1)}, u32[]{:S(2)}, u32[]{:S(2)}) %all-to-all-start.2) | async-done | bytes 786464 | tf_op jit(solution)/shard_map/feed_forward/all_to_all | solution.py:77
  201.4 4.9 %mix_back.1 = (bf16[2,4,3,64,512]{4,3,2,1,0:T(8,128)(2,1)S(1)}, bf16[2,4,3,64,512]{4,3,2,1,0:T(8,128)(2,1)S(1)}, bf16[2,4,3,64,512]{4,3,2,1,0:T(8,128)(2,1)S(1)}) custom-call(s32[8]{0:T(128)S(1)} %copy-done.3, bf16[4,3,64,512]{3,2,1,0:T(8,128)(2,1)S(1)} %all-to-all-done.2.refs_0_, bf16[3,256,1024]{2,1,0:T(8,128)(2,1)} %copy-done.10, ...), custom_call_target="tpu_custom_call" | custom-call | flops 49999998976 | bytes 1 | tf_op jit(solution)/shard_map/mixing_back/mix_back/pallas_call | solution.py:507
  209.4 1.9 collective-permute-done.39.refs_1_
  214.3 2.2 collective-permute-start.44
  216.6 2.2 collective-permute-start.43
  218.8 4.2 %collective-permute-done.44 = bf16[96,768]{1,0:T(8,128)(2,1)S(1)} collective-permute-done((bf16[96,768]{1,0:T(8,128)(2,1)S(1)}, bf16[96,768]{1,0:T(8,128)(2,1)S(1)}, u32[]{:S(2)}, u32[]{:S(2)}) %collective-permute-start.44) | collective-permute-done | bytes 147488 | tf_op jit(solution)/shard_map/weight_grads/ppermute | solution.py:71
  223.0 4.3 %collective-permute-done.42 = bf16[96,768]{1,0:T(8,128)(2,1)S(1)} collective-permute-done((bf16[96,768]{1,0:T(8,128)(2,1)S(1)}, bf16[96,768]{1,0:T(8,128)(2,1)S(1)}, u32[]{:S(2)}, u32[]{:S(2)}) %collective-permute-start.42) | collective-permute-done | bytes 147488 | tf_op jit(solution)/shard_map/weight_grads/ppermute | solution.py:71
  227.2 2.1 collective-permute-done.43
  229.3 2.0 collective-permute-done.40
  234.7 3.0 collective-permute-start.47
  239.1 5.3 %collective-permute-done.47.refs_3_ = bf16[3,64,512]{2,1,0:T(8,128)(2,1)S(1)} collective-permute-done((bf16[3,64,512]{2,1,0:T(8,128)(2,1)S(1)}, bf16[3,64,512]{2,1,0:T(8,128)(2,1)S(1)}, u32[]{:S(2)}, u32[]{:S(2)}) %collective-permute-start.47) | collective-permute-done | bytes 196640 | tf_op jit(solution)/shard_map/mixing_back/ppermute | solution.py:71
  244.4 9.1 %collective-permute-done.46.refs_2_ = bf16[3,64,512]{2,1,0:T(8,128)(2,1)S(1)} collective-permute-done((bf16[3,64,512]{2,1,0:T(8,128)(2,1)S(1)}, bf16[3,64,512]{2,1,0:T(8,128)(2,1)S(1)}, u32[]{:S(2)}, u32[]{:S(2)}) %collective-permute-start.46) | collective-permute-done | bytes 196640 | tf_op jit(solution)/shard_map/mixing_back/ppermute | solution.py:71
  254.7 1.9 value_grads.1
  257.8 3.8 %all-to-all-start.3 = ((bf16[4,3,64,512]{3,2,1,0:T(8,128)(2,1)}), bf16[4,3,64,512]{3,2,1,0:T(8,128)(2,1)S(1)}, u32[]{:S(2)}, u32[]{:S(2)}) async-start(bf16[4,3,64,512]{3,2,1,0:T(8,128)(2,1)} %fusion), calls=%async_computation.3 | async-start | bytes 1572864 | tf_op jit(solution)/shard_map/mixing_back/all_to_all | solution.py:77
  269.8 12.0 %collective-permute-done.51.refs_1_ = bf16[4,24,768]{2,1,0:T(8,128)(2,1)S(1)} collective-permute-done((bf16[4,24,768]{2,1,0:T(8,128)(2,1)S(1)}, bf16[4,24,768]{2,1,0:T(8,128)(2,1)S(1)}, u32[]{:S(2)}, u32[]{:S(2)}) %collective-permute-start.51) | collective-permute-done | bytes 147488 | tf_op jit(solution)/shard_map/value_grads/ppermute | solution.py:71
  286.2 2.4 collective-permute-start.58
  288.6 2.3 make_tokens_grad.1
  292.3 7.5 %collective-permute-done.58 = bf16[24,4608]{1,0:T(8,128)(2,1)S(1)} collective-permute-done((bf16[24,4608]{1,0:T(8,128)(2,1)S(1)}, bf16[24,4608]{1,0:T(8,128)(2,1)S(1)}, u32[]{:S(2)}, u32[]{:S(2)}) %collective-permute-start.58) | collective-permute-done | bytes 221216 | tf_op jit(solution)/shard_map/weight_grads/ppermute | solution.py:71
  299.8 7.4 %collective-permute-done.57 = bf16[24,4608]{1,0:T(8,128)(2,1)S(1)} collective-permute-done((bf16[24,4608]{1,0:T(8,128)(2,1)S(1)}, bf16[24,4608]{1,0:T(8,128)(2,1)S(1)}, u32[]{:S(2)}, u32[]{:S(2)}) %collective-permute-start.57) | collective-permute-done | bytes 221216 | tf_op jit(solution)/shard_map/weight_grads/ppermute | solution.py:71
  (256 shorter events, 68.3 us)
Async XLA Ops:
  4.6 11.5 %collective-permute-start.2 = (bf16[6,24,768]{2,1,0:T(8,128)(2,1)S(1)}, bf16[6,24,768]{2,1,0:T(8,128)(2,1)S(1)}, u32[]{:S(2)}, u32[]{:S(2)}) collective-permute-start(bf16[6,24,768]{2,1,0:T(8,128)(2,1)S(1)} %pad_maximum_fusion.8), channel_id=1, source_target_pairs={{0,12},{1,13},{2,14},{3,15},{4,8},{5,9},{6,10},{7,11},{8,4},{9,5},... | collective-permute-start | bytes 663560 | tf_op jit(solution)/shard_map/round_one/ppermute | solution.py:71
  9.8 18.8 %collective-permute-start.1 = (bf16[6,24,768]{2,1,0:T(8,128)(2,1)S(1)}, bf16[6,24,768]{2,1,0:T(8,128)(2,1)S(1)}, u32[]{:S(2)}, u32[]{:S(2)}) collective-permute-start(bf16[6,24,768]{2,1,0:T(8,128)(2,1)S(1)} %pad_maximum_fusion.8), channel_id=1, source_target_pairs={{0,8},{1,9},{2,10},{3,11},{4,12},{5,13},{6,14},{7,15},{8,0},{9,1},... | collective-permute-start | bytes 663560 | tf_op jit(solution)/shard_map/round_one/ppermute | solution.py:71
  9.8 18.8 %collective-permute-start = (bf16[6,24,768]{2,1,0:T(8,128)(2,1)S(1)}, bf16[6,24,768]{2,1,0:T(8,128)(2,1)S(1)}, u32[]{:S(2)}, u32[]{:S(2)}) collective-permute-start(bf16[6,24,768]{2,1,0:T(8,128)(2,1)S(1)} %pad_maximum_fusion.8), channel_id=1, source_target_pairs={{0,4},{1,5},{2,6},{3,7},{4,0},{5,1},{6,2},{7,3},{8,12},{9,13},{10,... | collective-permute-start | bytes 663560 | tf_op jit(solution)/shard_map/round_one/ppermute | solution.py:71
  31.7 22.8 %all-to-all-start = ((bf16[4,3,32,1024]{3,2,1,0:T(8,128)(2,1)}), bf16[4,3,32,1024]{3,2,1,0:T(8,128)(2,1)S(1)}, u32[]{:S(2)}, u32[]{:S(2)}) async-start(bf16[4,3,32,1024]{3,2,1,0:T(8,128)(2,1)} %mix_rows.1), calls=%async_computation | async-start | bytes 1572864 | tf_op jit(solution)/shard_map/round_two/all_to_all | solution.py:77
  41.6 12.9 %collective-permute-start.6 = (bf16[16,24,768]{2,1,0:T(8,128)(2,1)S(1)}, bf16[16,24,768]{2,1,0:T(8,128)(2,1)S(1)}, u32[]{:S(2)}, u32[]{:S(2)}) collective-permute-start(bf16[16,24,768]{2,1,0:T(8,128)(2,1)S(1)} %constant_dynamic-update-slice_fusion.rest_0_), channel_id=1, source_target_pairs={{0,1},{1,0},{2,3},{3,2},{4,5},{5,4},{6,7},{7,6},{8,9},{9,8},{10,11... | collective-permute-start | bytes 1769480 | tf_op jit(solution)/shard_map/round_two/ppermute | solution.py:71
  41.9 12.6 %collective-permute-start.7 = (bf16[4,3,24,768]{3,2,1,0:T(8,128)(2,1)S(1)}, bf16[4,3,24,768]{3,2,1,0:T(8,128)(2,1)S(1)}, u32[]{:S(2)}, u32[]{:S(2)}) collective-permute-start(bf16[4,3,24,768]{3,2,1,0:T(8,128)(2,1)S(1)} %slice.244), channel_id=1, source_target_pairs={{0,16},{1,17},{2,18},{3,19},{4,20},{5,21},{6,22},{7,23},{8,24},{9,... | collective-permute-start | bytes 1327112 | tf_op jit(solution)/shard_map/round_two/ppermute | solution.py:71
  42.5 9.2 %collective-permute-start.8 = (bf16[4,2,24,768]{3,2,1,0:T(8,128)(2,1)S(1)}, bf16[4,2,24,768]{3,2,1,0:T(8,128)(2,1)S(1)}, u32[]{:S(2)}, u32[]{:S(2)}) collective-permute-start(bf16[4,2,24,768]{3,2,1,0:T(8,128)(2,1)S(1)} %pad_maximum_fusion.7), channel_id=1, source_target_pairs={{0,2},{1,3},{2,0},{3,1},{4,6},{5,7},{6,4},{7,5},{8,10},{9,11},{10,... | collective-permute-start | bytes 884744 | tf_op jit(solution)/shard_map/round_two/ppermute | solution.py:71
  55.7 22.8 %collective-permute-start.13 = (bf16[8,2,24,768]{3,2,1,0:T(8,128)(2,1)S(1)}, bf16[8,2,24,768]{3,2,1,0:T(8,128)(2,1)S(1)}, u32[]{:S(2)}, u32[]{:S(2)}) collective-permute-start(bf16[8,2,24,768]{3,2,1,0:T(8,128)(2,1)S(1)} %pad_maximum_fusion.3), channel_id=1, source_target_pairs={{0,16},{1,17},{2,18},{3,19},{4,20},{5,21},{6,22},{7,23},{8,24},{9,... | collective-permute-start | bytes 1769480 | tf_op jit(solution)/shard_map/round_three/ppermute | solution.py:71
  56.2 22.2 %collective-permute-start.12 = (bf16[8,3,24,768]{3,2,1,0:T(8,128)(2,1)S(1)}, bf16[8,3,24,768]{3,2,1,0:T(8,128)(2,1)S(1)}, u32[]{:S(2)}, u32[]{:S(2)}) collective-permute-start(bf16[8,3,24,768]{3,2,1,0:T(8,128)(2,1)S(1)} %pad_maximum_fusion), channel_id=1, source_target_pairs={{0,2},{1,3},{2,0},{3,1},{4,6},{5,7},{6,4},{7,5},{8,10},{9,11},{10,... | collective-permute-start | bytes 2654216 | tf_op jit(solution)/shard_map/round_three/ppermute | solution.py:71
  59.2 10.1 %collective-permute-start.9 = (bf16[3,64,512]{2,1,0:T(8,128)(2,1)S(1)}, bf16[3,64,512]{2,1,0:T(8,128)(2,1)S(1)}, u32[]{:S(2)}, u32[]{:S(2)}) collective-permute-start(bf16[3,64,512]{2,1,0:T(8,128)(2,1)S(1)} %get-tuple-element.113), channel_id=1, source_target_pairs={{0,4},{1,5},{2,6},{3,7},{4,0},{5,1},{6,2},{7,3},{8,12},{9,13},{10,... | collective-permute-start | bytes 589832 | tf_op jit(solution)/shard_map/round_three/ppermute | solution.py:71
  61.3 17.2 %collective-permute-start.10 = (bf16[3,64,512]{2,1,0:T(8,128)(2,1)S(1)}, bf16[3,64,512]{2,1,0:T(8,128)(2,1)S(1)}, u32[]{:S(2)}, u32[]{:S(2)}) collective-permute-start(bf16[3,64,512]{2,1,0:T(8,128)(2,1)S(1)} %get-tuple-element.114), channel_id=1, source_target_pairs={{0,8},{1,9},{2,10},{3,11},{4,12},{5,13},{6,14},{7,15},{8,0},{9,1},... | collective-permute-start | bytes 589832 | tf_op jit(solution)/shard_map/round_three/ppermute | solution.py:71
  63.6 14.8 %collective-permute-start.11 = (bf16[3,64,512]{2,1,0:T(8,128)(2,1)S(1)}, bf16[3,64,512]{2,1,0:T(8,128)(2,1)S(1)}, u32[]{:S(2)}, u32[]{:S(2)}) collective-permute-start(bf16[3,64,512]{2,1,0:T(8,128)(2,1)S(1)} %get-tuple-element.115), channel_id=1, source_target_pairs={{0,12},{1,13},{2,14},{3,15},{4,8},{5,9},{6,10},{7,11},{8,4},{9,5},... | collective-permute-start | bytes 589832 | tf_op jit(solution)/shard_map/round_three/ppermute | solution.py:71
  69.3 24.5 %collective-permute-start.15 = (bf16[4,3,32,1024]{3,2,1,0:T(8,128)(2,1)S(1)}, bf16[4,3,32,1024]{3,2,1,0:T(8,128)(2,1)S(1)}, u32[]{:S(2)}, u32[]{:S(2)}) collective-permute-start(bf16[4,3,32,1024]{3,2,1,0:T(8,128)(2,1)S(1)} %all-to-all-done.refs_4_), channel_id=1, source_target_pairs={{0,16},{1,17},{2,18},{3,19},{4,20},{5,21},{6,22},{7,23},{8,24},{9,... | collective-permute-start | bytes 2359304 | tf_op jit(solution)/shard_map/round_four/ppermute | solution.py:71
  78.6 16.8 %collective-permute-start.14 = (bf16[4,3,64,512]{3,2,1,0:T(8,128)(2,1)S(1)}, bf16[4,3,64,512]{3,2,1,0:T(8,128)(2,1)S(1)}, u32[]{:S(2)}, u32[]{:S(2)}) collective-permute-start(bf16[4,3,64,512]{3,2,1,0:T(8,128)(2,1)S(1)} %stack_all.1.refs_0_), channel_id=1, source_target_pairs={{0,2},{1,3},{2,0},{3,1},{4,6},{5,7},{6,4},{7,5},{8,10},{9,11},{10,... | collective-permute-start | bytes 2359304 | tf_op jit(solution)/shard_map/round_four/ppermute | solution.py:71
  79.7 12.5 %collective-permute-start.17 = (bf16[96,768]{1,0:T(8,128)(2,1)S(1)}, bf16[96,768]{1,0:T(8,128)(2,1)S(1)}, u32[]{:S(2)}, u32[]{:S(2)}) collective-permute-start(bf16[96,768]{1,0:T(8,128)(2,1)S(1)} %copy-done.43), channel_id=1, source_target_pairs={{0,8},{1,9},{2,10},{3,11},{4,12},{5,13},{6,14},{7,15},{8,0},{9,1},... | collective-permute-start | bytes 442376 | tf_op jit(solution)/shard_map/round_four/ppermute | solution.py:71
  83.5 10.3 %collective-permute-start.18 = (bf16[96,768]{1,0:T(8,128)(2,1)S(1)}, bf16[96,768]{1,0:T(8,128)(2,1)S(1)}, u32[]{:S(2)}, u32[]{:S(2)}) collective-permute-start(bf16[96,768]{1,0:T(8,128)(2,1)S(1)} %copy-done.43), channel_id=1, source_target_pairs={{0,12},{1,13},{2,14},{3,15},{4,8},{5,9},{6,10},{7,11},{8,4},{9,5},... | collective-permute-start | bytes 442376 | tf_op jit(solution)/shard_map/round_four/ppermute | solution.py:71
  103.2 27.1 %collective-permute-start.21 = (bf16[16,3,24,768]{3,2,1,0:T(8,128)(2,1)S(1)}, bf16[16,3,24,768]{3,2,1,0:T(8,128)(2,1)}, u32[]{:S(2)}, u32[]{:S(2)}) collective-permute-start(bf16[16,3,24,768]{3,2,1,0:T(8,128)(2,1)S(1)} %constant_dynamic-update-slice_fusion.7.refs_0_), channel_id=1, source_target_pairs={{0,1},{1,0},{2,3},{3,2},{4,5},{5,4},{6,7},{7,6},{8,9},{9,8},{10,11... | collective-permute-start | bytes 5308424 | tf_op jit(solution)/shard_map/round_five/ppermute | solution.py:71
  103.4 26.3 %collective-permute-start.22 = (bf16[16,2,24,768]{3,2,1,0:T(8,128)(2,1)S(1)}, bf16[16,2,24,768]{3,2,1,0:T(8,128)(2,1)}, u32[]{:S(2)}, u32[]{:S(2)}) collective-permute-start(bf16[16,2,24,768]{3,2,1,0:T(8,128)(2,1)S(1)} %constant_dynamic-update-slice_fusion.9.refs_2_), channel_id=1, source_target_pairs={{0,1},{1,0},{2,3},{3,2},{4,5},{5,4},{6,7},{7,6},{8,9},{9,8},{10,11... | collective-permute-start | bytes 3538952 | tf_op jit(solution)/shard_map/round_five/ppermute | solution.py:71
  104.0 9.1 %collective-permute-start.23 = (bf16[4,48,768]{2,1,0:T(8,128)(2,1)S(1)}, bf16[4,48,768]{2,1,0:T(8,128)(2,1)S(1)}, u32[]{:S(2)}, u32[]{:S(2)}) collective-permute-start(bf16[4,48,768]{2,1,0:T(8,128)(2,1)S(1)} %get-tuple-element.220), channel_id=1, source_target_pairs={{0,16},{1,17},{2,18},{3,19},{4,20},{5,21},{6,22},{7,23},{8,24},{9,... | collective-permute-start | bytes 884744 | tf_op jit(solution)/shard_map/round_five/ppermute | solution.py:71
  113.1 14.7 %collective-permute-start.24 = (bf16[8,48,768]{2,1,0:T(8,128)(2,1)S(1)}, bf16[8,48,768]{2,1,0:T(8,128)(2,1)}, u32[]{:S(2)}, u32[]{:S(2)}) collective-permute-start(bf16[8,48,768]{2,1,0:T(8,128)(2,1)S(1)} %pad_maximum_fusion.5.refs_5_), channel_id=1, source_target_pairs={{0,2},{1,3},{2,0},{3,1},{4,6},{5,7},{6,4},{7,5},{8,10},{9,11},{10,... | collective-permute-start | bytes 1769480 | tf_op jit(solution)/shard_map/round_five/ppermute | solution.py:71
  115.2 14.5 %collective-permute-start.28 = (bf16[8,48,768]{2,1,0:T(8,128)(2,1)}, bf16[8,48,768]{2,1,0:T(8,128)(2,1)}, u32[]{:S(2)}, u32[]{:S(2)}) collective-permute-start(bf16[8,48,768]{2,1,0:T(8,128)(2,1)} %pad_maximum_fusion.6.refs_9_), channel_id=1, source_target_pairs={{0,16},{1,17},{2,18},{3,19},{4,20},{5,21},{6,22},{7,23},{8,24},{9,... | collective-permute-start | bytes 1769480 | tf_op jit(solution)/shard_map/round_five/ppermute | solution.py:71
  116.2 26.4 %all-to-all-start.1 = ((bf16[4,3,64,512]{3,2,1,0:T(8,128)(2,1)}), bf16[4,3,64,512]{3,2,1,0:T(8,128)(2,1)}, u32[]{:S(2)}, u32[]{:S(2)}) async-start(bf16[4,3,64,512]{3,2,1,0:T(8,128)(2,1)} %get-tuple-element.125), calls=%async_computation.1 | async-start | bytes 1572864 | tf_op jit(solution)/shard_map/round_five/all_to_all | solution.py:77
  122.7 15.0 %collective-permute-start.25 = (bf16[8,48,768]{2,1,0:T(8,128)(2,1)S(1)}, bf16[8,48,768]{2,1,0:T(8,128)(2,1)S(1)}, u32[]{:S(2)}, u32[]{:S(2)}) collective-permute-start(bf16[8,48,768]{2,1,0:T(8,128)(2,1)S(1)} %pad_maximum_fusion.5.refs_5_), channel_id=1, source_target_pairs={{0,1},{1,0},{2,3},{3,2},{4,5},{5,4},{6,7},{7,6},{8,9},{9,8},{10,11... | collective-permute-start | bytes 1769480 | tf_op jit(solution)/shard_map/round_five/ppermute | solution.py:71
  127.9 10.7 %collective-permute-start.29 = (bf16[8,48,768]{2,1,0:T(8,128)(2,1)}, bf16[8,48,768]{2,1,0:T(8,128)(2,1)}, u32[]{:S(2)}, u32[]{:S(2)}) collective-permute-start(bf16[8,48,768]{2,1,0:T(8,128)(2,1)} %pad_maximum_fusion.6.refs_9_), channel_id=1, source_target_pairs={{0,1},{1,0},{2,3},{3,2},{4,5},{5,4},{6,7},{7,6},{8,9},{9,8},{10,11... | collective-permute-start | bytes 1769480 | tf_op jit(solution)/shard_map/round_five/ppermute | solution.py:71
  129.7 12.8 %collective-permute-start.26 = (bf16[8,48,768]{2,1,0:T(8,128)(2,1)}, bf16[8,48,768]{2,1,0:T(8,128)(2,1)}, u32[]{:S(2)}, u32[]{:S(2)}) collective-permute-start(bf16[8,48,768]{2,1,0:T(8,128)(2,1)} %collective-permute-done.24.refs_6_), channel_id=1, source_target_pairs={{0,1},{1,0},{2,3},{3,2},{4,5},{5,4},{6,7},{7,6},{8,9},{9,8},{10,11... | collective-permute-start | bytes 1769480 | tf_op jit(solution)/shard_map/round_five/ppermute | solution.py:71
  129.7 12.8 %collective-permute-start.30 = (bf16[8,48,768]{2,1,0:T(8,128)(2,1)}, bf16[8,48,768]{2,1,0:T(8,128)(2,1)}, u32[]{:S(2)}, u32[]{:S(2)}) collective-permute-start(bf16[8,48,768]{2,1,0:T(8,128)(2,1)} %collective-permute-done.28.refs_10_), channel_id=1, source_target_pairs={{0,1},{1,0},{2,3},{3,2},{4,5},{5,4},{6,7},{7,6},{8,9},{9,8},{10,11... | collective-permute-start | bytes 1769480 | tf_op jit(solution)/shard_map/round_five/ppermute | solution.py:71
  173.4 13.3 %collective-permute-start.36 = (bf16[16,24,2304]{2,1,0:T(8,128)(2,1)}, bf16[16,24,2304]{2,1,0:T(8,128)(2,1)}, u32[]{:S(2)}, u32[]{:S(2)}) collective-permute-start(bf16[16,24,2304]{2,1,0:T(8,128)(2,1)} %get-tuple-element.150), channel_id=1, source_target_pairs={{0,1},{1,0},{2,3},{3,2},{4,5},{5,4},{6,7},{7,6},{8,9},{9,8},{10,11... | collective-permute-start | bytes 5308424 | tf_op jit(solution)/shard_map/weight_grads/ppermute | solution.py:71
  173.5 10.5 %collective-permute-start.35 = (bf16[16,24,1536]{2,1,0:T(8,128)(2,1)}, bf16[16,24,1536]{2,1,0:T(8,128)(2,1)}, u32[]{:S(2)}, u32[]{:S(2)}) collective-permute-start(bf16[16,24,1536]{2,1,0:T(8,128)(2,1)} %get-tuple-element.148), channel_id=1, source_target_pairs={{0,1},{1,0},{2,3},{3,2},{4,5},{5,4},{6,7},{7,6},{8,9},{9,8},{10,11... | collective-permute-start | bytes 3538952 | tf_op jit(solution)/shard_map/weight_grads/ppermute | solution.py:71
  174.0 24.1 %all-to-all-start.2 = ((bf16[4,3,64,512]{3,2,1,0:T(8,128)(2,1)}), bf16[4,3,64,512]{3,2,1,0:T(8,128)(2,1)S(1)}, u32[]{:S(2)}, u32[]{:S(2)}) async-start(bf16[4,3,64,512]{3,2,1,0:T(8,128)(2,1)} %get-tuple-element.144), calls=%async_computation.2 | async-start | bytes 1572864 | tf_op jit(solution)/shard_map/feed_forward/all_to_all | solution.py:77
  180.2 17.9 %collective-permute-start.32 = (bf16[8,48,768]{2,1,0:T(8,128)(2,1)}, bf16[8,48,768]{2,1,0:T(8,128)(2,1)S(1)}, u32[]{:S(2)}, u32[]{:S(2)}) collective-permute-start(bf16[8,48,768]{2,1,0:T(8,128)(2,1)} %get-tuple-element.208), channel_id=1, source_target_pairs={{0,2},{1,3},{2,0},{3,1},{4,6},{5,7},{6,4},{7,5},{8,10},{9,11},{10,... | collective-permute-start | bytes 1769480 | tf_op jit(solution)/shard_map/weight_grads/ppermute | solution.py:71
  182.4 15.7 %collective-permute-start.34 = (bf16[8,48,768]{2,1,0:T(8,128)(2,1)S(1)}, bf16[8,48,768]{2,1,0:T(8,128)(2,1)}, u32[]{:S(2)}, u32[]{:S(2)}) collective-permute-start(bf16[8,48,768]{2,1,0:T(8,128)(2,1)S(1)} %get-tuple-element.206), channel_id=1, source_target_pairs={{0,16},{1,17},{2,18},{3,19},{4,20},{5,21},{6,22},{7,23},{8,24},{9,... | collective-permute-start | bytes 1769480 | tf_op jit(solution)/shard_map/weight_grads/ppermute | solution.py:71
  207.9 21.3 %collective-permute-start.41 = (bf16[4,3,64,512]{3,2,1,0:T(8,128)(2,1)S(1)}, bf16[4,3,64,512]{3,2,1,0:T(8,128)(2,1)S(1)}, u32[]{:S(2)}, u32[]{:S(2)}) collective-permute-start(bf16[4,3,64,512]{3,2,1,0:T(8,128)(2,1)S(1)} %slice_bitcast_fusion), channel_id=1, source_target_pairs={{0,16},{1,17},{2,18},{3,19},{4,20},{5,21},{6,22},{7,23},{8,24},{9,... | collective-permute-start | bytes 2359304 | tf_op jit(solution)/shard_map/mixing_back/ppermute | solution.py:71
  211.7 19.6 %collective-permute-start.40 = (bf16[1,4,3,64,512]{4,3,2,1,0:T(8,128)(2,1)S(1)}, bf16[1,4,3,64,512]{4,3,2,1,0:T(8,128)(2,1)S(1)}, u32[]{:S(2)}, u32[]{:S(2)}) collective-permute-start(bf16[1,4,3,64,512]{4,3,2,1,0:T(8,128)(2,1)S(1)} %get-tuple-element.161), channel_id=1, source_target_pairs={{0,2},{1,3},{2,0},{3,1},{4,6},{5,7},{6,4},{7,5},{8,10},{9,11},{10,... | collective-permute-start | bytes 2359304 | tf_op jit(solution)/shard_map/mixing_back/ppermute | solution.py:71
  216.6 10.7 %collective-permute-start.42 = (bf16[96,768]{1,0:T(8,128)(2,1)S(1)}, bf16[96,768]{1,0:T(8,128)(2,1)S(1)}, u32[]{:S(2)}, u32[]{:S(2)}) collective-permute-start(bf16[96,768]{1,0:T(8,128)(2,1)S(1)} %get-tuple-element.217), channel_id=1, source_target_pairs={{0,4},{1,5},{2,6},{3,7},{4,0},{5,1},{6,2},{7,3},{8,12},{9,13},{10,... | collective-permute-start | bytes 442376 | tf_op jit(solution)/shard_map/weight_grads/ppermute | solution.py:71
  216.6 12.7 %collective-permute-start.43 = (bf16[96,768]{1,0:T(8,128)(2,1)S(1)}, bf16[96,768]{1,0:T(8,128)(2,1)S(1)}, u32[]{:S(2)}, u32[]{:S(2)}) collective-permute-start(bf16[96,768]{1,0:T(8,128)(2,1)S(1)} %get-tuple-element.218), channel_id=1, source_target_pairs={{0,8},{1,9},{2,10},{3,11},{4,12},{5,13},{6,14},{7,15},{8,0},{9,1},... | collective-permute-start | bytes 442376 | tf_op jit(solution)/shard_map/weight_grads/ppermute | solution.py:71
  232.5 21.0 %collective-permute-start.49 = (bf16[8,24,2304]{2,1,0:T(8,128)(2,1)S(1)}, bf16[8,24,2304]{2,1,0:T(8,128)(2,1)S(1)}, u32[]{:S(2)}, u32[]{:S(2)}) collective-permute-start(bf16[8,24,2304]{2,1,0:T(8,128)(2,1)S(1)} %copy-done.33), channel_id=1, source_target_pairs={{0,2},{1,3},{2,0},{3,1},{4,6},{5,7},{6,4},{7,5},{8,10},{9,11},{10,... | collective-permute-start | bytes 2654216 | tf_op jit(solution)/shard_map/weight_grads/ppermute | solution.py:71
  233.8 19.7 %collective-permute-start.48 = (bf16[8,24,1536]{2,1,0:T(8,128)(2,1)S(1)}, bf16[8,24,1536]{2,1,0:T(8,128)(2,1)S(1)}, u32[]{:S(2)}, u32[]{:S(2)}) collective-permute-start(bf16[8,24,1536]{2,1,0:T(8,128)(2,1)S(1)} %copy-done.34), channel_id=1, source_target_pairs={{0,16},{1,17},{2,18},{3,19},{4,20},{5,21},{6,22},{7,23},{8,24},{9,... | collective-permute-start | bytes 1769480 | tf_op jit(solution)/shard_map/weight_grads/ppermute | solution.py:71
  234.7 9.7 %collective-permute-start.47 = (bf16[3,64,512]{2,1,0:T(8,128)(2,1)S(1)}, bf16[3,64,512]{2,1,0:T(8,128)(2,1)S(1)}, u32[]{:S(2)}, u32[]{:S(2)}) collective-permute-start(bf16[3,64,512]{2,1,0:T(8,128)(2,1)S(1)} %get-tuple-element.212), channel_id=1, source_target_pairs={{0,12},{1,13},{2,14},{3,15},{4,8},{5,9},{6,10},{7,11},{8,4},{9,5},... | collective-permute-start | bytes 589832 | tf_op jit(solution)/shard_map/mixing_back/ppermute | solution.py:71
  237.7 15.8 %collective-permute-start.46 = (bf16[3,64,512]{2,1,0:T(8,128)(2,1)S(1)}, bf16[3,64,512]{2,1,0:T(8,128)(2,1)S(1)}, u32[]{:S(2)}, u32[]{:S(2)}) collective-permute-start(bf16[3,64,512]{2,1,0:T(8,128)(2,1)S(1)} %get-tuple-element.213), channel_id=1, source_target_pairs={{0,8},{1,9},{2,10},{3,11},{4,12},{5,13},{6,14},{7,15},{8,0},{9,1},... | collective-permute-start | bytes 589832 | tf_op jit(solution)/shard_map/mixing_back/ppermute | solution.py:71
  237.7 15.8 %collective-permute-start.45 = (bf16[3,64,512]{2,1,0:T(8,128)(2,1)S(1)}, bf16[3,64,512]{2,1,0:T(8,128)(2,1)S(1)}, u32[]{:S(2)}, u32[]{:S(2)}) collective-permute-start(bf16[3,64,512]{2,1,0:T(8,128)(2,1)S(1)} %get-tuple-element.214), channel_id=1, source_target_pairs={{0,4},{1,5},{2,6},{3,7},{4,0},{5,1},{6,2},{7,3},{8,12},{9,13},{10,... | collective-permute-start | bytes 589832 | tf_op jit(solution)/shard_map/mixing_back/ppermute | solution.py:71
  257.8 24.8 %all-to-all-start.3 = ((bf16[4,3,64,512]{3,2,1,0:T(8,128)(2,1)}), bf16[4,3,64,512]{3,2,1,0:T(8,128)(2,1)S(1)}, u32[]{:S(2)}, u32[]{:S(2)}) async-start(bf16[4,3,64,512]{3,2,1,0:T(8,128)(2,1)} %fusion), calls=%async_computation.3 | async-start | bytes 1572864 | tf_op jit(solution)/shard_map/mixing_back/all_to_all | solution.py:77
  263.2 19.4 %collective-permute-start.55 = (bf16[4,24,2304]{2,1,0:T(8,128)(2,1)S(1)}, bf16[4,24,2304]{2,1,0:T(8,128)(2,1)S(1)}, u32[]{:S(2)}, u32[]{:S(2)}) collective-permute-start(bf16[4,24,2304]{2,1,0:T(8,128)(2,1)S(1)} %add_convert_fusion.10), channel_id=1, source_target_pairs={{0,16},{1,17},{2,18},{3,19},{4,20},{5,21},{6,22},{7,23},{8,24},{9,... | collective-permute-start | bytes 1327112 | tf_op jit(solution)/shard_map/weight_grads/ppermute | solution.py:71
  264.1 17.8 %collective-permute-start.54 = (bf16[4,24,1536]{2,1,0:T(8,128)(2,1)S(1)}, bf16[4,24,1536]{2,1,0:T(8,128)(2,1)S(1)}, u32[]{:S(2)}, u32[]{:S(2)}) collective-permute-start(bf16[4,24,1536]{2,1,0:T(8,128)(2,1)S(1)} %add_convert_fusion.13), channel_id=1, source_target_pairs={{0,2},{1,3},{2,0},{3,1},{4,6},{5,7},{6,4},{7,5},{8,10},{9,11},{10,... | collective-permute-start | bytes 884744 | tf_op jit(solution)/shard_map/weight_grads/ppermute | solution.py:71
  265.5 16.3 %collective-permute-start.51 = (bf16[4,24,768]{2,1,0:T(8,128)(2,1)S(1)}, bf16[4,24,768]{2,1,0:T(8,128)(2,1)S(1)}, u32[]{:S(2)}, u32[]{:S(2)}) collective-permute-start(bf16[4,24,768]{2,1,0:T(8,128)(2,1)S(1)} %get-tuple-element.180), channel_id=1, source_target_pairs={{0,16},{1,17},{2,18},{3,19},{4,20},{5,21},{6,22},{7,23},{8,24},{9,... | collective-permute-start | bytes 442376 | tf_op jit(solution)/shard_map/value_grads/ppermute | solution.py:71
  266.0 15.8 %collective-permute-start.52 = (bf16[4,24,768]{2,1,0:T(8,128)(2,1)S(1)}, bf16[4,24,768]{2,1,0:T(8,128)(2,1)S(1)}, u32[]{:S(2)}, u32[]{:S(2)}) collective-permute-start(bf16[4,24,768]{2,1,0:T(8,128)(2,1)S(1)} %get-tuple-element.181), channel_id=1, source_target_pairs={{0,2},{1,3},{2,0},{3,1},{4,6},{5,7},{6,4},{7,5},{8,10},{9,11},{10,... | collective-permute-start | bytes 442376 | tf_op jit(solution)/shard_map/value_grads/ppermute | solution.py:71
  267.5 14.4 %collective-permute-start.53 = (bf16[4,24,768]{2,1,0:T(8,128)(2,1)S(1)}, bf16[4,24,768]{2,1,0:T(8,128)(2,1)S(1)}, u32[]{:S(2)}, u32[]{:S(2)}) collective-permute-start(bf16[4,24,768]{2,1,0:T(8,128)(2,1)S(1)} %get-tuple-element.182), channel_id=1, source_target_pairs={{0,18},{1,19},{2,16},{3,17},{4,22},{5,23},{6,20},{7,21},{8,26},{9,... | collective-permute-start | bytes 442376 | tf_op jit(solution)/shard_map/value_grads/ppermute | solution.py:71
  286.2 13.5 %collective-permute-start.58 = (bf16[24,4608]{1,0:T(8,128)(2,1)S(1)}, bf16[24,4608]{1,0:T(8,128)(2,1)S(1)}, u32[]{:S(2)}, u32[]{:S(2)}) collective-permute-start(bf16[24,4608]{1,0:T(8,128)(2,1)S(1)} %get-tuple-element.210), channel_id=1, source_target_pairs={{0,12},{1,13},{2,14},{3,15},{4,8},{5,9},{6,10},{7,11},{8,4},{9,5},... | collective-permute-start | bytes 663560 | tf_op jit(solution)/shard_map/weight_grads/ppermute | solution.py:71
  288.6 18.6 %collective-permute-start.57 = (bf16[24,4608]{1,0:T(8,128)(2,1)S(1)}, bf16[24,4608]{1,0:T(8,128)(2,1)S(1)}, u32[]{:S(2)}, u32[]{:S(2)}) collective-permute-start(bf16[24,4608]{1,0:T(8,128)(2,1)S(1)} %get-tuple-element.211), channel_id=1, source_target_pairs={{0,8},{1,9},{2,10},{3,11},{4,12},{5,13},{6,14},{7,15},{8,0},{9,1},... | collective-permute-start | bytes 663560 | tf_op jit(solution)/shard_map/weight_grads/ppermute | solution.py:71
  (71 other events, 571.6 us)

commit v4 on v3

--- a/solution.py
+++ b/solution.py
@@ -287,7 +287,7 @@
         ),
         out_shape=shape((width, kinds * width)),
         compiler_params=params(24),
-        cost_estimate=cost(width * width * kinds, 4 * width * width * kinds),
+        cost_estimate=pl.CostEstimate(flops=width, bytes_accessed=width, transcendentals=0),
         name="prepare_weights",
     )(lay.me, *ups)
 
@@ -649,6 +649,22 @@
     )(*parts)
 
 
+def pass_kernel(source, target):
+    del source, target
+
+
+def pass_on(array):
+    return pl.pallas_call(
+        pass_kernel,
+        out_shape=shape(array.shape, array.dtype),
+        in_specs=[pl.BlockSpec(memory_space=pl.ANY)],
+        out_specs=pl.BlockSpec(memory_space=pl.ANY),
+        input_output_aliases={0: 0},
+        cost_estimate=cost(0, 0),
+        name="pass_on",
+    )(array)
+
+
 def total_kernel(*refs):
     *parts, out = refs
     total = parts[0][...].astype(F32)
@@ -734,14 +750,15 @@
             one, two = wide[:, :SPLIT], wide[:, SPLIT:]
             four = [own, lay.swap(own, dp=1), lay.swap(own, x=1), lay.swap(own, dp=1, x=1)]
             one_other, two_other = lay.swap(one, dp=1), lay.swap(two, x=1)
+            four, one_other, two_other = tie((four, one_other, two_other))
             own = jnp.concatenate(four)
             w_value = [own, lay.swap(own, c=1)]
-            w_value, one_other, two_other, rows = tie((w_value, one_other, two_other, rows))
+            one, two = jnp.concatenate([one, one_other]), jnp.concatenate([two, two_other])
+            one_other, two_other = lay.swap(one, x=1), lay.swap(two, dp=1)
+            w_value, rows = tie((w_value, rows))
         with jax.named_scope("round_three"):
             normed_one, w_value, value_parts = make_values(lay, tokens, w_value)
             first = along_z(lay, value_parts)
-            one, two = jnp.concatenate([one, one_other]), jnp.concatenate([two, two_other])
-            one_other, two_other = lay.swap(one, x=1), lay.swap(two, dp=1)
             first, one_other, two_other = tie((first, one_other, two_other))
         with jax.named_scope("round_four"):
             values = stack_all(first)
@@ -751,20 +768,20 @@
             values_other, rows_other, tall = tie((values_other, rows_other, tall))
             rows = [rows, rows_other]
         with jax.named_scope("round_five"):
+            tall = stack_all(tall)
+            cut = tall.shape[1] // 2
+            three, four = tall[:, :cut], tall[:, cut:]
+            three_other, four_other = lay.swap(three, dp=1), lay.swap(four, x=1)
             values = [values, values_other, lay.swap(values, c=1), lay.swap(values_other, c=1)]
             mix_low, values, pieces = mix_values(lay, values, rows)
             pieces = lay.across_z(pieces)
-            tall, one, two, one_other, two_other = after(
-                (tall, one, two, one_other, two_other), mix_low
-            )
-            tall = jnp.stack(tall)
-            cut = tall.shape[1] // 2
-            three, four = tall[:, :cut], tall[:, cut:]
-            three_other, four_other = lay.swap(three, dp=1), lay.swap(four, x=1)
-            one, two = jnp.concatenate([one, one_other]), jnp.concatenate([two, two_other])
-            w_up = prepare_weights(lay, [one, lay.swap(one, c=1), two, lay.swap(two, c=1)])
+            values = pass_on(values)
+            three_other, four_other, values = tie((three_other, four_other, values))
             three, four = jnp.concatenate([three, three_other]), jnp.concatenate([four, four_other])
             three_other, four_other = lay.swap(three, x=1), lay.swap(four, dp=1)
+            one, two = jnp.concatenate([one, one_other]), jnp.concatenate([two, two_other])
+            w_up = [one, lay.swap(one, c=1), two, lay.swap(two, c=1)]
+            w_up = prepare_weights(lay, w_up)
             w_down = [three, three_other, four, four_other]
             w_down += [lay.swap(array, c=1) for array in w_down]
             w_down = [w_down[i] for i in (0, 1, 4, 5, 2, 3, 6, 7)]

time: 311 us -> 307 us (0.987)
  waiting for transfers between devices: 143 us -> 120 us
  other arithmetic: 26.3 us -> 39.4 us
  starting transfers between devices: 74.7 us -> 78.5 us
    ppermute x59, waiting for transfers between devices: 131 us -> 108 us  [swap(): lax.ppermute(array, AXES, [(i, i ^ mask) for i in range(self.devices)])]
    concatenate x1 -> x2, other arithmetic: 0.08 us -> 4.66 us  [on_device(): jnp.concatenate([one, one_other])]
    ppermute x59, starting transfers between devices: 56.9 us -> 61.3 us  [swap(): lax.ppermute(array, AXES, [(i, i ^ mask) for i in range(self.devices)])]
    convert_element_type x13, other arithmetic: 15 us -> 19.1 us  [add_low(): return (left.astype(F32) + right.astype(F32)).astype(BF16)]
    concatenate x1 -> x2, other arithmetic: 1.02 us -> 4.16 us  [on_device(): jnp.concatenate([two, two_other])]
    unnamed x116 -> x113, local copies, waits for them, and re-layouts: 12.4 us -> 13.3 us
  transfers between devices with their start and end apart: 63 -> 63, of which waited for: 29 -> 30; matrix products, arithmetic and copies ran while one was open for 5% -> 10% of each run, Pallas kernels for 5% -> 6%
where the time goes in v4:
time: 307 us; the launch traced here: 305 us
  waiting for transfers between devices  120 us (39%)
  starting transfers between devices  78.5 us (26%)
  Pallas kernels  52.3 us (17%)
  other arithmetic  39.4 us (13%)
  local copies, waits for them, and re-layouts  13.7 us (4%)
    ppermute x59, waiting for transfers between devices, swap(): lax.ppermute(array, AXES, [(i, i ^ mask) for i in range(self.devices)])  108 us
    ppermute x59, starting transfers between devices, swap(): lax.ppermute(array, AXES, [(i, i ^ mask) for i in range(self.devices)])  61.3 us
    pallas_call x1, Pallas kernels, middle(): pl.pallas_call(functools.partial(middle_kernel, positions=lay.positions,...  30.3 us
    convert_element_type x13, other arithmetic, add_low(): return (left.astype(F32) + right.astype(F32)).astype(BF16)  19.1 us
    all_to_all x4, starting transfers between devices, across_z(): return lax.all_to_all(array, 'seq', 0, 0, axis_index_groups=lines)  17.2 us
    unnamed x113, local copies, waits for them, and re-layouts  13.3 us
    all_to_all x4, waiting for transfers between devices, across_z(): return lax.all_to_all(array, 'seq', 0, 0, axis_index_groups=lines)  12.4 us
  transfers between devices with their start and end apart: 63, of which 30 were waited for; matrix products, arithmetic and copies ran while one was open for 10% of the time, Pallas kernels for 6%

profile of v4, /device:TPU:0, one launch (start us, length us, event | category | flops | bytes accessed | tf_op | source)
XLA Modules:
  0.0 305.3 jit_solution(4582310354798795390)
XLA Ops:
  4.6 5.1 %collective-permute-start.2 = (bf16[6,24,768]{2,1,0:T(8,128)(2,1)S(1)}, bf16[6,24,768]{2,1,0:T(8,128)(2,1)S(1)}, u32[]{:S(2)}, u32[]{:S(2)}) collective-permute-start(bf16[6,24,768]{2,1,0:T(8,128)(2,1)S(1)} %pad_maximum_fusion.9), channel_id=1, source_target_pairs={{0,12},{1,13},{2,14},{3,15},{4,8},{5,9},{6,10},{7,11},{8,4},{9,5},... | collective-permute-start | bytes 663560 | tf_op jit(solution)/shard_map/round_one/ppermute | solution.py:71
  11.9 1.9 mix_rows.1
  13.8 2.3 collective-permute-done.2
  16.2 12.4 %collective-permute-done.1 = bf16[6,24,768]{2,1,0:T(8,128)(2,1)S(1)} collective-permute-done((bf16[6,24,768]{2,1,0:T(8,128)(2,1)S(1)}, bf16[6,24,768]{2,1,0:T(8,128)(2,1)S(1)}, u32[]{:S(2)}, u32[]{:S(2)}) %collective-permute-start.1) | collective-permute-done | bytes 221216 | tf_op jit(solution)/shard_map/round_one/ppermute | solution.py:71
  35.6 3.7 %all-to-all-start = ((bf16[4,3,32,1024]{3,2,1,0:T(8,128)(2,1)}), bf16[4,3,32,1024]{3,2,1,0:T(8,128)(2,1)S(1)}, u32[]{:S(2)}, u32[]{:S(2)}) async-start(bf16[4,3,32,1024]{3,2,1,0:T(8,128)(2,1)} %mix_rows.1), calls=%async_computation | async-start | bytes 1572864 | tf_op jit(solution)/shard_map/round_two/all_to_all | solution.py:77
  39.3 3.7 %collective-permute-done.5 = bf16[4,24,768]{2,1,0:T(8,128)(2,1)S(1)} collective-permute-done((bf16[4,24,768]{2,1,0:T(8,128)(2,1)S(1)}, bf16[4,24,768]{2,1,0:T(8,128)(2,1)S(1)}, u32[]{:S(2)}, u32[]{:S(2)}) %collective-permute-start.5) | collective-permute-done | bytes 147488 | tf_op jit(solution)/shard_map/round_two/ppermute | solution.py:71
  46.6 1.9 pad_maximum_fusion.5
  50.0 2.0 pad_maximum_fusion.2
  53.5 3.9 %all-to-all-done.refs_4_ = bf16[4,3,32,1024]{3,2,1,0:T(8,128)(2,1)S(1)} async-done(((bf16[4,3,32,1024]{3,2,1,0:T(8,128)(2,1)}), bf16[4,3,32,1024]{3,2,1,0:T(8,128)(2,1)S(1)}, u32[]{:S(2)}, u32[]{:S(2)}) %all-to-all-start) | async-done | bytes 786464 | tf_op jit(solution)/shard_map/round_two/all_to_all | solution.py:77
  57.4 1.9 make_values.1
  59.4 2.0 collective-permute-start.10
  61.4 2.4 collective-permute-start.11
  66.0 8.0 %collective-permute-done.12 = bf16[8,3,24,768]{3,2,1,0:T(8,128)(2,1)} collective-permute-done((bf16[8,3,24,768]{3,2,1,0:T(8,128)(2,1)}, bf16[8,3,24,768]{3,2,1,0:T(8,128)(2,1)}, u32[]{:S(2)}, u32[]{:S(2)}) %collective-permute-start.12) | collective-permute-done | bytes 884768 | tf_op jit(solution)/shard_map/round_two/ppermute | solution.py:71
  74.0 2.0 collective-permute-done.10.refs_2_
  76.9 3.0 collective-permute-start.17
  80.0 2.4 collective-permute-start.18
  82.4 2.7 pad_maximum_fusion.refs_0_
  85.0 2.3 pad_maximum_fusion.1.refs_2_
  87.3 1.9 collective-permute-done.17.refs_2_
  90.9 2.0 collective-permute-done.14.refs_1_
  96.8 2.7 mix_values.1
  106.1 5.4 %all-to-all-start.1 = ((bf16[4,3,64,512]{3,2,1,0:T(8,128)(2,1)}), bf16[4,3,64,512]{3,2,1,0:T(8,128)(2,1)S(1)}, u32[]{:S(2)}, u32[]{:S(2)}) async-start(bf16[4,3,64,512]{3,2,1,0:T(8,128)(2,1)} %get-tuple-element.128), calls=%async_computation.1 | async-start | bytes 1572864 | tf_op jit(solution)/shard_map/round_five/all_to_all | solution.py:77
  112.1 6.7 %collective-permute-done.28.refs_10_ = bf16[8,48,768]{2,1,0:T(8,128)(2,1)} collective-permute-done((bf16[8,48,768]{2,1,0:T(8,128)(2,1)S(1)}, bf16[8,48,768]{2,1,0:T(8,128)(2,1)}, u32[]{:S(2)}, u32[]{:S(2)}) %collective-permute-start.28) | collective-permute-done | bytes 589856 | tf_op jit(solution)/shard_map/round_five/ppermute | solution.py:71
  120.0 5.6 %prepare_weights.1.refs_3_.refs_4_ = bf16[768,3840]{1,0:T(8,128)(2,1)S(1)} custom-call(s32[8]{0:T(128)S(1)} %stack.44.me, bf16[16,3,24,768]{3,2,1,0:T(8,128)(2,1)} %pad_maximum_fusion.refs_0_, bf16[16,3,24,768]{3,2,1,0:T(8,128)(2,1)} %collective-permute-done.21.refs_1_, bf16[16,2,24,768]{3,2,1,0:T(8,128)(2,1)} %pad_maximum_fusion.1.refs_2_, ...), custom_call_target="tpu_custom_call" | custom-call | flops 768 | bytes 768 | tf_op jit(solution)/shard_map/round_five/prepare_weights/pallas_call | solution.py:280
  125.6 2.5 copy-done
  131.5 30.3 %middle.1 = (bf16[512,768]{1,0:T(8,128)(2,1)}, f32[512,768]{1,0:T(8,128)}, bf16[4,3,64,512]{3,2,1,0:T(8,128)(2,1)}, bf16[16,24,1536]{2,1,0:T(8,128)(2,1)}, bf16[...) custom-call(s32[8]{0:T(128)} %copy-done.3, ...), custom_call_target="tpu_custom_call" | custom-call | flops 49999998976 | bytes 1 | tf_op jit(solution)/shard_map/feed_forward/middle/pallas_call | solution.py:429
  163.0 3.9 %all-to-all-start.2 = ((bf16[4,3,64,512]{3,2,1,0:T(8,128)(2,1)}), bf16[4,3,64,512]{3,2,1,0:T(8,128)(2,1)S(1)}, u32[]{:S(2)}, u32[]{:S(2)}) async-start(bf16[4,3,64,512]{3,2,1,0:T(8,128)(2,1)} %get-tuple-element.141), calls=%async_computation.2 | async-start | bytes 1572864 | tf_op jit(solution)/shard_map/feed_forward/all_to_all | solution.py:77
  166.8 2.5 add_convert_fusion.7
  173.9 2.7 add_convert_fusion.2
  176.7 3.1 %add_convert_fusion = (bf16[8,24,2304]{2,1,0:T(8,128)(2,1)}, bf16[8,24,2304]{2,1,0:T(8,128)(2,1)}) fusion(bf16[16,24,2304]{2,1,0:T(8,128)(2,1)} %collective-permute-done.36, bf16[16,24,2304]{2,1,0:T(8,128)(2,1)S(1)} %copy-done.26), kind=kLoop, calls=%fused_computation.1 | loop fusion | flops 3538944 | bytes 5308416 | tf_op jit(solution)/shard_map/weight_grads/convert_element_type | solution.py:81
  179.8 7.8 %all-to-all-done.2.refs_0_ = bf16[4,3,64,512]{3,2,1,0:T(8,128)(2,1)S(1)} async-done(((bf16[4,3,64,512]{3,2,1,0:T(8,128)(2,1)}), bf16[4,3,64,512]{3,2,1,0:T(8,128)(2,1)S(1)}, u32[]{:S(2)}, u32[]{:S(2)}) %all-to-all-start.2) | async-done | bytes 786464 | tf_op jit(solution)/shard_map/feed_forward/all_to_all | solution.py:77
  192.7 4.9 %mix_back.1 = (bf16[2,4,3,64,512]{4,3,2,1,0:T(8,128)(2,1)S(1)}, bf16[2,4,3,64,512]{4,3,2,1,0:T(8,128)(2,1)S(1)}, bf16[2,4,3,64,512]{4,3,2,1,0:T(8,128)(2,1)S(1)}) custom-call(s32[8]{0:T(128)S(1)} %copy-done.4, bf16[4,3,64,512]{3,2,1,0:T(8,128)(2,1)S(1)} %all-to-all-done.2.refs_0_, bf16[3,256,1024]{2,1,0:T(8,128)(2,1)} %copy-done.11, ...), custom_call_target="tpu_custom_call" | custom-call | flops 49999998976 | bytes 1 | tf_op jit(solution)/shard_map/mixing_back/mix_back/pallas_call | solution.py:507
  200.8 1.8 collective-permute-done.39.refs_1_
  205.9 3.1 %collective-permute-start.44 = (bf16[96,768]{1,0:T(8,128)(2,1)S(1)}, bf16[96,768]{1,0:T(8,128)(2,1)S(1)}, u32[]{:S(2)}, u32[]{:S(2)}) collective-permute-start(bf16[96,768]{1,0:T(8,128)(2,1)S(1)} %get-tuple-element.214), channel_id=1, source_target_pairs={{0,12},{1,13},{2,14},{3,15},{4,8},{5,9},{6,10},{7,11},{8,4},{9,5},... | collective-permute-start | bytes 442376 | tf_op jit(solution)/shard_map/weight_grads/ppermute | solution.py:71
  210.4 4.1 %collective-permute-done.44 = bf16[96,768]{1,0:T(8,128)(2,1)S(1)} collective-permute-done((bf16[96,768]{1,0:T(8,128)(2,1)S(1)}, bf16[96,768]{1,0:T(8,128)(2,1)S(1)}, u32[]{:S(2)}, u32[]{:S(2)}) %collective-permute-start.44) | collective-permute-done | bytes 147488 | tf_op jit(solution)/shard_map/weight_grads/ppermute | solution.py:71
  214.6 2.1 collective-permute-done.42
  216.6 6.3 %collective-permute-done.43 = bf16[96,768]{1,0:T(8,128)(2,1)S(1)} collective-permute-done((bf16[96,768]{1,0:T(8,128)(2,1)S(1)}, bf16[96,768]{1,0:T(8,128)(2,1)S(1)}, u32[]{:S(2)}, u32[]{:S(2)}) %collective-permute-start.43) | collective-permute-done | bytes 147488 | tf_op jit(solution)/shard_map/weight_grads/ppermute | solution.py:71
  226.8 2.2 collective-permute-start.47
  231.2 5.3 %collective-permute-done.47.refs_3_ = bf16[3,64,512]{2,1,0:T(8,128)(2,1)S(1)} collective-permute-done((bf16[3,64,512]{2,1,0:T(8,128)(2,1)S(1)}, bf16[3,64,512]{2,1,0:T(8,128)(2,1)S(1)}, u32[]{:S(2)}, u32[]{:S(2)}) %collective-permute-start.47) | collective-permute-done | bytes 196640 | tf_op jit(solution)/shard_map/mixing_back/ppermute | solution.py:71
  236.6 9.9 %collective-permute-done.46.refs_2_ = bf16[3,64,512]{2,1,0:T(8,128)(2,1)S(1)} collective-permute-done((bf16[3,64,512]{2,1,0:T(8,128)(2,1)S(1)}, bf16[3,64,512]{2,1,0:T(8,128)(2,1)S(1)}, u32[]{:S(2)}, u32[]{:S(2)}) %collective-permute-start.46) | collective-permute-done | bytes 196640 | tf_op jit(solution)/shard_map/mixing_back/ppermute | solution.py:71
  247.3 1.9 value_grads.1
  250.4 4.2 %all-to-all-start.3 = ((bf16[4,3,64,512]{3,2,1,0:T(8,128)(2,1)}), bf16[4,3,64,512]{3,2,1,0:T(8,128)(2,1)}, u32[]{:S(2)}, u32[]{:S(2)}) async-start(bf16[4,3,64,512]{3,2,1,0:T(8,128)(2,1)} %fusion), calls=%async_computation.3 | async-start | bytes 1572864 | tf_op jit(solution)/shard_map/mixing_back/all_to_all | solution.py:77
  262.7 13.3 %collective-permute-done.51.refs_1_ = bf16[4,24,768]{2,1,0:T(8,128)(2,1)S(1)} collective-permute-done((bf16[4,24,768]{2,1,0:T(8,128)(2,1)S(1)}, bf16[4,24,768]{2,1,0:T(8,128)(2,1)S(1)}, u32[]{:S(2)}, u32[]{:S(2)}) %collective-permute-start.51) | collective-permute-done | bytes 147488 | tf_op jit(solution)/shard_map/value_grads/ppermute | solution.py:71
  281.2 2.4 collective-permute-start.58
  283.6 2.3 make_tokens_grad.1
  285.8 2.5 bitcast_convert_fusion
  288.3 6.4 %collective-permute-done.58 = bf16[24,4608]{1,0:T(8,128)(2,1)S(1)} collective-permute-done((bf16[24,4608]{1,0:T(8,128)(2,1)S(1)}, bf16[24,4608]{1,0:T(8,128)(2,1)S(1)}, u32[]{:S(2)}, u32[]{:S(2)}) %collective-permute-start.58) | collective-permute-done | bytes 221216 | tf_op jit(solution)/shard_map/weight_grads/ppermute | solution.py:71
  294.7 7.7 %collective-permute-done.57 = bf16[24,4608]{1,0:T(8,128)(2,1)S(1)} collective-permute-done((bf16[24,4608]{1,0:T(8,128)(2,1)S(1)}, bf16[24,4608]{1,0:T(8,128)(2,1)S(1)}, u32[]{:S(2)}, u32[]{:S(2)}) %collective-permute-start.57) | collective-permute-done | bytes 221216 | tf_op jit(solution)/shard_map/weight_grads/ppermute | solution.py:71
  (254 shorter events, 82.9 us)
Async XLA Ops:
  4.6 11.5 %collective-permute-start.2 = (bf16[6,24,768]{2,1,0:T(8,128)(2,1)S(1)}, bf16[6,24,768]{2,1,0:T(8,128)(2,1)S(1)}, u32[]{:S(2)}, u32[]{:S(2)}) collective-permute-start(bf16[6,24,768]{2,1,0:T(8,128)(2,1)S(1)} %pad_maximum_fusion.9), channel_id=1, source_target_pairs={{0,12},{1,13},{2,14},{3,15},{4,8},{5,9},{6,10},{7,11},{8,4},{9,5},... | collective-permute-start | bytes 663560 | tf_op jit(solution)/shard_map/round_one/ppermute | solution.py:71
  9.8 18.8 %collective-permute-start.1 = (bf16[6,24,768]{2,1,0:T(8,128)(2,1)S(1)}, bf16[6,24,768]{2,1,0:T(8,128)(2,1)S(1)}, u32[]{:S(2)}, u32[]{:S(2)}) collective-permute-start(bf16[6,24,768]{2,1,0:T(8,128)(2,1)S(1)} %pad_maximum_fusion.9), channel_id=1, source_target_pairs={{0,8},{1,9},{2,10},{3,11},{4,12},{5,13},{6,14},{7,15},{8,0},{9,1},... | collective-permute-start | bytes 663560 | tf_op jit(solution)/shard_map/round_one/ppermute | solution.py:71
  9.8 18.8 %collective-permute-start = (bf16[6,24,768]{2,1,0:T(8,128)(2,1)S(1)}, bf16[6,24,768]{2,1,0:T(8,128)(2,1)S(1)}, u32[]{:S(2)}, u32[]{:S(2)}) collective-permute-start(bf16[6,24,768]{2,1,0:T(8,128)(2,1)S(1)} %pad_maximum_fusion.9), channel_id=1, source_target_pairs={{0,4},{1,5},{2,6},{3,7},{4,0},{5,1},{6,2},{7,3},{8,12},{9,13},{10,... | collective-permute-start | bytes 663560 | tf_op jit(solution)/shard_map/round_one/ppermute | solution.py:71
  28.8 17.6 %collective-permute-start.6 = (bf16[4,3,24,768]{3,2,1,0:T(8,128)(2,1)S(1)}, bf16[4,3,24,768]{3,2,1,0:T(8,128)(2,1)}, u32[]{:S(2)}, u32[]{:S(2)}) collective-permute-start(bf16[4,3,24,768]{3,2,1,0:T(8,128)(2,1)S(1)} %slice.244), channel_id=1, source_target_pairs={{0,16},{1,17},{2,18},{3,19},{4,20},{5,21},{6,22},{7,23},{8,24},{9,... | collective-permute-start | bytes 1327112 | tf_op jit(solution)/shard_map/round_two/ppermute | solution.py:71
  30.4 16.0 %collective-permute-start.7 = (bf16[4,2,24,768]{3,2,1,0:T(8,128)(2,1)S(1)}, bf16[4,2,24,768]{3,2,1,0:T(8,128)(2,1)}, u32[]{:S(2)}, u32[]{:S(2)}) collective-permute-start(bf16[4,2,24,768]{3,2,1,0:T(8,128)(2,1)S(1)} %pad_maximum_fusion.8), channel_id=1, source_target_pairs={{0,2},{1,3},{2,0},{3,1},{4,6},{5,7},{6,4},{7,5},{8,10},{9,11},{10,... | collective-permute-start | bytes 884744 | tf_op jit(solution)/shard_map/round_two/ppermute | solution.py:71
  32.0 11.0 %collective-permute-start.5 = (bf16[4,24,768]{2,1,0:T(8,128)(2,1)S(1)}, bf16[4,24,768]{2,1,0:T(8,128)(2,1)S(1)}, u32[]{:S(2)}, u32[]{:S(2)}) collective-permute-start(bf16[4,24,768]{2,1,0:T(8,128)(2,1)S(1)} %pad_maximum_fusion.11), channel_id=1, source_target_pairs={{0,18},{1,19},{2,16},{3,17},{4,22},{5,23},{6,20},{7,21},{8,26},{9,... | collective-permute-start | bytes 442376 | tf_op jit(solution)/shard_map/round_two/ppermute | solution.py:71
  32.6 12.0 %collective-permute-start.4 = (bf16[4,24,768]{2,1,0:T(8,128)(2,1)S(1)}, bf16[4,24,768]{2,1,0:T(8,128)(2,1)S(1)}, u32[]{:S(2)}, u32[]{:S(2)}) collective-permute-start(bf16[4,24,768]{2,1,0:T(8,128)(2,1)S(1)} %pad_maximum_fusion.11), channel_id=1, source_target_pairs={{0,2},{1,3},{2,0},{3,1},{4,6},{5,7},{6,4},{7,5},{8,10},{9,11},{10,... | collective-permute-start | bytes 442376 | tf_op jit(solution)/shard_map/round_two/ppermute | solution.py:71
  34.1 12.3 %collective-permute-start.3 = (bf16[4,24,768]{2,1,0:T(8,128)(2,1)S(1)}, bf16[4,24,768]{2,1,0:T(8,128)(2,1)S(1)}, u32[]{:S(2)}, u32[]{:S(2)}) collective-permute-start(bf16[4,24,768]{2,1,0:T(8,128)(2,1)S(1)} %pad_maximum_fusion.11), channel_id=1, source_target_pairs={{0,16},{1,17},{2,18},{3,19},{4,20},{5,21},{6,22},{7,23},{8,24},{9,... | collective-permute-start | bytes 442376 | tf_op jit(solution)/shard_map/round_two/ppermute | solution.py:71
  35.6 21.8 %all-to-all-start = ((bf16[4,3,32,1024]{3,2,1,0:T(8,128)(2,1)}), bf16[4,3,32,1024]{3,2,1,0:T(8,128)(2,1)S(1)}, u32[]{:S(2)}, u32[]{:S(2)}) async-start(bf16[4,3,32,1024]{3,2,1,0:T(8,128)(2,1)} %mix_rows.1), calls=%async_computation | async-start | bytes 1572864 | tf_op jit(solution)/shard_map/round_two/all_to_all | solution.py:77
  48.5 16.0 %collective-permute-start.13 = (bf16[8,2,24,768]{3,2,1,0:T(8,128)(2,1)}, bf16[8,2,24,768]{3,2,1,0:T(8,128)(2,1)}, u32[]{:S(2)}, u32[]{:S(2)}) collective-permute-start(bf16[8,2,24,768]{3,2,1,0:T(8,128)(2,1)} %pad_maximum_fusion.5), channel_id=1, source_target_pairs={{0,16},{1,17},{2,18},{3,19},{4,20},{5,21},{6,22},{7,23},{8,24},{9,... | collective-permute-start | bytes 1769480 | tf_op jit(solution)/shard_map/round_two/ppermute | solution.py:71
  52.0 22.0 %collective-permute-start.12 = (bf16[8,3,24,768]{3,2,1,0:T(8,128)(2,1)}, bf16[8,3,24,768]{3,2,1,0:T(8,128)(2,1)}, u32[]{:S(2)}, u32[]{:S(2)}) collective-permute-start(bf16[8,3,24,768]{3,2,1,0:T(8,128)(2,1)} %pad_maximum_fusion.2), channel_id=1, source_target_pairs={{0,2},{1,3},{2,0},{3,1},{4,6},{5,7},{6,4},{7,5},{8,10},{9,11},{10,... | collective-permute-start | bytes 2654216 | tf_op jit(solution)/shard_map/round_two/ppermute | solution.py:71
  59.3 14.7 %collective-permute-start.9 = (bf16[3,64,512]{2,1,0:T(8,128)(2,1)S(1)}, bf16[3,64,512]{2,1,0:T(8,128)(2,1)S(1)}, u32[]{:S(2)}, u32[]{:S(2)}) collective-permute-start(bf16[3,64,512]{2,1,0:T(8,128)(2,1)S(1)} %get-tuple-element.116), channel_id=1, source_target_pairs={{0,4},{1,5},{2,6},{3,7},{4,0},{5,1},{6,2},{7,3},{8,12},{9,13},{10,... | collective-permute-start | bytes 589832 | tf_op jit(solution)/shard_map/round_three/ppermute | solution.py:71
  59.4 16.6 %collective-permute-start.10 = (bf16[3,64,512]{2,1,0:T(8,128)(2,1)S(1)}, bf16[3,64,512]{2,1,0:T(8,128)(2,1)S(1)}, u32[]{:S(2)}, u32[]{:S(2)}) collective-permute-start(bf16[3,64,512]{2,1,0:T(8,128)(2,1)S(1)} %get-tuple-element.117), channel_id=1, source_target_pairs={{0,8},{1,9},{2,10},{3,11},{4,12},{5,13},{6,14},{7,15},{8,0},{9,1},... | collective-permute-start | bytes 589832 | tf_op jit(solution)/shard_map/round_three/ppermute | solution.py:71
  61.4 14.6 %collective-permute-start.11 = (bf16[3,64,512]{2,1,0:T(8,128)(2,1)S(1)}, bf16[3,64,512]{2,1,0:T(8,128)(2,1)S(1)}, u32[]{:S(2)}, u32[]{:S(2)}) collective-permute-start(bf16[3,64,512]{2,1,0:T(8,128)(2,1)S(1)} %get-tuple-element.118), channel_id=1, source_target_pairs={{0,12},{1,13},{2,14},{3,15},{4,8},{5,9},{6,10},{7,11},{8,4},{9,5},... | collective-permute-start | bytes 589832 | tf_op jit(solution)/shard_map/round_three/ppermute | solution.py:71
  64.4 26.5 %collective-permute-start.15 = (bf16[4,3,32,1024]{3,2,1,0:T(8,128)(2,1)S(1)}, bf16[4,3,32,1024]{3,2,1,0:T(8,128)(2,1)S(1)}, u32[]{:S(2)}, u32[]{:S(2)}) collective-permute-start(bf16[4,3,32,1024]{3,2,1,0:T(8,128)(2,1)S(1)} %all-to-all-done.refs_4_), channel_id=1, source_target_pairs={{0,16},{1,17},{2,18},{3,19},{4,20},{5,21},{6,22},{7,23},{8,24},{9,... | collective-permute-start | bytes 2359304 | tf_op jit(solution)/shard_map/round_four/ppermute | solution.py:71
  76.1 16.9 %collective-permute-start.14 = (bf16[4,3,64,512]{3,2,1,0:T(8,128)(2,1)S(1)}, bf16[4,3,64,512]{3,2,1,0:T(8,128)(2,1)S(1)}, u32[]{:S(2)}, u32[]{:S(2)}) collective-permute-start(bf16[4,3,64,512]{3,2,1,0:T(8,128)(2,1)S(1)} %stack_all.2.refs_0_), channel_id=1, source_target_pairs={{0,2},{1,3},{2,0},{3,1},{4,6},{5,7},{6,4},{7,5},{8,10},{9,11},{10,... | collective-permute-start | bytes 2359304 | tf_op jit(solution)/shard_map/round_four/ppermute | solution.py:71
  76.9 12.3 %collective-permute-start.17 = (bf16[96,768]{1,0:T(8,128)(2,1)S(1)}, bf16[96,768]{1,0:T(8,128)(2,1)S(1)}, u32[]{:S(2)}, u32[]{:S(2)}) collective-permute-start(bf16[96,768]{1,0:T(8,128)(2,1)S(1)} %copy-done.8), channel_id=1, source_target_pairs={{0,8},{1,9},{2,10},{3,11},{4,12},{5,13},{6,14},{7,15},{8,0},{9,1},... | collective-permute-start | bytes 442376 | tf_op jit(solution)/shard_map/round_four/ppermute | solution.py:71
  80.0 10.9 %collective-permute-start.18 = (bf16[96,768]{1,0:T(8,128)(2,1)S(1)}, bf16[96,768]{1,0:T(8,128)(2,1)S(1)}, u32[]{:S(2)}, u32[]{:S(2)}) collective-permute-start(bf16[96,768]{1,0:T(8,128)(2,1)S(1)} %copy-done.8), channel_id=1, source_target_pairs={{0,12},{1,13},{2,14},{3,15},{4,8},{5,9},{6,10},{7,11},{8,4},{9,5},... | collective-permute-start | bytes 442376 | tf_op jit(solution)/shard_map/round_four/ppermute | solution.py:71
  89.2 22.3 %collective-permute-start.22 = (bf16[16,2,24,768]{3,2,1,0:T(8,128)(2,1)}, bf16[16,2,24,768]{3,2,1,0:T(8,128)(2,1)}, u32[]{:S(2)}, u32[]{:S(2)}) collective-permute-start(bf16[16,2,24,768]{3,2,1,0:T(8,128)(2,1)} %pad_maximum_fusion.1.refs_2_), channel_id=1, source_target_pairs={{0,1},{1,0},{2,3},{3,2},{4,5},{5,4},{6,7},{7,6},{8,9},{9,8},{10,11... | collective-permute-start | bytes 3538952 | tf_op jit(solution)/shard_map/round_five/ppermute | solution.py:71
  90.9 29.0 %collective-permute-start.21 = (bf16[16,3,24,768]{3,2,1,0:T(8,128)(2,1)}, bf16[16,3,24,768]{3,2,1,0:T(8,128)(2,1)}, u32[]{:S(2)}, u32[]{:S(2)}) collective-permute-start(bf16[16,3,24,768]{3,2,1,0:T(8,128)(2,1)} %pad_maximum_fusion.refs_0_), channel_id=1, source_target_pairs={{0,1},{1,0},{2,3},{3,2},{4,5},{5,4},{6,7},{7,6},{8,9},{9,8},{10,11... | collective-permute-start | bytes 5308424 | tf_op jit(solution)/shard_map/round_five/ppermute | solution.py:71
  93.1 9.5 %collective-permute-start.24 = (bf16[4,48,768]{2,1,0:T(8,128)(2,1)S(1)}, bf16[4,48,768]{2,1,0:T(8,128)(2,1)S(1)}, u32[]{:S(2)}, u32[]{:S(2)}) collective-permute-start(bf16[4,48,768]{2,1,0:T(8,128)(2,1)S(1)} %get-tuple-element.217), channel_id=1, source_target_pairs={{0,2},{1,3},{2,0},{3,1},{4,6},{5,7},{6,4},{7,5},{8,10},{9,11},{10,... | collective-permute-start | bytes 884744 | tf_op jit(solution)/shard_map/round_five/ppermute | solution.py:71
  103.9 14.8 %collective-permute-start.28 = (bf16[8,48,768]{2,1,0:T(8,128)(2,1)S(1)}, bf16[8,48,768]{2,1,0:T(8,128)(2,1)}, u32[]{:S(2)}, u32[]{:S(2)}) collective-permute-start(bf16[8,48,768]{2,1,0:T(8,128)(2,1)S(1)} %pad_maximum_fusion.7.refs_9_), channel_id=1, source_target_pairs={{0,16},{1,17},{2,18},{3,19},{4,20},{5,21},{6,22},{7,23},{8,24},{9,... | collective-permute-start | bytes 1769480 | tf_op jit(solution)/shard_map/round_five/ppermute | solution.py:71
  105.5 14.4 %collective-permute-start.25 = (bf16[8,48,768]{2,1,0:T(8,128)(2,1)S(1)}, bf16[8,48,768]{2,1,0:T(8,128)(2,1)S(1)}, u32[]{:S(2)}, u32[]{:S(2)}) collective-permute-start(bf16[8,48,768]{2,1,0:T(8,128)(2,1)S(1)} %pad_maximum_fusion.6.refs_5_), channel_id=1, source_target_pairs={{0,2},{1,3},{2,0},{3,1},{4,6},{5,7},{6,4},{7,5},{8,10},{9,11},{10,... | collective-permute-start | bytes 1769480 | tf_op jit(solution)/shard_map/round_five/ppermute | solution.py:71
  106.1 24.5 %all-to-all-start.1 = ((bf16[4,3,64,512]{3,2,1,0:T(8,128)(2,1)}), bf16[4,3,64,512]{3,2,1,0:T(8,128)(2,1)S(1)}, u32[]{:S(2)}, u32[]{:S(2)}) async-start(bf16[4,3,64,512]{3,2,1,0:T(8,128)(2,1)} %get-tuple-element.128), calls=%async_computation.1 | async-start | bytes 1572864 | tf_op jit(solution)/shard_map/round_five/all_to_all | solution.py:77
  111.5 16.6 %collective-permute-start.29 = (bf16[8,48,768]{2,1,0:T(8,128)(2,1)S(1)}, bf16[8,48,768]{2,1,0:T(8,128)(2,1)S(1)}, u32[]{:S(2)}, u32[]{:S(2)}) collective-permute-start(bf16[8,48,768]{2,1,0:T(8,128)(2,1)S(1)} %pad_maximum_fusion.7.refs_9_), channel_id=1, source_target_pairs={{0,1},{1,0},{2,3},{3,2},{4,5},{5,4},{6,7},{7,6},{8,9},{9,8},{10,11... | collective-permute-start | bytes 1769480 | tf_op jit(solution)/shard_map/round_five/ppermute | solution.py:71
  111.5 16.6 %collective-permute-start.26 = (bf16[8,48,768]{2,1,0:T(8,128)(2,1)S(1)}, bf16[8,48,768]{2,1,0:T(8,128)(2,1)S(1)}, u32[]{:S(2)}, u32[]{:S(2)}) collective-permute-start(bf16[8,48,768]{2,1,0:T(8,128)(2,1)S(1)} %pad_maximum_fusion.6.refs_5_), channel_id=1, source_target_pairs={{0,1},{1,0},{2,3},{3,2},{4,5},{5,4},{6,7},{7,6},{8,9},{9,8},{10,11... | collective-permute-start | bytes 1769480 | tf_op jit(solution)/shard_map/round_five/ppermute | solution.py:71
  120.0 10.0 %collective-permute-start.27 = (bf16[8,48,768]{2,1,0:T(8,128)(2,1)S(1)}, bf16[8,48,768]{2,1,0:T(8,128)(2,1)}, u32[]{:S(2)}, u32[]{:S(2)}) collective-permute-start(bf16[8,48,768]{2,1,0:T(8,128)(2,1)S(1)} %collective-permute-done.25.refs_6_), channel_id=1, source_target_pairs={{0,1},{1,0},{2,3},{3,2},{4,5},{5,4},{6,7},{7,6},{8,9},{9,8},{10,11... | collective-permute-start | bytes 1769480 | tf_op jit(solution)/shard_map/round_five/ppermute | solution.py:71
  162.5 14.2 %collective-permute-start.36 = (bf16[16,24,2304]{2,1,0:T(8,128)(2,1)}, bf16[16,24,2304]{2,1,0:T(8,128)(2,1)}, u32[]{:S(2)}, u32[]{:S(2)}) collective-permute-start(bf16[16,24,2304]{2,1,0:T(8,128)(2,1)} %get-tuple-element.147), channel_id=1, source_target_pairs={{0,1},{1,0},{2,3},{3,2},{4,5},{5,4},{6,7},{7,6},{8,9},{9,8},{10,11... | collective-permute-start | bytes 5308424 | tf_op jit(solution)/shard_map/weight_grads/ppermute | solution.py:71
  162.5 11.4 %collective-permute-start.35 = (bf16[16,24,1536]{2,1,0:T(8,128)(2,1)}, bf16[16,24,1536]{2,1,0:T(8,128)(2,1)}, u32[]{:S(2)}, u32[]{:S(2)}) collective-permute-start(bf16[16,24,1536]{2,1,0:T(8,128)(2,1)} %get-tuple-element.145), channel_id=1, source_target_pairs={{0,1},{1,0},{2,3},{3,2},{4,5},{5,4},{6,7},{7,6},{8,9},{9,8},{10,11... | collective-permute-start | bytes 3538952 | tf_op jit(solution)/shard_map/weight_grads/ppermute | solution.py:71
  163.0 24.6 %all-to-all-start.2 = ((bf16[4,3,64,512]{3,2,1,0:T(8,128)(2,1)}), bf16[4,3,64,512]{3,2,1,0:T(8,128)(2,1)S(1)}, u32[]{:S(2)}, u32[]{:S(2)}) async-start(bf16[4,3,64,512]{3,2,1,0:T(8,128)(2,1)} %get-tuple-element.141), calls=%async_computation.2 | async-start | bytes 1572864 | tf_op jit(solution)/shard_map/feed_forward/all_to_all | solution.py:77
  169.3 18.2 %collective-permute-start.32 = (bf16[8,48,768]{2,1,0:T(8,128)(2,1)}, bf16[8,48,768]{2,1,0:T(8,128)(2,1)}, u32[]{:S(2)}, u32[]{:S(2)}) collective-permute-start(bf16[8,48,768]{2,1,0:T(8,128)(2,1)} %get-tuple-element.206), channel_id=1, source_target_pairs={{0,2},{1,3},{2,0},{3,1},{4,6},{5,7},{6,4},{7,5},{8,10},{9,11},{10,... | collective-permute-start | bytes 1769480 | tf_op jit(solution)/shard_map/weight_grads/ppermute | solution.py:71
  172.4 15.3 %collective-permute-start.34 = (bf16[8,48,768]{2,1,0:T(8,128)(2,1)S(1)}, bf16[8,48,768]{2,1,0:T(8,128)(2,1)}, u32[]{:S(2)}, u32[]{:S(2)}) collective-permute-start(bf16[8,48,768]{2,1,0:T(8,128)(2,1)S(1)} %get-tuple-element.204), channel_id=1, source_target_pairs={{0,16},{1,17},{2,18},{3,19},{4,20},{5,21},{6,22},{7,23},{8,24},{9,... | collective-permute-start | bytes 1769480 | tf_op jit(solution)/shard_map/weight_grads/ppermute | solution.py:71
  199.2 23.7 %collective-permute-start.41 = (bf16[4,3,64,512]{3,2,1,0:T(8,128)(2,1)S(1)}, bf16[4,3,64,512]{3,2,1,0:T(8,128)(2,1)S(1)}, u32[]{:S(2)}, u32[]{:S(2)}) collective-permute-start(bf16[4,3,64,512]{3,2,1,0:T(8,128)(2,1)S(1)} %slice_bitcast_fusion), channel_id=1, source_target_pairs={{0,16},{1,17},{2,18},{3,19},{4,20},{5,21},{6,22},{7,23},{8,24},{9,... | collective-permute-start | bytes 2359304 | tf_op jit(solution)/shard_map/mixing_back/ppermute | solution.py:71
  203.0 19.9 %collective-permute-start.40 = (bf16[1,4,3,64,512]{4,3,2,1,0:T(8,128)(2,1)S(1)}, bf16[1,4,3,64,512]{4,3,2,1,0:T(8,128)(2,1)S(1)}, u32[]{:S(2)}, u32[]{:S(2)}) collective-permute-start(bf16[1,4,3,64,512]{4,3,2,1,0:T(8,128)(2,1)S(1)} %get-tuple-element.159), channel_id=1, source_target_pairs={{0,2},{1,3},{2,0},{3,1},{4,6},{5,7},{6,4},{7,5},{8,10},{9,11},{10,... | collective-permute-start | bytes 2359304 | tf_op jit(solution)/shard_map/mixing_back/ppermute | solution.py:71
  209.1 13.8 %collective-permute-start.43 = (bf16[96,768]{1,0:T(8,128)(2,1)S(1)}, bf16[96,768]{1,0:T(8,128)(2,1)S(1)}, u32[]{:S(2)}, u32[]{:S(2)}) collective-permute-start(bf16[96,768]{1,0:T(8,128)(2,1)S(1)} %get-tuple-element.216), channel_id=1, source_target_pairs={{0,8},{1,9},{2,10},{3,11},{4,12},{5,13},{6,14},{7,15},{8,0},{9,1},... | collective-permute-start | bytes 442376 | tf_op jit(solution)/shard_map/weight_grads/ppermute | solution.py:71
  224.1 22.3 %collective-permute-start.49 = (bf16[8,24,2304]{2,1,0:T(8,128)(2,1)S(1)}, bf16[8,24,2304]{2,1,0:T(8,128)(2,1)}, u32[]{:S(2)}, u32[]{:S(2)}) collective-permute-start(bf16[8,24,2304]{2,1,0:T(8,128)(2,1)S(1)} %copy-done.30), channel_id=1, source_target_pairs={{0,2},{1,3},{2,0},{3,1},{4,6},{5,7},{6,4},{7,5},{8,10},{9,11},{10,... | collective-permute-start | bytes 2654216 | tf_op jit(solution)/shard_map/weight_grads/ppermute | solution.py:71
  225.2 21.2 %collective-permute-start.48 = (bf16[8,24,1536]{2,1,0:T(8,128)(2,1)S(1)}, bf16[8,24,1536]{2,1,0:T(8,128)(2,1)S(1)}, u32[]{:S(2)}, u32[]{:S(2)}) collective-permute-start(bf16[8,24,1536]{2,1,0:T(8,128)(2,1)S(1)} %copy-done.32), channel_id=1, source_target_pairs={{0,16},{1,17},{2,18},{3,19},{4,20},{5,21},{6,22},{7,23},{8,24},{9,... | collective-permute-start | bytes 1769480 | tf_op jit(solution)/shard_map/weight_grads/ppermute | solution.py:71
  226.8 9.8 %collective-permute-start.47 = (bf16[3,64,512]{2,1,0:T(8,128)(2,1)S(1)}, bf16[3,64,512]{2,1,0:T(8,128)(2,1)S(1)}, u32[]{:S(2)}, u32[]{:S(2)}) collective-permute-start(bf16[3,64,512]{2,1,0:T(8,128)(2,1)S(1)} %get-tuple-element.210), channel_id=1, source_target_pairs={{0,12},{1,13},{2,14},{3,15},{4,8},{5,9},{6,10},{7,11},{8,4},{9,5},... | collective-permute-start | bytes 589832 | tf_op jit(solution)/shard_map/mixing_back/ppermute | solution.py:71
  229.0 17.5 %collective-permute-start.46 = (bf16[3,64,512]{2,1,0:T(8,128)(2,1)S(1)}, bf16[3,64,512]{2,1,0:T(8,128)(2,1)S(1)}, u32[]{:S(2)}, u32[]{:S(2)}) collective-permute-start(bf16[3,64,512]{2,1,0:T(8,128)(2,1)S(1)} %get-tuple-element.211), channel_id=1, source_target_pairs={{0,8},{1,9},{2,10},{3,11},{4,12},{5,13},{6,14},{7,15},{8,0},{9,1},... | collective-permute-start | bytes 589832 | tf_op jit(solution)/shard_map/mixing_back/ppermute | solution.py:71
  230.3 16.2 %collective-permute-start.45 = (bf16[3,64,512]{2,1,0:T(8,128)(2,1)S(1)}, bf16[3,64,512]{2,1,0:T(8,128)(2,1)S(1)}, u32[]{:S(2)}, u32[]{:S(2)}) collective-permute-start(bf16[3,64,512]{2,1,0:T(8,128)(2,1)S(1)} %get-tuple-element.212), channel_id=1, source_target_pairs={{0,4},{1,5},{2,6},{3,7},{4,0},{5,1},{6,2},{7,3},{8,12},{9,13},{10,... | collective-permute-start | bytes 589832 | tf_op jit(solution)/shard_map/mixing_back/ppermute | solution.py:71
  250.4 26.3 %all-to-all-start.3 = ((bf16[4,3,64,512]{3,2,1,0:T(8,128)(2,1)}), bf16[4,3,64,512]{3,2,1,0:T(8,128)(2,1)}, u32[]{:S(2)}, u32[]{:S(2)}) async-start(bf16[4,3,64,512]{3,2,1,0:T(8,128)(2,1)} %fusion), calls=%async_computation.3 | async-start | bytes 1572864 | tf_op jit(solution)/shard_map/mixing_back/all_to_all | solution.py:77
  257.0 19.7 %collective-permute-start.55 = (bf16[4,24,2304]{2,1,0:T(8,128)(2,1)S(1)}, bf16[4,24,2304]{2,1,0:T(8,128)(2,1)}, u32[]{:S(2)}, u32[]{:S(2)}) collective-permute-start(bf16[4,24,2304]{2,1,0:T(8,128)(2,1)S(1)} %add_convert_fusion.10), channel_id=1, source_target_pairs={{0,16},{1,17},{2,18},{3,19},{4,20},{5,21},{6,22},{7,23},{8,24},{9,... | collective-permute-start | bytes 1327112 | tf_op jit(solution)/shard_map/weight_grads/ppermute | solution.py:71
  257.7 18.2 %collective-permute-start.54 = (bf16[4,24,1536]{2,1,0:T(8,128)(2,1)S(1)}, bf16[4,24,1536]{2,1,0:T(8,128)(2,1)S(1)}, u32[]{:S(2)}, u32[]{:S(2)}) collective-permute-start(bf16[4,24,1536]{2,1,0:T(8,128)(2,1)S(1)} %add_convert_fusion.13), channel_id=1, source_target_pairs={{0,2},{1,3},{2,0},{3,1},{4,6},{5,7},{6,4},{7,5},{8,10},{9,11},{10,... | collective-permute-start | bytes 884744 | tf_op jit(solution)/shard_map/weight_grads/ppermute | solution.py:71
  258.4 17.6 %collective-permute-start.51 = (bf16[4,24,768]{2,1,0:T(8,128)(2,1)S(1)}, bf16[4,24,768]{2,1,0:T(8,128)(2,1)S(1)}, u32[]{:S(2)}, u32[]{:S(2)}) collective-permute-start(bf16[4,24,768]{2,1,0:T(8,128)(2,1)S(1)} %get-tuple-element.178), channel_id=1, source_target_pairs={{0,16},{1,17},{2,18},{3,19},{4,20},{5,21},{6,22},{7,23},{8,24},{9,... | collective-permute-start | bytes 442376 | tf_op jit(solution)/shard_map/value_grads/ppermute | solution.py:71
  259.8 16.1 %collective-permute-start.52 = (bf16[4,24,768]{2,1,0:T(8,128)(2,1)S(1)}, bf16[4,24,768]{2,1,0:T(8,128)(2,1)S(1)}, u32[]{:S(2)}, u32[]{:S(2)}) collective-permute-start(bf16[4,24,768]{2,1,0:T(8,128)(2,1)S(1)} %get-tuple-element.179), channel_id=1, source_target_pairs={{0,2},{1,3},{2,0},{3,1},{4,6},{5,7},{6,4},{7,5},{8,10},{9,11},{10,... | collective-permute-start | bytes 442376 | tf_op jit(solution)/shard_map/value_grads/ppermute | solution.py:71
  261.3 14.7 %collective-permute-start.53 = (bf16[4,24,768]{2,1,0:T(8,128)(2,1)S(1)}, bf16[4,24,768]{2,1,0:T(8,128)(2,1)S(1)}, u32[]{:S(2)}, u32[]{:S(2)}) collective-permute-start(bf16[4,24,768]{2,1,0:T(8,128)(2,1)S(1)} %get-tuple-element.180), channel_id=1, source_target_pairs={{0,18},{1,19},{2,16},{3,17},{4,22},{5,23},{6,20},{7,21},{8,26},{9,... | collective-permute-start | bytes 442376 | tf_op jit(solution)/shard_map/value_grads/ppermute | solution.py:71
  281.2 13.5 %collective-permute-start.58 = (bf16[24,4608]{1,0:T(8,128)(2,1)S(1)}, bf16[24,4608]{1,0:T(8,128)(2,1)S(1)}, u32[]{:S(2)}, u32[]{:S(2)}) collective-permute-start(bf16[24,4608]{1,0:T(8,128)(2,1)S(1)} %get-tuple-element.208), channel_id=1, source_target_pairs={{0,12},{1,13},{2,14},{3,15},{4,8},{5,9},{6,10},{7,11},{8,4},{9,5},... | collective-permute-start | bytes 663560 | tf_op jit(solution)/shard_map/weight_grads/ppermute | solution.py:71
  283.5 18.9 %collective-permute-start.57 = (bf16[24,4608]{1,0:T(8,128)(2,1)S(1)}, bf16[24,4608]{1,0:T(8,128)(2,1)S(1)}, u32[]{:S(2)}, u32[]{:S(2)}) collective-permute-start(bf16[24,4608]{1,0:T(8,128)(2,1)S(1)} %get-tuple-element.209), channel_id=1, source_target_pairs={{0,8},{1,9},{2,10},{3,11},{4,12},{5,13},{6,14},{7,15},{8,0},{9,1},... | collective-permute-start | bytes 663560 | tf_op jit(solution)/shard_map/weight_grads/ppermute | solution.py:71
  (70 other events, 625.4 us)

commit v5 on v4

--- a/solution.py
+++ b/solution.py
@@ -13,7 +13,20 @@
 HEAD = 64
 GROUPS = 4
 EPS = 1e-06
-COST = 50_000_000_000
+SHARES = {
+    "mix_rows": 50000000000,
+    "make_values": 20000000000,
+    "mix_values": 50000000000,
+    "prepare_weights": 120000000000,
+    "middle": 50000000000,
+    "mix_back": 768,
+    "value_grads": 120000000000,
+    "make_tokens_grad": 8000000000,
+    "add_split": 768,
+    "stack_all": 50000000000,
+    "pass_on": 50000000000,
+    "add_all": 50000000000,
+}
 FIRST = 2
 SPLIT = 3
 MIB = 1 << 20
@@ -31,8 +44,8 @@
     return pltpu.CompilerParams(vmem_limit_bytes=mib * MIB)
 
 
-def cost(flops, moved, trans=0):
-    return pl.CostEstimate(flops=COST, bytes_accessed=1, transcendentals=0)
+def share(name):
+    return pl.CostEstimate(flops=SHARES[name], bytes_accessed=1, transcendentals=0)
 
 
 def shape(dims, kind=BF16):
@@ -142,7 +155,7 @@
         out_specs=vmem(),
         out_shape=shape((GROUPS, group, positions // 2, length)),
         compiler_params=params(24),
-        cost_estimate=cost(1e7, 4 * logits.size, logits.size),
+        cost_estimate=share("mix_rows"),
         name="mix_rows",
     )(lay.me, logits.reshape(GROUPS, group, positions, length))
 
@@ -205,7 +218,7 @@
         out_shape=outs,
         scratch_shapes=[pltpu.VMEM((GROUPS,) + piece, BF16), pltpu.VMEM((width // 128, rows, 128), F32)],
         compiler_params=params(24),
-        cost_estimate=cost(2 * rows * width * width, 6 * rows * width + 4 * width * width),
+        cost_estimate=share("make_values"),
         name="make_values",
     )(lay.me, tokens, *weight)
     normed = result[0]
@@ -250,7 +263,7 @@
             shape((GROUPS, group, positions, lanes)),
         ],
         compiler_params=params(40),
-        cost_estimate=cost(2 * group * GROUPS * positions * length * lanes, 8 * group * length * lanes),
+        cost_estimate=share("mix_values"),
         name="mix_values",
     )(lay.me, *inputs)
     return result
@@ -287,7 +300,7 @@
         ),
         out_shape=shape((width, kinds * width)),
         compiler_params=params(24),
-        cost_estimate=pl.CostEstimate(flops=width, bytes_accessed=width, transcendentals=0),
+        cost_estimate=share("prepare_weights"),
         name="prepare_weights",
     )(lay.me, *ups)
 
@@ -453,7 +466,7 @@
         ),
         out_shape=[shape(flat), shape(flat, F32), shape(piece)] + [shape(dims) for dims in grads],
         compiler_params=params(60),
-        cost_estimate=cost(12 * rows * width * hidden, 16 * width * hidden, rows * hidden),
+        cost_estimate=share("middle"),
         name="middle",
     )(lay.me, pieces, tokens, out_grad, *weights)
     return out[0], out[1], out[2], list(out[3:])
@@ -518,9 +531,7 @@
             pltpu.VMEM((GROUPS * positions, length), BF16),
         ],
         compiler_params=params(48),
-        cost_estimate=cost(
-            4 * group * GROUPS * positions * length * lanes, 8 * group * length * lanes
-        ),
+        cost_estimate=share("mix_back"),
         name="mix_back",
     )(lay.me, pieces, rows, values)
     return result[0], list(result[1:])
@@ -563,7 +574,7 @@
             pltpu.VMEM((width, width), F32),
         ],
         compiler_params=params(32),
-        cost_estimate=cost(2 * rows * width * width, 8 * rows * width),
+        cost_estimate=share("value_grads"),
         name="value_grads",
     )(lay.me, *pieces, normed)
 
@@ -585,29 +596,9 @@
         in_specs=[vmem()] * 4,
         out_specs=vmem(),
         compiler_params=params(24),
-        cost_estimate=cost(2 * rows * width * width, 12 * rows * width),
+        cost_estimate=share("make_tokens_grad"),
         name="make_tokens_grad",
     )(total, weight, tokens, residual_grad)
-
-
-def logits_out_kernel(me, *refs):
-    pieces, out = refs[:GROUPS], refs[GROUPS]
-    for k, piece in enumerate(pieces):
-        out[me[1] ^ k] = piece[...].astype(F32)
-
-
-def make_logits_grad(lay, pieces):
-    group, positions, part = pieces[0].shape
-    out = pl.pallas_call(
-        logits_out_kernel,
-        out_shape=shape((GROUPS, group, positions, part), F32),
-        in_specs=[smem()] + [vmem()] * GROUPS,
-        out_specs=vmem(),
-        compiler_params=params(16),
-        cost_estimate=cost(1e6, 24 * pieces[0].size),
-        name="make_logits_grad",
-    )(lay.me, *pieces)
-    return out.reshape(lay.heads, positions, part)
 
 
 def add_kernel(*refs):
@@ -626,7 +617,7 @@
         in_specs=[vmem()] * 2,
         out_specs=[vmem()] * parts,
         compiler_params=params(24),
-        cost_estimate=cost(left.size, 6 * left.size),
+        cost_estimate=share("add_split"),
         name="add_split",
     )(left, right)
 
@@ -644,7 +635,7 @@
         in_specs=[vmem()] * len(parts),
         out_specs=vmem(),
         compiler_params=params(24),
-        cost_estimate=cost(0, 4 * len(parts) * parts[0].size),
+        cost_estimate=share("stack_all"),
         name="stack_all",
     )(*parts)
 
@@ -660,7 +651,7 @@
         in_specs=[pl.BlockSpec(memory_space=pl.ANY)],
         out_specs=pl.BlockSpec(memory_space=pl.ANY),
         input_output_aliases={0: 0},
-        cost_estimate=cost(0, 0),
+        cost_estimate=share("pass_on"),
         name="pass_on",
     )(array)
 
@@ -680,7 +671,7 @@
         in_specs=[vmem()] * len(parts),
         out_specs=vmem(),
         compiler_params=params(24),
-        cost_estimate=cost(len(parts) * parts[0].size, 4 * len(parts) * parts[0].size),
+        cost_estimate=share("add_all"),
         name="add_all",
     )(*parts)
 

time: 307 us -> 304 us (level)
    unnamed x113 -> x107, local copies, waits for them, and re-layouts: 13.3 us -> 11.1 us
  transfers between devices with their start and end apart: 63 -> 63, of which waited for: 30 -> 30; matrix products, arithmetic and copies ran while one was open for 10% -> 10% of each run, Pallas kernels for 6% -> 7%
where the time goes in v5:
time: 304 us; the launch traced here: 303 us
  waiting for transfers between devices  120 us (39%)
  starting transfers between devices  78.5 us (26%)
  Pallas kernels  52.1 us (17%)
  other arithmetic  39.4 us (13%)
  local copies, waits for them, and re-layouts  11.5 us (4%)
    ppermute x59, waiting for transfers between devices, swap(): lax.ppermute(array, AXES, [(i, i ^ mask) for i in range(self.devices)])  105 us
    ppermute x59, starting transfers between devices, swap(): lax.ppermute(array, AXES, [(i, i ^ mask) for i in range(self.devices)])  61.3 us
    pallas_call x1, Pallas kernels, middle(): pl.pallas_call(functools.partial(middle_kernel, positions=lay.positions,...  30.3 us
    convert_element_type x13, other arithmetic, add_low(): return (left.astype(F32) + right.astype(F32)).astype(BF16)  19.2 us
    all_to_all x4, starting transfers between devices, across_z(): return lax.all_to_all(array, 'seq', 0, 0, axis_index_groups=lines)  17.2 us
    all_to_all x4, waiting for transfers between devices, across_z(): return lax.all_to_all(array, 'seq', 0, 0, axis_index_groups=lines)  14.7 us
    unnamed x107, local copies, waits for them, and re-layouts  11.1 us
  transfers between devices with their start and end apart: 63, of which 30 were waited for; matrix products, arithmetic and copies ran while one was open for 10% of the time, Pallas kernels for 7%

profile of v5, /device:TPU:0, one launch (start us, length us, event | category | flops | bytes accessed | tf_op | source)
XLA Modules:
  0.0 302.8 jit_solution(17464210062786610818)
XLA Ops:
  4.6 5.1 %collective-permute-start.2 = (bf16[6,24,768]{2,1,0:T(8,128)(2,1)S(1)}, bf16[6,24,768]{2,1,0:T(8,128)(2,1)S(1)}, u32[]{:S(2)}, u32[]{:S(2)}) collective-permute-start(bf16[6,24,768]{2,1,0:T(8,128)(2,1)S(1)} %pad_maximum_fusion.9), channel_id=1, source_target_pairs={{0,12},{1,13},{2,14},{3,15},{4,8},{5,9},{6,10},{7,11},{8,4},{9,5},... | collective-permute-start | bytes 663560 | tf_op jit(solution)/shard_map/round_one/ppermute | solution.py:84
  11.9 1.9 mix_rows.1
  13.8 2.3 collective-permute-done.2
  16.2 12.4 %collective-permute-done.1 = bf16[6,24,768]{2,1,0:T(8,128)(2,1)S(1)} collective-permute-done((bf16[6,24,768]{2,1,0:T(8,128)(2,1)S(1)}, bf16[6,24,768]{2,1,0:T(8,128)(2,1)S(1)}, u32[]{:S(2)}, u32[]{:S(2)}) %collective-permute-start.1) | collective-permute-done | bytes 221216 | tf_op jit(solution)/shard_map/round_one/ppermute | solution.py:84
  35.6 3.7 %all-to-all-start = ((bf16[4,3,32,1024]{3,2,1,0:T(8,128)(2,1)}), bf16[4,3,32,1024]{3,2,1,0:T(8,128)(2,1)S(1)}, u32[]{:S(2)}, u32[]{:S(2)}) async-start(bf16[4,3,32,1024]{3,2,1,0:T(8,128)(2,1)} %mix_rows.1), calls=%async_computation | async-start | bytes 1572864 | tf_op jit(solution)/shard_map/round_two/all_to_all | solution.py:90
  39.3 3.7 %collective-permute-done.5 = bf16[4,24,768]{2,1,0:T(8,128)(2,1)S(1)} collective-permute-done((bf16[4,24,768]{2,1,0:T(8,128)(2,1)S(1)}, bf16[4,24,768]{2,1,0:T(8,128)(2,1)S(1)}, u32[]{:S(2)}, u32[]{:S(2)}) %collective-permute-start.5) | collective-permute-done | bytes 147488 | tf_op jit(solution)/shard_map/round_two/ppermute | solution.py:84
  46.6 1.9 pad_maximum_fusion.5
  50.0 2.0 pad_maximum_fusion.2
  53.5 3.9 %all-to-all-done.refs_4_ = bf16[4,3,32,1024]{3,2,1,0:T(8,128)(2,1)S(1)} async-done(((bf16[4,3,32,1024]{3,2,1,0:T(8,128)(2,1)}), bf16[4,3,32,1024]{3,2,1,0:T(8,128)(2,1)S(1)}, u32[]{:S(2)}, u32[]{:S(2)}) %all-to-all-start) | async-done | bytes 786464 | tf_op jit(solution)/shard_map/round_two/all_to_all | solution.py:90
  57.4 2.0 make_values.1
  59.4 2.0 collective-permute-start.10
  61.4 2.4 collective-permute-start.11
  66.0 8.0 %collective-permute-done.12 = bf16[8,3,24,768]{3,2,1,0:T(8,128)(2,1)} collective-permute-done((bf16[8,3,24,768]{3,2,1,0:T(8,128)(2,1)}, bf16[8,3,24,768]{3,2,1,0:T(8,128)(2,1)}, u32[]{:S(2)}, u32[]{:S(2)}) %collective-permute-start.12) | collective-permute-done | bytes 884768 | tf_op jit(solution)/shard_map/round_two/ppermute | solution.py:84
  74.0 2.0 collective-permute-done.10.refs_2_
  77.0 3.0 collective-permute-start.17
  80.0 2.4 collective-permute-start.18
  82.4 2.7 pad_maximum_fusion.refs_0_
  85.0 2.3 pad_maximum_fusion.1.refs_2_
  87.3 1.9 collective-permute-done.17.refs_2_
  91.0 2.0 collective-permute-done.14.refs_1_
  96.8 2.7 mix_values.1
  106.6 5.4 %all-to-all-start.1 = ((bf16[4,3,64,512]{3,2,1,0:T(8,128)(2,1)}), bf16[4,3,64,512]{3,2,1,0:T(8,128)(2,1)S(1)}, u32[]{:S(2)}, u32[]{:S(2)}) async-start(bf16[4,3,64,512]{3,2,1,0:T(8,128)(2,1)} %get-tuple-element.128), calls=%async_computation.1 | async-start | bytes 1572864 | tf_op jit(solution)/shard_map/round_five/all_to_all | solution.py:90
  112.3 7.0 %collective-permute-done.28.refs_10_ = bf16[8,48,768]{2,1,0:T(8,128)(2,1)} collective-permute-done((bf16[8,48,768]{2,1,0:T(8,128)(2,1)S(1)}, bf16[8,48,768]{2,1,0:T(8,128)(2,1)}, u32[]{:S(2)}, u32[]{:S(2)}) %collective-permute-start.28) | collective-permute-done | bytes 589856 | tf_op jit(solution)/shard_map/round_five/ppermute | solution.py:84
  120.5 5.6 %prepare_weights.1.refs_3_.refs_4_ = bf16[768,3840]{1,0:T(8,128)(2,1)S(1)} custom-call(s32[8]{0:T(128)S(1)} %stack.44.me, bf16[16,3,24,768]{3,2,1,0:T(8,128)(2,1)} %pad_maximum_fusion.refs_0_, bf16[16,3,24,768]{3,2,1,0:T(8,128)(2,1)} %collective-permute-done.21.refs_1_, bf16[16,2,24,768]{3,2,1,0:T(8,128)(2,1)} %pad_maximum_fusion.1.refs_2_, ...), custom_call_target="tpu_custom_call" | custom-call | flops 120000004096 | bytes 1 | tf_op jit(solution)/shard_map/round_five/prepare_weights/pallas_call | solution.py:293
  126.1 2.5 copy-done.11
  130.2 2.6 all-to-all-done.1.refs_0_
  133.7 30.3 %middle.1 = (bf16[512,768]{1,0:T(8,128)(2,1)}, f32[512,768]{1,0:T(8,128)}, bf16[4,3,64,512]{3,2,1,0:T(8,128)(2,1)}, bf16[16,24,1536]{2,1,0:T(8,128)(2,1)}, bf16[...) custom-call(s32[8]{0:T(128)} %copy-done.2, ...), custom_call_target="tpu_custom_call" | custom-call | flops 49999998976 | bytes 1 | tf_op jit(solution)/shard_map/feed_forward/middle/pallas_call | solution.py:442
  165.1 3.7 %all-to-all-start.2 = ((bf16[4,3,64,512]{3,2,1,0:T(8,128)(2,1)}), bf16[4,3,64,512]{3,2,1,0:T(8,128)(2,1)S(1)}, u32[]{:S(2)}, u32[]{:S(2)}) async-start(bf16[4,3,64,512]{3,2,1,0:T(8,128)(2,1)} %get-tuple-element.141), calls=%async_computation.2 | async-start | bytes 1572864 | tf_op jit(solution)/shard_map/feed_forward/all_to_all | solution.py:90
  168.8 2.5 add_convert_fusion.7
  175.0 2.7 add_convert_fusion.2
  177.8 3.1 %add_convert_fusion = (bf16[8,24,2304]{2,1,0:T(8,128)(2,1)}, bf16[8,24,2304]{2,1,0:T(8,128)(2,1)}) fusion(bf16[16,24,2304]{2,1,0:T(8,128)(2,1)} %collective-permute-done.36, bf16[16,24,2304]{2,1,0:T(8,128)(2,1)S(1)} %copy-done.23), kind=kLoop, calls=%fused_computation.1 | loop fusion | flops 3538944 | bytes 5308416 | tf_op jit(solution)/shard_map/weight_grads/convert_element_type | solution.py:94
  180.9 8.3 %all-to-all-done.2.refs_0_ = bf16[4,3,64,512]{3,2,1,0:T(8,128)(2,1)S(1)} async-done(((bf16[4,3,64,512]{3,2,1,0:T(8,128)(2,1)}), bf16[4,3,64,512]{3,2,1,0:T(8,128)(2,1)S(1)}, u32[]{:S(2)}, u32[]{:S(2)}) %all-to-all-start.2) | async-done | bytes 786464 | tf_op jit(solution)/shard_map/feed_forward/all_to_all | solution.py:90
  193.9 4.8 %mix_back.1 = (bf16[2,4,3,64,512]{4,3,2,1,0:T(8,128)(2,1)S(1)}, bf16[2,4,3,64,512]{4,3,2,1,0:T(8,128)(2,1)S(1)}, bf16[2,4,3,64,512]{4,3,2,1,0:T(8,128)(2,1)S(1)}) custom-call(s32[8]{0:T(128)S(1)} %copy-done.3, bf16[4,3,64,512]{3,2,1,0:T(8,128)(2,1)S(1)} %all-to-all-done.2.refs_0_, bf16[3,256,1024]{2,1,0:T(8,128)(2,1)} %copy-done.1, ...), custom_call_target="tpu_custom_call" | custom-call | flops 768 | bytes 1 | tf_op jit(solution)/shard_map/mixing_back/mix_back/pallas_call | solution.py:520
  207.4 2.2 collective-permute-start.44
  209.5 2.3 collective-permute-start.43
  211.8 4.2 %collective-permute-done.44 = bf16[96,768]{1,0:T(8,128)(2,1)S(1)} collective-permute-done((bf16[96,768]{1,0:T(8,128)(2,1)S(1)}, bf16[96,768]{1,0:T(8,128)(2,1)S(1)}, u32[]{:S(2)}, u32[]{:S(2)}) %collective-permute-start.44) | collective-permute-done | bytes 147488 | tf_op jit(solution)/shard_map/weight_grads/ppermute | solution.py:84
  216.0 3.1 %collective-permute-done.42 = bf16[96,768]{1,0:T(8,128)(2,1)S(1)} collective-permute-done((bf16[96,768]{1,0:T(8,128)(2,1)S(1)}, bf16[96,768]{1,0:T(8,128)(2,1)S(1)}, u32[]{:S(2)}, u32[]{:S(2)}) %collective-permute-start.42) | collective-permute-done | bytes 147488 | tf_op jit(solution)/shard_map/weight_grads/ppermute | solution.py:84
  219.1 4.2 %collective-permute-done.43 = bf16[96,768]{1,0:T(8,128)(2,1)S(1)} collective-permute-done((bf16[96,768]{1,0:T(8,128)(2,1)S(1)}, bf16[96,768]{1,0:T(8,128)(2,1)S(1)}, u32[]{:S(2)}, u32[]{:S(2)}) %collective-permute-start.43) | collective-permute-done | bytes 147488 | tf_op jit(solution)/shard_map/weight_grads/ppermute | solution.py:84
  226.4 2.2 collective-permute-start.47
  230.9 5.3 %collective-permute-done.47.refs_3_ = bf16[3,64,512]{2,1,0:T(8,128)(2,1)S(1)} collective-permute-done((bf16[3,64,512]{2,1,0:T(8,128)(2,1)S(1)}, bf16[3,64,512]{2,1,0:T(8,128)(2,1)S(1)}, u32[]{:S(2)}, u32[]{:S(2)}) %collective-permute-start.47) | collective-permute-done | bytes 196640 | tf_op jit(solution)/shard_map/mixing_back/ppermute | solution.py:84
  236.2 9.3 %collective-permute-done.46.refs_2_ = bf16[3,64,512]{2,1,0:T(8,128)(2,1)S(1)} collective-permute-done((bf16[3,64,512]{2,1,0:T(8,128)(2,1)S(1)}, bf16[3,64,512]{2,1,0:T(8,128)(2,1)S(1)}, u32[]{:S(2)}, u32[]{:S(2)}) %collective-permute-start.46) | collective-permute-done | bytes 196640 | tf_op jit(solution)/shard_map/mixing_back/ppermute | solution.py:84
  248.6 4.3 %all-to-all-start.3 = ((bf16[4,3,64,512]{3,2,1,0:T(8,128)(2,1)}), bf16[4,3,64,512]{3,2,1,0:T(8,128)(2,1)}, u32[]{:S(2)}, u32[]{:S(2)}) async-start(bf16[4,3,64,512]{3,2,1,0:T(8,128)(2,1)} %fusion), calls=%async_computation.3 | async-start | bytes 1572864 | tf_op jit(solution)/shard_map/mixing_back/all_to_all | solution.py:90
  260.8 12.6 %collective-permute-done.51.refs_1_ = bf16[4,24,768]{2,1,0:T(8,128)(2,1)S(1)} collective-permute-done((bf16[4,24,768]{2,1,0:T(8,128)(2,1)S(1)}, bf16[4,24,768]{2,1,0:T(8,128)(2,1)S(1)}, u32[]{:S(2)}, u32[]{:S(2)}) %collective-permute-start.51) | collective-permute-done | bytes 147488 | tf_op jit(solution)/shard_map/value_grads/ppermute | solution.py:84
  278.6 2.4 collective-permute-start.58
  281.0 2.2 make_tokens_grad.1
  283.2 2.5 bitcast_convert_fusion
  285.7 6.4 %collective-permute-done.58 = bf16[24,4608]{1,0:T(8,128)(2,1)S(1)} collective-permute-done((bf16[24,4608]{1,0:T(8,128)(2,1)S(1)}, bf16[24,4608]{1,0:T(8,128)(2,1)S(1)}, u32[]{:S(2)}, u32[]{:S(2)}) %collective-permute-start.58) | collective-permute-done | bytes 221216 | tf_op jit(solution)/shard_map/weight_grads/ppermute | solution.py:84
  292.1 7.8 %collective-permute-done.57 = bf16[24,4608]{1,0:T(8,128)(2,1)S(1)} collective-permute-done((bf16[24,4608]{1,0:T(8,128)(2,1)S(1)}, bf16[24,4608]{1,0:T(8,128)(2,1)S(1)}, u32[]{:S(2)}, u32[]{:S(2)}) %collective-permute-start.57) | collective-permute-done | bytes 221216 | tf_op jit(solution)/shard_map/weight_grads/ppermute | solution.py:84
  (248 shorter events, 81.8 us)
Async XLA Ops:
  4.6 11.5 %collective-permute-start.2 = (bf16[6,24,768]{2,1,0:T(8,128)(2,1)S(1)}, bf16[6,24,768]{2,1,0:T(8,128)(2,1)S(1)}, u32[]{:S(2)}, u32[]{:S(2)}) collective-permute-start(bf16[6,24,768]{2,1,0:T(8,128)(2,1)S(1)} %pad_maximum_fusion.9), channel_id=1, source_target_pairs={{0,12},{1,13},{2,14},{3,15},{4,8},{5,9},{6,10},{7,11},{8,4},{9,5},... | collective-permute-start | bytes 663560 | tf_op jit(solution)/shard_map/round_one/ppermute | solution.py:84
  9.8 18.8 %collective-permute-start.1 = (bf16[6,24,768]{2,1,0:T(8,128)(2,1)S(1)}, bf16[6,24,768]{2,1,0:T(8,128)(2,1)S(1)}, u32[]{:S(2)}, u32[]{:S(2)}) collective-permute-start(bf16[6,24,768]{2,1,0:T(8,128)(2,1)S(1)} %pad_maximum_fusion.9), channel_id=1, source_target_pairs={{0,8},{1,9},{2,10},{3,11},{4,12},{5,13},{6,14},{7,15},{8,0},{9,1},... | collective-permute-start | bytes 663560 | tf_op jit(solution)/shard_map/round_one/ppermute | solution.py:84
  9.8 18.8 %collective-permute-start = (bf16[6,24,768]{2,1,0:T(8,128)(2,1)S(1)}, bf16[6,24,768]{2,1,0:T(8,128)(2,1)S(1)}, u32[]{:S(2)}, u32[]{:S(2)}) collective-permute-start(bf16[6,24,768]{2,1,0:T(8,128)(2,1)S(1)} %pad_maximum_fusion.9), channel_id=1, source_target_pairs={{0,4},{1,5},{2,6},{3,7},{4,0},{5,1},{6,2},{7,3},{8,12},{9,13},{10,... | collective-permute-start | bytes 663560 | tf_op jit(solution)/shard_map/round_one/ppermute | solution.py:84
  28.8 17.6 %collective-permute-start.6 = (bf16[4,3,24,768]{3,2,1,0:T(8,128)(2,1)S(1)}, bf16[4,3,24,768]{3,2,1,0:T(8,128)(2,1)}, u32[]{:S(2)}, u32[]{:S(2)}) collective-permute-start(bf16[4,3,24,768]{3,2,1,0:T(8,128)(2,1)S(1)} %slice.244), channel_id=1, source_target_pairs={{0,16},{1,17},{2,18},{3,19},{4,20},{5,21},{6,22},{7,23},{8,24},{9,... | collective-permute-start | bytes 1327112 | tf_op jit(solution)/shard_map/round_two/ppermute | solution.py:84
  30.4 16.0 %collective-permute-start.7 = (bf16[4,2,24,768]{3,2,1,0:T(8,128)(2,1)S(1)}, bf16[4,2,24,768]{3,2,1,0:T(8,128)(2,1)}, u32[]{:S(2)}, u32[]{:S(2)}) collective-permute-start(bf16[4,2,24,768]{3,2,1,0:T(8,128)(2,1)S(1)} %pad_maximum_fusion.8), channel_id=1, source_target_pairs={{0,2},{1,3},{2,0},{3,1},{4,6},{5,7},{6,4},{7,5},{8,10},{9,11},{10,... | collective-permute-start | bytes 884744 | tf_op jit(solution)/shard_map/round_two/ppermute | solution.py:84
  32.0 11.0 %collective-permute-start.5 = (bf16[4,24,768]{2,1,0:T(8,128)(2,1)S(1)}, bf16[4,24,768]{2,1,0:T(8,128)(2,1)S(1)}, u32[]{:S(2)}, u32[]{:S(2)}) collective-permute-start(bf16[4,24,768]{2,1,0:T(8,128)(2,1)S(1)} %pad_maximum_fusion.11), channel_id=1, source_target_pairs={{0,18},{1,19},{2,16},{3,17},{4,22},{5,23},{6,20},{7,21},{8,26},{9,... | collective-permute-start | bytes 442376 | tf_op jit(solution)/shard_map/round_two/ppermute | solution.py:84
  32.6 12.0 %collective-permute-start.4 = (bf16[4,24,768]{2,1,0:T(8,128)(2,1)S(1)}, bf16[4,24,768]{2,1,0:T(8,128)(2,1)S(1)}, u32[]{:S(2)}, u32[]{:S(2)}) collective-permute-start(bf16[4,24,768]{2,1,0:T(8,128)(2,1)S(1)} %pad_maximum_fusion.11), channel_id=1, source_target_pairs={{0,2},{1,3},{2,0},{3,1},{4,6},{5,7},{6,4},{7,5},{8,10},{9,11},{10,... | collective-permute-start | bytes 442376 | tf_op jit(solution)/shard_map/round_two/ppermute | solution.py:84
  34.1 12.3 %collective-permute-start.3 = (bf16[4,24,768]{2,1,0:T(8,128)(2,1)S(1)}, bf16[4,24,768]{2,1,0:T(8,128)(2,1)S(1)}, u32[]{:S(2)}, u32[]{:S(2)}) collective-permute-start(bf16[4,24,768]{2,1,0:T(8,128)(2,1)S(1)} %pad_maximum_fusion.11), channel_id=1, source_target_pairs={{0,16},{1,17},{2,18},{3,19},{4,20},{5,21},{6,22},{7,23},{8,24},{9,... | collective-permute-start | bytes 442376 | tf_op jit(solution)/shard_map/round_two/ppermute | solution.py:84
  35.6 21.8 %all-to-all-start = ((bf16[4,3,32,1024]{3,2,1,0:T(8,128)(2,1)}), bf16[4,3,32,1024]{3,2,1,0:T(8,128)(2,1)S(1)}, u32[]{:S(2)}, u32[]{:S(2)}) async-start(bf16[4,3,32,1024]{3,2,1,0:T(8,128)(2,1)} %mix_rows.1), calls=%async_computation | async-start | bytes 1572864 | tf_op jit(solution)/shard_map/round_two/all_to_all | solution.py:90
  48.5 16.0 %collective-permute-start.13 = (bf16[8,2,24,768]{3,2,1,0:T(8,128)(2,1)}, bf16[8,2,24,768]{3,2,1,0:T(8,128)(2,1)}, u32[]{:S(2)}, u32[]{:S(2)}) collective-permute-start(bf16[8,2,24,768]{3,2,1,0:T(8,128)(2,1)} %pad_maximum_fusion.5), channel_id=1, source_target_pairs={{0,16},{1,17},{2,18},{3,19},{4,20},{5,21},{6,22},{7,23},{8,24},{9,... | collective-permute-start | bytes 1769480 | tf_op jit(solution)/shard_map/round_two/ppermute | solution.py:84
  52.0 22.0 %collective-permute-start.12 = (bf16[8,3,24,768]{3,2,1,0:T(8,128)(2,1)}, bf16[8,3,24,768]{3,2,1,0:T(8,128)(2,1)}, u32[]{:S(2)}, u32[]{:S(2)}) collective-permute-start(bf16[8,3,24,768]{3,2,1,0:T(8,128)(2,1)} %pad_maximum_fusion.2), channel_id=1, source_target_pairs={{0,2},{1,3},{2,0},{3,1},{4,6},{5,7},{6,4},{7,5},{8,10},{9,11},{10,... | collective-permute-start | bytes 2654216 | tf_op jit(solution)/shard_map/round_two/ppermute | solution.py:84
  59.3 14.7 %collective-permute-start.9 = (bf16[3,64,512]{2,1,0:T(8,128)(2,1)S(1)}, bf16[3,64,512]{2,1,0:T(8,128)(2,1)S(1)}, u32[]{:S(2)}, u32[]{:S(2)}) collective-permute-start(bf16[3,64,512]{2,1,0:T(8,128)(2,1)S(1)} %get-tuple-element.116), channel_id=1, source_target_pairs={{0,4},{1,5},{2,6},{3,7},{4,0},{5,1},{6,2},{7,3},{8,12},{9,13},{10,... | collective-permute-start | bytes 589832 | tf_op jit(solution)/shard_map/round_three/ppermute | solution.py:84
  59.4 16.6 %collective-permute-start.10 = (bf16[3,64,512]{2,1,0:T(8,128)(2,1)S(1)}, bf16[3,64,512]{2,1,0:T(8,128)(2,1)S(1)}, u32[]{:S(2)}, u32[]{:S(2)}) collective-permute-start(bf16[3,64,512]{2,1,0:T(8,128)(2,1)S(1)} %get-tuple-element.117), channel_id=1, source_target_pairs={{0,8},{1,9},{2,10},{3,11},{4,12},{5,13},{6,14},{7,15},{8,0},{9,1},... | collective-permute-start | bytes 589832 | tf_op jit(solution)/shard_map/round_three/ppermute | solution.py:84
  61.4 14.6 %collective-permute-start.11 = (bf16[3,64,512]{2,1,0:T(8,128)(2,1)S(1)}, bf16[3,64,512]{2,1,0:T(8,128)(2,1)S(1)}, u32[]{:S(2)}, u32[]{:S(2)}) collective-permute-start(bf16[3,64,512]{2,1,0:T(8,128)(2,1)S(1)} %get-tuple-element.118), channel_id=1, source_target_pairs={{0,12},{1,13},{2,14},{3,15},{4,8},{5,9},{6,10},{7,11},{8,4},{9,5},... | collective-permute-start | bytes 589832 | tf_op jit(solution)/shard_map/round_three/ppermute | solution.py:84
  64.4 26.5 %collective-permute-start.15 = (bf16[4,3,32,1024]{3,2,1,0:T(8,128)(2,1)S(1)}, bf16[4,3,32,1024]{3,2,1,0:T(8,128)(2,1)S(1)}, u32[]{:S(2)}, u32[]{:S(2)}) collective-permute-start(bf16[4,3,32,1024]{3,2,1,0:T(8,128)(2,1)S(1)} %all-to-all-done.refs_4_), channel_id=1, source_target_pairs={{0,16},{1,17},{2,18},{3,19},{4,20},{5,21},{6,22},{7,23},{8,24},{9,... | collective-permute-start | bytes 2359304 | tf_op jit(solution)/shard_map/round_four/ppermute | solution.py:84
  76.1 16.9 %collective-permute-start.14 = (bf16[4,3,64,512]{3,2,1,0:T(8,128)(2,1)S(1)}, bf16[4,3,64,512]{3,2,1,0:T(8,128)(2,1)S(1)}, u32[]{:S(2)}, u32[]{:S(2)}) collective-permute-start(bf16[4,3,64,512]{3,2,1,0:T(8,128)(2,1)S(1)} %stack_all.2.refs_0_), channel_id=1, source_target_pairs={{0,2},{1,3},{2,0},{3,1},{4,6},{5,7},{6,4},{7,5},{8,10},{9,11},{10,... | collective-permute-start | bytes 2359304 | tf_op jit(solution)/shard_map/round_four/ppermute | solution.py:84
  77.0 12.3 %collective-permute-start.17 = (bf16[96,768]{1,0:T(8,128)(2,1)S(1)}, bf16[96,768]{1,0:T(8,128)(2,1)S(1)}, u32[]{:S(2)}, u32[]{:S(2)}) collective-permute-start(bf16[96,768]{1,0:T(8,128)(2,1)S(1)} %copy-done.7), channel_id=1, source_target_pairs={{0,8},{1,9},{2,10},{3,11},{4,12},{5,13},{6,14},{7,15},{8,0},{9,1},... | collective-permute-start | bytes 442376 | tf_op jit(solution)/shard_map/round_four/ppermute | solution.py:84
  80.0 10.9 %collective-permute-start.18 = (bf16[96,768]{1,0:T(8,128)(2,1)S(1)}, bf16[96,768]{1,0:T(8,128)(2,1)S(1)}, u32[]{:S(2)}, u32[]{:S(2)}) collective-permute-start(bf16[96,768]{1,0:T(8,128)(2,1)S(1)} %copy-done.7), channel_id=1, source_target_pairs={{0,12},{1,13},{2,14},{3,15},{4,8},{5,9},{6,10},{7,11},{8,4},{9,5},... | collective-permute-start | bytes 442376 | tf_op jit(solution)/shard_map/round_four/ppermute | solution.py:84
  89.2 22.8 %collective-permute-start.22 = (bf16[16,2,24,768]{3,2,1,0:T(8,128)(2,1)}, bf16[16,2,24,768]{3,2,1,0:T(8,128)(2,1)}, u32[]{:S(2)}, u32[]{:S(2)}) collective-permute-start(bf16[16,2,24,768]{3,2,1,0:T(8,128)(2,1)} %pad_maximum_fusion.1.refs_2_), channel_id=1, source_target_pairs={{0,1},{1,0},{2,3},{3,2},{4,5},{5,4},{6,7},{7,6},{8,9},{9,8},{10,11... | collective-permute-start | bytes 3538952 | tf_op jit(solution)/shard_map/round_five/ppermute | solution.py:84
  90.9 29.5 %collective-permute-start.21 = (bf16[16,3,24,768]{3,2,1,0:T(8,128)(2,1)}, bf16[16,3,24,768]{3,2,1,0:T(8,128)(2,1)}, u32[]{:S(2)}, u32[]{:S(2)}) collective-permute-start(bf16[16,3,24,768]{3,2,1,0:T(8,128)(2,1)} %pad_maximum_fusion.refs_0_), channel_id=1, source_target_pairs={{0,1},{1,0},{2,3},{3,2},{4,5},{5,4},{6,7},{7,6},{8,9},{9,8},{10,11... | collective-permute-start | bytes 5308424 | tf_op jit(solution)/shard_map/round_five/ppermute | solution.py:84
  104.5 14.7 %collective-permute-start.28 = (bf16[8,48,768]{2,1,0:T(8,128)(2,1)S(1)}, bf16[8,48,768]{2,1,0:T(8,128)(2,1)}, u32[]{:S(2)}, u32[]{:S(2)}) collective-permute-start(bf16[8,48,768]{2,1,0:T(8,128)(2,1)S(1)} %pad_maximum_fusion.7.refs_9_), channel_id=1, source_target_pairs={{0,16},{1,17},{2,18},{3,19},{4,20},{5,21},{6,22},{7,23},{8,24},{9,... | collective-permute-start | bytes 1769480 | tf_op jit(solution)/shard_map/round_five/ppermute | solution.py:84
  106.0 14.4 %collective-permute-start.25 = (bf16[8,48,768]{2,1,0:T(8,128)(2,1)S(1)}, bf16[8,48,768]{2,1,0:T(8,128)(2,1)S(1)}, u32[]{:S(2)}, u32[]{:S(2)}) collective-permute-start(bf16[8,48,768]{2,1,0:T(8,128)(2,1)S(1)} %pad_maximum_fusion.6.refs_5_), channel_id=1, source_target_pairs={{0,2},{1,3},{2,0},{3,1},{4,6},{5,7},{6,4},{7,5},{8,10},{9,11},{10,... | collective-permute-start | bytes 1769480 | tf_op jit(solution)/shard_map/round_five/ppermute | solution.py:84
  106.6 22.0 %collective-permute-start.29 = (bf16[8,48,768]{2,1,0:T(8,128)(2,1)S(1)}, bf16[8,48,768]{2,1,0:T(8,128)(2,1)}, u32[]{:S(2)}, u32[]{:S(2)}) collective-permute-start(bf16[8,48,768]{2,1,0:T(8,128)(2,1)S(1)} %pad_maximum_fusion.7.refs_9_), channel_id=1, source_target_pairs={{0,1},{1,0},{2,3},{3,2},{4,5},{5,4},{6,7},{7,6},{8,9},{9,8},{10,11... | collective-permute-start | bytes 1769480 | tf_op jit(solution)/shard_map/round_five/ppermute | solution.py:84
  106.6 26.2 %all-to-all-start.1 = ((bf16[4,3,64,512]{3,2,1,0:T(8,128)(2,1)}), bf16[4,3,64,512]{3,2,1,0:T(8,128)(2,1)S(1)}, u32[]{:S(2)}, u32[]{:S(2)}) async-start(bf16[4,3,64,512]{3,2,1,0:T(8,128)(2,1)} %get-tuple-element.128), calls=%async_computation.1 | async-start | bytes 1572864 | tf_op jit(solution)/shard_map/round_five/all_to_all | solution.py:90
  112.0 16.6 %collective-permute-start.26 = (bf16[8,48,768]{2,1,0:T(8,128)(2,1)S(1)}, bf16[8,48,768]{2,1,0:T(8,128)(2,1)S(1)}, u32[]{:S(2)}, u32[]{:S(2)}) collective-permute-start(bf16[8,48,768]{2,1,0:T(8,128)(2,1)S(1)} %pad_maximum_fusion.6.refs_5_), channel_id=1, source_target_pairs={{0,1},{1,0},{2,3},{3,2},{4,5},{5,4},{6,7},{7,6},{8,9},{9,8},{10,11... | collective-permute-start | bytes 1769480 | tf_op jit(solution)/shard_map/round_five/ppermute | solution.py:84
  120.5 9.8 %collective-permute-start.27 = (bf16[8,48,768]{2,1,0:T(8,128)(2,1)S(1)}, bf16[8,48,768]{2,1,0:T(8,128)(2,1)}, u32[]{:S(2)}, u32[]{:S(2)}) collective-permute-start(bf16[8,48,768]{2,1,0:T(8,128)(2,1)S(1)} %collective-permute-done.25.refs_6_), channel_id=1, source_target_pairs={{0,1},{1,0},{2,3},{3,2},{4,5},{5,4},{6,7},{7,6},{8,9},{9,8},{10,11... | collective-permute-start | bytes 1769480 | tf_op jit(solution)/shard_map/round_five/ppermute | solution.py:84
  164.6 13.2 %collective-permute-start.36 = (bf16[16,24,2304]{2,1,0:T(8,128)(2,1)}, bf16[16,24,2304]{2,1,0:T(8,128)(2,1)}, u32[]{:S(2)}, u32[]{:S(2)}) collective-permute-start(bf16[16,24,2304]{2,1,0:T(8,128)(2,1)} %get-tuple-element.147), channel_id=1, source_target_pairs={{0,1},{1,0},{2,3},{3,2},{4,5},{5,4},{6,7},{7,6},{8,9},{9,8},{10,11... | collective-permute-start | bytes 5308424 | tf_op jit(solution)/shard_map/weight_grads/ppermute | solution.py:84
  164.7 10.4 %collective-permute-start.35 = (bf16[16,24,1536]{2,1,0:T(8,128)(2,1)}, bf16[16,24,1536]{2,1,0:T(8,128)(2,1)}, u32[]{:S(2)}, u32[]{:S(2)}) collective-permute-start(bf16[16,24,1536]{2,1,0:T(8,128)(2,1)} %get-tuple-element.145), channel_id=1, source_target_pairs={{0,1},{1,0},{2,3},{3,2},{4,5},{5,4},{6,7},{7,6},{8,9},{9,8},{10,11... | collective-permute-start | bytes 3538952 | tf_op jit(solution)/shard_map/weight_grads/ppermute | solution.py:84
  165.1 24.1 %all-to-all-start.2 = ((bf16[4,3,64,512]{3,2,1,0:T(8,128)(2,1)}), bf16[4,3,64,512]{3,2,1,0:T(8,128)(2,1)S(1)}, u32[]{:S(2)}, u32[]{:S(2)}) async-start(bf16[4,3,64,512]{3,2,1,0:T(8,128)(2,1)} %get-tuple-element.141), calls=%async_computation.2 | async-start | bytes 1572864 | tf_op jit(solution)/shard_map/feed_forward/all_to_all | solution.py:90
  171.3 17.9 %collective-permute-start.32 = (bf16[8,48,768]{2,1,0:T(8,128)(2,1)}, bf16[8,48,768]{2,1,0:T(8,128)(2,1)}, u32[]{:S(2)}, u32[]{:S(2)}) collective-permute-start(bf16[8,48,768]{2,1,0:T(8,128)(2,1)} %get-tuple-element.206), channel_id=1, source_target_pairs={{0,2},{1,3},{2,0},{3,1},{4,6},{5,7},{6,4},{7,5},{8,10},{9,11},{10,... | collective-permute-start | bytes 1769480 | tf_op jit(solution)/shard_map/weight_grads/ppermute | solution.py:84
  173.5 15.7 %collective-permute-start.34 = (bf16[8,48,768]{2,1,0:T(8,128)(2,1)S(1)}, bf16[8,48,768]{2,1,0:T(8,128)(2,1)}, u32[]{:S(2)}, u32[]{:S(2)}) collective-permute-start(bf16[8,48,768]{2,1,0:T(8,128)(2,1)S(1)} %get-tuple-element.204), channel_id=1, source_target_pairs={{0,16},{1,17},{2,18},{3,19},{4,20},{5,21},{6,22},{7,23},{8,24},{9,... | collective-permute-start | bytes 1769480 | tf_op jit(solution)/shard_map/weight_grads/ppermute | solution.py:84
  200.0 23.2 %collective-permute-start.41 = (bf16[4,3,64,512]{3,2,1,0:T(8,128)(2,1)S(1)}, bf16[4,3,64,512]{3,2,1,0:T(8,128)(2,1)S(1)}, u32[]{:S(2)}, u32[]{:S(2)}) collective-permute-start(bf16[4,3,64,512]{3,2,1,0:T(8,128)(2,1)S(1)} %slice_bitcast_fusion), channel_id=1, source_target_pairs={{0,16},{1,17},{2,18},{3,19},{4,20},{5,21},{6,22},{7,23},{8,24},{9,... | collective-permute-start | bytes 2359304 | tf_op jit(solution)/shard_map/mixing_back/ppermute | solution.py:84
  203.7 19.6 %collective-permute-start.40 = (bf16[1,4,3,64,512]{4,3,2,1,0:T(8,128)(2,1)S(1)}, bf16[1,4,3,64,512]{4,3,2,1,0:T(8,128)(2,1)S(1)}, u32[]{:S(2)}, u32[]{:S(2)}) collective-permute-start(bf16[1,4,3,64,512]{4,3,2,1,0:T(8,128)(2,1)S(1)} %get-tuple-element.159), channel_id=1, source_target_pairs={{0,2},{1,3},{2,0},{3,1},{4,6},{5,7},{6,4},{7,5},{8,10},{9,11},{10,... | collective-permute-start | bytes 2359304 | tf_op jit(solution)/shard_map/mixing_back/ppermute | solution.py:84
  209.5 9.6 %collective-permute-start.42 = (bf16[96,768]{1,0:T(8,128)(2,1)S(1)}, bf16[96,768]{1,0:T(8,128)(2,1)S(1)}, u32[]{:S(2)}, u32[]{:S(2)}) collective-permute-start(bf16[96,768]{1,0:T(8,128)(2,1)S(1)} %get-tuple-element.215), channel_id=1, source_target_pairs={{0,4},{1,5},{2,6},{3,7},{4,0},{5,1},{6,2},{7,3},{8,12},{9,13},{10,... | collective-permute-start | bytes 442376 | tf_op jit(solution)/shard_map/weight_grads/ppermute | solution.py:84
  209.5 13.7 %collective-permute-start.43 = (bf16[96,768]{1,0:T(8,128)(2,1)S(1)}, bf16[96,768]{1,0:T(8,128)(2,1)S(1)}, u32[]{:S(2)}, u32[]{:S(2)}) collective-permute-start(bf16[96,768]{1,0:T(8,128)(2,1)S(1)} %get-tuple-element.216), channel_id=1, source_target_pairs={{0,8},{1,9},{2,10},{3,11},{4,12},{5,13},{6,14},{7,15},{8,0},{9,1},... | collective-permute-start | bytes 442376 | tf_op jit(solution)/shard_map/weight_grads/ppermute | solution.py:84
  223.6 21.9 %collective-permute-start.49 = (bf16[8,24,2304]{2,1,0:T(8,128)(2,1)S(1)}, bf16[8,24,2304]{2,1,0:T(8,128)(2,1)}, u32[]{:S(2)}, u32[]{:S(2)}) collective-permute-start(bf16[8,24,2304]{2,1,0:T(8,128)(2,1)S(1)} %copy-done.27), channel_id=1, source_target_pairs={{0,2},{1,3},{2,0},{3,1},{4,6},{5,7},{6,4},{7,5},{8,10},{9,11},{10,... | collective-permute-start | bytes 2654216 | tf_op jit(solution)/shard_map/weight_grads/ppermute | solution.py:84
  224.9 20.6 %collective-permute-start.48 = (bf16[8,24,1536]{2,1,0:T(8,128)(2,1)S(1)}, bf16[8,24,1536]{2,1,0:T(8,128)(2,1)S(1)}, u32[]{:S(2)}, u32[]{:S(2)}) collective-permute-start(bf16[8,24,1536]{2,1,0:T(8,128)(2,1)S(1)} %copy-done.29), channel_id=1, source_target_pairs={{0,16},{1,17},{2,18},{3,19},{4,20},{5,21},{6,22},{7,23},{8,24},{9,... | collective-permute-start | bytes 1769480 | tf_op jit(solution)/shard_map/weight_grads/ppermute | solution.py:84
  226.4 9.7 %collective-permute-start.47 = (bf16[3,64,512]{2,1,0:T(8,128)(2,1)S(1)}, bf16[3,64,512]{2,1,0:T(8,128)(2,1)S(1)}, u32[]{:S(2)}, u32[]{:S(2)}) collective-permute-start(bf16[3,64,512]{2,1,0:T(8,128)(2,1)S(1)} %get-tuple-element.210), channel_id=1, source_target_pairs={{0,12},{1,13},{2,14},{3,15},{4,8},{5,9},{6,10},{7,11},{8,4},{9,5},... | collective-permute-start | bytes 589832 | tf_op jit(solution)/shard_map/mixing_back/ppermute | solution.py:84
  228.6 16.9 %collective-permute-start.46 = (bf16[3,64,512]{2,1,0:T(8,128)(2,1)S(1)}, bf16[3,64,512]{2,1,0:T(8,128)(2,1)S(1)}, u32[]{:S(2)}, u32[]{:S(2)}) collective-permute-start(bf16[3,64,512]{2,1,0:T(8,128)(2,1)S(1)} %get-tuple-element.211), channel_id=1, source_target_pairs={{0,8},{1,9},{2,10},{3,11},{4,12},{5,13},{6,14},{7,15},{8,0},{9,1},... | collective-permute-start | bytes 589832 | tf_op jit(solution)/shard_map/mixing_back/ppermute | solution.py:84
  229.3 16.2 %collective-permute-start.45 = (bf16[3,64,512]{2,1,0:T(8,128)(2,1)S(1)}, bf16[3,64,512]{2,1,0:T(8,128)(2,1)S(1)}, u32[]{:S(2)}, u32[]{:S(2)}) collective-permute-start(bf16[3,64,512]{2,1,0:T(8,128)(2,1)S(1)} %get-tuple-element.212), channel_id=1, source_target_pairs={{0,4},{1,5},{2,6},{3,7},{4,0},{5,1},{6,2},{7,3},{8,12},{9,13},{10,... | collective-permute-start | bytes 589832 | tf_op jit(solution)/shard_map/mixing_back/ppermute | solution.py:84
  248.6 25.5 %all-to-all-start.3 = ((bf16[4,3,64,512]{3,2,1,0:T(8,128)(2,1)}), bf16[4,3,64,512]{3,2,1,0:T(8,128)(2,1)}, u32[]{:S(2)}, u32[]{:S(2)}) async-start(bf16[4,3,64,512]{3,2,1,0:T(8,128)(2,1)} %fusion), calls=%async_computation.3 | async-start | bytes 1572864 | tf_op jit(solution)/shard_map/mixing_back/all_to_all | solution.py:90
  254.5 19.7 %collective-permute-start.55 = (bf16[4,24,2304]{2,1,0:T(8,128)(2,1)S(1)}, bf16[4,24,2304]{2,1,0:T(8,128)(2,1)}, u32[]{:S(2)}, u32[]{:S(2)}) collective-permute-start(bf16[4,24,2304]{2,1,0:T(8,128)(2,1)S(1)} %add_convert_fusion.10), channel_id=1, source_target_pairs={{0,16},{1,17},{2,18},{3,19},{4,20},{5,21},{6,22},{7,23},{8,24},{9,... | collective-permute-start | bytes 1327112 | tf_op jit(solution)/shard_map/weight_grads/ppermute | solution.py:84
  255.2 18.2 %collective-permute-start.54 = (bf16[4,24,1536]{2,1,0:T(8,128)(2,1)S(1)}, bf16[4,24,1536]{2,1,0:T(8,128)(2,1)S(1)}, u32[]{:S(2)}, u32[]{:S(2)}) collective-permute-start(bf16[4,24,1536]{2,1,0:T(8,128)(2,1)S(1)} %add_convert_fusion.13), channel_id=1, source_target_pairs={{0,2},{1,3},{2,0},{3,1},{4,6},{5,7},{6,4},{7,5},{8,10},{9,11},{10,... | collective-permute-start | bytes 884744 | tf_op jit(solution)/shard_map/weight_grads/ppermute | solution.py:84
  256.5 16.9 %collective-permute-start.51 = (bf16[4,24,768]{2,1,0:T(8,128)(2,1)S(1)}, bf16[4,24,768]{2,1,0:T(8,128)(2,1)S(1)}, u32[]{:S(2)}, u32[]{:S(2)}) collective-permute-start(bf16[4,24,768]{2,1,0:T(8,128)(2,1)S(1)} %get-tuple-element.178), channel_id=1, source_target_pairs={{0,16},{1,17},{2,18},{3,19},{4,20},{5,21},{6,22},{7,23},{8,24},{9,... | collective-permute-start | bytes 442376 | tf_op jit(solution)/shard_map/value_grads/ppermute | solution.py:84
  257.1 16.3 %collective-permute-start.52 = (bf16[4,24,768]{2,1,0:T(8,128)(2,1)S(1)}, bf16[4,24,768]{2,1,0:T(8,128)(2,1)S(1)}, u32[]{:S(2)}, u32[]{:S(2)}) collective-permute-start(bf16[4,24,768]{2,1,0:T(8,128)(2,1)S(1)} %get-tuple-element.179), channel_id=1, source_target_pairs={{0,2},{1,3},{2,0},{3,1},{4,6},{5,7},{6,4},{7,5},{8,10},{9,11},{10,... | collective-permute-start | bytes 442376 | tf_op jit(solution)/shard_map/value_grads/ppermute | solution.py:84
  258.7 14.7 %collective-permute-start.53 = (bf16[4,24,768]{2,1,0:T(8,128)(2,1)S(1)}, bf16[4,24,768]{2,1,0:T(8,128)(2,1)S(1)}, u32[]{:S(2)}, u32[]{:S(2)}) collective-permute-start(bf16[4,24,768]{2,1,0:T(8,128)(2,1)S(1)} %get-tuple-element.180), channel_id=1, source_target_pairs={{0,18},{1,19},{2,16},{3,17},{4,22},{5,23},{6,20},{7,21},{8,26},{9,... | collective-permute-start | bytes 442376 | tf_op jit(solution)/shard_map/value_grads/ppermute | solution.py:84
  278.6 13.5 %collective-permute-start.58 = (bf16[24,4608]{1,0:T(8,128)(2,1)S(1)}, bf16[24,4608]{1,0:T(8,128)(2,1)S(1)}, u32[]{:S(2)}, u32[]{:S(2)}) collective-permute-start(bf16[24,4608]{1,0:T(8,128)(2,1)S(1)} %get-tuple-element.208), channel_id=1, source_target_pairs={{0,12},{1,13},{2,14},{3,15},{4,8},{5,9},{6,10},{7,11},{8,4},{9,5},... | collective-permute-start | bytes 663560 | tf_op jit(solution)/shard_map/weight_grads/ppermute | solution.py:84
  280.9 18.9 %collective-permute-start.57 = (bf16[24,4608]{1,0:T(8,128)(2,1)S(1)}, bf16[24,4608]{1,0:T(8,128)(2,1)S(1)}, u32[]{:S(2)}, u32[]{:S(2)}) collective-permute-start(bf16[24,4608]{1,0:T(8,128)(2,1)S(1)} %get-tuple-element.209), channel_id=1, source_target_pairs={{0,8},{1,9},{2,10},{3,11},{4,12},{5,13},{6,14},{7,15},{8,0},{9,1},... | collective-permute-start | bytes 663560 | tf_op jit(solution)/shard_map/weight_grads/ppermute | solution.py:84
  (67 other events, 632.5 us)

commit v6 on v5

--- a/solution.py
+++ b/solution.py
@@ -15,6 +15,7 @@
 EPS = 1e-06
 SHARES = {
     "mix_rows": 50000000000,
+    "finish": 768,
     "make_values": 20000000000,
     "mix_values": 50000000000,
     "prepare_weights": 120000000000,
@@ -599,6 +600,40 @@
         cost_estimate=share("make_tokens_grad"),
         name="make_tokens_grad",
     )(total, weight, tokens, residual_grad)
+
+
+def finish_kernel(*refs):
+    parts, (gain_one, gain_two, value_weight, up_weight) = refs[:GROUPS], refs[GROUPS : GROUPS + 4]
+    value_out, up_out, out_out, one_out, two_out = refs[GROUPS + 4 :]
+    total = parts[0][...].astype(F32)
+    for part in parts[1:]:
+        total = total + part[...].astype(F32)
+    width = value_out.shape[1]
+    value_sum, up_sum = total[:, :width], total[:, width:-width]
+    value_out[...] = gain_one[...] * value_sum
+    up_out[...] = gain_two[...] * up_sum
+    out_out[...] = total[:, -width:]
+    one_out[...] = jnp.sum(value_sum * value_weight[...].astype(F32), axis=1, keepdims=True)
+    two_out[...] = jnp.sum(up_sum * up_weight[...].astype(F32), axis=1, keepdims=True)
+
+
+def finish(parts, gain_one, gain_two, value_weight, up_weight):
+    rows, width = value_weight.shape
+    return pl.pallas_call(
+        finish_kernel,
+        out_shape=[
+            shape((rows, width), F32),
+            shape(up_weight.shape, F32),
+            shape((rows, width), F32),
+            shape((rows, 1), F32),
+            shape((rows, 1), F32),
+        ],
+        in_specs=[vmem()] * (GROUPS + 4),
+        out_specs=[vmem()] * 5,
+        compiler_params=params(16),
+        cost_estimate=share("finish"),
+        name="finish",
+    )(*parts, gain_one, gain_two, value_weight, up_weight)
 
 
 def add_kernel(*refs):
@@ -846,8 +881,11 @@
             own = add_all([own[0]] + list(parts))
         with jax.named_scope("weight_grads"):
             last = jnp.concatenate([own, add_low(a_own, a_other), add_low(b_own, b_other)], axis=2)
-            last = sum_z(lay, last)
-            value_sum, up_sum, out_wgrad = last[:, :width], last[:, width:-width], last[:, -width:]
+            last = [last[0]] + [lay.swap(last[k], z=k) for k in range(1, GROUPS)]
+            value_wgrad, up_grad, out_wgrad, gain_one_grad, gain_two_grad = finish(
+                last, gain_one, gain_two, value_weight, up_weight
+            )
+            gain_one_grad, gain_two_grad = gain_one_grad[:, 0], gain_two_grad[:, 0]
             down_grad = c_sum[0].astype(F32)
             for part in c_rest:
                 down_grad = down_grad + part.astype(F32)
@@ -873,9 +911,9 @@
             up_sum, down_grad, out_wgrad = (scatter_sum(grad) for grad in grads)
     with jax.named_scope("value_grads"):
         tokens_grad = make_tokens_grad(total, w_value, tokens, residual_grad)
+    if not small:
         value_wgrad = gain_one * value_sum
         gain_one_grad = jnp.sum(value_sum * value_weight.astype(F32), axis=1)
-    with jax.named_scope("weight_grads"):
         up_grad = gain_two * up_sum
         gain_two_grad = jnp.sum(up_sum * up_weight.astype(F32), axis=1)
     return (

time: 304 us -> 302 us (level)
  waiting for transfers between devices: 120 us -> 116 us
    ppermute x59, waiting for transfers between devices: 105 us -> 97.9 us  [swap(): lax.ppermute(array, AXES, [(i, i ^ mask) for i in range(self.devices)])]
    ppermute x59, starting transfers between devices: 61.3 us -> 57.8 us  [swap(): lax.ppermute(array, AXES, [(i, i ^ mask) for i in range(self.devices)])]
    all_to_all x4, waiting for transfers between devices: 14.7 us -> 17.8 us  [across_z(): return lax.all_to_all(array, 'seq', 0, 0, axis_index_groups=lines)]
    unnamed x107 -> x91, local copies, waits for them, and re-layouts: 11.1 us -> 10.4 us
  transfers between devices with their start and end apart: 63 -> 63, of which waited for: 30 -> 24; matrix products, arithmetic and copies ran while one was open for 10% -> 11% of each run, Pallas kernels for 7% -> 7%
where the time goes in v6:
time: 302 us; the launch traced here: 300 us
  waiting for transfers between devices  116 us (38%)
  starting transfers between devices  77.4 us (26%)
  Pallas kernels  53.3 us (18%)
  other arithmetic  41.4 us (14%)
  local copies, waits for them, and re-layouts  11 us (4%)
    ppermute x59, waiting for transfers between devices, swap(): lax.ppermute(array, AXES, [(i, i ^ mask) for i in range(self.devices)])  97.9 us
    ppermute x59, starting transfers between devices, swap(): lax.ppermute(array, AXES, [(i, i ^ mask) for i in range(self.devices)])  57.8 us
    pallas_call x1, Pallas kernels, middle(): pl.pallas_call(functools.partial(middle_kernel, positions=lay.positions,...  30.4 us
    convert_element_type x13, other arithmetic, add_low(): return (left.astype(F32) + right.astype(F32)).astype(BF16)  20.7 us
    all_to_all x4, starting transfers between devices, across_z(): return lax.all_to_all(array, 'seq', 0, 0, axis_index_groups=lines)  19.6 us
    all_to_all x4, waiting for transfers between devices, across_z(): return lax.all_to_all(array, 'seq', 0, 0, axis_index_groups=lines)  17.8 us
    unnamed x91, local copies, waits for them, and re-layouts  10.4 us
  transfers between devices with their start and end apart: 63, of which 24 were waited for; matrix products, arithmetic and copies ran while one was open for 11% of the time, Pallas kernels for 7%

profile of v6, /device:TPU:0, one launch (start us, length us, event | category | flops | bytes accessed | tf_op | source)
XLA Modules:
  0.0 300.3 jit_solution(766410796598406681)
XLA Ops:
  5.6 3.1 %collective-permute-start = (bf16[6,24,768]{2,1,0:T(8,128)(2,1)S(1)}, bf16[6,24,768]{2,1,0:T(8,128)(2,1)S(1)}, u32[]{:S(2)}, u32[]{:S(2)}) collective-permute-start(bf16[6,24,768]{2,1,0:T(8,128)(2,1)S(1)} %pad_maximum_fusion.9), channel_id=1, source_target_pairs={{0,4},{1,5},{2,6},{3,7},{4,0},{5,1},{6,2},{7,3},{8,12},{9,13},{10,... | collective-permute-start | bytes 663560 | tf_op jit(solution)/shard_map/round_one/ppermute | solution.py:85
  8.7 2.6 collective-permute-start.1
  12.8 1.9 mix_rows.1
  14.7 3.4 %collective-permute-done = bf16[6,24,768]{2,1,0:T(8,128)(2,1)S(1)} collective-permute-done((bf16[6,24,768]{2,1,0:T(8,128)(2,1)S(1)}, bf16[6,24,768]{2,1,0:T(8,128)(2,1)S(1)}, u32[]{:S(2)}, u32[]{:S(2)}) %collective-permute-start) | collective-permute-done | bytes 221216 | tf_op jit(solution)/shard_map/round_one/ppermute | solution.py:85
  18.1 9.3 %collective-permute-done.1 = bf16[6,24,768]{2,1,0:T(8,128)(2,1)S(1)} collective-permute-done((bf16[6,24,768]{2,1,0:T(8,128)(2,1)S(1)}, bf16[6,24,768]{2,1,0:T(8,128)(2,1)S(1)}, u32[]{:S(2)}, u32[]{:S(2)}) %collective-permute-start.1) | collective-permute-done | bytes 221216 | tf_op jit(solution)/shard_map/round_one/ppermute | solution.py:85
  32.1 2.4 collective-permute-start.5
  34.5 6.2 %all-to-all-start = ((bf16[4,3,32,1024]{3,2,1,0:T(8,128)(2,1)}), bf16[4,3,32,1024]{3,2,1,0:T(8,128)(2,1)S(1)}, u32[]{:S(2)}, u32[]{:S(2)}) async-start(bf16[4,3,32,1024]{3,2,1,0:T(8,128)(2,1)} %mix_rows.1), calls=%async_computation | async-start | bytes 1572864 | tf_op jit(solution)/shard_map/round_two/all_to_all | solution.py:91
  40.7 2.9 collective-permute-done.3
  43.7 1.9 pad_maximum_fusion.5
  47.1 2.0 pad_maximum_fusion.2
  50.6 7.6 %all-to-all-done.refs_4_ = bf16[4,3,32,1024]{3,2,1,0:T(8,128)(2,1)S(1)} async-done(((bf16[4,3,32,1024]{3,2,1,0:T(8,128)(2,1)}), bf16[4,3,32,1024]{3,2,1,0:T(8,128)(2,1)S(1)}, u32[]{:S(2)}, u32[]{:S(2)}) %all-to-all-start) | async-done | bytes 786464 | tf_op jit(solution)/shard_map/round_two/all_to_all | solution.py:91
  58.2 2.0 make_values.1
  61.8 1.9 collective-permute-start.9
  64.3 6.9 %collective-permute-done.12 = bf16[8,3,24,768]{3,2,1,0:T(8,128)(2,1)} collective-permute-done((bf16[8,3,24,768]{3,2,1,0:T(8,128)(2,1)}, bf16[8,3,24,768]{3,2,1,0:T(8,128)(2,1)}, u32[]{:S(2)}, u32[]{:S(2)}) %collective-permute-start.12) | collective-permute-done | bytes 884768 | tf_op jit(solution)/shard_map/round_two/ppermute | solution.py:85
  71.2 2.3 collective-permute-done.10.refs_2_
  75.8 3.3 %collective-permute-start.16 = (bf16[96,768]{1,0:T(8,128)(2,1)S(1)}, bf16[96,768]{1,0:T(8,128)(2,1)S(1)}, u32[]{:S(2)}, u32[]{:S(2)}) collective-permute-start(bf16[96,768]{1,0:T(8,128)(2,1)S(1)} %copy-done.9), channel_id=1, source_target_pairs={{0,4},{1,5},{2,6},{3,7},{4,0},{5,1},{6,2},{7,3},{8,12},{9,13},{10,... | collective-permute-start | bytes 442376 | tf_op jit(solution)/shard_map/round_four/ppermute | solution.py:85
  81.4 2.7 pad_maximum_fusion.refs_0_
  84.1 2.3 pad_maximum_fusion.1.refs_2_
  86.3 6.5 %collective-permute-done.17.refs_2_ = bf16[96,768]{1,0:T(8,128)(2,1)S(1)} collective-permute-done((bf16[96,768]{1,0:T(8,128)(2,1)S(1)}, bf16[96,768]{1,0:T(8,128)(2,1)S(1)}, u32[]{:S(2)}, u32[]{:S(2)}) %collective-permute-start.17) | collective-permute-done | bytes 147488 | tf_op jit(solution)/shard_map/round_four/ppermute | solution.py:85
  95.1 2.8 collective-permute-done.20.refs_3_
  97.9 2.7 mix_values.1
  107.0 5.4 %all-to-all-start.1 = ((bf16[4,3,64,512]{3,2,1,0:T(8,128)(2,1)}), bf16[4,3,64,512]{3,2,1,0:T(8,128)(2,1)S(1)}, u32[]{:S(2)}, u32[]{:S(2)}) async-start(bf16[4,3,64,512]{3,2,1,0:T(8,128)(2,1)} %get-tuple-element.133), calls=%async_computation.1 | async-start | bytes 1572864 | tf_op jit(solution)/shard_map/round_five/all_to_all | solution.py:91
  112.7 7.2 %collective-permute-done.28.refs_10_ = bf16[8,48,768]{2,1,0:T(8,128)(2,1)} collective-permute-done((bf16[8,48,768]{2,1,0:T(8,128)(2,1)S(1)}, bf16[8,48,768]{2,1,0:T(8,128)(2,1)}, u32[]{:S(2)}, u32[]{:S(2)}) %collective-permute-start.28) | collective-permute-done | bytes 589856 | tf_op jit(solution)/shard_map/round_five/ppermute | solution.py:85
  121.1 5.6 %prepare_weights.1.refs_3_.refs_4_ = bf16[768,3840]{1,0:T(8,128)(2,1)S(1)} custom-call(s32[8]{0:T(128)S(1)} %stack.44.me, bf16[16,3,24,768]{3,2,1,0:T(8,128)(2,1)} %pad_maximum_fusion.refs_0_, bf16[16,3,24,768]{3,2,1,0:T(8,128)(2,1)} %collective-permute-done.21.refs_1_, bf16[16,2,24,768]{3,2,1,0:T(8,128)(2,1)} %pad_maximum_fusion.1.refs_2_, ...), custom_call_target="tpu_custom_call" | custom-call | flops 120000004096 | bytes 1 | tf_op jit(solution)/shard_map/round_five/prepare_weights/pallas_call | solution.py:294
  126.7 2.5 copy-done.13
  130.8 2.4 all-to-all-done.1.refs_0_
  134.1 30.4 %middle.1 = (bf16[512,768]{1,0:T(8,128)(2,1)}, f32[512,768]{1,0:T(8,128)}, bf16[4,3,64,512]{3,2,1,0:T(8,128)(2,1)}, bf16[16,24,1536]{2,1,0:T(8,128)(2,1)}, bf16[...) custom-call(s32[8]{0:T(128)} %copy-done.4, ...), custom_call_target="tpu_custom_call" | custom-call | flops 49999998976 | bytes 1 | tf_op jit(solution)/shard_map/feed_forward/middle/pallas_call | solution.py:443
  165.6 3.7 %all-to-all-start.2 = ((bf16[4,3,64,512]{3,2,1,0:T(8,128)(2,1)}), bf16[4,3,64,512]{3,2,1,0:T(8,128)(2,1)S(1)}, u32[]{:S(2)}, u32[]{:S(2)}) async-start(bf16[4,3,64,512]{3,2,1,0:T(8,128)(2,1)} %get-tuple-element.146), calls=%async_computation.2 | async-start | bytes 1572864 | tf_op jit(solution)/shard_map/feed_forward/all_to_all | solution.py:91
  169.4 2.4 add_convert_fusion.3
  176.1 2.7 add_convert_fusion.2
  178.8 3.1 %add_convert_fusion = (bf16[8,24,2304]{2,1,0:T(8,128)(2,1)}, bf16[8,24,2304]{2,1,0:T(8,128)(2,1)}) fusion(bf16[16,24,2304]{2,1,0:T(8,128)(2,1)} %collective-permute-done.36, bf16[16,24,2304]{2,1,0:T(8,128)(2,1)S(1)} %copy-done.24), kind=kLoop, calls=%fused_computation.1 | loop fusion | flops 3538944 | bytes 5308416 | tf_op jit(solution)/shard_map/weight_grads/convert_element_type | solution.py:95
  181.9 7.9 %all-to-all-done.2.refs_0_ = bf16[4,3,64,512]{3,2,1,0:T(8,128)(2,1)S(1)} async-done(((bf16[4,3,64,512]{3,2,1,0:T(8,128)(2,1)}), bf16[4,3,64,512]{3,2,1,0:T(8,128)(2,1)S(1)}, u32[]{:S(2)}, u32[]{:S(2)}) %all-to-all-start.2) | async-done | bytes 786464 | tf_op jit(solution)/shard_map/feed_forward/all_to_all | solution.py:91
  194.5 4.8 %mix_back.1 = (bf16[2,4,3,64,512]{4,3,2,1,0:T(8,128)(2,1)S(1)}, bf16[2,4,3,64,512]{4,3,2,1,0:T(8,128)(2,1)S(1)}, bf16[2,4,3,64,512]{4,3,2,1,0:T(8,128)(2,1)S(1)}) custom-call(s32[8]{0:T(128)S(1)} %copy-done.5, bf16[4,3,64,512]{3,2,1,0:T(8,128)(2,1)S(1)} %all-to-all-done.2.refs_0_, bf16[3,256,1024]{2,1,0:T(8,128)(2,1)} %copy-done.1, ...), custom_call_target="tpu_custom_call" | custom-call | flops 768 | bytes 1 | tf_op jit(solution)/shard_map/mixing_back/mix_back/pallas_call | solution.py:521
  199.2 2.1 collective-permute-done.37
  202.5 2.2 collective-permute-done.39.refs_1_
  212.5 2.9 collective-permute-done.42
  215.4 8.2 %collective-permute-done.43 = bf16[96,768]{1,0:T(8,128)(2,1)S(1)} collective-permute-done((bf16[96,768]{1,0:T(8,128)(2,1)S(1)}, bf16[96,768]{1,0:T(8,128)(2,1)S(1)}, u32[]{:S(2)}, u32[]{:S(2)}) %collective-permute-start.43) | collective-permute-done | bytes 147488 | tf_op jit(solution)/shard_map/weight_grads/ppermute | solution.py:85
  231.1 3.8 %collective-permute-done.45.refs_1_ = bf16[3,64,512]{2,1,0:T(8,128)(2,1)S(1)} collective-permute-done((bf16[3,64,512]{2,1,0:T(8,128)(2,1)S(1)}, bf16[3,64,512]{2,1,0:T(8,128)(2,1)S(1)}, u32[]{:S(2)}, u32[]{:S(2)}) %collective-permute-start.45) | collective-permute-done | bytes 196640 | tf_op jit(solution)/shard_map/mixing_back/ppermute | solution.py:85
  234.9 9.6 %collective-permute-done.46.refs_2_ = bf16[3,64,512]{2,1,0:T(8,128)(2,1)S(1)} collective-permute-done((bf16[3,64,512]{2,1,0:T(8,128)(2,1)S(1)}, bf16[3,64,512]{2,1,0:T(8,128)(2,1)S(1)}, u32[]{:S(2)}, u32[]{:S(2)}) %collective-permute-start.46) | collective-permute-done | bytes 196640 | tf_op jit(solution)/shard_map/mixing_back/ppermute | solution.py:85
  246.0 1.9 value_grads.1
  249.1 4.3 %all-to-all-start.3 = ((bf16[4,3,64,512]{3,2,1,0:T(8,128)(2,1)}), bf16[4,3,64,512]{3,2,1,0:T(8,128)(2,1)}, u32[]{:S(2)}, u32[]{:S(2)}) async-start(bf16[4,3,64,512]{3,2,1,0:T(8,128)(2,1)} %fusion), calls=%async_computation.3 | async-start | bytes 1572864 | tf_op jit(solution)/shard_map/mixing_back/all_to_all | solution.py:91
  253.6 2.0 add_convert_fusion.10
  261.6 1.8 fusion.2
  263.5 11.3 %collective-permute-done.51.refs_1_ = bf16[4,24,768]{2,1,0:T(8,128)(2,1)S(1)} collective-permute-done((bf16[4,24,768]{2,1,0:T(8,128)(2,1)S(1)}, bf16[4,24,768]{2,1,0:T(8,128)(2,1)S(1)}, u32[]{:S(2)}, u32[]{:S(2)}) %collective-permute-start.51) | collective-permute-done | bytes 147488 | tf_op jit(solution)/shard_map/value_grads/ppermute | solution.py:85
  279.3 2.4 collective-permute-start.57
  282.0 2.2 make_tokens_grad.1
  284.3 2.5 bitcast_convert_fusion
  288.5 9.6 %collective-permute-done.57.refs_2_ = bf16[24,4608]{1,0:T(8,128)(2,1)S(1)} collective-permute-done((bf16[24,4608]{1,0:T(8,128)(2,1)S(1)}, bf16[24,4608]{1,0:T(8,128)(2,1)S(1)}, u32[]{:S(2)}, u32[]{:S(2)}) %collective-permute-start.57) | collective-permute-done | bytes 221216 | tf_op jit(solution)/shard_map/weight_grads/ppermute | solution.py:85
  (234 shorter events, 77.5 us)
Async XLA Ops:
  5.6 12.5 %collective-permute-start = (bf16[6,24,768]{2,1,0:T(8,128)(2,1)S(1)}, bf16[6,24,768]{2,1,0:T(8,128)(2,1)S(1)}, u32[]{:S(2)}, u32[]{:S(2)}) collective-permute-start(bf16[6,24,768]{2,1,0:T(8,128)(2,1)S(1)} %pad_maximum_fusion.9), channel_id=1, source_target_pairs={{0,4},{1,5},{2,6},{3,7},{4,0},{5,1},{6,2},{7,3},{8,12},{9,13},{10,... | collective-permute-start | bytes 663560 | tf_op jit(solution)/shard_map/round_one/ppermute | solution.py:85
  8.7 18.7 %collective-permute-start.1 = (bf16[6,24,768]{2,1,0:T(8,128)(2,1)S(1)}, bf16[6,24,768]{2,1,0:T(8,128)(2,1)S(1)}, u32[]{:S(2)}, u32[]{:S(2)}) collective-permute-start(bf16[6,24,768]{2,1,0:T(8,128)(2,1)S(1)} %pad_maximum_fusion.9), channel_id=1, source_target_pairs={{0,8},{1,9},{2,10},{3,11},{4,12},{5,13},{6,14},{7,15},{8,0},{9,1},... | collective-permute-start | bytes 663560 | tf_op jit(solution)/shard_map/round_one/ppermute | solution.py:85
  11.3 16.1 %collective-permute-start.2 = (bf16[6,24,768]{2,1,0:T(8,128)(2,1)S(1)}, bf16[6,24,768]{2,1,0:T(8,128)(2,1)S(1)}, u32[]{:S(2)}, u32[]{:S(2)}) collective-permute-start(bf16[6,24,768]{2,1,0:T(8,128)(2,1)S(1)} %pad_maximum_fusion.9), channel_id=1, source_target_pairs={{0,12},{1,13},{2,14},{3,15},{4,8},{5,9},{6,10},{7,11},{8,4},{9,5},... | collective-permute-start | bytes 663560 | tf_op jit(solution)/shard_map/round_one/ppermute | solution.py:85
  27.7 15.8 %collective-permute-start.6 = (bf16[4,3,24,768]{3,2,1,0:T(8,128)(2,1)S(1)}, bf16[4,3,24,768]{3,2,1,0:T(8,128)(2,1)}, u32[]{:S(2)}, u32[]{:S(2)}) collective-permute-start(bf16[4,3,24,768]{3,2,1,0:T(8,128)(2,1)S(1)} %slice.232), channel_id=1, source_target_pairs={{0,16},{1,17},{2,18},{3,19},{4,20},{5,21},{6,22},{7,23},{8,24},{9,... | collective-permute-start | bytes 1327112 | tf_op jit(solution)/shard_map/round_two/ppermute | solution.py:85
  29.3 14.2 %collective-permute-start.7 = (bf16[4,2,24,768]{3,2,1,0:T(8,128)(2,1)S(1)}, bf16[4,2,24,768]{3,2,1,0:T(8,128)(2,1)}, u32[]{:S(2)}, u32[]{:S(2)}) collective-permute-start(bf16[4,2,24,768]{3,2,1,0:T(8,128)(2,1)S(1)} %pad_maximum_fusion.8), channel_id=1, source_target_pairs={{0,2},{1,3},{2,0},{3,1},{4,6},{5,7},{6,4},{7,5},{8,10},{9,11},{10,... | collective-permute-start | bytes 884744 | tf_op jit(solution)/shard_map/round_two/ppermute | solution.py:85
  31.0 12.6 %collective-permute-start.3 = (bf16[4,24,768]{2,1,0:T(8,128)(2,1)S(1)}, bf16[4,24,768]{2,1,0:T(8,128)(2,1)S(1)}, u32[]{:S(2)}, u32[]{:S(2)}) collective-permute-start(bf16[4,24,768]{2,1,0:T(8,128)(2,1)S(1)} %pad_maximum_fusion.11), channel_id=1, source_target_pairs={{0,16},{1,17},{2,18},{3,19},{4,20},{5,21},{6,22},{7,23},{8,24},{9,... | collective-permute-start | bytes 442376 | tf_op jit(solution)/shard_map/round_two/ppermute | solution.py:85
  31.5 12.0 %collective-permute-start.4 = (bf16[4,24,768]{2,1,0:T(8,128)(2,1)S(1)}, bf16[4,24,768]{2,1,0:T(8,128)(2,1)S(1)}, u32[]{:S(2)}, u32[]{:S(2)}) collective-permute-start(bf16[4,24,768]{2,1,0:T(8,128)(2,1)S(1)} %pad_maximum_fusion.11), channel_id=1, source_target_pairs={{0,2},{1,3},{2,0},{3,1},{4,6},{5,7},{6,4},{7,5},{8,10},{9,11},{10,... | collective-permute-start | bytes 442376 | tf_op jit(solution)/shard_map/round_two/ppermute | solution.py:85
  32.1 11.5 %collective-permute-start.5 = (bf16[4,24,768]{2,1,0:T(8,128)(2,1)S(1)}, bf16[4,24,768]{2,1,0:T(8,128)(2,1)S(1)}, u32[]{:S(2)}, u32[]{:S(2)}) collective-permute-start(bf16[4,24,768]{2,1,0:T(8,128)(2,1)S(1)} %pad_maximum_fusion.11), channel_id=1, source_target_pairs={{0,18},{1,19},{2,16},{3,17},{4,22},{5,23},{6,20},{7,21},{8,26},{9,... | collective-permute-start | bytes 442376 | tf_op jit(solution)/shard_map/round_two/ppermute | solution.py:85
  34.5 23.7 %all-to-all-start = ((bf16[4,3,32,1024]{3,2,1,0:T(8,128)(2,1)}), bf16[4,3,32,1024]{3,2,1,0:T(8,128)(2,1)S(1)}, u32[]{:S(2)}, u32[]{:S(2)}) async-start(bf16[4,3,32,1024]{3,2,1,0:T(8,128)(2,1)} %mix_rows.1), calls=%async_computation | async-start | bytes 1572864 | tf_op jit(solution)/shard_map/round_two/all_to_all | solution.py:91
  45.6 18.1 %collective-permute-start.13 = (bf16[8,2,24,768]{3,2,1,0:T(8,128)(2,1)}, bf16[8,2,24,768]{3,2,1,0:T(8,128)(2,1)}, u32[]{:S(2)}, u32[]{:S(2)}) collective-permute-start(bf16[8,2,24,768]{3,2,1,0:T(8,128)(2,1)} %pad_maximum_fusion.5), channel_id=1, source_target_pairs={{0,16},{1,17},{2,18},{3,19},{4,20},{5,21},{6,22},{7,23},{8,24},{9,... | collective-permute-start | bytes 1769480 | tf_op jit(solution)/shard_map/round_two/ppermute | solution.py:85
  49.1 22.0 %collective-permute-start.12 = (bf16[8,3,24,768]{3,2,1,0:T(8,128)(2,1)}, bf16[8,3,24,768]{3,2,1,0:T(8,128)(2,1)}, u32[]{:S(2)}, u32[]{:S(2)}) collective-permute-start(bf16[8,3,24,768]{3,2,1,0:T(8,128)(2,1)} %pad_maximum_fusion.2), channel_id=1, source_target_pairs={{0,2},{1,3},{2,0},{3,1},{4,6},{5,7},{6,4},{7,5},{8,10},{9,11},{10,... | collective-permute-start | bytes 2654216 | tf_op jit(solution)/shard_map/round_two/ppermute | solution.py:85
  60.2 13.3 %collective-permute-start.10 = (bf16[3,64,512]{2,1,0:T(8,128)(2,1)S(1)}, bf16[3,64,512]{2,1,0:T(8,128)(2,1)S(1)}, u32[]{:S(2)}, u32[]{:S(2)}) collective-permute-start(bf16[3,64,512]{2,1,0:T(8,128)(2,1)S(1)} %get-tuple-element.122), channel_id=1, source_target_pairs={{0,8},{1,9},{2,10},{3,11},{4,12},{5,13},{6,14},{7,15},{8,0},{9,1},... | collective-permute-start | bytes 589832 | tf_op jit(solution)/shard_map/round_three/ppermute | solution.py:85
  60.3 13.2 %collective-permute-start.11 = (bf16[3,64,512]{2,1,0:T(8,128)(2,1)S(1)}, bf16[3,64,512]{2,1,0:T(8,128)(2,1)S(1)}, u32[]{:S(2)}, u32[]{:S(2)}) collective-permute-start(bf16[3,64,512]{2,1,0:T(8,128)(2,1)S(1)} %get-tuple-element.123), channel_id=1, source_target_pairs={{0,12},{1,13},{2,14},{3,15},{4,8},{5,9},{6,10},{7,11},{8,4},{9,5},... | collective-permute-start | bytes 589832 | tf_op jit(solution)/shard_map/round_three/ppermute | solution.py:85
  61.8 13.0 %collective-permute-start.9 = (bf16[3,64,512]{2,1,0:T(8,128)(2,1)S(1)}, bf16[3,64,512]{2,1,0:T(8,128)(2,1)S(1)}, u32[]{:S(2)}, u32[]{:S(2)}) collective-permute-start(bf16[3,64,512]{2,1,0:T(8,128)(2,1)S(1)} %get-tuple-element.121), channel_id=1, source_target_pairs={{0,4},{1,5},{2,6},{3,7},{4,0},{5,1},{6,2},{7,3},{8,12},{9,13},{10,... | collective-permute-start | bytes 589832 | tf_op jit(solution)/shard_map/round_three/ppermute | solution.py:85
  63.8 29.6 %collective-permute-start.15 = (bf16[4,3,32,1024]{3,2,1,0:T(8,128)(2,1)S(1)}, bf16[4,3,32,1024]{3,2,1,0:T(8,128)(2,1)S(1)}, u32[]{:S(2)}, u32[]{:S(2)}) collective-permute-start(bf16[4,3,32,1024]{3,2,1,0:T(8,128)(2,1)S(1)} %all-to-all-done.refs_4_), channel_id=1, source_target_pairs={{0,16},{1,17},{2,18},{3,19},{4,20},{5,21},{6,22},{7,23},{8,24},{9,... | collective-permute-start | bytes 2359304 | tf_op jit(solution)/shard_map/round_four/ppermute | solution.py:85
  74.9 18.4 %collective-permute-start.14 = (bf16[4,3,64,512]{3,2,1,0:T(8,128)(2,1)S(1)}, bf16[4,3,64,512]{3,2,1,0:T(8,128)(2,1)S(1)}, u32[]{:S(2)}, u32[]{:S(2)}) collective-permute-start(bf16[4,3,64,512]{3,2,1,0:T(8,128)(2,1)S(1)} %stack_all.2.refs_0_), channel_id=1, source_target_pairs={{0,2},{1,3},{2,0},{3,1},{4,6},{5,7},{6,4},{7,5},{8,10},{9,11},{10,... | collective-permute-start | bytes 2359304 | tf_op jit(solution)/shard_map/round_four/ppermute | solution.py:85
  75.8 10.6 %collective-permute-start.16 = (bf16[96,768]{1,0:T(8,128)(2,1)S(1)}, bf16[96,768]{1,0:T(8,128)(2,1)S(1)}, u32[]{:S(2)}, u32[]{:S(2)}) collective-permute-start(bf16[96,768]{1,0:T(8,128)(2,1)S(1)} %copy-done.9), channel_id=1, source_target_pairs={{0,4},{1,5},{2,6},{3,7},{4,0},{5,1},{6,2},{7,3},{8,12},{9,13},{10,... | collective-permute-start | bytes 442376 | tf_op jit(solution)/shard_map/round_four/ppermute | solution.py:85
  79.0 13.8 %collective-permute-start.17 = (bf16[96,768]{1,0:T(8,128)(2,1)S(1)}, bf16[96,768]{1,0:T(8,128)(2,1)S(1)}, u32[]{:S(2)}, u32[]{:S(2)}) collective-permute-start(bf16[96,768]{1,0:T(8,128)(2,1)S(1)} %copy-done.9), channel_id=1, source_target_pairs={{0,8},{1,9},{2,10},{3,11},{4,12},{5,13},{6,14},{7,15},{8,0},{9,1},... | collective-permute-start | bytes 442376 | tf_op jit(solution)/shard_map/round_four/ppermute | solution.py:85
  79.7 13.1 %collective-permute-start.18 = (bf16[96,768]{1,0:T(8,128)(2,1)S(1)}, bf16[96,768]{1,0:T(8,128)(2,1)S(1)}, u32[]{:S(2)}, u32[]{:S(2)}) collective-permute-start(bf16[96,768]{1,0:T(8,128)(2,1)S(1)} %copy-done.9), channel_id=1, source_target_pairs={{0,12},{1,13},{2,14},{3,15},{4,8},{5,9},{6,10},{7,11},{8,4},{9,5},... | collective-permute-start | bytes 442376 | tf_op jit(solution)/shard_map/round_four/ppermute | solution.py:85
  92.8 19.6 %collective-permute-start.22 = (bf16[16,2,24,768]{3,2,1,0:T(8,128)(2,1)}, bf16[16,2,24,768]{3,2,1,0:T(8,128)(2,1)}, u32[]{:S(2)}, u32[]{:S(2)}) collective-permute-start(bf16[16,2,24,768]{3,2,1,0:T(8,128)(2,1)} %pad_maximum_fusion.1.refs_2_), channel_id=1, source_target_pairs={{0,1},{1,0},{2,3},{3,2},{4,5},{5,4},{6,7},{7,6},{8,9},{9,8},{10,11... | collective-permute-start | bytes 3538952 | tf_op jit(solution)/shard_map/round_five/ppermute | solution.py:85
  92.8 28.2 %collective-permute-start.21 = (bf16[16,3,24,768]{3,2,1,0:T(8,128)(2,1)}, bf16[16,3,24,768]{3,2,1,0:T(8,128)(2,1)}, u32[]{:S(2)}, u32[]{:S(2)}) collective-permute-start(bf16[16,3,24,768]{3,2,1,0:T(8,128)(2,1)} %pad_maximum_fusion.refs_0_), channel_id=1, source_target_pairs={{0,1},{1,0},{2,3},{3,2},{4,5},{5,4},{6,7},{7,6},{8,9},{9,8},{10,11... | collective-permute-start | bytes 5308424 | tf_op jit(solution)/shard_map/round_five/ppermute | solution.py:85
  104.3 15.5 %collective-permute-start.28 = (bf16[8,48,768]{2,1,0:T(8,128)(2,1)S(1)}, bf16[8,48,768]{2,1,0:T(8,128)(2,1)}, u32[]{:S(2)}, u32[]{:S(2)}) collective-permute-start(bf16[8,48,768]{2,1,0:T(8,128)(2,1)S(1)} %pad_maximum_fusion.7.refs_9_), channel_id=1, source_target_pairs={{0,16},{1,17},{2,18},{3,19},{4,20},{5,21},{6,22},{7,23},{8,24},{9,... | collective-permute-start | bytes 1769480 | tf_op jit(solution)/shard_map/round_five/ppermute | solution.py:85
  105.9 15.2 %collective-permute-start.25 = (bf16[8,48,768]{2,1,0:T(8,128)(2,1)S(1)}, bf16[8,48,768]{2,1,0:T(8,128)(2,1)S(1)}, u32[]{:S(2)}, u32[]{:S(2)}) collective-permute-start(bf16[8,48,768]{2,1,0:T(8,128)(2,1)S(1)} %pad_maximum_fusion.6.refs_5_), channel_id=1, source_target_pairs={{0,2},{1,3},{2,0},{3,1},{4,6},{5,7},{6,4},{7,5},{8,10},{9,11},{10,... | collective-permute-start | bytes 1769480 | tf_op jit(solution)/shard_map/round_five/ppermute | solution.py:85
  107.0 22.2 %collective-permute-start.29 = (bf16[8,48,768]{2,1,0:T(8,128)(2,1)S(1)}, bf16[8,48,768]{2,1,0:T(8,128)(2,1)}, u32[]{:S(2)}, u32[]{:S(2)}) collective-permute-start(bf16[8,48,768]{2,1,0:T(8,128)(2,1)S(1)} %pad_maximum_fusion.7.refs_9_), channel_id=1, source_target_pairs={{0,1},{1,0},{2,3},{3,2},{4,5},{5,4},{6,7},{7,6},{8,9},{9,8},{10,11... | collective-permute-start | bytes 1769480 | tf_op jit(solution)/shard_map/round_five/ppermute | solution.py:85
  107.0 26.3 %all-to-all-start.1 = ((bf16[4,3,64,512]{3,2,1,0:T(8,128)(2,1)}), bf16[4,3,64,512]{3,2,1,0:T(8,128)(2,1)S(1)}, u32[]{:S(2)}, u32[]{:S(2)}) async-start(bf16[4,3,64,512]{3,2,1,0:T(8,128)(2,1)} %get-tuple-element.133), calls=%async_computation.1 | async-start | bytes 1572864 | tf_op jit(solution)/shard_map/round_five/all_to_all | solution.py:91
  112.4 16.8 %collective-permute-start.26 = (bf16[8,48,768]{2,1,0:T(8,128)(2,1)S(1)}, bf16[8,48,768]{2,1,0:T(8,128)(2,1)S(1)}, u32[]{:S(2)}, u32[]{:S(2)}) collective-permute-start(bf16[8,48,768]{2,1,0:T(8,128)(2,1)S(1)} %pad_maximum_fusion.6.refs_5_), channel_id=1, source_target_pairs={{0,1},{1,0},{2,3},{3,2},{4,5},{5,4},{6,7},{7,6},{8,9},{9,8},{10,11... | collective-permute-start | bytes 1769480 | tf_op jit(solution)/shard_map/round_five/ppermute | solution.py:85
  165.1 13.6 %collective-permute-start.36 = (bf16[16,24,2304]{2,1,0:T(8,128)(2,1)}, bf16[16,24,2304]{2,1,0:T(8,128)(2,1)}, u32[]{:S(2)}, u32[]{:S(2)}) collective-permute-start(bf16[16,24,2304]{2,1,0:T(8,128)(2,1)} %get-tuple-element.152), channel_id=1, source_target_pairs={{0,1},{1,0},{2,3},{3,2},{4,5},{5,4},{6,7},{7,6},{8,9},{9,8},{10,11... | collective-permute-start | bytes 5308424 | tf_op jit(solution)/shard_map/weight_grads/ppermute | solution.py:85
  165.2 10.8 %collective-permute-start.35 = (bf16[16,24,1536]{2,1,0:T(8,128)(2,1)}, bf16[16,24,1536]{2,1,0:T(8,128)(2,1)}, u32[]{:S(2)}, u32[]{:S(2)}) collective-permute-start(bf16[16,24,1536]{2,1,0:T(8,128)(2,1)} %get-tuple-element.150), channel_id=1, source_target_pairs={{0,1},{1,0},{2,3},{3,2},{4,5},{5,4},{6,7},{7,6},{8,9},{9,8},{10,11... | collective-permute-start | bytes 3538952 | tf_op jit(solution)/shard_map/weight_grads/ppermute | solution.py:85
  165.6 24.1 %all-to-all-start.2 = ((bf16[4,3,64,512]{3,2,1,0:T(8,128)(2,1)}), bf16[4,3,64,512]{3,2,1,0:T(8,128)(2,1)S(1)}, u32[]{:S(2)}, u32[]{:S(2)}) async-start(bf16[4,3,64,512]{3,2,1,0:T(8,128)(2,1)} %get-tuple-element.146), calls=%async_computation.2 | async-start | bytes 1572864 | tf_op jit(solution)/shard_map/feed_forward/all_to_all | solution.py:91
  171.8 17.9 %collective-permute-start.34 = (bf16[8,48,768]{2,1,0:T(8,128)(2,1)}, bf16[8,48,768]{2,1,0:T(8,128)(2,1)}, u32[]{:S(2)}, u32[]{:S(2)}) collective-permute-start(bf16[8,48,768]{2,1,0:T(8,128)(2,1)} %get-tuple-element.214), channel_id=1, source_target_pairs={{0,16},{1,17},{2,18},{3,19},{4,20},{5,21},{6,22},{7,23},{8,24},{9,... | collective-permute-start | bytes 1769480 | tf_op jit(solution)/shard_map/weight_grads/ppermute | solution.py:85
  174.5 15.3 %collective-permute-start.32 = (bf16[8,48,768]{2,1,0:T(8,128)(2,1)S(1)}, bf16[8,48,768]{2,1,0:T(8,128)(2,1)}, u32[]{:S(2)}, u32[]{:S(2)}) collective-permute-start(bf16[8,48,768]{2,1,0:T(8,128)(2,1)S(1)} %get-tuple-element.216), channel_id=1, source_target_pairs={{0,2},{1,3},{2,0},{3,1},{4,6},{5,7},{6,4},{7,5},{8,10},{9,11},{10,... | collective-permute-start | bytes 1769480 | tf_op jit(solution)/shard_map/weight_grads/ppermute | solution.py:85
  201.4 22.1 %collective-permute-start.41 = (bf16[4,3,64,512]{3,2,1,0:T(8,128)(2,1)S(1)}, bf16[4,3,64,512]{3,2,1,0:T(8,128)(2,1)S(1)}, u32[]{:S(2)}, u32[]{:S(2)}) collective-permute-start(bf16[4,3,64,512]{3,2,1,0:T(8,128)(2,1)S(1)} %slice_bitcast_fusion), channel_id=1, source_target_pairs={{0,16},{1,17},{2,18},{3,19},{4,20},{5,21},{6,22},{7,23},{8,24},{9,... | collective-permute-start | bytes 2359304 | tf_op jit(solution)/shard_map/mixing_back/ppermute | solution.py:85
  205.1 19.6 %collective-permute-start.40 = (bf16[1,4,3,64,512]{4,3,2,1,0:T(8,128)(2,1)S(1)}, bf16[1,4,3,64,512]{4,3,2,1,0:T(8,128)(2,1)S(1)}, u32[]{:S(2)}, u32[]{:S(2)}) collective-permute-start(bf16[1,4,3,64,512]{4,3,2,1,0:T(8,128)(2,1)S(1)} %get-tuple-element.164), channel_id=1, source_target_pairs={{0,2},{1,3},{2,0},{3,1},{4,6},{5,7},{6,4},{7,5},{8,10},{9,11},{10,... | collective-permute-start | bytes 2359304 | tf_op jit(solution)/shard_map/mixing_back/ppermute | solution.py:85
  209.8 13.7 %collective-permute-start.43 = (bf16[96,768]{1,0:T(8,128)(2,1)S(1)}, bf16[96,768]{1,0:T(8,128)(2,1)S(1)}, u32[]{:S(2)}, u32[]{:S(2)}) collective-permute-start(bf16[96,768]{1,0:T(8,128)(2,1)S(1)} %get-tuple-element.227), channel_id=1, source_target_pairs={{0,8},{1,9},{2,10},{3,11},{4,12},{5,13},{6,14},{7,15},{8,0},{9,1},... | collective-permute-start | bytes 442376 | tf_op jit(solution)/shard_map/weight_grads/ppermute | solution.py:85
  211.3 12.3 %collective-permute-start.44 = (bf16[96,768]{1,0:T(8,128)(2,1)S(1)}, bf16[96,768]{1,0:T(8,128)(2,1)S(1)}, u32[]{:S(2)}, u32[]{:S(2)}) collective-permute-start(bf16[96,768]{1,0:T(8,128)(2,1)S(1)} %get-tuple-element.225), channel_id=1, source_target_pairs={{0,12},{1,13},{2,14},{3,15},{4,8},{5,9},{6,10},{7,11},{8,4},{9,5},... | collective-permute-start | bytes 442376 | tf_op jit(solution)/shard_map/weight_grads/ppermute | solution.py:85
  224.9 21.0 %collective-permute-start.49 = (bf16[8,24,2304]{2,1,0:T(8,128)(2,1)S(1)}, bf16[8,24,2304]{2,1,0:T(8,128)(2,1)}, u32[]{:S(2)}, u32[]{:S(2)}) collective-permute-start(bf16[8,24,2304]{2,1,0:T(8,128)(2,1)S(1)} %copy-done.28), channel_id=1, source_target_pairs={{0,2},{1,3},{2,0},{3,1},{4,6},{5,7},{6,4},{7,5},{8,10},{9,11},{10,... | collective-permute-start | bytes 2654216 | tf_op jit(solution)/shard_map/weight_grads/ppermute | solution.py:85
  225.6 18.9 %collective-permute-start.48 = (bf16[8,24,1536]{2,1,0:T(8,128)(2,1)S(1)}, bf16[8,24,1536]{2,1,0:T(8,128)(2,1)S(1)}, u32[]{:S(2)}, u32[]{:S(2)}) collective-permute-start(bf16[8,24,1536]{2,1,0:T(8,128)(2,1)S(1)} %copy-done.30), channel_id=1, source_target_pairs={{0,16},{1,17},{2,18},{3,19},{4,20},{5,21},{6,22},{7,23},{8,24},{9,... | collective-permute-start | bytes 1769480 | tf_op jit(solution)/shard_map/weight_grads/ppermute | solution.py:85
  228.2 16.3 %collective-permute-start.46 = (bf16[3,64,512]{2,1,0:T(8,128)(2,1)S(1)}, bf16[3,64,512]{2,1,0:T(8,128)(2,1)S(1)}, u32[]{:S(2)}, u32[]{:S(2)}) collective-permute-start(bf16[3,64,512]{2,1,0:T(8,128)(2,1)S(1)} %get-tuple-element.222), channel_id=1, source_target_pairs={{0,8},{1,9},{2,10},{3,11},{4,12},{5,13},{6,14},{7,15},{8,0},{9,1},... | collective-permute-start | bytes 589832 | tf_op jit(solution)/shard_map/mixing_back/ppermute | solution.py:85
  229.9 14.6 %collective-permute-start.47 = (bf16[3,64,512]{2,1,0:T(8,128)(2,1)S(1)}, bf16[3,64,512]{2,1,0:T(8,128)(2,1)S(1)}, u32[]{:S(2)}, u32[]{:S(2)}) collective-permute-start(bf16[3,64,512]{2,1,0:T(8,128)(2,1)S(1)} %get-tuple-element.221), channel_id=1, source_target_pairs={{0,12},{1,13},{2,14},{3,15},{4,8},{5,9},{6,10},{7,11},{8,4},{9,5},... | collective-permute-start | bytes 589832 | tf_op jit(solution)/shard_map/mixing_back/ppermute | solution.py:85
  249.1 25.7 %all-to-all-start.3 = ((bf16[4,3,64,512]{3,2,1,0:T(8,128)(2,1)}), bf16[4,3,64,512]{3,2,1,0:T(8,128)(2,1)}, u32[]{:S(2)}, u32[]{:S(2)}) async-start(bf16[4,3,64,512]{3,2,1,0:T(8,128)(2,1)} %fusion), calls=%async_computation.3 | async-start | bytes 1572864 | tf_op jit(solution)/shard_map/mixing_back/all_to_all | solution.py:91
  255.6 19.1 %collective-permute-start.55 = (bf16[4,24,2304]{2,1,0:T(8,128)(2,1)}, bf16[4,24,2304]{2,1,0:T(8,128)(2,1)}, u32[]{:S(2)}, u32[]{:S(2)}) collective-permute-start(bf16[4,24,2304]{2,1,0:T(8,128)(2,1)} %add_convert_fusion.10), channel_id=1, source_target_pairs={{0,16},{1,17},{2,18},{3,19},{4,20},{5,21},{6,22},{7,23},{8,24},{9,... | collective-permute-start | bytes 1327112 | tf_op jit(solution)/shard_map/weight_grads/ppermute | solution.py:85
  257.4 17.3 %collective-permute-start.54 = (bf16[4,24,1536]{2,1,0:T(8,128)(2,1)}, bf16[4,24,1536]{2,1,0:T(8,128)(2,1)}, u32[]{:S(2)}, u32[]{:S(2)}) collective-permute-start(bf16[4,24,1536]{2,1,0:T(8,128)(2,1)} %add_convert_fusion.13), channel_id=1, source_target_pairs={{0,2},{1,3},{2,0},{3,1},{4,6},{5,7},{6,4},{7,5},{8,10},{9,11},{10,... | collective-permute-start | bytes 884744 | tf_op jit(solution)/shard_map/weight_grads/ppermute | solution.py:85
  258.1 16.6 %collective-permute-start.51 = (bf16[4,24,768]{2,1,0:T(8,128)(2,1)S(1)}, bf16[4,24,768]{2,1,0:T(8,128)(2,1)S(1)}, u32[]{:S(2)}, u32[]{:S(2)}) collective-permute-start(bf16[4,24,768]{2,1,0:T(8,128)(2,1)S(1)} %get-tuple-element.183), channel_id=1, source_target_pairs={{0,16},{1,17},{2,18},{3,19},{4,20},{5,21},{6,22},{7,23},{8,24},{9,... | collective-permute-start | bytes 442376 | tf_op jit(solution)/shard_map/value_grads/ppermute | solution.py:85
  259.2 15.6 %collective-permute-start.52 = (bf16[4,24,768]{2,1,0:T(8,128)(2,1)S(1)}, bf16[4,24,768]{2,1,0:T(8,128)(2,1)S(1)}, u32[]{:S(2)}, u32[]{:S(2)}) collective-permute-start(bf16[4,24,768]{2,1,0:T(8,128)(2,1)S(1)} %get-tuple-element.184), channel_id=1, source_target_pairs={{0,2},{1,3},{2,0},{3,1},{4,6},{5,7},{6,4},{7,5},{8,10},{9,11},{10,... | collective-permute-start | bytes 442376 | tf_op jit(solution)/shard_map/value_grads/ppermute | solution.py:85
  260.6 14.1 %collective-permute-start.53 = (bf16[4,24,768]{2,1,0:T(8,128)(2,1)S(1)}, bf16[4,24,768]{2,1,0:T(8,128)(2,1)S(1)}, u32[]{:S(2)}, u32[]{:S(2)}) collective-permute-start(bf16[4,24,768]{2,1,0:T(8,128)(2,1)S(1)} %get-tuple-element.185), channel_id=1, source_target_pairs={{0,18},{1,19},{2,16},{3,17},{4,22},{5,23},{6,20},{7,21},{8,26},{9,... | collective-permute-start | bytes 442376 | tf_op jit(solution)/shard_map/value_grads/ppermute | solution.py:85
  277.6 10.9 %collective-permute-start.56 = (bf16[24,4608]{1,0:T(8,128)(2,1)S(1)}, bf16[24,4608]{1,0:T(8,128)(2,1)S(1)}, u32[]{:S(2)}, u32[]{:S(2)}) collective-permute-start(bf16[24,4608]{1,0:T(8,128)(2,1)S(1)} %get-tuple-element.219), channel_id=1, source_target_pairs={{0,4},{1,5},{2,6},{3,7},{4,0},{5,1},{6,2},{7,3},{8,12},{9,13},{10,... | collective-permute-start | bytes 663560 | tf_op jit(solution)/shard_map/weight_grads/ppermute | solution.py:85
  279.3 18.7 %collective-permute-start.57 = (bf16[24,4608]{1,0:T(8,128)(2,1)S(1)}, bf16[24,4608]{1,0:T(8,128)(2,1)S(1)}, u32[]{:S(2)}, u32[]{:S(2)}) collective-permute-start(bf16[24,4608]{1,0:T(8,128)(2,1)S(1)} %get-tuple-element.218), channel_id=1, source_target_pairs={{0,8},{1,9},{2,10},{3,11},{4,12},{5,13},{6,14},{7,15},{8,0},{9,1},... | collective-permute-start | bytes 663560 | tf_op jit(solution)/shard_map/weight_grads/ppermute | solution.py:85
  281.7 16.4 %collective-permute-start.58 = (bf16[24,4608]{1,0:T(8,128)(2,1)S(1)}, bf16[24,4608]{1,0:T(8,128)(2,1)S(1)}, u32[]{:S(2)}, u32[]{:S(2)}) collective-permute-start(bf16[24,4608]{1,0:T(8,128)(2,1)S(1)} %get-tuple-element.217), channel_id=1, source_target_pairs={{0,12},{1,13},{2,14},{3,15},{4,8},{5,9},{6,10},{7,11},{8,4},{9,5},... | collective-permute-start | bytes 663560 | tf_op jit(solution)/shard_map/weight_grads/ppermute | solution.py:85
  (59 other events, 555.6 us)

commit v7 on v6

--- a/solution.py
+++ b/solution.py
@@ -29,7 +29,7 @@
     "add_all": 50000000000,
 }
 FIRST = 2
-SPLIT = 3
+SPLIT = 2
 MIB = 1 << 20
 
 

time: 302 us -> 302 us (level)
    unnamed x91 -> x97, local copies, waits for them, and re-layouts: 10.4 us -> 11.1 us
  transfers between devices with their start and end apart: 63 -> 63, of which waited for: 24 -> 26; matrix products, arithmetic and copies ran while one was open for 11% -> 10% of each run, Pallas kernels for 7% -> 6%
where the time goes in v7:
time: 302 us; the launch traced here: 300 us
  waiting for transfers between devices  117 us (39%)
  starting transfers between devices  76.8 us (25%)
  Pallas kernels  52.4 us (17%)
  other arithmetic  40.4 us (13%)
  local copies, waits for them, and re-layouts  11.7 us (4%)
    ppermute x59, waiting for transfers between devices, swap(): lax.ppermute(array, AXES, [(i, i ^ mask) for i in range(self.devices)])  99.6 us
    ppermute x59, starting transfers between devices, swap(): lax.ppermute(array, AXES, [(i, i ^ mask) for i in range(self.devices)])  58.1 us
    pallas_call x1, Pallas kernels, middle(): pl.pallas_call(functools.partial(middle_kernel, positions=lay.positions,...  30.3 us
    convert_element_type x13, other arithmetic, add_low(): return (left.astype(F32) + right.astype(F32)).astype(BF16)  20.7 us
    all_to_all x4, starting transfers between devices, across_z(): return lax.all_to_all(array, 'seq', 0, 0, axis_index_groups=lines)  18.7 us
    all_to_all x4, waiting for transfers between devices, across_z(): return lax.all_to_all(array, 'seq', 0, 0, axis_index_groups=lines)  17.9 us
    unnamed x97, local copies, waits for them, and re-layouts  11.1 us
  transfers between devices with their start and end apart: 63, of which 26 were waited for; matrix products, arithmetic and copies ran while one was open for 10% of the time, Pallas kernels for 6%

profile of v7, /device:TPU:0, one launch (start us, length us, event | category | flops | bytes accessed | tf_op | source)
XLA Modules:
  0.0 300.1 jit_solution(11789018180436494177)
XLA Ops:
  5.6 3.1 %collective-permute-start = (bf16[6,24,768]{2,1,0:T(8,128)(2,1)S(1)}, bf16[6,24,768]{2,1,0:T(8,128)(2,1)S(1)}, u32[]{:S(2)}, u32[]{:S(2)}) collective-permute-start(bf16[6,24,768]{2,1,0:T(8,128)(2,1)S(1)} %pad_maximum_fusion.11), channel_id=1, source_target_pairs={{0,4},{1,5},{2,6},{3,7},{4,0},{5,1},{6,2},{7,3},{8,12},{9,13},{10,... | collective-permute-start | bytes 663560 | tf_op jit(solution)/shard_map/round_one/ppermute | solution.py:85
  8.7 2.6 collective-permute-start.1
  12.8 1.9 mix_rows.1
  14.7 3.4 %collective-permute-done = bf16[6,24,768]{2,1,0:T(8,128)(2,1)S(1)} collective-permute-done((bf16[6,24,768]{2,1,0:T(8,128)(2,1)S(1)}, bf16[6,24,768]{2,1,0:T(8,128)(2,1)S(1)}, u32[]{:S(2)}, u32[]{:S(2)}) %collective-permute-start) | collective-permute-done | bytes 221216 | tf_op jit(solution)/shard_map/round_one/ppermute | solution.py:85
  18.1 9.3 %collective-permute-done.1 = bf16[6,24,768]{2,1,0:T(8,128)(2,1)S(1)} collective-permute-done((bf16[6,24,768]{2,1,0:T(8,128)(2,1)S(1)}, bf16[6,24,768]{2,1,0:T(8,128)(2,1)S(1)}, u32[]{:S(2)}, u32[]{:S(2)}) %collective-permute-start.1) | collective-permute-done | bytes 221216 | tf_op jit(solution)/shard_map/round_one/ppermute | solution.py:85
  32.0 2.4 collective-permute-start.5
  34.4 6.2 %all-to-all-start = ((bf16[4,3,32,1024]{3,2,1,0:T(8,128)(2,1)}), bf16[4,3,32,1024]{3,2,1,0:T(8,128)(2,1)S(1)}, u32[]{:S(2)}, u32[]{:S(2)}) async-start(bf16[4,3,32,1024]{3,2,1,0:T(8,128)(2,1)} %mix_rows.1), calls=%async_computation | async-start | bytes 1572864 | tf_op jit(solution)/shard_map/round_two/all_to_all | solution.py:91
  41.9 2.5 collective-permute-done.5
  45.3 2.1 pad_maximum_fusion.2
  50.3 7.8 %all-to-all-done.refs_4_ = bf16[4,3,32,1024]{3,2,1,0:T(8,128)(2,1)S(1)} async-done(((bf16[4,3,32,1024]{3,2,1,0:T(8,128)(2,1)}), bf16[4,3,32,1024]{3,2,1,0:T(8,128)(2,1)S(1)}, u32[]{:S(2)}, u32[]{:S(2)}) %all-to-all-start) | async-done | bytes 786464 | tf_op jit(solution)/shard_map/round_two/all_to_all | solution.py:91
  58.1 2.0 make_values.1
  61.7 1.9 collective-permute-start.9
  66.0 4.2 %collective-permute-done.13 = bf16[8,3,24,768]{3,2,1,0:T(8,128)(2,1)} collective-permute-done((bf16[8,3,24,768]{3,2,1,0:T(8,128)(2,1)}, bf16[8,3,24,768]{3,2,1,0:T(8,128)(2,1)}, u32[]{:S(2)}, u32[]{:S(2)}) %collective-permute-start.13) | collective-permute-done | bytes 884768 | tf_op jit(solution)/shard_map/round_two/ppermute | solution.py:85
  70.2 3.2 %collective-permute-done.10.refs_2_ = bf16[3,64,512]{2,1,0:T(8,128)(2,1)S(1)} collective-permute-done((bf16[3,64,512]{2,1,0:T(8,128)(2,1)S(1)}, bf16[3,64,512]{2,1,0:T(8,128)(2,1)S(1)}, u32[]{:S(2)}, u32[]{:S(2)}) %collective-permute-start.10) | collective-permute-done | bytes 196640 | tf_op jit(solution)/shard_map/round_three/ppermute | solution.py:85
  75.7 2.9 collective-permute-start.16
  81.1 2.7 pad_maximum_fusion.refs_2_
  83.8 2.2 pad_maximum_fusion.1.refs_0_
  86.0 6.5 %collective-permute-done.17.refs_2_ = bf16[96,768]{1,0:T(8,128)(2,1)S(1)} collective-permute-done((bf16[96,768]{1,0:T(8,128)(2,1)S(1)}, bf16[96,768]{1,0:T(8,128)(2,1)S(1)}, u32[]{:S(2)}, u32[]{:S(2)}) %collective-permute-start.17) | collective-permute-done | bytes 147488 | tf_op jit(solution)/shard_map/round_four/ppermute | solution.py:85
  95.2 3.3 %collective-permute-done.20.refs_3_ = bf16[4,3,64,512]{3,2,1,0:T(8,128)(2,1)S(1)} collective-permute-done((bf16[4,3,64,512]{3,2,1,0:T(8,128)(2,1)S(1)}, bf16[4,3,64,512]{3,2,1,0:T(8,128)(2,1)S(1)}, u32[]{:S(2)}, u32[]{:S(2)}) %collective-permute-start.20) | collective-permute-done | bytes 786464 | tf_op jit(solution)/shard_map/round_five/ppermute | solution.py:85
  98.4 2.7 mix_values.1
  107.9 4.5 %all-to-all-start.1 = ((bf16[4,3,64,512]{3,2,1,0:T(8,128)(2,1)}), bf16[4,3,64,512]{3,2,1,0:T(8,128)(2,1)S(1)}, u32[]{:S(2)}, u32[]{:S(2)}) async-start(bf16[4,3,64,512]{3,2,1,0:T(8,128)(2,1)} %get-tuple-element.133), calls=%async_computation.1 | async-start | bytes 1572864 | tf_op jit(solution)/shard_map/round_five/all_to_all | solution.py:91
  112.6 7.8 %collective-permute-done.28.refs_10_ = bf16[8,48,768]{2,1,0:T(8,128)(2,1)} collective-permute-done((bf16[8,48,768]{2,1,0:T(8,128)(2,1)S(1)}, bf16[8,48,768]{2,1,0:T(8,128)(2,1)}, u32[]{:S(2)}, u32[]{:S(2)}) %collective-permute-start.28) | collective-permute-done | bytes 589856 | tf_op jit(solution)/shard_map/round_five/ppermute | solution.py:85
  121.9 4.9 %prepare_weights.1.refs_3_.refs_4_ = bf16[768,3840]{1,0:T(8,128)(2,1)S(1)} custom-call(s32[8]{0:T(128)S(1)} %stack.44.me, bf16[16,2,24,768]{3,2,1,0:T(8,128)(2,1)} %pad_maximum_fusion.1.refs_0_, bf16[16,2,24,768]{3,2,1,0:T(8,128)(2,1)} %collective-permute-done.21.refs_1_, bf16[16,3,24,768]{3,2,1,0:T(8,128)(2,1)} %pad_maximum_fusion.refs_2_, ...), custom_call_target="tpu_custom_call" | custom-call | flops 120000004096 | bytes 1 | tf_op jit(solution)/shard_map/round_five/prepare_weights/pallas_call | solution.py:294
  126.8 2.5 copy-done.13
  130.9 2.2 all-to-all-done.1.refs_0_
  134.0 30.3 %middle.1 = (bf16[512,768]{1,0:T(8,128)(2,1)}, f32[512,768]{1,0:T(8,128)}, bf16[4,3,64,512]{3,2,1,0:T(8,128)(2,1)}, bf16[16,24,1536]{2,1,0:T(8,128)(2,1)}, bf16[...) custom-call(s32[8]{0:T(128)} %copy-done.4, ...), custom_call_target="tpu_custom_call" | custom-call | flops 49999998976 | bytes 1 | tf_op jit(solution)/shard_map/feed_forward/middle/pallas_call | solution.py:443
  165.4 3.7 %all-to-all-start.2 = ((bf16[4,3,64,512]{3,2,1,0:T(8,128)(2,1)}), bf16[4,3,64,512]{3,2,1,0:T(8,128)(2,1)S(1)}, u32[]{:S(2)}, u32[]{:S(2)}) async-start(bf16[4,3,64,512]{3,2,1,0:T(8,128)(2,1)} %get-tuple-element.146), calls=%async_computation.2 | async-start | bytes 1572864 | tf_op jit(solution)/shard_map/feed_forward/all_to_all | solution.py:91
  169.2 2.5 add_convert_fusion.3
  175.9 2.7 add_convert_fusion.2
  178.6 3.1 %add_convert_fusion = (bf16[8,24,2304]{2,1,0:T(8,128)(2,1)}, bf16[8,24,2304]{2,1,0:T(8,128)(2,1)}) fusion(bf16[16,24,2304]{2,1,0:T(8,128)(2,1)} %collective-permute-done.36, bf16[16,24,2304]{2,1,0:T(8,128)(2,1)S(1)} %copy-done.24), kind=kLoop, calls=%fused_computation.1 | loop fusion | flops 3538944 | bytes 5308416 | tf_op jit(solution)/shard_map/weight_grads/convert_element_type | solution.py:95
  181.7 7.8 %all-to-all-done.2.refs_0_ = bf16[4,3,64,512]{3,2,1,0:T(8,128)(2,1)S(1)} async-done(((bf16[4,3,64,512]{3,2,1,0:T(8,128)(2,1)}), bf16[4,3,64,512]{3,2,1,0:T(8,128)(2,1)S(1)}, u32[]{:S(2)}, u32[]{:S(2)}) %all-to-all-start.2) | async-done | bytes 786464 | tf_op jit(solution)/shard_map/feed_forward/all_to_all | solution.py:91
  194.3 4.8 %mix_back.1 = (bf16[2,4,3,64,512]{4,3,2,1,0:T(8,128)(2,1)S(1)}, bf16[2,4,3,64,512]{4,3,2,1,0:T(8,128)(2,1)S(1)}, bf16[2,4,3,64,512]{4,3,2,1,0:T(8,128)(2,1)S(1)}) custom-call(s32[8]{0:T(128)S(1)} %copy-done.5, bf16[4,3,64,512]{3,2,1,0:T(8,128)(2,1)S(1)} %all-to-all-done.2.refs_0_, bf16[3,256,1024]{2,1,0:T(8,128)(2,1)} %copy-done.1, ...), custom_call_target="tpu_custom_call" | custom-call | flops 768 | bytes 1 | tf_op jit(solution)/shard_map/mixing_back/mix_back/pallas_call | solution.py:521
  199.0 2.1 collective-permute-done.37
  202.2 2.4 collective-permute-done.39.refs_1_
  208.7 2.4 collective-permute-start.43
  212.3 3.6 %collective-permute-done.42 = bf16[96,768]{1,0:T(8,128)(2,1)S(1)} collective-permute-done((bf16[96,768]{1,0:T(8,128)(2,1)S(1)}, bf16[96,768]{1,0:T(8,128)(2,1)S(1)}, u32[]{:S(2)}, u32[]{:S(2)}) %collective-permute-start.42) | collective-permute-done | bytes 147488 | tf_op jit(solution)/shard_map/weight_grads/ppermute | solution.py:85
  215.9 6.8 %collective-permute-done.43 = bf16[96,768]{1,0:T(8,128)(2,1)S(1)} collective-permute-done((bf16[96,768]{1,0:T(8,128)(2,1)S(1)}, bf16[96,768]{1,0:T(8,128)(2,1)S(1)}, u32[]{:S(2)}, u32[]{:S(2)}) %collective-permute-start.43) | collective-permute-done | bytes 147488 | tf_op jit(solution)/shard_map/weight_grads/ppermute | solution.py:85
  222.7 1.9 collective-permute-done.40
  230.9 3.8 %collective-permute-done.45.refs_1_ = bf16[3,64,512]{2,1,0:T(8,128)(2,1)S(1)} collective-permute-done((bf16[3,64,512]{2,1,0:T(8,128)(2,1)S(1)}, bf16[3,64,512]{2,1,0:T(8,128)(2,1)S(1)}, u32[]{:S(2)}, u32[]{:S(2)}) %collective-permute-start.45) | collective-permute-done | bytes 196640 | tf_op jit(solution)/shard_map/mixing_back/ppermute | solution.py:85
  234.6 9.5 %collective-permute-done.46.refs_2_ = bf16[3,64,512]{2,1,0:T(8,128)(2,1)S(1)} collective-permute-done((bf16[3,64,512]{2,1,0:T(8,128)(2,1)S(1)}, bf16[3,64,512]{2,1,0:T(8,128)(2,1)S(1)}, u32[]{:S(2)}, u32[]{:S(2)}) %collective-permute-start.46) | collective-permute-done | bytes 196640 | tf_op jit(solution)/shard_map/mixing_back/ppermute | solution.py:85
  245.8 1.9 value_grads.1
  248.9 4.3 %all-to-all-start.3 = ((bf16[4,3,64,512]{3,2,1,0:T(8,128)(2,1)}), bf16[4,3,64,512]{3,2,1,0:T(8,128)(2,1)}, u32[]{:S(2)}, u32[]{:S(2)}) async-start(bf16[4,3,64,512]{3,2,1,0:T(8,128)(2,1)} %fusion), calls=%async_computation.3 | async-start | bytes 1572864 | tf_op jit(solution)/shard_map/mixing_back/all_to_all | solution.py:91
  253.5 2.0 add_convert_fusion.10
  263.3 11.3 %collective-permute-done.51.refs_1_ = bf16[4,24,768]{2,1,0:T(8,128)(2,1)S(1)} collective-permute-done((bf16[4,24,768]{2,1,0:T(8,128)(2,1)S(1)}, bf16[4,24,768]{2,1,0:T(8,128)(2,1)S(1)}, u32[]{:S(2)}, u32[]{:S(2)}) %collective-permute-start.51) | collective-permute-done | bytes 147488 | tf_op jit(solution)/shard_map/value_grads/ppermute | solution.py:85
  279.2 2.4 collective-permute-start.57
  281.9 2.2 make_tokens_grad.1
  284.1 2.5 bitcast_convert_fusion
  288.3 9.6 %collective-permute-done.57.refs_2_ = bf16[24,4608]{1,0:T(8,128)(2,1)S(1)} collective-permute-done((bf16[24,4608]{1,0:T(8,128)(2,1)S(1)}, bf16[24,4608]{1,0:T(8,128)(2,1)S(1)}, u32[]{:S(2)}, u32[]{:S(2)}) %collective-permute-start.57) | collective-permute-done | bytes 221216 | tf_op jit(solution)/shard_map/weight_grads/ppermute | solution.py:85
  (239 shorter events, 80.4 us)
Async XLA Ops:
  5.6 12.5 %collective-permute-start = (bf16[6,24,768]{2,1,0:T(8,128)(2,1)S(1)}, bf16[6,24,768]{2,1,0:T(8,128)(2,1)S(1)}, u32[]{:S(2)}, u32[]{:S(2)}) collective-permute-start(bf16[6,24,768]{2,1,0:T(8,128)(2,1)S(1)} %pad_maximum_fusion.11), channel_id=1, source_target_pairs={{0,4},{1,5},{2,6},{3,7},{4,0},{5,1},{6,2},{7,3},{8,12},{9,13},{10,... | collective-permute-start | bytes 663560 | tf_op jit(solution)/shard_map/round_one/ppermute | solution.py:85
  8.7 18.7 %collective-permute-start.1 = (bf16[6,24,768]{2,1,0:T(8,128)(2,1)S(1)}, bf16[6,24,768]{2,1,0:T(8,128)(2,1)S(1)}, u32[]{:S(2)}, u32[]{:S(2)}) collective-permute-start(bf16[6,24,768]{2,1,0:T(8,128)(2,1)S(1)} %pad_maximum_fusion.11), channel_id=1, source_target_pairs={{0,8},{1,9},{2,10},{3,11},{4,12},{5,13},{6,14},{7,15},{8,0},{9,1},... | collective-permute-start | bytes 663560 | tf_op jit(solution)/shard_map/round_one/ppermute | solution.py:85
  11.3 16.1 %collective-permute-start.2 = (bf16[6,24,768]{2,1,0:T(8,128)(2,1)S(1)}, bf16[6,24,768]{2,1,0:T(8,128)(2,1)S(1)}, u32[]{:S(2)}, u32[]{:S(2)}) collective-permute-start(bf16[6,24,768]{2,1,0:T(8,128)(2,1)S(1)} %pad_maximum_fusion.11), channel_id=1, source_target_pairs={{0,12},{1,13},{2,14},{3,15},{4,8},{5,9},{6,10},{7,11},{8,4},{9,5},... | collective-permute-start | bytes 663560 | tf_op jit(solution)/shard_map/round_one/ppermute | solution.py:85
  27.6 17.5 %collective-permute-start.7 = (bf16[4,3,24,768]{3,2,1,0:T(8,128)(2,1)S(1)}, bf16[4,3,24,768]{3,2,1,0:T(8,128)(2,1)}, u32[]{:S(2)}, u32[]{:S(2)}) collective-permute-start(bf16[4,3,24,768]{3,2,1,0:T(8,128)(2,1)S(1)} %pad_maximum_fusion.7), channel_id=1, source_target_pairs={{0,2},{1,3},{2,0},{3,1},{4,6},{5,7},{6,4},{7,5},{8,10},{9,11},{10,... | collective-permute-start | bytes 1327112 | tf_op jit(solution)/shard_map/round_two/ppermute | solution.py:85
  29.2 15.2 %collective-permute-start.6 = (bf16[4,2,24,768]{3,2,1,0:T(8,128)(2,1)S(1)}, bf16[4,2,24,768]{3,2,1,0:T(8,128)(2,1)S(1)}, u32[]{:S(2)}, u32[]{:S(2)}) collective-permute-start(bf16[4,2,24,768]{3,2,1,0:T(8,128)(2,1)S(1)} %pad_maximum_fusion.10), channel_id=1, source_target_pairs={{0,16},{1,17},{2,18},{3,19},{4,20},{5,21},{6,22},{7,23},{8,24},{9,... | collective-permute-start | bytes 884744 | tf_op jit(solution)/shard_map/round_two/ppermute | solution.py:85
  31.4 10.4 %collective-permute-start.4 = (bf16[4,24,768]{2,1,0:T(8,128)(2,1)S(1)}, bf16[4,24,768]{2,1,0:T(8,128)(2,1)S(1)}, u32[]{:S(2)}, u32[]{:S(2)}) collective-permute-start(bf16[4,24,768]{2,1,0:T(8,128)(2,1)S(1)} %pad_maximum_fusion.13), channel_id=1, source_target_pairs={{0,2},{1,3},{2,0},{3,1},{4,6},{5,7},{6,4},{7,5},{8,10},{9,11},{10,... | collective-permute-start | bytes 442376 | tf_op jit(solution)/shard_map/round_two/ppermute | solution.py:85
  32.0 12.4 %collective-permute-start.5 = (bf16[4,24,768]{2,1,0:T(8,128)(2,1)S(1)}, bf16[4,24,768]{2,1,0:T(8,128)(2,1)S(1)}, u32[]{:S(2)}, u32[]{:S(2)}) collective-permute-start(bf16[4,24,768]{2,1,0:T(8,128)(2,1)S(1)} %pad_maximum_fusion.13), channel_id=1, source_target_pairs={{0,18},{1,19},{2,16},{3,17},{4,22},{5,23},{6,20},{7,21},{8,26},{9,... | collective-permute-start | bytes 442376 | tf_op jit(solution)/shard_map/round_two/ppermute | solution.py:85
  34.4 23.7 %all-to-all-start = ((bf16[4,3,32,1024]{3,2,1,0:T(8,128)(2,1)}), bf16[4,3,32,1024]{3,2,1,0:T(8,128)(2,1)S(1)}, u32[]{:S(2)}, u32[]{:S(2)}) async-start(bf16[4,3,32,1024]{3,2,1,0:T(8,128)(2,1)} %mix_rows.1), calls=%async_computation | async-start | bytes 1572864 | tf_op jit(solution)/shard_map/round_two/all_to_all | solution.py:91
  47.4 22.8 %collective-permute-start.13 = (bf16[8,3,24,768]{3,2,1,0:T(8,128)(2,1)}, bf16[8,3,24,768]{3,2,1,0:T(8,128)(2,1)}, u32[]{:S(2)}, u32[]{:S(2)}) collective-permute-start(bf16[8,3,24,768]{3,2,1,0:T(8,128)(2,1)} %pad_maximum_fusion.2), channel_id=1, source_target_pairs={{0,16},{1,17},{2,18},{3,19},{4,20},{5,21},{6,22},{7,23},{8,24},{9,... | collective-permute-start | bytes 2654216 | tf_op jit(solution)/shard_map/round_two/ppermute | solution.py:85
  48.8 15.6 %collective-permute-start.12 = (bf16[8,2,24,768]{3,2,1,0:T(8,128)(2,1)}, bf16[8,2,24,768]{3,2,1,0:T(8,128)(2,1)}, u32[]{:S(2)}, u32[]{:S(2)}) collective-permute-start(bf16[8,2,24,768]{3,2,1,0:T(8,128)(2,1)} %pad_maximum_fusion.4), channel_id=1, source_target_pairs={{0,2},{1,3},{2,0},{3,1},{4,6},{5,7},{6,4},{7,5},{8,10},{9,11},{10,... | collective-permute-start | bytes 1769480 | tf_op jit(solution)/shard_map/round_two/ppermute | solution.py:85
  60.1 13.3 %collective-permute-start.10 = (bf16[3,64,512]{2,1,0:T(8,128)(2,1)S(1)}, bf16[3,64,512]{2,1,0:T(8,128)(2,1)S(1)}, u32[]{:S(2)}, u32[]{:S(2)}) collective-permute-start(bf16[3,64,512]{2,1,0:T(8,128)(2,1)S(1)} %get-tuple-element.122), channel_id=1, source_target_pairs={{0,8},{1,9},{2,10},{3,11},{4,12},{5,13},{6,14},{7,15},{8,0},{9,1},... | collective-permute-start | bytes 589832 | tf_op jit(solution)/shard_map/round_three/ppermute | solution.py:85
  60.2 13.3 %collective-permute-start.11 = (bf16[3,64,512]{2,1,0:T(8,128)(2,1)S(1)}, bf16[3,64,512]{2,1,0:T(8,128)(2,1)S(1)}, u32[]{:S(2)}, u32[]{:S(2)}) collective-permute-start(bf16[3,64,512]{2,1,0:T(8,128)(2,1)S(1)} %get-tuple-element.123), channel_id=1, source_target_pairs={{0,12},{1,13},{2,14},{3,15},{4,8},{5,9},{6,10},{7,11},{8,4},{9,5},... | collective-permute-start | bytes 589832 | tf_op jit(solution)/shard_map/round_three/ppermute | solution.py:85
  61.7 13.0 %collective-permute-start.9 = (bf16[3,64,512]{2,1,0:T(8,128)(2,1)S(1)}, bf16[3,64,512]{2,1,0:T(8,128)(2,1)S(1)}, u32[]{:S(2)}, u32[]{:S(2)}) collective-permute-start(bf16[3,64,512]{2,1,0:T(8,128)(2,1)S(1)} %get-tuple-element.121), channel_id=1, source_target_pairs={{0,4},{1,5},{2,6},{3,7},{4,0},{5,1},{6,2},{7,3},{8,12},{9,13},{10,... | collective-permute-start | bytes 589832 | tf_op jit(solution)/shard_map/round_three/ppermute | solution.py:85
  64.4 28.6 %collective-permute-start.15 = (bf16[4,3,32,1024]{3,2,1,0:T(8,128)(2,1)S(1)}, bf16[4,3,32,1024]{3,2,1,0:T(8,128)(2,1)S(1)}, u32[]{:S(2)}, u32[]{:S(2)}) collective-permute-start(bf16[4,3,32,1024]{3,2,1,0:T(8,128)(2,1)S(1)} %all-to-all-done.refs_4_), channel_id=1, source_target_pairs={{0,16},{1,17},{2,18},{3,19},{4,20},{5,21},{6,22},{7,23},{8,24},{9,... | collective-permute-start | bytes 2359304 | tf_op jit(solution)/shard_map/round_four/ppermute | solution.py:85
  74.9 18.2 %collective-permute-start.14 = (bf16[4,3,64,512]{3,2,1,0:T(8,128)(2,1)S(1)}, bf16[4,3,64,512]{3,2,1,0:T(8,128)(2,1)S(1)}, u32[]{:S(2)}, u32[]{:S(2)}) collective-permute-start(bf16[4,3,64,512]{3,2,1,0:T(8,128)(2,1)S(1)} %stack_all.2.refs_0_), channel_id=1, source_target_pairs={{0,2},{1,3},{2,0},{3,1},{4,6},{5,7},{6,4},{7,5},{8,10},{9,11},{10,... | collective-permute-start | bytes 2359304 | tf_op jit(solution)/shard_map/round_four/ppermute | solution.py:85
  78.6 13.9 %collective-permute-start.17 = (bf16[96,768]{1,0:T(8,128)(2,1)S(1)}, bf16[96,768]{1,0:T(8,128)(2,1)S(1)}, u32[]{:S(2)}, u32[]{:S(2)}) collective-permute-start(bf16[96,768]{1,0:T(8,128)(2,1)S(1)} %copy-done.9), channel_id=1, source_target_pairs={{0,8},{1,9},{2,10},{3,11},{4,12},{5,13},{6,14},{7,15},{8,0},{9,1},... | collective-permute-start | bytes 442376 | tf_op jit(solution)/shard_map/round_four/ppermute | solution.py:85
  79.6 12.9 %collective-permute-start.18 = (bf16[96,768]{1,0:T(8,128)(2,1)S(1)}, bf16[96,768]{1,0:T(8,128)(2,1)S(1)}, u32[]{:S(2)}, u32[]{:S(2)}) collective-permute-start(bf16[96,768]{1,0:T(8,128)(2,1)S(1)} %copy-done.9), channel_id=1, source_target_pairs={{0,12},{1,13},{2,14},{3,15},{4,8},{5,9},{6,10},{7,11},{8,4},{9,5},... | collective-permute-start | bytes 442376 | tf_op jit(solution)/shard_map/round_four/ppermute | solution.py:85
  92.5 29.4 %collective-permute-start.22 = (bf16[16,3,24,768]{3,2,1,0:T(8,128)(2,1)}, bf16[16,3,24,768]{3,2,1,0:T(8,128)(2,1)}, u32[]{:S(2)}, u32[]{:S(2)}) collective-permute-start(bf16[16,3,24,768]{3,2,1,0:T(8,128)(2,1)} %pad_maximum_fusion.refs_2_), channel_id=1, source_target_pairs={{0,1},{1,0},{2,3},{3,2},{4,5},{5,4},{6,7},{7,6},{8,9},{9,8},{10,11... | collective-permute-start | bytes 5308424 | tf_op jit(solution)/shard_map/round_five/ppermute | solution.py:85
  92.5 19.9 %collective-permute-start.21 = (bf16[16,2,24,768]{3,2,1,0:T(8,128)(2,1)}, bf16[16,2,24,768]{3,2,1,0:T(8,128)(2,1)}, u32[]{:S(2)}, u32[]{:S(2)}) collective-permute-start(bf16[16,2,24,768]{3,2,1,0:T(8,128)(2,1)} %pad_maximum_fusion.1.refs_0_), channel_id=1, source_target_pairs={{0,1},{1,0},{2,3},{3,2},{4,5},{5,4},{6,7},{7,6},{8,9},{9,8},{10,11... | collective-permute-start | bytes 3538952 | tf_op jit(solution)/shard_map/round_five/ppermute | solution.py:85
  93.2 10.8 %collective-permute-start.23 = (bf16[4,48,768]{2,1,0:T(8,128)(2,1)S(1)}, bf16[4,48,768]{2,1,0:T(8,128)(2,1)S(1)}, u32[]{:S(2)}, u32[]{:S(2)}) collective-permute-start(bf16[4,48,768]{2,1,0:T(8,128)(2,1)S(1)} %get-tuple-element.229), channel_id=1, source_target_pairs={{0,16},{1,17},{2,18},{3,19},{4,20},{5,21},{6,22},{7,23},{8,24},{9,... | collective-permute-start | bytes 884744 | tf_op jit(solution)/shard_map/round_five/ppermute | solution.py:85
  94.3 10.5 %collective-permute-start.24 = (bf16[4,48,768]{2,1,0:T(8,128)(2,1)S(1)}, bf16[4,48,768]{2,1,0:T(8,128)(2,1)S(1)}, u32[]{:S(2)}, u32[]{:S(2)}) collective-permute-start(bf16[4,48,768]{2,1,0:T(8,128)(2,1)S(1)} %get-tuple-element.228), channel_id=1, source_target_pairs={{0,2},{1,3},{2,0},{3,1},{4,6},{5,7},{6,4},{7,5},{8,10},{9,11},{10,... | collective-permute-start | bytes 884744 | tf_op jit(solution)/shard_map/round_five/ppermute | solution.py:85
  104.8 15.5 %collective-permute-start.28 = (bf16[8,48,768]{2,1,0:T(8,128)(2,1)S(1)}, bf16[8,48,768]{2,1,0:T(8,128)(2,1)}, u32[]{:S(2)}, u32[]{:S(2)}) collective-permute-start(bf16[8,48,768]{2,1,0:T(8,128)(2,1)S(1)} %pad_maximum_fusion.6.refs_9_), channel_id=1, source_target_pairs={{0,16},{1,17},{2,18},{3,19},{4,20},{5,21},{6,22},{7,23},{8,24},{9,... | collective-permute-start | bytes 1769480 | tf_op jit(solution)/shard_map/round_five/ppermute | solution.py:85
  106.7 15.2 %collective-permute-start.25 = (bf16[8,48,768]{2,1,0:T(8,128)(2,1)S(1)}, bf16[8,48,768]{2,1,0:T(8,128)(2,1)S(1)}, u32[]{:S(2)}, u32[]{:S(2)}) collective-permute-start(bf16[8,48,768]{2,1,0:T(8,128)(2,1)S(1)} %pad_maximum_fusion.5.refs_5_), channel_id=1, source_target_pairs={{0,2},{1,3},{2,0},{3,1},{4,6},{5,7},{6,4},{7,5},{8,10},{9,11},{10,... | collective-permute-start | bytes 1769480 | tf_op jit(solution)/shard_map/round_five/ppermute | solution.py:85
  107.9 21.4 %collective-permute-start.29 = (bf16[8,48,768]{2,1,0:T(8,128)(2,1)S(1)}, bf16[8,48,768]{2,1,0:T(8,128)(2,1)}, u32[]{:S(2)}, u32[]{:S(2)}) collective-permute-start(bf16[8,48,768]{2,1,0:T(8,128)(2,1)S(1)} %pad_maximum_fusion.6.refs_9_), channel_id=1, source_target_pairs={{0,1},{1,0},{2,3},{3,2},{4,5},{5,4},{6,7},{7,6},{8,9},{9,8},{10,11... | collective-permute-start | bytes 1769480 | tf_op jit(solution)/shard_map/round_five/ppermute | solution.py:85
  107.9 25.3 %all-to-all-start.1 = ((bf16[4,3,64,512]{3,2,1,0:T(8,128)(2,1)}), bf16[4,3,64,512]{3,2,1,0:T(8,128)(2,1)S(1)}, u32[]{:S(2)}, u32[]{:S(2)}) async-start(bf16[4,3,64,512]{3,2,1,0:T(8,128)(2,1)} %get-tuple-element.133), calls=%async_computation.1 | async-start | bytes 1572864 | tf_op jit(solution)/shard_map/round_five/all_to_all | solution.py:91
  112.4 16.9 %collective-permute-start.26 = (bf16[8,48,768]{2,1,0:T(8,128)(2,1)S(1)}, bf16[8,48,768]{2,1,0:T(8,128)(2,1)S(1)}, u32[]{:S(2)}, u32[]{:S(2)}) collective-permute-start(bf16[8,48,768]{2,1,0:T(8,128)(2,1)S(1)} %pad_maximum_fusion.5.refs_5_), channel_id=1, source_target_pairs={{0,1},{1,0},{2,3},{3,2},{4,5},{5,4},{6,7},{7,6},{8,9},{9,8},{10,11... | collective-permute-start | bytes 1769480 | tf_op jit(solution)/shard_map/round_five/ppermute | solution.py:85
  164.9 13.7 %collective-permute-start.36 = (bf16[16,24,2304]{2,1,0:T(8,128)(2,1)}, bf16[16,24,2304]{2,1,0:T(8,128)(2,1)}, u32[]{:S(2)}, u32[]{:S(2)}) collective-permute-start(bf16[16,24,2304]{2,1,0:T(8,128)(2,1)} %get-tuple-element.152), channel_id=1, source_target_pairs={{0,1},{1,0},{2,3},{3,2},{4,5},{5,4},{6,7},{7,6},{8,9},{9,8},{10,11... | collective-permute-start | bytes 5308424 | tf_op jit(solution)/shard_map/weight_grads/ppermute | solution.py:85
  165.0 10.8 %collective-permute-start.35 = (bf16[16,24,1536]{2,1,0:T(8,128)(2,1)}, bf16[16,24,1536]{2,1,0:T(8,128)(2,1)}, u32[]{:S(2)}, u32[]{:S(2)}) collective-permute-start(bf16[16,24,1536]{2,1,0:T(8,128)(2,1)} %get-tuple-element.150), channel_id=1, source_target_pairs={{0,1},{1,0},{2,3},{3,2},{4,5},{5,4},{6,7},{7,6},{8,9},{9,8},{10,11... | collective-permute-start | bytes 3538952 | tf_op jit(solution)/shard_map/weight_grads/ppermute | solution.py:85
  165.4 24.1 %all-to-all-start.2 = ((bf16[4,3,64,512]{3,2,1,0:T(8,128)(2,1)}), bf16[4,3,64,512]{3,2,1,0:T(8,128)(2,1)S(1)}, u32[]{:S(2)}, u32[]{:S(2)}) async-start(bf16[4,3,64,512]{3,2,1,0:T(8,128)(2,1)} %get-tuple-element.146), calls=%async_computation.2 | async-start | bytes 1572864 | tf_op jit(solution)/shard_map/feed_forward/all_to_all | solution.py:91
  171.6 17.9 %collective-permute-start.34 = (bf16[8,48,768]{2,1,0:T(8,128)(2,1)}, bf16[8,48,768]{2,1,0:T(8,128)(2,1)}, u32[]{:S(2)}, u32[]{:S(2)}) collective-permute-start(bf16[8,48,768]{2,1,0:T(8,128)(2,1)} %get-tuple-element.214), channel_id=1, source_target_pairs={{0,16},{1,17},{2,18},{3,19},{4,20},{5,21},{6,22},{7,23},{8,24},{9,... | collective-permute-start | bytes 1769480 | tf_op jit(solution)/shard_map/weight_grads/ppermute | solution.py:85
  174.3 15.2 %collective-permute-start.32 = (bf16[8,48,768]{2,1,0:T(8,128)(2,1)S(1)}, bf16[8,48,768]{2,1,0:T(8,128)(2,1)}, u32[]{:S(2)}, u32[]{:S(2)}) collective-permute-start(bf16[8,48,768]{2,1,0:T(8,128)(2,1)S(1)} %get-tuple-element.216), channel_id=1, source_target_pairs={{0,2},{1,3},{2,0},{3,1},{4,6},{5,7},{6,4},{7,5},{8,10},{9,11},{10,... | collective-permute-start | bytes 1769480 | tf_op jit(solution)/shard_map/weight_grads/ppermute | solution.py:85
  201.2 21.4 %collective-permute-start.41 = (bf16[4,3,64,512]{3,2,1,0:T(8,128)(2,1)S(1)}, bf16[4,3,64,512]{3,2,1,0:T(8,128)(2,1)S(1)}, u32[]{:S(2)}, u32[]{:S(2)}) collective-permute-start(bf16[4,3,64,512]{3,2,1,0:T(8,128)(2,1)S(1)} %slice_bitcast_fusion), channel_id=1, source_target_pairs={{0,16},{1,17},{2,18},{3,19},{4,20},{5,21},{6,22},{7,23},{8,24},{9,... | collective-permute-start | bytes 2359304 | tf_op jit(solution)/shard_map/mixing_back/ppermute | solution.py:85
  204.9 19.6 %collective-permute-start.40 = (bf16[1,4,3,64,512]{4,3,2,1,0:T(8,128)(2,1)S(1)}, bf16[1,4,3,64,512]{4,3,2,1,0:T(8,128)(2,1)S(1)}, u32[]{:S(2)}, u32[]{:S(2)}) collective-permute-start(bf16[1,4,3,64,512]{4,3,2,1,0:T(8,128)(2,1)S(1)} %get-tuple-element.164), channel_id=1, source_target_pairs={{0,2},{1,3},{2,0},{3,1},{4,6},{5,7},{6,4},{7,5},{8,10},{9,11},{10,... | collective-permute-start | bytes 2359304 | tf_op jit(solution)/shard_map/mixing_back/ppermute | solution.py:85
  208.7 14.0 %collective-permute-start.43 = (bf16[96,768]{1,0:T(8,128)(2,1)S(1)}, bf16[96,768]{1,0:T(8,128)(2,1)S(1)}, u32[]{:S(2)}, u32[]{:S(2)}) collective-permute-start(bf16[96,768]{1,0:T(8,128)(2,1)S(1)} %get-tuple-element.227), channel_id=1, source_target_pairs={{0,8},{1,9},{2,10},{3,11},{4,12},{5,13},{6,14},{7,15},{8,0},{9,1},... | collective-permute-start | bytes 442376 | tf_op jit(solution)/shard_map/weight_grads/ppermute | solution.py:85
  211.0 11.6 %collective-permute-start.44 = (bf16[96,768]{1,0:T(8,128)(2,1)S(1)}, bf16[96,768]{1,0:T(8,128)(2,1)S(1)}, u32[]{:S(2)}, u32[]{:S(2)}) collective-permute-start(bf16[96,768]{1,0:T(8,128)(2,1)S(1)} %get-tuple-element.225), channel_id=1, source_target_pairs={{0,12},{1,13},{2,14},{3,15},{4,8},{5,9},{6,10},{7,11},{8,4},{9,5},... | collective-permute-start | bytes 442376 | tf_op jit(solution)/shard_map/weight_grads/ppermute | solution.py:85
  224.8 21.0 %collective-permute-start.49 = (bf16[8,24,2304]{2,1,0:T(8,128)(2,1)S(1)}, bf16[8,24,2304]{2,1,0:T(8,128)(2,1)}, u32[]{:S(2)}, u32[]{:S(2)}) collective-permute-start(bf16[8,24,2304]{2,1,0:T(8,128)(2,1)S(1)} %copy-done.31), channel_id=1, source_target_pairs={{0,2},{1,3},{2,0},{3,1},{4,6},{5,7},{6,4},{7,5},{8,10},{9,11},{10,... | collective-permute-start | bytes 2654216 | tf_op jit(solution)/shard_map/weight_grads/ppermute | solution.py:85
  225.4 18.8 %collective-permute-start.48 = (bf16[8,24,1536]{2,1,0:T(8,128)(2,1)S(1)}, bf16[8,24,1536]{2,1,0:T(8,128)(2,1)S(1)}, u32[]{:S(2)}, u32[]{:S(2)}) collective-permute-start(bf16[8,24,1536]{2,1,0:T(8,128)(2,1)S(1)} %copy-done.33), channel_id=1, source_target_pairs={{0,16},{1,17},{2,18},{3,19},{4,20},{5,21},{6,22},{7,23},{8,24},{9,... | collective-permute-start | bytes 1769480 | tf_op jit(solution)/shard_map/weight_grads/ppermute | solution.py:85
  228.0 16.2 %collective-permute-start.46 = (bf16[3,64,512]{2,1,0:T(8,128)(2,1)S(1)}, bf16[3,64,512]{2,1,0:T(8,128)(2,1)S(1)}, u32[]{:S(2)}, u32[]{:S(2)}) collective-permute-start(bf16[3,64,512]{2,1,0:T(8,128)(2,1)S(1)} %get-tuple-element.222), channel_id=1, source_target_pairs={{0,8},{1,9},{2,10},{3,11},{4,12},{5,13},{6,14},{7,15},{8,0},{9,1},... | collective-permute-start | bytes 589832 | tf_op jit(solution)/shard_map/mixing_back/ppermute | solution.py:85
  229.7 14.5 %collective-permute-start.47 = (bf16[3,64,512]{2,1,0:T(8,128)(2,1)S(1)}, bf16[3,64,512]{2,1,0:T(8,128)(2,1)S(1)}, u32[]{:S(2)}, u32[]{:S(2)}) collective-permute-start(bf16[3,64,512]{2,1,0:T(8,128)(2,1)S(1)} %get-tuple-element.221), channel_id=1, source_target_pairs={{0,12},{1,13},{2,14},{3,15},{4,8},{5,9},{6,10},{7,11},{8,4},{9,5},... | collective-permute-start | bytes 589832 | tf_op jit(solution)/shard_map/mixing_back/ppermute | solution.py:85
  248.9 25.7 %all-to-all-start.3 = ((bf16[4,3,64,512]{3,2,1,0:T(8,128)(2,1)}), bf16[4,3,64,512]{3,2,1,0:T(8,128)(2,1)}, u32[]{:S(2)}, u32[]{:S(2)}) async-start(bf16[4,3,64,512]{3,2,1,0:T(8,128)(2,1)} %fusion), calls=%async_computation.3 | async-start | bytes 1572864 | tf_op jit(solution)/shard_map/mixing_back/all_to_all | solution.py:91
  255.5 19.1 %collective-permute-start.55 = (bf16[4,24,2304]{2,1,0:T(8,128)(2,1)}, bf16[4,24,2304]{2,1,0:T(8,128)(2,1)}, u32[]{:S(2)}, u32[]{:S(2)}) collective-permute-start(bf16[4,24,2304]{2,1,0:T(8,128)(2,1)} %add_convert_fusion.10), channel_id=1, source_target_pairs={{0,16},{1,17},{2,18},{3,19},{4,20},{5,21},{6,22},{7,23},{8,24},{9,... | collective-permute-start | bytes 1327112 | tf_op jit(solution)/shard_map/weight_grads/ppermute | solution.py:85
  257.2 17.4 %collective-permute-start.54 = (bf16[4,24,1536]{2,1,0:T(8,128)(2,1)}, bf16[4,24,1536]{2,1,0:T(8,128)(2,1)}, u32[]{:S(2)}, u32[]{:S(2)}) collective-permute-start(bf16[4,24,1536]{2,1,0:T(8,128)(2,1)} %add_convert_fusion.13), channel_id=1, source_target_pairs={{0,2},{1,3},{2,0},{3,1},{4,6},{5,7},{6,4},{7,5},{8,10},{9,11},{10,... | collective-permute-start | bytes 884744 | tf_op jit(solution)/shard_map/weight_grads/ppermute | solution.py:85
  257.9 16.7 %collective-permute-start.51 = (bf16[4,24,768]{2,1,0:T(8,128)(2,1)S(1)}, bf16[4,24,768]{2,1,0:T(8,128)(2,1)S(1)}, u32[]{:S(2)}, u32[]{:S(2)}) collective-permute-start(bf16[4,24,768]{2,1,0:T(8,128)(2,1)S(1)} %get-tuple-element.183), channel_id=1, source_target_pairs={{0,16},{1,17},{2,18},{3,19},{4,20},{5,21},{6,22},{7,23},{8,24},{9,... | collective-permute-start | bytes 442376 | tf_op jit(solution)/shard_map/value_grads/ppermute | solution.py:85
  259.0 15.6 %collective-permute-start.52 = (bf16[4,24,768]{2,1,0:T(8,128)(2,1)S(1)}, bf16[4,24,768]{2,1,0:T(8,128)(2,1)S(1)}, u32[]{:S(2)}, u32[]{:S(2)}) collective-permute-start(bf16[4,24,768]{2,1,0:T(8,128)(2,1)S(1)} %get-tuple-element.184), channel_id=1, source_target_pairs={{0,2},{1,3},{2,0},{3,1},{4,6},{5,7},{6,4},{7,5},{8,10},{9,11},{10,... | collective-permute-start | bytes 442376 | tf_op jit(solution)/shard_map/value_grads/ppermute | solution.py:85
  260.5 14.1 %collective-permute-start.53 = (bf16[4,24,768]{2,1,0:T(8,128)(2,1)S(1)}, bf16[4,24,768]{2,1,0:T(8,128)(2,1)S(1)}, u32[]{:S(2)}, u32[]{:S(2)}) collective-permute-start(bf16[4,24,768]{2,1,0:T(8,128)(2,1)S(1)} %get-tuple-element.185), channel_id=1, source_target_pairs={{0,18},{1,19},{2,16},{3,17},{4,22},{5,23},{6,20},{7,21},{8,26},{9,... | collective-permute-start | bytes 442376 | tf_op jit(solution)/shard_map/value_grads/ppermute | solution.py:85
  277.4 10.9 %collective-permute-start.56 = (bf16[24,4608]{1,0:T(8,128)(2,1)S(1)}, bf16[24,4608]{1,0:T(8,128)(2,1)S(1)}, u32[]{:S(2)}, u32[]{:S(2)}) collective-permute-start(bf16[24,4608]{1,0:T(8,128)(2,1)S(1)} %get-tuple-element.219), channel_id=1, source_target_pairs={{0,4},{1,5},{2,6},{3,7},{4,0},{5,1},{6,2},{7,3},{8,12},{9,13},{10,... | collective-permute-start | bytes 663560 | tf_op jit(solution)/shard_map/weight_grads/ppermute | solution.py:85
  279.2 18.7 %collective-permute-start.57 = (bf16[24,4608]{1,0:T(8,128)(2,1)S(1)}, bf16[24,4608]{1,0:T(8,128)(2,1)S(1)}, u32[]{:S(2)}, u32[]{:S(2)}) collective-permute-start(bf16[24,4608]{1,0:T(8,128)(2,1)S(1)} %get-tuple-element.218), channel_id=1, source_target_pairs={{0,8},{1,9},{2,10},{3,11},{4,12},{5,13},{6,14},{7,15},{8,0},{9,1},... | collective-permute-start | bytes 663560 | tf_op jit(solution)/shard_map/weight_grads/ppermute | solution.py:85
  281.5 16.4 %collective-permute-start.58 = (bf16[24,4608]{1,0:T(8,128)(2,1)S(1)}, bf16[24,4608]{1,0:T(8,128)(2,1)S(1)}, u32[]{:S(2)}, u32[]{:S(2)}) collective-permute-start(bf16[24,4608]{1,0:T(8,128)(2,1)S(1)} %get-tuple-element.217), channel_id=1, source_target_pairs={{0,12},{1,13},{2,14},{3,15},{4,8},{5,9},{6,10},{7,11},{8,4},{9,5},... | collective-permute-start | bytes 663560 | tf_op jit(solution)/shard_map/weight_grads/ppermute | solution.py:85
  (62 other events, 566.9 us)
